TPU v7x, 32 devices: a whole 2x2x4 slice. The times are simulated.
32 devices in a mesh: rep: 2 (over x), pg: 16 (over z, y, core).
Axes of the slice: x: 2, y: 2, z: 4, core: 2. Of those that a mesh axis runs over, the one named last changes fastest.
Arguments:
- queries: bfloat16 [32, 128, 4096], P(('rep', 'pg')), parts along dimension 0, may hold values from -6 to 6
- block_kv: bfloat16 [32, 128, 1024], P(('rep', 'pg')), parts along dimension 0, may hold values from -6 to 6
- pool_kv: bfloat16 [32, 16, 32, 1024], P(('rep', 'pg')), parts along dimension 0, may hold values from -6 to 6
- prefix_len: int32 [32], P('rep'), parts along dimension 0, may hold values from 0 to 512, as said below
- assignment: int32 [32], P('rep'), parts along dimension 0, may hold values from 0 to 15, each once
- stripe_map: int32 [32, 16], P('rep'), parts along dimension 0, may hold values from 0 to 15, each once within a row
- owner_map: int32 [32, 16], P('rep'), parts along dimension 0, may hold values from 0 to 15, each once within a row
Outputs:
- attended: bfloat16 [32, 128, 4096], P(('rep', 'pg')), parts along dimension 0
- decode_kv: bfloat16 [32, 16, 8, 1024], P(('rep', 'pg')), parts along dimension 0
There are 2 independent parts, one for each index of `rep`. A program takes and returns all parts, laid end to end along the dimension named above; each array names one. Nothing has to cross between parts.
Inputs may be any that keep to these rules, and one draw needn't show every extreme that they name: `prefix_len`: some request has exactly 512. `assignment`: each group computes a different request. `stripe_map`: each row names every device once. `owner_map`: each row names every device once.
All inputs are finite; a program needn't handle non-finite values.
Results may differ from a plain program's by a relative error of at most 0.0079.
Values may be sent and summed in bfloat16 or wider, within the bound.
No kernel may reach another device: no remote copies, remote signals or barrier semaphores. Data moves between devices by JAX's collectives and lax.ppermute only.
A program may use at most 64 MiB of HBM per device.

v0:
```python
import functools
import math

import jax
import jax.numpy as jnp
import numpy as np
from jax import lax
from jax.experimental import pallas as pl
from jax.experimental.pallas import tpu as pltpu
from jax.sharding import PartitionSpec as P

Q_HEADS = 32
KV_HEADS = 4
HEAD_DIM = 128
PER_KV = Q_HEADS // KV_HEADS
KV_WIDTH = KV_HEADS * HEAD_DIM
WIDTH = 2 * KV_WIDTH

ROPE_BASE = 1000000.0
MASKED = -1e30
SCALE = HEAD_DIM ** -0.5 / math.log(2.0)
CHUNK = 256
LATE = 4
LATE_CHUNK = 256
AHEAD = 4

SMEM = pl.BlockSpec(memory_space=pltpu.SMEM)
VMEM = pl.BlockSpec(memory_space=pltpu.VMEM)
ANY = pl.BlockSpec(memory_space=pl.ANY)


def params(mib):
    return pltpu.CompilerParams(vmem_limit_bytes=mib * 1024 * 1024)


def column(head):
    return slice(head * HEAD_DIM, (head + 1) * HEAD_DIM)


def order_of(groups):
    half = groups // 2
    far, near = list(range(half, 2 * half)), list(range(half - 1, 0, -1))
    order = [(far if kind == "f" else near).pop(0) for kind in "fffnfnfnfnnffnn"]
    order.insert(groups - LATE - 1, 0)
    return order


def rotation_tables(rows):
    half = HEAD_DIM // 2
    freqs = np.tile(ROPE_BASE ** (-np.arange(half, dtype=np.float64) / half), 2)
    angles = np.arange(rows, dtype=np.float64)[:, None] * freqs[None, :]
    parts = [np.cos(angles), np.sin(angles), np.tile(freqs, (8, 1))]
    return jnp.asarray(np.concatenate(parts, axis=0).astype(np.float32))


def rotation(table_ref, length):
    rows = (table_ref.shape[0] - 8) // 2
    start = length.astype(jnp.float32) * table_ref[2 * rows : 2 * rows + 8, :]
    cos_start, sin_start = jnp.cos(start)[0:1], jnp.sin(start)[0:1]
    cos_row, sin_row = table_ref[0:rows, :], table_ref[rows : 2 * rows, :]
    lane = lax.broadcasted_iota(jnp.int32, (1, HEAD_DIM), 1)
    sign = jnp.where(lane < HEAD_DIM // 2, -1.0, 1.0)
    cosine = cos_row * cos_start - sin_row * sin_start
    return cosine, sin_row * (cos_start * sign) + cos_row * (sin_start * sign)


def turn(x, cosine, sine):
    x = x.astype(jnp.float32)
    return (x * cosine + pltpu.roll(x, HEAD_DIM // 2, 1) * sine).astype(jnp.bfloat16)


def info_rows(new_count):
    sizes = [("cos", new_count), ("sin", new_count), ("bias", 8), ("scalars", 8), ("new", 2 * KV_HEADS * new_count)]
    at, rows = 0, {}
    for name, size in sizes:
        rows[name] = at
        at += size
    return rows, at


def fresh_rows(info_ref, base, residue, new_count, count, quarter, lanes):
    groups = new_count // count
    stack = [
        info_ref[pl.ds(base + (head + lanes) * new_count + residue, count, stride=groups), :]
        for head in range(0, 2 * KV_HEADS, quarter)
    ]
    return jnp.concatenate(stack, axis=0)


def front_kernel(
    order, me_ref, assign_any, length_any, owner_any, stripe_any, block_any, table_any, pool_any, *refs
):
    groups, slots, width = pool_any.shape
    send_refs, info_any, refs = refs[:AHEAD], refs[AHEAD], refs[AHEAD + 1 :]
    (assign_ref, length_ref, owner_ref, stripe_ref, residue_ref, block_ref, table_ref, pack_ref, info_ref,
     small_sems, pool_sems, send_sems, info_sems) = refs
    new_count = block_any.shape[0]
    count = new_count // groups
    quarter = width * count // slots // HEAD_DIM
    at, rows = info_rows(new_count)
    pairs = [
        (assign_any, assign_ref), (length_any, length_ref), (owner_any, owner_ref), (stripe_any, stripe_ref),
        (block_any, block_ref), (table_any, table_ref),
    ]
    smalls = [pltpu.make_async_copy(*pair, small_sems.at[i]) for i, pair in enumerate(pairs)]
    for copy in smalls:
        copy.start()
    me = me_ref[0]
    smalls[0].wait()
    pool_copies = [
        pltpu.make_async_copy(
            pool_any.at[assign_ref[me ^ order[p]]], pack_ref.at[p, :, pl.ds(0, width)], pool_sems.at[p]
        )
        for p in range(AHEAD)
    ]
    for copy in pool_copies:
        copy.start()
    for copy in smalls[1:]:
        copy.wait()
    request = assign_ref[me]
    length = length_ref[request]
    for residue in range(groups):
        residue_ref[owner_ref[request, residue]] = residue
    cosine, sine = rotation(table_ref, length)
    for head in range(KV_HEADS):
        low = at["new"] + head * new_count
        info_ref[low : low + new_count] = turn(block_ref[:, column(head)], cosine, sine).astype(jnp.float32)
        low += KV_HEADS * new_count
        info_ref[low : low + new_count] = block_ref[:, column(KV_HEADS + head)].astype(jnp.float32)

    def info_copy(part, low, high):
        part_rows = pl.ds(low, high - low)
        return pltpu.make_async_copy(info_ref.at[part_rows], info_any.at[part_rows], info_sems.at[part])

    info_copy(0, at["new"], rows).start()
    sends = []
    for p in range(AHEAD):
        for lanes in range(quarter):
            pack_ref[p, :, width + lanes * HEAD_DIM : width + (lanes + 1) * HEAD_DIM] = fresh_rows(
                info_ref, at["new"], residue_ref[me ^ order[p]], new_count, count, quarter, lanes
            ).astype(jnp.bfloat16)
        pool_copies[p].wait()
        sends.append(pltpu.make_async_copy(pack_ref.at[p], send_refs[p], send_sems.at[p]))
        sends[-1].start()
    info_ref[at["cos"] : at["cos"] + new_count] = cosine
    info_ref[at["sin"] : at["sin"] + new_count] = sine
    per_row = HEAD_DIM // slots
    row = lax.broadcasted_iota(jnp.int32, (8, HEAD_DIM), 0)
    lane = lax.broadcasted_iota(jnp.int32, (8, HEAD_DIM), 1)
    piece, slot = row * per_row + lane // slots, lane % slots
    holder, requests, residues = jnp.zeros_like(lane), jnp.zeros_like(lane), jnp.zeros_like(lane)
    for p in range(groups):
        other = me ^ order[p]
        holder = jnp.where(piece == p, other, holder)
        requests = jnp.where(lane == p, assign_ref[other], requests)
        residues = jnp.where(lane == p, residue_ref[other], residues)
    bias = jnp.full((8, HEAD_DIM), MASKED, jnp.float32)
    for residue in range(groups):
        live = (holder == stripe_ref[request, residue]) & (slot * groups + residue < length)
        bias = jnp.where(live, 0.0, bias)
    info_ref[at["bias"] : at["bias"] + 8] = bias
    scalars = jnp.where(row == 0, requests, residues)
    info_ref[at["scalars"] : at["scalars"] + 8] = scalars.astype(jnp.float32)
    info_copy(1, 0, at["new"]).start()
    for copy in sends:
        copy.wait()
    info_copy(0, at["new"], rows).wait()
    info_copy(1, 0, at["new"]).wait()


def front(order, me, assignment, prefix_len, owner_map, stripe_map, block_kv, table, pool):
    groups, slots, width = pool.shape
    new_count = block_kv.shape[0]
    count = new_count // groups
    block = jax.ShapeDtypeStruct((slots, width + width * count // slots), jnp.bfloat16)
    info = jax.ShapeDtypeStruct((info_rows(new_count)[1], HEAD_DIM), jnp.float32)
    *blocks, info = pl.pallas_call(
        functools.partial(front_kernel, order),
        out_shape=[block] * AHEAD + [info],
        in_specs=[SMEM] + [ANY] * 7,
        out_specs=[ANY] * (AHEAD + 1),
        scratch_shapes=[
            pltpu.SMEM(assignment.shape, jnp.int32),
            pltpu.SMEM(prefix_len.shape, jnp.int32),
            pltpu.SMEM(owner_map.shape, jnp.int32),
            pltpu.SMEM(stripe_map.shape, jnp.int32),
            pltpu.SMEM(assignment.shape, jnp.int32),
            pltpu.VMEM(block_kv.shape, jnp.bfloat16),
            pltpu.VMEM(table.shape, jnp.float32),
            pltpu.VMEM((AHEAD,) + block.shape, jnp.bfloat16),
            pltpu.VMEM(info.shape, jnp.float32),
            pltpu.SemaphoreType.DMA((6,)),
            pltpu.SemaphoreType.DMA((AHEAD,)),
            pltpu.SemaphoreType.DMA((AHEAD,)),
            pltpu.SemaphoreType.DMA((2,)),
        ],
        compiler_params=params(60),
        name="front",
    )(me, assignment, prefix_len, owner_map, stripe_map, block_kv, table, pool)
    return blocks, info


def query_kernel(order, info_ref, q_ref, pool_ref, *refs):
    groups, slots, width = pool_ref.shape
    sent = groups - 1 - AHEAD
    send_refs, refs = refs[:sent], refs[sent:]
    rot_ref, own_ref, fresh_ref, bias_ref, request_ref, scalar_ref, scalar_sem = refs
    new_count = q_ref.shape[0]
    count = new_count // groups
    quarter = fresh_ref.shape[1] // HEAD_DIM
    at, _ = info_rows(new_count)
    scalar_copy = pltpu.make_async_copy(info_ref.at[pl.ds(at["scalars"], 8)], scalar_ref, scalar_sem)
    scalar_copy.start()
    cosine = info_ref[at["cos"] : at["cos"] + new_count]
    sine = info_ref[at["sin"] : at["sin"] + new_count]
    for row in range(bias_ref.shape[1] // HEAD_DIM):
        line = info_ref[at["bias"] + row : at["bias"] + row + 1]
        bias_ref[:, column(row)] = jnp.broadcast_to(line, (8, HEAD_DIM))
    request_ref[...] = info_ref[at["scalars"] : at["scalars"] + 8].astype(jnp.int32)
    for head in range(2 * KV_HEADS):
        rows = at["new"] + head * new_count
        own_ref[head, slots : slots + new_count] = info_ref[rows : rows + new_count].astype(jnp.bfloat16)
    for head in range(Q_HEADS):
        rows = slice((head % PER_KV) * new_count, (head % PER_KV + 1) * new_count)
        rot_ref[head // PER_KV, rows, :] = turn(q_ref[:, column(head)], cosine, sine)
    scalar_copy.wait()
    sends = list(send_refs)
    for p in range(AHEAD, groups):
        request = scalar_ref[0, p].astype(jnp.int32)
        residue = scalar_ref[1, p].astype(jnp.int32)
        if order[p] == 0:
            target, base = fresh_ref, 0
            for head in range(2 * KV_HEADS):
                own_ref[head, 0:slots] = pool_ref[request, :, column(head)]
        else:
            target, base = sends.pop(0), width
            target[:, 0:width] = pool_ref[request]
        for lanes in range(quarter):
            target[:, base + lanes * HEAD_DIM : base + (lanes + 1) * HEAD_DIM] = fresh_rows(
                info_ref, at["new"], residue, new_count, count, quarter, lanes
            ).astype(jnp.bfloat16)


def rotate_queries(order, info, queries, pool):
    groups, slots, width = pool.shape
    new_count = queries.shape[0]
    spare = width * (new_count // groups) // slots
    sent = groups - 1 - AHEAD
    outs = pl.pallas_call(
        functools.partial(query_kernel, order),
        out_shape=[jax.ShapeDtypeStruct((slots, width + spare), jnp.bfloat16)] * sent
        + [
            jax.ShapeDtypeStruct((KV_HEADS, PER_KV * new_count, HEAD_DIM), jnp.bfloat16),
            jax.ShapeDtypeStruct((2 * KV_HEADS, slots + new_count, HEAD_DIM), jnp.bfloat16),
            jax.ShapeDtypeStruct((slots, spare), jnp.bfloat16),
            jax.ShapeDtypeStruct((8, groups * slots), jnp.float32),
            jax.ShapeDtypeStruct((8, HEAD_DIM), jnp.int32),
        ],
        in_specs=[VMEM] * 3,
        out_specs=[VMEM] * (sent + 5),
        scratch_shapes=[pltpu.SMEM((8, HEAD_DIM), jnp.float32), pltpu.SemaphoreType.DMA],
        compiler_params=params(32),
        name="rotate_queries",
    )(info, queries, pool)
    return outs[:sent], outs[sent:]


def attend_kernel(pieces, first, early, final, unpack, size, *refs):
    rot_ref, bias_ref, refs = refs[0], refs[1], refs[2:]
    if early:
        (sum_in, total_in, high_in), refs = refs[:3], refs[3:]
    else:
        own_ref, refs = refs[0], refs[1:]
    got_refs, refs = refs[:pieces], refs[pieces:]
    fresh_refs = [got.at[:, pl.ds(WIDTH, got.shape[1] - WIDTH)] for got in got_refs] if unpack else []
    if unpack:
        request_vmem, refs = refs[0], refs[1:]
        if early:
            refs = refs[1:]
        else:
            fresh_refs, refs = fresh_refs + [refs[0]], refs[1:]
    if final:
        out_ref, refs = refs[0], refs[1:]
    else:
        (sum_out, total_out, high_out), refs = refs[:3], refs[3:]
    if unpack:
        (decode_ref, rows_ref, request_ref, request_sem, decode_sems), refs = refs[:5], refs[5:]
        count = rows_ref.shape[1]
        request_copy = pltpu.make_async_copy(request_vmem, request_ref, request_sem)
        request_copy.start()
    if final:
        done_ref, out_sems = refs
    new_count = rot_ref.shape[1] // PER_KV
    slots = got_refs[0].shape[0]
    span = pieces * slots
    if not early:
        span += own_ref.shape[1] - new_count
        token = lax.broadcasted_iota(jnp.int32, (size, new_count), 0) % new_count
        causal = jnp.where(lax.broadcasted_iota(jnp.int32, (size, new_count), 1) <= token, 0.0, MASKED)
    bias = bias_ref[0:1, first * slots : first * slots + span]
    per_head = PER_KV * new_count // size
    total_chunks = KV_HEADS * per_head
    heads_in = size // new_count
    keys, values = {}, {}
    scores, weights, factors = {}, {}, {}

    def place(at):
        head, chunk = divmod(at, per_head)
        return head, chunk, slice(chunk * size, (chunk + 1) * size)

    def score(at):
        head, chunk, rows = place(at)
        if chunk == 0:
            key_parts = [got[:, column(head)] for got in got_refs]
            value_parts = [got[:, column(KV_HEADS + head)] for got in got_refs]
            if not early:
                key_parts.append(own_ref[head])
                value_parts.append(own_ref[KV_HEADS + head])
            keys[head] = jnp.concatenate(key_parts, axis=0)
            value = jnp.concatenate(value_parts, axis=0)
            values[head] = jnp.concatenate([value, jnp.ones_like(value)], axis=1)
        scores[at] = lax.dot_general(
            rot_ref[head, rows, :], keys[head], (((1,), (1,)), ((), ())), preferred_element_type=jnp.float32
        )

    def weigh(at):
        head, chunk, rows = place(at)
        values_at = scores.pop(at)
        if early:
            values_at = values_at * SCALE + bias
        else:
            values_at = jnp.concatenate(
                [values_at[:, :span] * SCALE + bias, values_at[:, span:] * SCALE + causal], axis=1
            )
        high = jnp.max(values_at, axis=1, keepdims=True)
        if early:
            high_before = high_in[head, rows, :]
            high = jnp.maximum(high_before, high)
            factors[at] = jnp.exp2(high_before - high)
            high = jnp.concatenate([high] * (span // HEAD_DIM), axis=1)
        elif not final:
            high_out[head, rows, :] = jnp.broadcast_to(high, (size, HEAD_DIM))
        weights[at] = jnp.exp2(values_at - high).astype(jnp.bfloat16)

    def out_copy(at):
        head, chunk, rows = place(at)
        width = heads_in * HEAD_DIM
        return pltpu.make_async_copy(
            done_ref.at[at], out_ref.at[:, pl.ds(at * width, width)], out_sems.at[at]
        )

    def finish(at, summed):
        head, chunk, rows = place(at)
        summed, total = summed[:, :HEAD_DIM], summed[:, HEAD_DIM:]
        if early:
            factor = factors.pop(at)
            summed = summed + sum_in[head, rows, :] * factor
            total = total + total_in[head, rows, :] * factor
        if not final:
            sum_out[head, rows, :] = summed
            total_out[head, rows, :] = total
            return
        about = pl.reciprocal(total, approx=True)
        result = (summed * (about * (2.0 - total * about))).astype(jnp.bfloat16)
        for row in range(heads_in):
            done_ref[at, :, column(row)] = result[row * new_count : (row + 1) * new_count]
        out_copy(at).start()

    def decode_copy(p):
        return pltpu.make_async_copy(
            rows_ref.at[p], decode_ref.at[request_ref[0, first + p]], decode_sems.at[p]
        )

    score(0)
    for at in range(total_chunks + 1):
        if at + 1 < total_chunks:
            score(at + 1)
        if at >= 1:
            summed = jnp.dot(
                weights.pop(at - 1), values[(at - 1) // per_head], preferred_element_type=jnp.float32
            )
        if at < total_chunks:
            weigh(at)
        if at >= 1:
            finish(at - 1, summed)
        if unpack and at == 1:
            request_copy.wait()
            for p, fresh_ref in enumerate(fresh_refs):
                stack = fresh_ref[...]
                quarter = stack.shape[1]
                for part in range(stack.shape[0] // count):
                    rows_ref[p, :, part * quarter : (part + 1) * quarter] = stack[
                        part * count : (part + 1) * count
                    ]
                decode_copy(p).start()
    for p in range(len(fresh_refs)):
        decode_copy(p).wait()
    if final:
        for at in range(total_chunks):
            out_copy(at).wait()


def attend(rot, bias, own, got, first=0, sums=None, final=True, requests=None, fresh=None, decode=None, size=CHUNK):
    rows = rot.shape[1]
    new_count = rows // PER_KV
    pieces = len(got)
    early, unpack = sums is not None, requests is not None
    operands = [rot, bias] + (list(sums) if early else [own]) + list(got)
    specs = [VMEM] * len(operands)
    shapes, out_specs, scratch, aliases = [], [], [], {}
    if unpack:
        operands.append(requests)
        specs.append(VMEM)
        if early:
            operands.append(decode)
            specs.append(ANY)
            aliases = {len(operands) - 1: 1 if final else 3}
        else:
            operands.append(fresh)
            specs.append(VMEM)
    if final:
        shapes.append(jax.ShapeDtypeStruct((new_count, Q_HEADS * HEAD_DIM), jnp.bfloat16))
        out_specs.append(ANY)
    else:
        shapes += [jax.ShapeDtypeStruct((KV_HEADS, rows, HEAD_DIM), jnp.float32)] * 3
        out_specs += [VMEM] * 3
    if unpack:
        slots = got[0].shape[0]
        count = (got[0].shape[1] - WIDTH) * slots // WIDTH
        unpacked = pieces if early else pieces + 1
        shapes.append(jax.ShapeDtypeStruct((new_count // count, count, WIDTH), jnp.bfloat16))
        out_specs.append(ANY)
        scratch += [
            pltpu.VMEM((unpacked, count, WIDTH), jnp.bfloat16),
            pltpu.SMEM(requests.shape, jnp.int32),
            pltpu.SemaphoreType.DMA,
            pltpu.SemaphoreType.DMA((unpacked,)),
        ]
    if final:
        chunks = KV_HEADS * rows // size
        scratch += [
            pltpu.VMEM((chunks, new_count, size // new_count * HEAD_DIM), jnp.bfloat16),
            pltpu.SemaphoreType.DMA((chunks,)),
        ]
    return pl.pallas_call(
        functools.partial(attend_kernel, pieces, first, early, final, unpack, size),
        out_shape=tuple(shapes),
        in_specs=specs,
        out_specs=tuple(out_specs),
        scratch_shapes=scratch,
        input_output_aliases=aliases,
        compiler_params=params(32),
        name="attend_late" if early else "attend",
    )(*operands)


def inverse(table):
    places = jnp.arange(table.shape[0], dtype=jnp.int32)
    return jnp.sum(jnp.where(table[None, :] == places[:, None], places, 0), axis=1)


def rotate(rows, positions, heads):
    half = HEAD_DIM // 2
    freqs = ROPE_BASE ** (-jnp.arange(half, dtype=jnp.float32) / half)
    angles = positions.astype(jnp.float32)[:, None] * freqs[None, :]
    cosine = jnp.concatenate([jnp.cos(angles)] * 2, axis=-1)[:, None, :]
    sine = jnp.concatenate([-jnp.sin(angles), jnp.sin(angles)], axis=-1)[:, None, :]
    split = rows.astype(jnp.float32).reshape(rows.shape[0], heads, HEAD_DIM)
    turned = jnp.roll(split, half, axis=-1)
    return (split * cosine + turned * sine).astype(jnp.bfloat16)


def small_pieces(me, assignment, prefix_len, stripe_map, owner_map, queries, block_kv, pool):
    groups, slots, width = pool.shape
    new_count = block_kv.shape[0]
    count = new_count // groups
    request = assignment[me[0]]
    length = prefix_len[request]
    positions = length + jnp.arange(new_count, dtype=jnp.int32)
    rot = rotate(queries, positions, Q_HEADS).reshape(new_count, KV_HEADS, PER_KV, HEAD_DIM)
    rot = jnp.transpose(rot, (1, 2, 0, 3)).reshape(KV_HEADS, PER_KV * new_count, HEAD_DIM)
    new_keys = rotate(block_kv[:, :KV_WIDTH], positions, KV_HEADS).reshape(new_count, KV_WIDTH)
    new_kv = jnp.concatenate([new_keys, block_kv[:, KV_WIDTH:]], axis=1)
    own = jnp.transpose(new_kv.reshape(new_count, 2 * KV_HEADS, HEAD_DIM), (1, 0, 2))
    spread = jnp.transpose(new_kv.reshape(count, groups, width), (1, 0, 2))
    send = jnp.concatenate([pool[assignment], spread[inverse(owner_map[request])]], axis=1)
    got = lax.all_to_all(send, "pg", split_axis=0, concat_axis=0, tiled=True)
    located = jnp.arange(slots, dtype=jnp.int32)[None, :] * groups + inverse(stripe_map[request])[:, None]
    bias = jnp.where(located < length, 0.0, MASKED).astype(jnp.float32).reshape(1, groups * slots)
    keys = got[:, :slots].reshape(groups * slots, width)
    (attended,) = attend(rot, jnp.broadcast_to(bias, (8, groups * slots)), own, [keys])
    return attended, got[inverse(assignment), slots:]


def shards(queries, block_kv, pool_kv, prefix_len, assignment, stripe_map, owner_map):
    queries, block_kv, pool = queries[0], block_kv[0], pool_kv[0]
    groups, slots, width = pool.shape
    new_count = queries.shape[0]
    count = new_count // groups
    me = lax.axis_index("pg").astype(jnp.int32).reshape(1)
    if groups != 16 or slots % 16 or HEAD_DIM % slots or count % 8 or slots % count:
        attended, decode_kv = small_pieces(
            me, assignment, prefix_len, stripe_map, owner_map, queries, block_kv, pool
        )
        return (attended[None], decode_kv[None])
    order = order_of(groups)
    table = rotation_tables(new_count)
    first_blocks, info = front(order, me, assignment, prefix_len, owner_map, stripe_map, block_kv, table, pool)
    other_blocks, (rot, own, fresh, bias, requests) = rotate_queries(order, info, queries, pool)
    got = []
    for block, t in zip(list(first_blocks) + list(other_blocks), [t for t in order if t]):
        got.append(lax.ppermute(block, "pg", [(source, source ^ t) for source in range(groups)]))
    soon = groups - LATE - 1
    *sums, decode_kv = attend(rot, bias, own, got[:soon], final=False, requests=requests, fresh=fresh)
    attended, decode_kv = attend(
        rot, bias, None, got[soon:], first=soon + 1, sums=sums, requests=requests, decode=decode_kv, size=LATE_CHUNK
    )
    return (attended[None], decode_kv[None])


def solution(mesh):
    return jax.shard_map(
        shards,
        mesh=mesh,
        in_specs=(
            P(("rep", "pg"), None, None),
            P(("rep", "pg"), None, None),
            P(("rep", "pg"), None, None, None),
            P("rep"),
            P("rep"),
            P("rep", None),
            P("rep", None),
        ),
        out_specs=(P(("rep", "pg"), None, None), P(("rep", "pg"), None, None, None)),
        check_vma=False,
    )
```

profile of v0, /device:TPU:0, one launch (start us, length us, event | category | flops | bytes accessed | tf_op | source)
XLA Modules:
  0.0 42.4 jit_solution(1997890912283071522)
XLA Ops:
  0.6 2.6 %front.1 = (bf16[32,1280]{1,0:T(8,128)(2,1)}, bf16[32,1280]{1,0:T(8,128)(2,1)}, bf16[32,1280]{1,0:T(8,128)(2,1)}, bf16[32,1280]{1,0:T(8,128)(2,1)}, f32[1296,128]{1,0:T(8,128)}) custom-call(s32[1]{0:T(128)} %bitcast.me_ref, s32[16]{0:T(128)} %assign_any.1, s32[16]{0:T(128)} %length_any.1, s32[16,16]{1,0:T(8,128)} %owner_any.1, s32[16,16]{1,0:T(8,128)} %stripe_any.1, ...), custom_call_target="tpu_custom_call" | custom-call | tf_op jit(solution)/shard_map/front/pallas_call | solution.py:177
  3.3 4.1 %collective-permute-start = (bf16[32,1280]{1,0:T(8,128)(2,1)}, bf16[32,1280]{1,0:T(8,128)(2,1)S(1)}, u32[]{:S(2)}, u32[]{:S(2)}) collective-permute-start(bf16[32,1280]{1,0:T(8,128)(2,1)} %get-tuple-element.33), channel_id=1, source_target_pairs={{0,8},{1,9},{2,10},{3,11},{4,12},{5,13},{6,14},{7,15},{8,0},{9,1},... | collective-permute-start | bytes 245768 | tf_op jit(solution)/shard_map/ppermute | solution.py:512
  7.4 3.0 %collective-permute-start.2 = (bf16[32,1280]{1,0:T(8,128)(2,1)}, bf16[32,1280]{1,0:T(8,128)(2,1)S(1)}, u32[]{:S(2)}, u32[]{:S(2)}) collective-permute-start(bf16[32,1280]{1,0:T(8,128)(2,1)} %get-tuple-element.35), channel_id=1, source_target_pairs={{0,10},{1,11},{2,8},{3,9},{4,14},{5,15},{6,12},{7,13},{8,2},{9,3},... | collective-permute-start | bytes 245768 | tf_op jit(solution)/shard_map/ppermute | solution.py:512
  10.4 1.8 %collective-permute-start.3 = (bf16[32,1280]{1,0:T(8,128)(2,1)}, bf16[32,1280]{1,0:T(8,128)(2,1)S(1)}, u32[]{:S(2)}, u32[]{:S(2)}) collective-permute-start(bf16[32,1280]{1,0:T(8,128)(2,1)} %get-tuple-element.36), channel_id=1, source_target_pairs={{0,7},{1,6},{2,5},{3,4},{4,3},{5,2},{6,1},{7,0},{8,15},{9,14},{10,... | collective-permute-start | bytes 245768 | tf_op jit(solution)/shard_map/ppermute | solution.py:512
  12.2 1.2 %copy-done.1 = bf16[1,128,4096]{2,1,0:T(8,128)(2,1)S(1)} copy-done((bf16[1,128,4096]{2,1,0:T(8,128)(2,1)S(1)}, bf16[1,128,4096]{2,1,0:T(8,128)(2,1)}, u32[]{:S(2)}) %copy-start.1) | copy-done | bytes 1048600
  13.4 1.1 %copy-done.2 = f32[1296,128]{1,0:T(8,128)S(1)} copy-done((f32[1296,128]{1,0:T(8,128)S(1)}, f32[1296,128]{1,0:T(8,128)}, u32[]{:S(2)}) %copy-start.2) | copy-done | bytes 663576
  14.5 0.9 %rotate_queries.1 = (bf16[32,1280]{1,0:T(8,128)(2,1)S(1)}, bf16[32,1280]{1,0:T(8,128)(2,1)S(1)}, bf16[32,1280]{1,0:T(8,128)(2,1)S(1)}, bf16[32,1280]{1,0:T(8,128...) custom-call(f32[1296,128]{1,0:T(8,128)S(1)} %copy-done.2, ...), custom_call_target="tpu_custom_call" | custom-call | tf_op jit(solution)/shard_map/rotate_queries/pallas_call | solution.py:249
  15.4 1.3 %collective-permute-start.4 = (bf16[32,1280]{1,0:T(8,128)(2,1)S(1)}, bf16[32,1280]{1,0:T(8,128)(2,1)S(1)}, u32[]{:S(2)}, u32[]{:S(2)}) collective-permute-start(bf16[32,1280]{1,0:T(8,128)(2,1)S(1)} %get-tuple-element.37), channel_id=1, source_target_pairs={{0,11},{1,10},{2,9},{3,8},{4,15},{5,14},{6,13},{7,12},{8,3},{9,2},... | collective-permute-start | bytes 245768 | tf_op jit(solution)/shard_map/ppermute | solution.py:512
  16.7 0.0 collective-permute-done.refs_3_
  16.7 0.4 %collective-permute-start.5 = (bf16[32,1280]{1,0:T(8,128)(2,1)S(1)}, bf16[32,1280]{1,0:T(8,128)(2,1)S(1)}, u32[]{:S(2)}, u32[]{:S(2)}) collective-permute-start(bf16[32,1280]{1,0:T(8,128)(2,1)S(1)} %get-tuple-element.38), channel_id=1, source_target_pairs={{0,6},{1,7},{2,4},{3,5},{4,2},{5,3},{6,0},{7,1},{8,14},{9,15},{10,... | collective-permute-start | bytes 245768 | tf_op jit(solution)/shard_map/ppermute | solution.py:512
  17.2 0.0 collective-permute-done.1.refs_4_
  17.2 3.3 %collective-permute-start.6 = (bf16[32,1280]{1,0:T(8,128)(2,1)S(1)}, bf16[32,1280]{1,0:T(8,128)(2,1)S(1)}, u32[]{:S(2)}, u32[]{:S(2)}) collective-permute-start(bf16[32,1280]{1,0:T(8,128)(2,1)S(1)} %get-tuple-element.39), channel_id=1, source_target_pairs={{0,12},{1,13},{2,14},{3,15},{4,8},{5,9},{6,10},{7,11},{8,4},{9,5},... | collective-permute-start | bytes 245768 | tf_op jit(solution)/shard_map/ppermute | solution.py:512
  20.5 0.0 collective-permute-done.2.refs_5_
  20.5 0.2 collective-permute-start.7
  20.7 0.0 collective-permute-done.3.refs_6_
  20.7 4.0 %collective-permute-start.8 = (bf16[32,1280]{1,0:T(8,128)(2,1)S(1)}, bf16[32,1280]{1,0:T(8,128)(2,1)S(1)}, u32[]{:S(2)}, u32[]{:S(2)}) collective-permute-start(bf16[32,1280]{1,0:T(8,128)(2,1)S(1)} %get-tuple-element.41), channel_id=1, source_target_pairs={{0,13},{1,12},{2,15},{3,14},{4,9},{5,8},{6,11},{7,10},{8,5},{9,4},... | collective-permute-start | bytes 245768 | tf_op jit(solution)/shard_map/ppermute | solution.py:512
  24.7 1.4 %collective-permute-start.9 = (bf16[32,1280]{1,0:T(8,128)(2,1)S(1)}, bf16[32,1280]{1,0:T(8,128)(2,1)S(1)}, u32[]{:S(2)}, u32[]{:S(2)}) collective-permute-start(bf16[32,1280]{1,0:T(8,128)(2,1)S(1)} %get-tuple-element.42), channel_id=1, source_target_pairs={{0,4},{1,5},{2,6},{3,7},{4,0},{5,1},{6,2},{7,3},{8,12},{9,13},{10,... | collective-permute-start | bytes 245768 | tf_op jit(solution)/shard_map/ppermute | solution.py:512
  26.1 4.6 %collective-permute-start.11 = (bf16[32,1280]{1,0:T(8,128)(2,1)S(1)}, bf16[32,1280]{1,0:T(8,128)(2,1)S(1)}, u32[]{:S(2)}, u32[]{:S(2)}) collective-permute-start(bf16[32,1280]{1,0:T(8,128)(2,1)S(1)} %get-tuple-element.49), channel_id=1, source_target_pairs={{0,14},{1,15},{2,12},{3,13},{4,10},{5,11},{6,8},{7,9},{8,6},{9,7},... | collective-permute-start | bytes 245768 | tf_op jit(solution)/shard_map/ppermute | solution.py:512
  30.7 2.4 %collective-permute-start.12 = (bf16[32,1280]{1,0:T(8,128)(2,1)S(1)}, bf16[32,1280]{1,0:T(8,128)(2,1)S(1)}, u32[]{:S(2)}, u32[]{:S(2)}) collective-permute-start(bf16[32,1280]{1,0:T(8,128)(2,1)S(1)} %get-tuple-element.50), channel_id=1, source_target_pairs={{0,15},{1,14},{2,13},{3,12},{4,11},{5,10},{6,9},{7,8},{8,7},{9,6},... | collective-permute-start | bytes 245768 | tf_op jit(solution)/shard_map/ppermute | solution.py:512
  33.1 0.1 collective-permute-start.14
  33.2 3.7 %attend.1 = (f32[4,1024,128]{2,1,0:T(8,128)S(1)}, f32[4,1024,128]{2,1,0:T(8,128)S(1)}, f32[4,1024,128]{2,1,0:T(8,128)S(1)}, bf16[16,8,1024]{2,1,0:T(8,128)(2,1)}) custom-call(bf16[4,1024,128]{2,1,0:T(8,128)(2,1)S(1)} %get-tuple-element.30.refs_0_, f32[8,512]{1,0:T(8,128)S(1)} %get-tuple-element.31.refs_1_, ...), custom_call_target="tpu_custom_call" | custom-call | tf_op jit(solution)/shard_map/attend/pallas_call | solution.py:445
  36.9 0.4 %collective-permute-done.12.refs_6_ = bf16[32,1280]{1,0:T(8,128)(2,1)S(1)} collective-permute-done((bf16[32,1280]{1,0:T(8,128)(2,1)S(1)}, bf16[32,1280]{1,0:T(8,128)(2,1)S(1)}, u32[]{:S(2)}, u32[]{:S(2)}) %collective-permute-start.12) | collective-permute-done | bytes 81952 | tf_op jit(solution)/shard_map/ppermute | solution.py:512
  37.4 1.8 %collective-permute-done.13.refs_7_ = bf16[32,1280]{1,0:T(8,128)(2,1)S(1)} collective-permute-done((bf16[32,1280]{1,0:T(8,128)(2,1)S(1)}, bf16[32,1280]{1,0:T(8,128)(2,1)S(1)}, u32[]{:S(2)}, u32[]{:S(2)}) %collective-permute-start.13) | collective-permute-done | bytes 81952 | tf_op jit(solution)/shard_map/ppermute | solution.py:512
  39.2 3.2 %attend_late.1 = (bf16[128,4096]{1,0:T(8,128)(2,1)}, bf16[16,8,1024]{2,1,0:T(8,128)(2,1)}) custom-call(bf16[4,1024,128]{2,1,0:T(8,128)(2,1)S(1)} %get-tuple-element.30.refs_0_, f32[8,512]{1,0:T(8,128)S(1)} %get-tuple-element.31.refs_1_, f32[4,1024,128]{2,1,0:T(8,128)S(1)} %get-tuple-element.46.refs_2_, ...), custom_call_target="tpu_custom_call", output_to_operand_aliasing={{1}: (10, {})} | custom-call | tf_op jit(solution)/shard_map/attend_late/pallas_call | solution.py:445
  (16 shorter events, 0.0 us)
Async XLA Ops:
  0.6 11.6 %copy-start = (bf16[1,16,32,1024]{3,2,1,0:T(8,128)(2,1)S(1)}, bf16[1,16,32,1024]{3,2,1,0:T(8,128)(2,1)}, u32[]{:S(2)}) copy-start(bf16[1,16,32,1024]{3,2,1,0:T(8,128)(2,1)} %param.10) | copy-start | bytes 3145732
  3.3 13.5 %collective-permute-start = (bf16[32,1280]{1,0:T(8,128)(2,1)}, bf16[32,1280]{1,0:T(8,128)(2,1)S(1)}, u32[]{:S(2)}, u32[]{:S(2)}) collective-permute-start(bf16[32,1280]{1,0:T(8,128)(2,1)} %get-tuple-element.33), channel_id=1, source_target_pairs={{0,8},{1,9},{2,10},{3,11},{4,12},{5,13},{6,14},{7,15},{8,0},{9,1},... | collective-permute-start | bytes 245768 | tf_op jit(solution)/shard_map/ppermute | solution.py:512
  7.4 9.8 %collective-permute-start.1 = (bf16[32,1280]{1,0:T(8,128)(2,1)}, bf16[32,1280]{1,0:T(8,128)(2,1)S(1)}, u32[]{:S(2)}, u32[]{:S(2)}) collective-permute-start(bf16[32,1280]{1,0:T(8,128)(2,1)} %get-tuple-element.34), channel_id=1, source_target_pairs={{0,9},{1,8},{2,11},{3,10},{4,13},{5,12},{6,15},{7,14},{8,1},{9,0},... | collective-permute-start | bytes 245768 | tf_op jit(solution)/shard_map/ppermute | solution.py:512
  7.4 13.1 %collective-permute-start.2 = (bf16[32,1280]{1,0:T(8,128)(2,1)}, bf16[32,1280]{1,0:T(8,128)(2,1)S(1)}, u32[]{:S(2)}, u32[]{:S(2)}) collective-permute-start(bf16[32,1280]{1,0:T(8,128)(2,1)} %get-tuple-element.35), channel_id=1, source_target_pairs={{0,10},{1,11},{2,8},{3,9},{4,14},{5,15},{6,12},{7,13},{8,2},{9,3},... | collective-permute-start | bytes 245768 | tf_op jit(solution)/shard_map/ppermute | solution.py:512
  10.4 10.3 %collective-permute-start.3 = (bf16[32,1280]{1,0:T(8,128)(2,1)}, bf16[32,1280]{1,0:T(8,128)(2,1)S(1)}, u32[]{:S(2)}, u32[]{:S(2)}) collective-permute-start(bf16[32,1280]{1,0:T(8,128)(2,1)} %get-tuple-element.36), channel_id=1, source_target_pairs={{0,7},{1,6},{2,5},{3,4},{4,3},{5,2},{6,1},{7,0},{8,15},{9,14},{10,... | collective-permute-start | bytes 245768 | tf_op jit(solution)/shard_map/ppermute | solution.py:512
  12.2 1.2 %copy-start.1 = (bf16[1,128,4096]{2,1,0:T(8,128)(2,1)S(1)}, bf16[1,128,4096]{2,1,0:T(8,128)(2,1)}, u32[]{:S(2)}) copy-start(bf16[1,128,4096]{2,1,0:T(8,128)(2,1)} %param.8) | copy-start | bytes 3145732
  13.4 1.1 %copy-start.2 = (f32[1296,128]{1,0:T(8,128)S(1)}, f32[1296,128]{1,0:T(8,128)}, u32[]{:S(2)}) copy-start(f32[1296,128]{1,0:T(8,128)} %get-tuple-element.29.info_ref) | copy-start | bytes 1990660
  15.4 9.3 %collective-permute-start.4 = (bf16[32,1280]{1,0:T(8,128)(2,1)S(1)}, bf16[32,1280]{1,0:T(8,128)(2,1)S(1)}, u32[]{:S(2)}, u32[]{:S(2)}) collective-permute-start(bf16[32,1280]{1,0:T(8,128)(2,1)S(1)} %get-tuple-element.37), channel_id=1, source_target_pairs={{0,11},{1,10},{2,9},{3,8},{4,15},{5,14},{6,13},{7,12},{8,3},{9,2},... | collective-permute-start | bytes 245768 | tf_op jit(solution)/shard_map/ppermute | solution.py:512
  16.7 9.4 %collective-permute-start.5 = (bf16[32,1280]{1,0:T(8,128)(2,1)S(1)}, bf16[32,1280]{1,0:T(8,128)(2,1)S(1)}, u32[]{:S(2)}, u32[]{:S(2)}) collective-permute-start(bf16[32,1280]{1,0:T(8,128)(2,1)S(1)} %get-tuple-element.38), channel_id=1, source_target_pairs={{0,6},{1,7},{2,4},{3,5},{4,2},{5,3},{6,0},{7,1},{8,14},{9,15},{10,... | collective-permute-start | bytes 245768 | tf_op jit(solution)/shard_map/ppermute | solution.py:512
  17.2 8.9 %collective-permute-start.6 = (bf16[32,1280]{1,0:T(8,128)(2,1)S(1)}, bf16[32,1280]{1,0:T(8,128)(2,1)S(1)}, u32[]{:S(2)}, u32[]{:S(2)}) collective-permute-start(bf16[32,1280]{1,0:T(8,128)(2,1)S(1)} %get-tuple-element.39), channel_id=1, source_target_pairs={{0,12},{1,13},{2,14},{3,15},{4,8},{5,9},{6,10},{7,11},{8,4},{9,5},... | collective-permute-start | bytes 245768 | tf_op jit(solution)/shard_map/ppermute | solution.py:512
  20.5 10.2 %collective-permute-start.7 = (bf16[32,1280]{1,0:T(8,128)(2,1)S(1)}, bf16[32,1280]{1,0:T(8,128)(2,1)S(1)}, u32[]{:S(2)}, u32[]{:S(2)}) collective-permute-start(bf16[32,1280]{1,0:T(8,128)(2,1)S(1)} %get-tuple-element.40), channel_id=1, source_target_pairs={{0,5},{1,4},{2,7},{3,6},{4,1},{5,0},{6,3},{7,2},{8,13},{9,12},{10,... | collective-permute-start | bytes 245768 | tf_op jit(solution)/shard_map/ppermute | solution.py:512
  20.7 12.4 %collective-permute-start.8 = (bf16[32,1280]{1,0:T(8,128)(2,1)S(1)}, bf16[32,1280]{1,0:T(8,128)(2,1)S(1)}, u32[]{:S(2)}, u32[]{:S(2)}) collective-permute-start(bf16[32,1280]{1,0:T(8,128)(2,1)S(1)} %get-tuple-element.41), channel_id=1, source_target_pairs={{0,13},{1,12},{2,15},{3,14},{4,9},{5,8},{6,11},{7,10},{8,5},{9,4},... | collective-permute-start | bytes 245768 | tf_op jit(solution)/shard_map/ppermute | solution.py:512
  24.7 8.3 %collective-permute-start.9 = (bf16[32,1280]{1,0:T(8,128)(2,1)S(1)}, bf16[32,1280]{1,0:T(8,128)(2,1)S(1)}, u32[]{:S(2)}, u32[]{:S(2)}) collective-permute-start(bf16[32,1280]{1,0:T(8,128)(2,1)S(1)} %get-tuple-element.42), channel_id=1, source_target_pairs={{0,4},{1,5},{2,6},{3,7},{4,0},{5,1},{6,2},{7,3},{8,12},{9,13},{10,... | collective-permute-start | bytes 245768 | tf_op jit(solution)/shard_map/ppermute | solution.py:512
  26.1 7.1 %collective-permute-start.10 = (bf16[32,1280]{1,0:T(8,128)(2,1)S(1)}, bf16[32,1280]{1,0:T(8,128)(2,1)S(1)}, u32[]{:S(2)}, u32[]{:S(2)}) collective-permute-start(bf16[32,1280]{1,0:T(8,128)(2,1)S(1)} %get-tuple-element.43), channel_id=1, source_target_pairs={{0,3},{1,2},{2,1},{3,0},{4,7},{5,6},{6,5},{7,4},{8,11},{9,10},{10,... | collective-permute-start | bytes 245768 | tf_op jit(solution)/shard_map/ppermute | solution.py:512
  26.1 10.8 %collective-permute-start.11 = (bf16[32,1280]{1,0:T(8,128)(2,1)S(1)}, bf16[32,1280]{1,0:T(8,128)(2,1)S(1)}, u32[]{:S(2)}, u32[]{:S(2)}) collective-permute-start(bf16[32,1280]{1,0:T(8,128)(2,1)S(1)} %get-tuple-element.49), channel_id=1, source_target_pairs={{0,14},{1,15},{2,12},{3,13},{4,10},{5,11},{6,8},{7,9},{8,6},{9,7},... | collective-permute-start | bytes 245768 | tf_op jit(solution)/shard_map/ppermute | solution.py:512
  30.7 6.7 %collective-permute-start.12 = (bf16[32,1280]{1,0:T(8,128)(2,1)S(1)}, bf16[32,1280]{1,0:T(8,128)(2,1)S(1)}, u32[]{:S(2)}, u32[]{:S(2)}) collective-permute-start(bf16[32,1280]{1,0:T(8,128)(2,1)S(1)} %get-tuple-element.50), channel_id=1, source_target_pairs={{0,15},{1,14},{2,13},{3,12},{4,11},{5,10},{6,9},{7,8},{8,7},{9,6},... | collective-permute-start | bytes 245768 | tf_op jit(solution)/shard_map/ppermute | solution.py:512
  33.1 6.1 %collective-permute-start.13 = (bf16[32,1280]{1,0:T(8,128)(2,1)S(1)}, bf16[32,1280]{1,0:T(8,128)(2,1)S(1)}, u32[]{:S(2)}, u32[]{:S(2)}) collective-permute-start(bf16[32,1280]{1,0:T(8,128)(2,1)S(1)} %get-tuple-element.51), channel_id=1, source_target_pairs={{0,2},{1,3},{2,0},{3,1},{4,6},{5,7},{6,4},{7,5},{8,10},{9,11},{10,... | collective-permute-start | bytes 245768 | tf_op jit(solution)/shard_map/ppermute | solution.py:512
  33.1 6.1 %collective-permute-start.14 = (bf16[32,1280]{1,0:T(8,128)(2,1)S(1)}, bf16[32,1280]{1,0:T(8,128)(2,1)S(1)}, u32[]{:S(2)}, u32[]{:S(2)}) collective-permute-start(bf16[32,1280]{1,0:T(8,128)(2,1)S(1)} %get-tuple-element.52), channel_id=1, source_target_pairs={{0,1},{1,0},{2,3},{3,2},{4,5},{5,4},{6,7},{7,6},{8,9},{9,8},{10,11... | collective-permute-start | bytes 245768 | tf_op jit(solution)/shard_map/ppermute | solution.py:512
where the time goes:
time: 42.6 us; the launch traced here: 42.4 us
  starting transfers between devices  26.7 us (63%)
  Pallas kernels  10.4 us (24%)
  waiting for transfers between devices  2.33 us (5%)
  local copies, waits for them, and re-layouts  2.32 us (5%)
  between operations  0.7 us (2%)
    ppermute x15, starting transfers between devices, shards(): lax.ppermute(block, 'pg', [(source, source ^ t) for source in range(group...  26.7 us
    pallas_call x2, Pallas kernels, attend(): pl.pallas_call(functools.partial(attend_kernel, pieces, first, early, fin...  6.88 us
    pallas_call x1, Pallas kernels, front(): pl.pallas_call(functools.partial(front_kernel, order), out_shape=[block]...  2.6 us
    ppermute x15, waiting for transfers between devices, shards(): lax.ppermute(block, 'pg', [(source, source ^ t) for source in range(group...  2.33 us
    unnamed x6, local copies, waits for them, and re-layouts  2.32 us
    pallas_call x1, Pallas kernels, rotate_queries(): pl.pallas_call(functools.partial(query_kernel, order), out_shape=[jax.Sha...  0.87 us
  transfers between devices with their start and end apart: 15, of which 2 were waited for; matrix products, arithmetic and copies ran while one was open for 0% of the time, Pallas kernels for 11%

commit v1 on v0

--- a/solution.py
+++ b/solution.py
@@ -40,7 +40,7 @@
 def order_of(groups):
     half = groups // 2
     far, near = list(range(half, 2 * half)), list(range(half - 1, 0, -1))
-    order = [(far if kind == "f" else near).pop(0) for kind in "fffnfnfnfnnffnn"]
+    order = [(far if kind == "f" else near).pop(0) for kind in "fnfnfnfnfnnffnf"]
     order.insert(groups - LATE - 1, 0)
     return order
 
@@ -92,7 +92,7 @@
 ):
     groups, slots, width = pool_any.shape
     send_refs, info_any, refs = refs[:AHEAD], refs[AHEAD], refs[AHEAD + 1 :]
-    (assign_ref, length_ref, owner_ref, stripe_ref, residue_ref, block_ref, table_ref, pack_ref, info_ref,
+    (assign_ref, length_ref, owner_ref, stripe_ref, residue_ref, block_ref, table_ref, pool_ref, pack_ref, info_ref,
      small_sems, pool_sems, send_sems, info_sems) = refs
     new_count = block_any.shape[0]
     count = new_count // groups
@@ -105,17 +105,14 @@
     smalls = [pltpu.make_async_copy(*pair, small_sems.at[i]) for i, pair in enumerate(pairs)]
     for copy in smalls:
         copy.start()
-    me = me_ref[0]
-    smalls[0].wait()
     pool_copies = [
-        pltpu.make_async_copy(
-            pool_any.at[assign_ref[me ^ order[p]]], pack_ref.at[p, :, pl.ds(0, width)], pool_sems.at[p]
-        )
-        for p in range(AHEAD)
+        pltpu.make_async_copy(pool_any.at[pl.ds(low, 4)], pool_ref.at[pl.ds(low, 4)], pool_sems.at[low // 4])
+        for low in range(0, groups, 4)
     ]
     for copy in pool_copies:
         copy.start()
-    for copy in smalls[1:]:
+    me = me_ref[0]
+    for copy in smalls:
         copy.wait()
     request = assign_ref[me]
     length = length_ref[request]
@@ -133,13 +130,15 @@
         return pltpu.make_async_copy(info_ref.at[part_rows], info_any.at[part_rows], info_sems.at[part])
 
     info_copy(0, at["new"], rows).start()
+    for copy in pool_copies:
+        copy.wait()
     sends = []
     for p in range(AHEAD):
+        pack_ref[p, :, 0:width] = pool_ref[assign_ref[me ^ order[p]]]
         for lanes in range(quarter):
             pack_ref[p, :, width + lanes * HEAD_DIM : width + (lanes + 1) * HEAD_DIM] = fresh_rows(
                 info_ref, at["new"], residue_ref[me ^ order[p]], new_count, count, quarter, lanes
             ).astype(jnp.bfloat16)
-        pool_copies[p].wait()
         sends.append(pltpu.make_async_copy(pack_ref.at[p], send_refs[p], send_sems.at[p]))
         sends[-1].start()
     info_ref[at["cos"] : at["cos"] + new_count] = cosine
@@ -187,10 +186,11 @@
             pltpu.SMEM(assignment.shape, jnp.int32),
             pltpu.VMEM(block_kv.shape, jnp.bfloat16),
             pltpu.VMEM(table.shape, jnp.float32),
+            pltpu.VMEM(pool.shape, jnp.bfloat16),
             pltpu.VMEM((AHEAD,) + block.shape, jnp.bfloat16),
             pltpu.VMEM(info.shape, jnp.float32),
             pltpu.SemaphoreType.DMA((6,)),
-            pltpu.SemaphoreType.DMA((AHEAD,)),
+            pltpu.SemaphoreType.DMA((groups // 4,)),
             pltpu.SemaphoreType.DMA((AHEAD,)),
             pltpu.SemaphoreType.DMA((2,)),
         ],
@@ -265,192 +265,244 @@
     return outs[:sent], outs[sent:]
 
 
-def attend_kernel(pieces, first, early, final, unpack, size, *refs):
-    rot_ref, bias_ref, refs = refs[0], refs[1], refs[2:]
-    if early:
-        (sum_in, total_in, high_in), refs = refs[:3], refs[3:]
-    else:
-        own_ref, refs = refs[0], refs[1:]
-    got_refs, refs = refs[:pieces], refs[pieces:]
-    fresh_refs = [got.at[:, pl.ds(WIDTH, got.shape[1] - WIDTH)] for got in got_refs] if unpack else []
-    if unpack:
-        request_vmem, refs = refs[0], refs[1:]
-        if early:
-            refs = refs[1:]
-        else:
-            fresh_refs, refs = fresh_refs + [refs[0]], refs[1:]
-    if final:
-        out_ref, refs = refs[0], refs[1:]
-    else:
-        (sum_out, total_out, high_out), refs = refs[:3], refs[3:]
-    if unpack:
-        (decode_ref, rows_ref, request_ref, request_sem, decode_sems), refs = refs[:5], refs[5:]
-        count = rows_ref.shape[1]
-        request_copy = pltpu.make_async_copy(request_vmem, request_ref, request_sem)
-        request_copy.start()
-    if final:
-        done_ref, out_sems = refs
-    new_count = rot_ref.shape[1] // PER_KV
-    slots = got_refs[0].shape[0]
-    span = pieces * slots
-    if not early:
-        span += own_ref.shape[1] - new_count
-        token = lax.broadcasted_iota(jnp.int32, (size, new_count), 0) % new_count
-        causal = jnp.where(lax.broadcasted_iota(jnp.int32, (size, new_count), 1) <= token, 0.0, MASKED)
-    bias = bias_ref[0:1, first * slots : first * slots + span]
-    per_head = PER_KV * new_count // size
-    total_chunks = KV_HEADS * per_head
-    heads_in = size // new_count
-    keys, values = {}, {}
-    scores, weights, factors = {}, {}, {}
-
-    def place(at):
-        head, chunk = divmod(at, per_head)
-        return head, chunk, slice(chunk * size, (chunk + 1) * size)
-
-    def score(at):
-        head, chunk, rows = place(at)
-        if chunk == 0:
-            key_parts = [got[:, column(head)] for got in got_refs]
-            value_parts = [got[:, column(KV_HEADS + head)] for got in got_refs]
-            if not early:
-                key_parts.append(own_ref[head])
-                value_parts.append(own_ref[KV_HEADS + head])
-            keys[head] = jnp.concatenate(key_parts, axis=0)
-            value = jnp.concatenate(value_parts, axis=0)
-            values[head] = jnp.concatenate([value, jnp.ones_like(value)], axis=1)
-        scores[at] = lax.dot_general(
-            rot_ref[head, rows, :], keys[head], (((1,), (1,)), ((), ())), preferred_element_type=jnp.float32
-        )
-
-    def weigh(at):
-        head, chunk, rows = place(at)
-        values_at = scores.pop(at)
-        if early:
-            values_at = values_at * SCALE + bias
-        else:
-            values_at = jnp.concatenate(
-                [values_at[:, :span] * SCALE + bias, values_at[:, span:] * SCALE + causal], axis=1
-            )
-        high = jnp.max(values_at, axis=1, keepdims=True)
-        if early:
-            high_before = high_in[head, rows, :]
-            high = jnp.maximum(high_before, high)
-            factors[at] = jnp.exp2(high_before - high)
-            high = jnp.concatenate([high] * (span // HEAD_DIM), axis=1)
-        elif not final:
-            high_out[head, rows, :] = jnp.broadcast_to(high, (size, HEAD_DIM))
-        weights[at] = jnp.exp2(values_at - high).astype(jnp.bfloat16)
-
-    def out_copy(at):
-        head, chunk, rows = place(at)
-        width = heads_in * HEAD_DIM
-        return pltpu.make_async_copy(
-            done_ref.at[at], out_ref.at[:, pl.ds(at * width, width)], out_sems.at[at]
-        )
-
-    def finish(at, summed):
-        head, chunk, rows = place(at)
-        summed, total = summed[:, :HEAD_DIM], summed[:, HEAD_DIM:]
-        if early:
-            factor = factors.pop(at)
-            summed = summed + sum_in[head, rows, :] * factor
-            total = total + total_in[head, rows, :] * factor
-        if not final:
-            sum_out[head, rows, :] = summed
-            total_out[head, rows, :] = total
-            return
-        about = pl.reciprocal(total, approx=True)
-        result = (summed * (about * (2.0 - total * about))).astype(jnp.bfloat16)
-        for row in range(heads_in):
-            done_ref[at, :, column(row)] = result[row * new_count : (row + 1) * new_count]
-        out_copy(at).start()
+def quotient(summed, total):
+    about = pl.reciprocal(total, approx=True)
+    return summed * (about * (2.0 - total * about))
+
+
+def join_keys(keys, values, got_refs, own_ref, head):
+    key_parts = [got[:, column(head)] for got in got_refs]
+    value_parts = [got[:, column(KV_HEADS + head)] for got in got_refs]
+    if own_ref is not None:
+        key_parts.append(own_ref[head])
+        value_parts.append(own_ref[KV_HEADS + head])
+    keys[head] = jnp.concatenate(key_parts, axis=0)
+    value = jnp.concatenate(value_parts, axis=0)
+    values[head] = jnp.concatenate([value, jnp.ones_like(value)], axis=1)
+
+
+def dot_keys(query, keys):
+    return lax.dot_general(query, keys, (((1,), (1,)), ((), ())), preferred_element_type=jnp.float32)
+
+
+def staged(total, score, weigh, mix, finish, beside=None):
+    scores, weights = {0: score(0)}, {}
+    for at in range(total + 1):
+        if at + 1 < total:
+            scores[at + 1] = score(at + 1)
+        if at >= 1:
+            mixed = mix(at - 1, weights.pop(at - 1))
+        if at < total:
+            weights[at] = weigh(at, scores.pop(at))
+        if at >= 1:
+            finish(at - 1, mixed)
+        if at == 1 and beside is not None:
+            beside()
+
+
+def unpacking(fresh_refs, first, request_vmem, decode_ref, rows_ref, request_ref, request_sem, decode_sems):
+    count = rows_ref.shape[1]
+    request_copy = pltpu.make_async_copy(request_vmem, request_ref, request_sem)
+    request_copy.start()
 
     def decode_copy(p):
         return pltpu.make_async_copy(
             rows_ref.at[p], decode_ref.at[request_ref[0, first + p]], decode_sems.at[p]
         )
 
-    score(0)
-    for at in range(total_chunks + 1):
-        if at + 1 < total_chunks:
-            score(at + 1)
-        if at >= 1:
-            summed = jnp.dot(
-                weights.pop(at - 1), values[(at - 1) // per_head], preferred_element_type=jnp.float32
-            )
-        if at < total_chunks:
-            weigh(at)
-        if at >= 1:
-            finish(at - 1, summed)
-        if unpack and at == 1:
-            request_copy.wait()
-            for p, fresh_ref in enumerate(fresh_refs):
-                stack = fresh_ref[...]
-                quarter = stack.shape[1]
-                for part in range(stack.shape[0] // count):
-                    rows_ref[p, :, part * quarter : (part + 1) * quarter] = stack[
-                        part * count : (part + 1) * count
-                    ]
-                decode_copy(p).start()
-    for p in range(len(fresh_refs)):
-        decode_copy(p).wait()
-    if final:
-        for at in range(total_chunks):
-            out_copy(at).wait()
-
-
-def attend(rot, bias, own, got, first=0, sums=None, final=True, requests=None, fresh=None, decode=None, size=CHUNK):
-    rows = rot.shape[1]
-    new_count = rows // PER_KV
-    pieces = len(got)
-    early, unpack = sums is not None, requests is not None
-    operands = [rot, bias] + (list(sums) if early else [own]) + list(got)
-    specs = [VMEM] * len(operands)
-    shapes, out_specs, scratch, aliases = [], [], [], {}
+    def start():
+        request_copy.wait()
+        for p, fresh_ref in enumerate(fresh_refs):
+            stack = fresh_ref[...]
+            quarter = stack.shape[1]
+            for part in range(stack.shape[0] // count):
+                rows_ref[p, :, part * quarter : (part + 1) * quarter] = stack[part * count : (part + 1) * count]
+            decode_copy(p).start()
+
+    def wait():
+        for p in range(len(fresh_refs)):
+            decode_copy(p).wait()
+
+    return start, wait
+
+
+def spare_part(got):
+    return got.at[:, pl.ds(WIDTH, got.shape[1] - WIDTH)]
+
+
+def attend_kernel(pieces, unpack, rot_ref, bias_ref, own_ref, *refs):
+    got_refs, refs = refs[:pieces], refs[pieces:]
+    start, wait = None, None
     if unpack:
-        operands.append(requests)
-        specs.append(VMEM)
-        if early:
-            operands.append(decode)
-            specs.append(ANY)
-            aliases = {len(operands) - 1: 1 if final else 3}
-        else:
-            operands.append(fresh)
-            specs.append(VMEM)
-    if final:
-        shapes.append(jax.ShapeDtypeStruct((new_count, Q_HEADS * HEAD_DIM), jnp.bfloat16))
-        out_specs.append(ANY)
+        request_vmem, fresh_ref, result_ref, level_ref, decode_ref, *scratch = refs
+        fresh_refs = [spare_part(got) for got in got_refs] + [fresh_ref]
+        start, wait = unpacking(fresh_refs, 0, request_vmem, decode_ref, *scratch)
     else:
-        shapes += [jax.ShapeDtypeStruct((KV_HEADS, rows, HEAD_DIM), jnp.float32)] * 3
-        out_specs += [VMEM] * 3
+        result_ref, level_ref = refs
+    new_count = rot_ref.shape[1] // PER_KV
+    span = pieces * got_refs[0].shape[0] + own_ref.shape[1] - new_count
+    token = lax.broadcasted_iota(jnp.int32, (CHUNK, new_count), 0) % new_count
+    causal = jnp.where(lax.broadcasted_iota(jnp.int32, (CHUNK, new_count), 1) <= token, 0.0, MASKED)
+    bias = bias_ref[0:1, 0:span]
+    per_head = PER_KV * new_count // CHUNK
+    keys, values, highs = {}, {}, {}
+
+    def place(at):
+        return at // per_head, slice(at % per_head * CHUNK, (at % per_head + 1) * CHUNK)
+
+    def score(at):
+        head, rows = place(at)
+        if at % per_head == 0:
+            join_keys(keys, values, got_refs, own_ref, head)
+        return dot_keys(rot_ref[head, rows, :], keys[head])
+
+    def weigh(at, scores):
+        scores = jnp.concatenate([scores[:, :span] * SCALE + bias, scores[:, span:] * SCALE + causal], axis=1)
+        highs[at] = jnp.max(scores, axis=1, keepdims=True)
+        return jnp.exp2(scores - highs[at]).astype(jnp.bfloat16)
+
+    def mix(at, weights):
+        return jnp.dot(weights, values[at // per_head], preferred_element_type=jnp.float32)
+
+    def finish(at, mixed):
+        head, rows = place(at)
+        total = mixed[:, HEAD_DIM:]
+        result_ref[head, rows, :] = quotient(mixed[:, :HEAD_DIM], total)
+        level_ref[head, rows, :] = highs.pop(at) + jnp.log2(total)
+
+    staged(KV_HEADS * per_head, score, weigh, mix, finish, start)
     if unpack:
+        wait()
+
+
+def attend(rot, bias, own, got, requests=None, fresh=None):
+    rows, new_count = rot.shape[1], rot.shape[1] // PER_KV
+    operands = [rot, bias, own, *got]
+    shapes = [jax.ShapeDtypeStruct((KV_HEADS, rows, HEAD_DIM), jnp.float32)] * 2
+    out_specs, scratch = [VMEM] * 2, []
+    if requests is not None:
+        operands += [requests, fresh]
         slots = got[0].shape[0]
         count = (got[0].shape[1] - WIDTH) * slots // WIDTH
-        unpacked = pieces if early else pieces + 1
         shapes.append(jax.ShapeDtypeStruct((new_count // count, count, WIDTH), jnp.bfloat16))
         out_specs.append(ANY)
-        scratch += [
-            pltpu.VMEM((unpacked, count, WIDTH), jnp.bfloat16),
-            pltpu.SMEM(requests.shape, jnp.int32),
-            pltpu.SemaphoreType.DMA,
-            pltpu.SemaphoreType.DMA((unpacked,)),
-        ]
-    if final:
-        chunks = KV_HEADS * rows // size
-        scratch += [
-            pltpu.VMEM((chunks, new_count, size // new_count * HEAD_DIM), jnp.bfloat16),
+        scratch = unpack_scratch(len(got) + 1, count, requests)
+    return pl.pallas_call(
+        functools.partial(attend_kernel, len(got), requests is not None),
+        out_shape=tuple(shapes),
+        in_specs=[VMEM] * len(operands),
+        out_specs=tuple(out_specs),
+        scratch_shapes=scratch,
+        compiler_params=params(32),
+        name="attend",
+    )(*operands)
+
+
+def unpack_scratch(pieces, count, requests):
+    return [
+        pltpu.VMEM((pieces, count, WIDTH), jnp.bfloat16),
+        pltpu.SMEM(requests.shape, jnp.int32),
+        pltpu.SemaphoreType.DMA,
+        pltpu.SemaphoreType.DMA((pieces,)),
+    ]
+
+
+HEADROOM = 96.0
+
+
+def late_kernel(pieces, first, rot_ref, bias_ref, result_ref, level_ref, *refs):
+    got_refs, refs = refs[:pieces], refs[pieces:]
+    request_vmem, _, out_ref, decode_ref, done_ref, out_sems, *scratch = refs
+    start, wait = unpacking([spare_part(got) for got in got_refs], first, request_vmem, decode_ref, *scratch)
+    slots = got_refs[0].shape[0]
+    new_count = out_ref.shape[0]
+    size = LATE_CHUNK
+    heads_in = size // new_count
+    bias = bias_ref[0:1, first * slots : (first + pieces) * slots]
+    per_head = PER_KV * new_count // size
+    chunks = KV_HEADS * per_head
+    keys, values, excess = {}, {}, []
+
+    def place(at):
+        return at // per_head, slice(at % per_head * size, (at % per_head + 1) * size)
+
+    def out_copy(at):
+        width = heads_in * HEAD_DIM
+        return pltpu.make_async_copy(
+            done_ref.at[at], out_ref.at[:, pl.ds(pl.multiple_of(at * width, width), width)], out_sems.at[at]
+        )
+
+    def store(at, result):
+        for row in range(heads_in):
+            done_ref[at, :, column(row)] = result[row * new_count : (row + 1) * new_count].astype(jnp.bfloat16)
+        out_copy(at).start()
+
+    def score(at):
+        head, rows = place(at)
+        if at % per_head == 0:
+            join_keys(keys, values, got_refs, None, head)
+        return dot_keys(rot_ref[head, rows, :], keys[head])
+
+    def weigh(at, scores):
+        head, rows = place(at)
+        powers = scores * SCALE + bias - level_ref[head, rows, :]
+        excess.append(jnp.max(powers.reshape(size // 8, 8, HEAD_DIM), axis=0))
+        return jnp.exp2(powers).astype(jnp.bfloat16)
+
+    def mix(at, weights):
+        return jnp.dot(weights, values[at // per_head], preferred_element_type=jnp.float32)
+
+    def finish(at, mixed):
+        head, rows = place(at)
+        store(at, quotient(result_ref[head, rows, :] + mixed[:, :HEAD_DIM], 1.0 + mixed[:, HEAD_DIM:]))
+
+    staged(chunks, score, weigh, mix, finish, start)
+    most = jnp.max(functools.reduce(jnp.maximum, excess))
+    wait()
+    for at in range(chunks):
+        out_copy(at).wait()
+
+    @pl.when(most > HEADROOM)
+    def _():
+        for head in range(KV_HEADS):
+
+            def again(chunk, carry, head=head):
+                rows = pl.ds(pl.multiple_of(chunk * size, size), size)
+                scores = dot_keys(rot_ref[head, rows, :], keys[head]) * SCALE + bias
+                level = level_ref[head, rows, :]
+                high = jnp.maximum(level, jnp.max(scores, axis=1, keepdims=True))
+                factor = jnp.exp2(level - high)
+                weights = jnp.exp2(scores - high).astype(jnp.bfloat16)
+                mixed = jnp.dot(weights, values[head], preferred_element_type=jnp.float32)
+                at = head * per_head + chunk
+                summed = result_ref[head, rows, :] * factor + mixed[:, :HEAD_DIM]
+                store(at, quotient(summed, factor + mixed[:, HEAD_DIM:]))
+                out_copy(at).wait()
+                return carry
+
+            lax.fori_loop(0, per_head, again, 0)
+
+
+def attend_late(rot, bias, result, level, got, first, requests, decode):
+    rows, new_count = rot.shape[1], rot.shape[1] // PER_KV
+    operands = [rot, bias, result, level, *got, requests, decode]
+    chunks = KV_HEADS * rows // LATE_CHUNK
+    return pl.pallas_call(
+        functools.partial(late_kernel, len(got), first),
+        out_shape=(
+            jax.ShapeDtypeStruct((new_count, Q_HEADS * HEAD_DIM), jnp.bfloat16),
+            jax.ShapeDtypeStruct(decode.shape, jnp.bfloat16),
+        ),
+        in_specs=[VMEM] * (len(operands) - 1) + [ANY],
+        out_specs=(ANY, ANY),
+        scratch_shapes=[
+            pltpu.VMEM((chunks, new_count, LATE_CHUNK // new_count * HEAD_DIM), jnp.bfloat16),
             pltpu.SemaphoreType.DMA((chunks,)),
         ]
-    return pl.pallas_call(
-        functools.partial(attend_kernel, pieces, first, early, final, unpack, size),
-        out_shape=tuple(shapes),
-        in_specs=specs,
-        out_specs=tuple(out_specs),
-        scratch_shapes=scratch,
-        input_output_aliases=aliases,
+        + unpack_scratch(len(got), decode.shape[1], requests),
+        input_output_aliases={len(operands) - 1: 1},
         compiler_params=params(32),
-        name="attend_late" if early else "attend",
+        name="attend_late",
     )(*operands)
 
 
@@ -488,7 +540,9 @@
     located = jnp.arange(slots, dtype=jnp.int32)[None, :] * groups + inverse(stripe_map[request])[:, None]
     bias = jnp.where(located < length, 0.0, MASKED).astype(jnp.float32).reshape(1, groups * slots)
     keys = got[:, :slots].reshape(groups * slots, width)
-    (attended,) = attend(rot, jnp.broadcast_to(bias, (8, groups * slots)), own, [keys])
+    result, _ = attend(rot, jnp.broadcast_to(bias, (8, groups * slots)), own, [keys])
+    result = result.astype(jnp.bfloat16).reshape(KV_HEADS, PER_KV, new_count, HEAD_DIM)
+    attended = jnp.transpose(result, (2, 0, 1, 3)).reshape(new_count, Q_HEADS * HEAD_DIM)
     return attended, got[inverse(assignment), slots:]
 
 
@@ -511,10 +565,8 @@
     for block, t in zip(list(first_blocks) + list(other_blocks), [t for t in order if t]):
         got.append(lax.ppermute(block, "pg", [(source, source ^ t) for source in range(groups)]))
     soon = groups - LATE - 1
-    *sums, decode_kv = attend(rot, bias, own, got[:soon], final=False, requests=requests, fresh=fresh)
-    attended, decode_kv = attend(
-        rot, bias, None, got[soon:], first=soon + 1, sums=sums, requests=requests, decode=decode_kv, size=LATE_CHUNK
-    )
+    result, level, decode_kv = attend(rot, bias, own, got[:soon], requests, fresh)
+    attended, decode_kv = attend_late(rot, bias, result, level, got[soon:], soon + 1, requests, decode_kv)
     return (attended[None], decode_kv[None])
 
 

time: 42.6 us -> 40.1 us (0.941)
  waiting for transfers between devices: 2.33 us -> 0.67 us
  Pallas kernels: 10.4 us -> 9.89 us
    ppermute x15, waiting for transfers between devices: 2.33 us -> 0.67 us  [shards(): lax.ppermute(block, 'pg', [(source, source ^ t) for source in range(group...]
  transfers between devices with their start and end apart: 15 -> 15, of which waited for: 2 -> 2; matrix products, arithmetic and copies ran while one was open for 0% -> 0% of each run, Pallas kernels for 11% -> 12%
where the time goes in v1:
time: 40.1 us; the launch traced here: 39.9 us
  starting transfers between devices  26.3 us (66%)
  Pallas kernels  9.89 us (25%)
  local copies, waits for them, and re-layouts  2.32 us (6%)
  between operations  0.71 us (2%)
  waiting for transfers between devices  0.67 us (2%)
    ppermute x15, starting transfers between devices, shards(): lax.ppermute(block, 'pg', [(source, source ^ t) for source in range(group...  26.3 us
    pallas_call x1, Pallas kernels, attend(): pl.pallas_call(functools.partial(attend_kernel, len(got), requests is not...  3.87 us
    pallas_call x1, Pallas kernels, attend_late(): pl.pallas_call(functools.partial(late_kernel, len(got), first), out_shape...  2.62 us
    pallas_call x1, Pallas kernels, front(): pl.pallas_call(functools.partial(front_kernel, order), out_shape=[block]...  2.53 us
    unnamed x6, local copies, waits for them, and re-layouts  2.32 us
    pallas_call x1, Pallas kernels, rotate_queries(): pl.pallas_call(functools.partial(query_kernel, order), out_shape=[jax.Sha...  0.88 us
  transfers between devices with their start and end apart: 15, of which 2 were waited for; matrix products, arithmetic and copies ran while one was open for 0% of the time, Pallas kernels for 12%

profile of v1, /device:TPU:0, one launch (start us, length us, event | category | flops | bytes accessed | tf_op | source)
XLA Modules:
  0.0 39.9 jit_solution(14077217579626925479)
XLA Ops:
  0.6 2.5 %front.1 = (bf16[32,1280]{1,0:T(8,128)(2,1)}, bf16[32,1280]{1,0:T(8,128)(2,1)}, bf16[32,1280]{1,0:T(8,128)(2,1)}, bf16[32,1280]{1,0:T(8,128)(2,1)}, f32[1296,128]{1,0:T(8,128)}) custom-call(s32[1]{0:T(128)} %bitcast.me_ref, s32[16]{0:T(128)} %assign_any.1, s32[16]{0:T(128)} %length_any.1, s32[16,16]{1,0:T(8,128)} %owner_any.1, s32[16,16]{1,0:T(8,128)} %stripe_any.1, ...), custom_call_target="tpu_custom_call" | custom-call | tf_op jit(solution)/shard_map/front/pallas_call | solution.py:176
  3.2 4.1 %collective-permute-start = (bf16[32,1280]{1,0:T(8,128)(2,1)}, bf16[32,1280]{1,0:T(8,128)(2,1)S(1)}, u32[]{:S(2)}, u32[]{:S(2)}) collective-permute-start(bf16[32,1280]{1,0:T(8,128)(2,1)} %get-tuple-element.32), channel_id=1, source_target_pairs={{0,8},{1,9},{2,10},{3,11},{4,12},{5,13},{6,14},{7,15},{8,0},{9,1},... | collective-permute-start | bytes 245768 | tf_op jit(solution)/shard_map/ppermute | solution.py:566
  7.3 1.7 %collective-permute-start.1 = (bf16[32,1280]{1,0:T(8,128)(2,1)}, bf16[32,1280]{1,0:T(8,128)(2,1)S(1)}, u32[]{:S(2)}, u32[]{:S(2)}) collective-permute-start(bf16[32,1280]{1,0:T(8,128)(2,1)} %get-tuple-element.33), channel_id=1, source_target_pairs={{0,7},{1,6},{2,5},{3,4},{4,3},{5,2},{6,1},{7,0},{8,15},{9,14},{10,... | collective-permute-start | bytes 245768 | tf_op jit(solution)/shard_map/ppermute | solution.py:566
  9.0 0.9 %collective-permute-start.2 = (bf16[32,1280]{1,0:T(8,128)(2,1)}, bf16[32,1280]{1,0:T(8,128)(2,1)S(1)}, u32[]{:S(2)}, u32[]{:S(2)}) collective-permute-start(bf16[32,1280]{1,0:T(8,128)(2,1)} %get-tuple-element.34), channel_id=1, source_target_pairs={{0,9},{1,8},{2,11},{3,10},{4,13},{5,12},{6,15},{7,14},{8,1},{9,0},... | collective-permute-start | bytes 245768 | tf_op jit(solution)/shard_map/ppermute | solution.py:566
  9.9 0.1 collective-permute-start.3
  10.0 1.2 %copy-done.1 = bf16[1,128,4096]{2,1,0:T(8,128)(2,1)S(1)} copy-done((bf16[1,128,4096]{2,1,0:T(8,128)(2,1)S(1)}, bf16[1,128,4096]{2,1,0:T(8,128)(2,1)}, u32[]{:S(2)}) %copy-start.1) | copy-done | bytes 1048600
  11.2 1.1 %copy-done.2 = f32[1296,128]{1,0:T(8,128)S(1)} copy-done((f32[1296,128]{1,0:T(8,128)S(1)}, f32[1296,128]{1,0:T(8,128)}, u32[]{:S(2)}) %copy-start.2) | copy-done | bytes 663576
  12.3 0.9 %rotate_queries.1 = (bf16[32,1280]{1,0:T(8,128)(2,1)S(1)}, bf16[32,1280]{1,0:T(8,128)(2,1)S(1)}, bf16[32,1280]{1,0:T(8,128)(2,1)S(1)}, bf16[32,1280]{1,0:T(8,128...) custom-call(f32[1296,128]{1,0:T(8,128)S(1)} %copy-done.2, ...), custom_call_target="tpu_custom_call" | custom-call | tf_op jit(solution)/shard_map/rotate_queries/pallas_call | solution.py:249
  13.2 3.9 %collective-permute-start.4 = (bf16[32,1280]{1,0:T(8,128)(2,1)S(1)}, bf16[32,1280]{1,0:T(8,128)(2,1)S(1)}, u32[]{:S(2)}, u32[]{:S(2)}) collective-permute-start(bf16[32,1280]{1,0:T(8,128)(2,1)S(1)} %get-tuple-element.36), channel_id=1, source_target_pairs={{0,10},{1,11},{2,8},{3,9},{4,14},{5,15},{6,12},{7,13},{8,2},{9,3},... | collective-permute-start | bytes 245768 | tf_op jit(solution)/shard_map/ppermute | solution.py:566
  17.1 0.0 collective-permute-done.refs_0_
  17.1 0.2 collective-permute-start.5
  17.3 0.0 collective-permute-done.1.refs_1_
  17.3 1.4 %collective-permute-start.6 = (bf16[32,1280]{1,0:T(8,128)(2,1)S(1)}, bf16[32,1280]{1,0:T(8,128)(2,1)S(1)}, u32[]{:S(2)}, u32[]{:S(2)}) collective-permute-start(bf16[32,1280]{1,0:T(8,128)(2,1)S(1)} %get-tuple-element.38), channel_id=1, source_target_pairs={{0,11},{1,10},{2,9},{3,8},{4,15},{5,14},{6,13},{7,12},{8,3},{9,2},... | collective-permute-start | bytes 245768 | tf_op jit(solution)/shard_map/ppermute | solution.py:566
  18.7 0.3 collective-permute-start.7
  18.9 0.0 collective-permute-done.3.refs_3_
  18.9 3.8 %collective-permute-start.8 = (bf16[32,1280]{1,0:T(8,128)(2,1)S(1)}, bf16[32,1280]{1,0:T(8,128)(2,1)S(1)}, u32[]{:S(2)}, u32[]{:S(2)}) collective-permute-start(bf16[32,1280]{1,0:T(8,128)(2,1)S(1)} %get-tuple-element.40), channel_id=1, source_target_pairs={{0,12},{1,13},{2,14},{3,15},{4,8},{5,9},{6,10},{7,11},{8,4},{9,5},... | collective-permute-start | bytes 245768 | tf_op jit(solution)/shard_map/ppermute | solution.py:566
  22.7 0.5 %collective-permute-done.5.refs_5_ = bf16[32,1280]{1,0:T(8,128)(2,1)S(1)} collective-permute-done((bf16[32,1280]{1,0:T(8,128)(2,1)S(1)}, bf16[32,1280]{1,0:T(8,128)(2,1)S(1)}, u32[]{:S(2)}, u32[]{:S(2)}) %collective-permute-start.5) | collective-permute-done | bytes 81952 | tf_op jit(solution)/shard_map/ppermute | solution.py:566
  23.2 1.1 %collective-permute-start.10 = (bf16[32,1280]{1,0:T(8,128)(2,1)S(1)}, bf16[32,1280]{1,0:T(8,128)(2,1)S(1)}, u32[]{:S(2)}, u32[]{:S(2)}) collective-permute-start(bf16[32,1280]{1,0:T(8,128)(2,1)S(1)} %get-tuple-element.42), channel_id=1, source_target_pairs={{0,2},{1,3},{2,0},{3,1},{4,6},{5,7},{6,4},{7,5},{8,10},{9,11},{10,... | collective-permute-start | bytes 245768 | tf_op jit(solution)/shard_map/ppermute | solution.py:566
  24.3 4.0 %collective-permute-start.11 = (bf16[32,1280]{1,0:T(8,128)(2,1)S(1)}, bf16[32,1280]{1,0:T(8,128)(2,1)S(1)}, u32[]{:S(2)}, u32[]{:S(2)}) collective-permute-start(bf16[32,1280]{1,0:T(8,128)(2,1)S(1)} %get-tuple-element.47), channel_id=1, source_target_pairs={{0,13},{1,12},{2,15},{3,14},{4,9},{5,8},{6,11},{7,10},{8,5},{9,4},... | collective-permute-start | bytes 245768 | tf_op jit(solution)/shard_map/ppermute | solution.py:566
  28.3 1.9 %collective-permute-start.12 = (bf16[32,1280]{1,0:T(8,128)(2,1)S(1)}, bf16[32,1280]{1,0:T(8,128)(2,1)S(1)}, u32[]{:S(2)}, u32[]{:S(2)}) collective-permute-start(bf16[32,1280]{1,0:T(8,128)(2,1)S(1)} %get-tuple-element.48), channel_id=1, source_target_pairs={{0,14},{1,15},{2,12},{3,13},{4,10},{5,11},{6,8},{7,9},{8,6},{9,7},... | collective-permute-start | bytes 245768 | tf_op jit(solution)/shard_map/ppermute | solution.py:566
  30.3 2.9 %collective-permute-start.14 = (bf16[32,1280]{1,0:T(8,128)(2,1)S(1)}, bf16[32,1280]{1,0:T(8,128)(2,1)S(1)}, u32[]{:S(2)}, u32[]{:S(2)}) collective-permute-start(bf16[32,1280]{1,0:T(8,128)(2,1)S(1)} %get-tuple-element.50), channel_id=1, source_target_pairs={{0,15},{1,14},{2,13},{3,12},{4,11},{5,10},{6,9},{7,8},{8,7},{9,6},... | collective-permute-start | bytes 245768 | tf_op jit(solution)/shard_map/ppermute | solution.py:566
  33.2 3.9 %attend.1 = (f32[4,1024,128]{2,1,0:T(8,128)S(1)}, f32[4,1024,128]{2,1,0:T(8,128)S(1)}, bf16[16,8,1024]{2,1,0:T(8,128)(2,1)}) custom-call(bf16[4,1024,128]{2,1,0:T(8,128)(2,1)S(1)} %get-tuple-element.29.rot_ref, f32[8,512]{1,0:T(8,128)S(1)} %get-tuple-element.30.bias_ref, bf16[8,160,128]{2,1,0:T(8,128)(2,1)S(1)} %get-tuple-element.31.own_ref, ...), custom_call_target="tpu_custom_call" | custom-call | tf_op jit(solution)/shard_map/attend/pallas_call | solution.py:390
  37.1 0.1 collective-permute-done.14.refs_3_
  37.2 2.6 %attend_late.1 = (bf16[128,4096]{1,0:T(8,128)(2,1)}, bf16[16,8,1024]{2,1,0:T(8,128)(2,1)}) custom-call(bf16[4,1024,128]{2,1,0:T(8,128)(2,1)S(1)} %get-tuple-element.29.rot_ref, f32[8,512]{1,0:T(8,128)S(1)} %get-tuple-element.30.bias_ref, f32[4,1024,128]{2,1,0:T(8,128)S(1)} %get-tuple-element.45.result_ref, ...), custom_call_target="tpu_custom_call", output_to_operand_aliasing={{1}: (9, {})} | custom-call | tf_op jit(solution)/shard_map/attend_late/pallas_call | solution.py:490
  (16 shorter events, 0.0 us)
Async XLA Ops:
  0.6 9.4 %copy-start = (bf16[1,16,32,1024]{3,2,1,0:T(8,128)(2,1)S(1)}, bf16[1,16,32,1024]{3,2,1,0:T(8,128)(2,1)}, u32[]{:S(2)}) copy-start(bf16[1,16,32,1024]{3,2,1,0:T(8,128)(2,1)} %param.10) | copy-start | bytes 3145732
  3.2 13.9 %collective-permute-start = (bf16[32,1280]{1,0:T(8,128)(2,1)}, bf16[32,1280]{1,0:T(8,128)(2,1)S(1)}, u32[]{:S(2)}, u32[]{:S(2)}) collective-permute-start(bf16[32,1280]{1,0:T(8,128)(2,1)} %get-tuple-element.32), channel_id=1, source_target_pairs={{0,8},{1,9},{2,10},{3,11},{4,12},{5,13},{6,14},{7,15},{8,0},{9,1},... | collective-permute-start | bytes 245768 | tf_op jit(solution)/shard_map/ppermute | solution.py:566
  7.3 10.0 %collective-permute-start.1 = (bf16[32,1280]{1,0:T(8,128)(2,1)}, bf16[32,1280]{1,0:T(8,128)(2,1)S(1)}, u32[]{:S(2)}, u32[]{:S(2)}) collective-permute-start(bf16[32,1280]{1,0:T(8,128)(2,1)} %get-tuple-element.33), channel_id=1, source_target_pairs={{0,7},{1,6},{2,5},{3,4},{4,3},{5,2},{6,1},{7,0},{8,15},{9,14},{10,... | collective-permute-start | bytes 245768 | tf_op jit(solution)/shard_map/ppermute | solution.py:566
  9.0 9.7 %collective-permute-start.2 = (bf16[32,1280]{1,0:T(8,128)(2,1)}, bf16[32,1280]{1,0:T(8,128)(2,1)S(1)}, u32[]{:S(2)}, u32[]{:S(2)}) collective-permute-start(bf16[32,1280]{1,0:T(8,128)(2,1)} %get-tuple-element.34), channel_id=1, source_target_pairs={{0,9},{1,8},{2,11},{3,10},{4,13},{5,12},{6,15},{7,14},{8,1},{9,0},... | collective-permute-start | bytes 245768 | tf_op jit(solution)/shard_map/ppermute | solution.py:566
  9.9 9.1 %collective-permute-start.3 = (bf16[32,1280]{1,0:T(8,128)(2,1)}, bf16[32,1280]{1,0:T(8,128)(2,1)S(1)}, u32[]{:S(2)}, u32[]{:S(2)}) collective-permute-start(bf16[32,1280]{1,0:T(8,128)(2,1)} %get-tuple-element.35), channel_id=1, source_target_pairs={{0,6},{1,7},{2,4},{3,5},{4,2},{5,3},{6,0},{7,1},{8,14},{9,15},{10,... | collective-permute-start | bytes 245768 | tf_op jit(solution)/shard_map/ppermute | solution.py:566
  10.0 1.2 %copy-start.1 = (bf16[1,128,4096]{2,1,0:T(8,128)(2,1)S(1)}, bf16[1,128,4096]{2,1,0:T(8,128)(2,1)}, u32[]{:S(2)}) copy-start(bf16[1,128,4096]{2,1,0:T(8,128)(2,1)} %param.8) | copy-start | bytes 3145732
  11.2 1.1 %copy-start.2 = (f32[1296,128]{1,0:T(8,128)S(1)}, f32[1296,128]{1,0:T(8,128)}, u32[]{:S(2)}) copy-start(f32[1296,128]{1,0:T(8,128)} %get-tuple-element.28.info_ref) | copy-start | bytes 1990660
  13.2 9.5 %collective-permute-start.4 = (bf16[32,1280]{1,0:T(8,128)(2,1)S(1)}, bf16[32,1280]{1,0:T(8,128)(2,1)S(1)}, u32[]{:S(2)}, u32[]{:S(2)}) collective-permute-start(bf16[32,1280]{1,0:T(8,128)(2,1)S(1)} %get-tuple-element.36), channel_id=1, source_target_pairs={{0,10},{1,11},{2,8},{3,9},{4,14},{5,15},{6,12},{7,13},{8,2},{9,3},... | collective-permute-start | bytes 245768 | tf_op jit(solution)/shard_map/ppermute | solution.py:566
  17.1 6.2 %collective-permute-start.5 = (bf16[32,1280]{1,0:T(8,128)(2,1)S(1)}, bf16[32,1280]{1,0:T(8,128)(2,1)S(1)}, u32[]{:S(2)}, u32[]{:S(2)}) collective-permute-start(bf16[32,1280]{1,0:T(8,128)(2,1)S(1)} %get-tuple-element.37), channel_id=1, source_target_pairs={{0,5},{1,4},{2,7},{3,6},{4,1},{5,0},{6,3},{7,2},{8,13},{9,12},{10,... | collective-permute-start | bytes 245768 | tf_op jit(solution)/shard_map/ppermute | solution.py:566
  17.3 7.1 %collective-permute-start.6 = (bf16[32,1280]{1,0:T(8,128)(2,1)S(1)}, bf16[32,1280]{1,0:T(8,128)(2,1)S(1)}, u32[]{:S(2)}, u32[]{:S(2)}) collective-permute-start(bf16[32,1280]{1,0:T(8,128)(2,1)S(1)} %get-tuple-element.38), channel_id=1, source_target_pairs={{0,11},{1,10},{2,9},{3,8},{4,15},{5,14},{6,13},{7,12},{8,3},{9,2},... | collective-permute-start | bytes 245768 | tf_op jit(solution)/shard_map/ppermute | solution.py:566
  18.7 9.7 %collective-permute-start.7 = (bf16[32,1280]{1,0:T(8,128)(2,1)S(1)}, bf16[32,1280]{1,0:T(8,128)(2,1)S(1)}, u32[]{:S(2)}, u32[]{:S(2)}) collective-permute-start(bf16[32,1280]{1,0:T(8,128)(2,1)S(1)} %get-tuple-element.39), channel_id=1, source_target_pairs={{0,4},{1,5},{2,6},{3,7},{4,0},{5,1},{6,2},{7,3},{8,12},{9,13},{10,... | collective-permute-start | bytes 245768 | tf_op jit(solution)/shard_map/ppermute | solution.py:566
  18.9 11.3 %collective-permute-start.8 = (bf16[32,1280]{1,0:T(8,128)(2,1)S(1)}, bf16[32,1280]{1,0:T(8,128)(2,1)S(1)}, u32[]{:S(2)}, u32[]{:S(2)}) collective-permute-start(bf16[32,1280]{1,0:T(8,128)(2,1)S(1)} %get-tuple-element.40), channel_id=1, source_target_pairs={{0,12},{1,13},{2,14},{3,15},{4,8},{5,9},{6,10},{7,11},{8,4},{9,5},... | collective-permute-start | bytes 245768 | tf_op jit(solution)/shard_map/ppermute | solution.py:566
  22.7 7.6 %collective-permute-start.9 = (bf16[32,1280]{1,0:T(8,128)(2,1)S(1)}, bf16[32,1280]{1,0:T(8,128)(2,1)S(1)}, u32[]{:S(2)}, u32[]{:S(2)}) collective-permute-start(bf16[32,1280]{1,0:T(8,128)(2,1)S(1)} %get-tuple-element.41), channel_id=1, source_target_pairs={{0,3},{1,2},{2,1},{3,0},{4,7},{5,6},{6,5},{7,4},{8,11},{9,10},{10,... | collective-permute-start | bytes 245768 | tf_op jit(solution)/shard_map/ppermute | solution.py:566
  23.2 10.0 %collective-permute-start.10 = (bf16[32,1280]{1,0:T(8,128)(2,1)S(1)}, bf16[32,1280]{1,0:T(8,128)(2,1)S(1)}, u32[]{:S(2)}, u32[]{:S(2)}) collective-permute-start(bf16[32,1280]{1,0:T(8,128)(2,1)S(1)} %get-tuple-element.42), channel_id=1, source_target_pairs={{0,2},{1,3},{2,0},{3,1},{4,6},{5,7},{6,4},{7,5},{8,10},{9,11},{10,... | collective-permute-start | bytes 245768 | tf_op jit(solution)/shard_map/ppermute | solution.py:566
  24.3 12.8 %collective-permute-start.11 = (bf16[32,1280]{1,0:T(8,128)(2,1)S(1)}, bf16[32,1280]{1,0:T(8,128)(2,1)S(1)}, u32[]{:S(2)}, u32[]{:S(2)}) collective-permute-start(bf16[32,1280]{1,0:T(8,128)(2,1)S(1)} %get-tuple-element.47), channel_id=1, source_target_pairs={{0,13},{1,12},{2,15},{3,14},{4,9},{5,8},{6,11},{7,10},{8,5},{9,4},... | collective-permute-start | bytes 245768 | tf_op jit(solution)/shard_map/ppermute | solution.py:566
  28.3 8.7 %collective-permute-start.12 = (bf16[32,1280]{1,0:T(8,128)(2,1)S(1)}, bf16[32,1280]{1,0:T(8,128)(2,1)S(1)}, u32[]{:S(2)}, u32[]{:S(2)}) collective-permute-start(bf16[32,1280]{1,0:T(8,128)(2,1)S(1)} %get-tuple-element.48), channel_id=1, source_target_pairs={{0,14},{1,15},{2,12},{3,13},{4,10},{5,11},{6,8},{7,9},{8,6},{9,7},... | collective-permute-start | bytes 245768 | tf_op jit(solution)/shard_map/ppermute | solution.py:566
  30.3 6.8 %collective-permute-start.13 = (bf16[32,1280]{1,0:T(8,128)(2,1)S(1)}, bf16[32,1280]{1,0:T(8,128)(2,1)S(1)}, u32[]{:S(2)}, u32[]{:S(2)}) collective-permute-start(bf16[32,1280]{1,0:T(8,128)(2,1)S(1)} %get-tuple-element.49), channel_id=1, source_target_pairs={{0,1},{1,0},{2,3},{3,2},{4,5},{5,4},{6,7},{7,6},{8,9},{9,8},{10,11... | collective-permute-start | bytes 245768 | tf_op jit(solution)/shard_map/ppermute | solution.py:566
  30.3 6.9 %collective-permute-start.14 = (bf16[32,1280]{1,0:T(8,128)(2,1)S(1)}, bf16[32,1280]{1,0:T(8,128)(2,1)S(1)}, u32[]{:S(2)}, u32[]{:S(2)}) collective-permute-start(bf16[32,1280]{1,0:T(8,128)(2,1)S(1)} %get-tuple-element.50), channel_id=1, source_target_pairs={{0,15},{1,14},{2,13},{3,12},{4,11},{5,10},{6,9},{7,8},{8,7},{9,6},... | collective-permute-start | bytes 245768 | tf_op jit(solution)/shard_map/ppermute | solution.py:566

commit v2 on v1

--- a/solution.py
+++ b/solution.py
@@ -20,7 +20,6 @@
 MASKED = -1e30
 SCALE = HEAD_DIM ** -0.5 / math.log(2.0)
 CHUNK = 256
-LATE = 4
 LATE_CHUNK = 256
 AHEAD = 4
 
@@ -37,12 +36,18 @@
     return slice(head * HEAD_DIM, (head + 1) * HEAD_DIM)
 
 
-def order_of(groups):
+def far_partners(groups):
+    quarter = groups // 4
+    next_to, beyond = list(range(2 * quarter, 3 * quarter)), list(range(3 * quarter, 4 * quarter))
+    order = []
+    for at in range(quarter):
+        order += [next_to[at ^ (at >> 1)], beyond[(at ^ (at >> 1)) ^ 1]]
+    return order
+
+
+def holder_of(p, me, groups, far):
     half = groups // 2
-    far, near = list(range(half, 2 * half)), list(range(half - 1, 0, -1))
-    order = [(far if kind == "f" else near).pop(0) for kind in "fnfnfnfnfnnffnf"]
-    order.insert(groups - LATE - 1, 0)
-    return order
+    return me // half * half + p if p < half else me ^ far[p - half]
 
 
 def rotation_tables(rows):
@@ -88,7 +93,7 @@
 
 
 def front_kernel(
-    order, me_ref, assign_any, length_any, owner_any, stripe_any, block_any, table_any, pool_any, *refs
+    far, me_ref, assign_any, length_any, owner_any, stripe_any, block_any, table_any, pool_any, *refs
 ):
     groups, slots, width = pool_any.shape
     send_refs, info_any, refs = refs[:AHEAD], refs[AHEAD], refs[AHEAD + 1 :]
@@ -134,10 +139,10 @@
         copy.wait()
     sends = []
     for p in range(AHEAD):
-        pack_ref[p, :, 0:width] = pool_ref[assign_ref[me ^ order[p]]]
+        pack_ref[p, :, 0:width] = pool_ref[assign_ref[me ^ far[p]]]
         for lanes in range(quarter):
             pack_ref[p, :, width + lanes * HEAD_DIM : width + (lanes + 1) * HEAD_DIM] = fresh_rows(
-                info_ref, at["new"], residue_ref[me ^ order[p]], new_count, count, quarter, lanes
+                info_ref, at["new"], residue_ref[me ^ far[p]], new_count, count, quarter, lanes
             ).astype(jnp.bfloat16)
         sends.append(pltpu.make_async_copy(pack_ref.at[p], send_refs[p], send_sems.at[p]))
         sends[-1].start()
@@ -149,7 +154,7 @@
     piece, slot = row * per_row + lane // slots, lane % slots
     holder, requests, residues = jnp.zeros_like(lane), jnp.zeros_like(lane), jnp.zeros_like(lane)
     for p in range(groups):
-        other = me ^ order[p]
+        other = holder_of(p, me, groups, far)
         holder = jnp.where(piece == p, other, holder)
         requests = jnp.where(lane == p, assign_ref[other], requests)
         residues = jnp.where(lane == p, residue_ref[other], residues)
@@ -167,14 +172,14 @@
     info_copy(1, 0, at["new"]).wait()
 
 
-def front(order, me, assignment, prefix_len, owner_map, stripe_map, block_kv, table, pool):
+def front(far, me, assignment, prefix_len, owner_map, stripe_map, block_kv, table, pool):
     groups, slots, width = pool.shape
     new_count = block_kv.shape[0]
     count = new_count // groups
     block = jax.ShapeDtypeStruct((slots, width + width * count // slots), jnp.bfloat16)
     info = jax.ShapeDtypeStruct((info_rows(new_count)[1], HEAD_DIM), jnp.float32)
     *blocks, info = pl.pallas_call(
-        functools.partial(front_kernel, order),
+        functools.partial(front_kernel, far),
         out_shape=[block] * AHEAD + [info],
         in_specs=[SMEM] + [ANY] * 7,
         out_specs=[ANY] * (AHEAD + 1),
@@ -200,14 +205,14 @@
     return blocks, info
 
 
-def query_kernel(order, info_ref, q_ref, pool_ref, *refs):
+def query_kernel(info_ref, q_ref, pool_ref, near_ref, *refs):
     groups, slots, width = pool_ref.shape
-    sent = groups - 1 - AHEAD
-    send_refs, refs = refs[:sent], refs[sent:]
-    rot_ref, own_ref, fresh_ref, bias_ref, request_ref, scalar_ref, scalar_sem = refs
+    half = groups // 2
+    send_refs, refs = refs[: half - AHEAD], refs[half - AHEAD :]
+    rot_ref, own_ref, bias_ref, request_ref, scalar_ref, scalar_sem = refs
     new_count = q_ref.shape[0]
     count = new_count // groups
-    quarter = fresh_ref.shape[1] // HEAD_DIM
+    quarter = width * count // slots // HEAD_DIM
     at, _ = info_rows(new_count)
     scalar_copy = pltpu.make_async_copy(info_ref.at[pl.ds(at["scalars"], 8)], scalar_ref, scalar_sem)
     scalar_copy.start()
@@ -219,40 +224,35 @@
     request_ref[...] = info_ref[at["scalars"] : at["scalars"] + 8].astype(jnp.int32)
     for head in range(2 * KV_HEADS):
         rows = at["new"] + head * new_count
-        own_ref[head, slots : slots + new_count] = info_ref[rows : rows + new_count].astype(jnp.bfloat16)
+        own_ref[head] = info_ref[rows : rows + new_count].astype(jnp.bfloat16)
     for head in range(Q_HEADS):
         rows = slice((head % PER_KV) * new_count, (head % PER_KV + 1) * new_count)
         rot_ref[head // PER_KV, rows, :] = turn(q_ref[:, column(head)], cosine, sine)
     scalar_copy.wait()
-    sends = list(send_refs)
-    for p in range(AHEAD, groups):
-        request = scalar_ref[0, p].astype(jnp.int32)
+    targets = [near_ref.at[p] for p in range(half)] + [None] * AHEAD + list(send_refs)
+    for p, target in enumerate(targets):
+        if target is None:
+            continue
+        target[:, 0:width] = pool_ref[scalar_ref[0, p].astype(jnp.int32)]
         residue = scalar_ref[1, p].astype(jnp.int32)
-        if order[p] == 0:
-            target, base = fresh_ref, 0
-            for head in range(2 * KV_HEADS):
-                own_ref[head, 0:slots] = pool_ref[request, :, column(head)]
-        else:
-            target, base = sends.pop(0), width
-            target[:, 0:width] = pool_ref[request]
         for lanes in range(quarter):
-            target[:, base + lanes * HEAD_DIM : base + (lanes + 1) * HEAD_DIM] = fresh_rows(
+            target[:, width + lanes * HEAD_DIM : width + (lanes + 1) * HEAD_DIM] = fresh_rows(
                 info_ref, at["new"], residue, new_count, count, quarter, lanes
             ).astype(jnp.bfloat16)
 
 
-def rotate_queries(order, info, queries, pool):
+def rotate_queries(info, queries, pool):
     groups, slots, width = pool.shape
     new_count = queries.shape[0]
-    spare = width * (new_count // groups) // slots
-    sent = groups - 1 - AHEAD
-    outs = pl.pallas_call(
-        functools.partial(query_kernel, order),
-        out_shape=[jax.ShapeDtypeStruct((slots, width + spare), jnp.bfloat16)] * sent
+    block = (slots, width + width * (new_count // groups) // slots)
+    sent = groups // 2 - AHEAD
+    near, *outs = pl.pallas_call(
+        query_kernel,
+        out_shape=[jax.ShapeDtypeStruct((groups // 2,) + block, jnp.bfloat16)]
+        + [jax.ShapeDtypeStruct(block, jnp.bfloat16)] * sent
         + [
             jax.ShapeDtypeStruct((KV_HEADS, PER_KV * new_count, HEAD_DIM), jnp.bfloat16),
-            jax.ShapeDtypeStruct((2 * KV_HEADS, slots + new_count, HEAD_DIM), jnp.bfloat16),
-            jax.ShapeDtypeStruct((slots, spare), jnp.bfloat16),
+            jax.ShapeDtypeStruct((2 * KV_HEADS, new_count, HEAD_DIM), jnp.bfloat16),
             jax.ShapeDtypeStruct((8, groups * slots), jnp.float32),
             jax.ShapeDtypeStruct((8, HEAD_DIM), jnp.int32),
         ],
@@ -262,7 +262,7 @@
         compiler_params=params(32),
         name="rotate_queries",
     )(info, queries, pool)
-    return outs[:sent], outs[sent:]
+    return near, outs[:sent], outs[sent:]
 
 
 def quotient(summed, total):
@@ -330,17 +330,23 @@
     return got.at[:, pl.ds(WIDTH, got.shape[1] - WIDTH)]
 
 
-def attend_kernel(pieces, unpack, rot_ref, bias_ref, own_ref, *refs):
-    got_refs, refs = refs[:pieces], refs[pieces:]
+def pieces_of(refs):
+    pieces = []
+    for ref in refs:
+        pieces += [ref] if len(ref.shape) == 2 else [ref.at[i] for i in range(ref.shape[0])]
+    return pieces
+
+
+def attend_kernel(arrays, unpack, rot_ref, bias_ref, own_ref, *refs):
+    got_refs, refs = pieces_of(refs[:arrays]), refs[arrays:]
     start, wait = None, None
     if unpack:
-        request_vmem, fresh_ref, result_ref, level_ref, decode_ref, *scratch = refs
-        fresh_refs = [spare_part(got) for got in got_refs] + [fresh_ref]
-        start, wait = unpacking(fresh_refs, 0, request_vmem, decode_ref, *scratch)
+        request_vmem, result_ref, level_ref, decode_ref, *scratch = refs
+        start, wait = unpacking([spare_part(got) for got in got_refs], 0, request_vmem, decode_ref, *scratch)
     else:
         result_ref, level_ref = refs
     new_count = rot_ref.shape[1] // PER_KV
-    span = pieces * got_refs[0].shape[0] + own_ref.shape[1] - new_count
+    span = len(got_refs) * got_refs[0].shape[0]
     token = lax.broadcasted_iota(jnp.int32, (CHUNK, new_count), 0) % new_count
     causal = jnp.where(lax.broadcasted_iota(jnp.int32, (CHUNK, new_count), 1) <= token, 0.0, MASKED)
     bias = bias_ref[0:1, 0:span]
@@ -375,18 +381,18 @@
         wait()
 
 
-def attend(rot, bias, own, got, requests=None, fresh=None):
+def attend(rot, bias, own, got, requests=None):
     rows, new_count = rot.shape[1], rot.shape[1] // PER_KV
     operands = [rot, bias, own, *got]
     shapes = [jax.ShapeDtypeStruct((KV_HEADS, rows, HEAD_DIM), jnp.float32)] * 2
     out_specs, scratch = [VMEM] * 2, []
     if requests is not None:
-        operands += [requests, fresh]
-        slots = got[0].shape[0]
-        count = (got[0].shape[1] - WIDTH) * slots // WIDTH
+        operands.append(requests)
+        slots, width = got[-1].shape
+        count = (width - WIDTH) * slots // WIDTH
         shapes.append(jax.ShapeDtypeStruct((new_count // count, count, WIDTH), jnp.bfloat16))
         out_specs.append(ANY)
-        scratch = unpack_scratch(len(got) + 1, count, requests)
+        scratch = unpack_scratch(len(pieces_of(got)), count, requests)
     return pl.pallas_call(
         functools.partial(attend_kernel, len(got), requests is not None),
         out_shape=tuple(shapes),
@@ -557,16 +563,18 @@
             me, assignment, prefix_len, stripe_map, owner_map, queries, block_kv, pool
         )
         return (attended[None], decode_kv[None])
-    order = order_of(groups)
+    half = groups // 2
+    far = far_partners(groups)
     table = rotation_tables(new_count)
-    first_blocks, info = front(order, me, assignment, prefix_len, owner_map, stripe_map, block_kv, table, pool)
-    other_blocks, (rot, own, fresh, bias, requests) = rotate_queries(order, info, queries, pool)
+    blocks, info = front(far, me, assignment, prefix_len, owner_map, stripe_map, block_kv, table, pool)
+    near, other_blocks, (rot, own, bias, requests) = rotate_queries(info, queries, pool)
     got = []
-    for block, t in zip(list(first_blocks) + list(other_blocks), [t for t in order if t]):
+    for block, t in zip(list(blocks) + list(other_blocks), far):
         got.append(lax.ppermute(block, "pg", [(source, source ^ t) for source in range(groups)]))
-    soon = groups - LATE - 1
-    result, level, decode_kv = attend(rot, bias, own, got[:soon], requests, fresh)
-    attended, decode_kv = attend_late(rot, bias, result, level, got[soon:], soon + 1, requests, decode_kv)
+    halves = [list(range(low, low + half)) for low in range(0, groups, half)]
+    got_near = lax.all_to_all(near, "pg", split_axis=0, concat_axis=0, axis_index_groups=halves, tiled=True)
+    result, level, decode_kv = attend(rot, bias, own, [got_near] + got[:AHEAD], requests)
+    attended, decode_kv = attend_late(rot, bias, result, level, got[AHEAD:], half + AHEAD, requests, decode_kv)
     return (attended[None], decode_kv[None])
 
 

time: 40.1 us -> 48.1 us (1.20)
  starting transfers between devices: 26.3 us -> 30.8 us
  waiting for transfers between devices: 0.67 us -> 3.34 us
  Pallas kernels: 9.89 us -> 10.6 us
    all_to_all x0 -> x1, starting transfers between devices: none -> 5.27 us  [shards(): lax.all_to_all(near, 'pg', split_axis=0, concat_axis=0, axis_index_groups...]
    ppermute x15 -> x8, waiting for transfers between devices: 0.67 us -> 3.34 us  [shards(): lax.ppermute(block, 'pg', [(source, source ^ t) for source in range(group...]
    pallas_call x2, Pallas kernels: 3.4 us -> 4.26 us  [the longest x1 2.53 us: front(): pl.pallas_call(functools.partial(front_kernel, far), out_shape=[block] *...]
    ppermute x15 -> x8, starting transfers between devices: 26.3 us -> 25.5 us  [shards(): lax.ppermute(block, 'pg', [(source, source ^ t) for source in range(group...]
    unnamed x6 -> x14, local copies, waits for them, and re-layouts: 2.32 us -> 2.33 us
  transfers between devices with their start and end apart: 15 -> 9, of which waited for: 2 -> 3; matrix products, arithmetic and copies ran while one was open for 0% -> 0% of each run, Pallas kernels for 12% -> 8%
where the time goes in v2:
time: 48.1 us; the launch traced here: 47.8 us
  starting transfers between devices  30.8 us (64%)
  Pallas kernels  10.6 us (22%)
  waiting for transfers between devices  3.34 us (7%)
  local copies, waits for them, and re-layouts  2.33 us (5%)
  between operations  0.72 us (1%)
    ppermute x8, starting transfers between devices, shards(): lax.ppermute(block, 'pg', [(source, source ^ t) for source in range(group...  25.5 us
    all_to_all x1, starting transfers between devices, shards(): lax.all_to_all(near, 'pg', split_axis=0, concat_axis=0, axis_index_groups...  5.27 us
    pallas_call x1, Pallas kernels, attend(): pl.pallas_call(functools.partial(attend_kernel, len(got), requests is not...  3.73 us
    ppermute x8, waiting for transfers between devices, shards(): lax.ppermute(block, 'pg', [(source, source ^ t) for source in range(group...  3.34 us
    pallas_call x1, Pallas kernels, attend_late(): pl.pallas_call(functools.partial(late_kernel, len(got), first), out_shape...  2.62 us
    pallas_call x1, Pallas kernels, front(): pl.pallas_call(functools.partial(front_kernel, far), out_shape=[block] *...  2.53 us
    unnamed x14, local copies, waits for them, and re-layouts  2.33 us
    pallas_call x1, Pallas kernels, rotate_queries(): pl.pallas_call(query_kernel, out_shape=[jax.ShapeDtypeStruct((groups // 2...  1.74 us
  transfers between devices with their start and end apart: 9, of which 3 were waited for; matrix products, arithmetic and copies ran while one was open for 0% of the time, Pallas kernels for 8%

profile of v2, /device:TPU:0, one launch (start us, length us, event | category | flops | bytes accessed | tf_op | source)
XLA Modules:
  0.0 47.8 jit_solution(6700820835629775094)
XLA Ops:
  0.6 2.5 %front.1 = (bf16[32,1280]{1,0:T(8,128)(2,1)}, bf16[32,1280]{1,0:T(8,128)(2,1)}, bf16[32,1280]{1,0:T(8,128)(2,1)}, bf16[32,1280]{1,0:T(8,128)(2,1)}, f32[1296,128]{1,0:T(8,128)}) custom-call(s32[1]{0:T(128)} %bitcast.me_ref, s32[16]{0:T(128)} %assign_any.1, s32[16]{0:T(128)} %length_any.1, s32[16,16]{1,0:T(8,128)} %owner_any.1, s32[16,16]{1,0:T(8,128)} %stripe_any.1, ...), custom_call_target="tpu_custom_call" | custom-call | tf_op jit(solution)/shard_map/front/pallas_call | solution.py:181
  3.2 0.0 copy-start.1
  3.2 1.2 %copy-done.1 = bf16[1,128,4096]{2,1,0:T(8,128)(2,1)S(1)} copy-done((bf16[1,128,4096]{2,1,0:T(8,128)(2,1)S(1)}, bf16[1,128,4096]{2,1,0:T(8,128)(2,1)}, u32[]{:S(2)}) %copy-start.1) | copy-done | bytes 1048600
  4.4 1.1 %copy-done.2 = f32[1296,128]{1,0:T(8,128)S(1)} copy-done((f32[1296,128]{1,0:T(8,128)S(1)}, f32[1296,128]{1,0:T(8,128)}, u32[]{:S(2)}) %copy-start.2) | copy-done | bytes 663576
  5.5 1.7 %rotate_queries.1 = (bf16[8,32,1280]{2,1,0:T(8,128)(2,1)}, bf16[32,1280]{1,0:T(8,128)(2,1)S(1)}, bf16[32,1280]{1,0:T(8,128)(2,1)S(1)}, bf16[32,1280]{1,0:T(8,128...) custom-call(f32[1296,128]{1,0:T(8,128)S(1)} %copy-done.2, ...), custom_call_target="tpu_custom_call" | custom-call | tf_op jit(solution)/shard_map/rotate_queries/pallas_call | solution.py:249
  7.3 5.3 %all-to-all-start = ((bf16[8,32,1280]{2,1,0:T(8,128)(2,1)}), bf16[8,32,1280]{2,1,0:T(8,128)(2,1)S(1)}, u32[]{:S(2)}, u32[]{:S(2)}) async-start(bf16[8,32,1280]{2,1,0:T(8,128)(2,1)} %get-tuple-element.25), calls=%async_computation | async-start | bytes 1310720 | tf_op jit(solution)/shard_map/all_to_all | solution.py:575
  12.5 2.6 %collective-permute-start = (bf16[32,1280]{1,0:T(8,128)(2,1)S(1)}, bf16[32,1280]{1,0:T(8,128)(2,1)S(1)}, u32[]{:S(2)}, u32[]{:S(2)}) collective-permute-start(bf16[32,1280]{1,0:T(8,128)(2,1)S(1)} %copy-done.6), channel_id=1, source_target_pairs={{0,8},{1,9},{2,10},{3,11},{4,12},{5,13},{6,14},{7,15},{8,0},{9,1},... | collective-permute-start | bytes 245768 | tf_op jit(solution)/shard_map/ppermute | solution.py:573
  15.2 1.2 %collective-permute-start.1 = (bf16[32,1280]{1,0:T(8,128)(2,1)S(1)}, bf16[32,1280]{1,0:T(8,128)(2,1)S(1)}, u32[]{:S(2)}, u32[]{:S(2)}) collective-permute-start(bf16[32,1280]{1,0:T(8,128)(2,1)S(1)} %copy-done.5), channel_id=1, source_target_pairs={{0,13},{1,12},{2,15},{3,14},{4,9},{5,8},{6,11},{7,10},{8,5},{9,4},... | collective-permute-start | bytes 245768 | tf_op jit(solution)/shard_map/ppermute | solution.py:573
  16.4 1.9 %collective-permute-start.2 = (bf16[32,1280]{1,0:T(8,128)(2,1)S(1)}, bf16[32,1280]{1,0:T(8,128)(2,1)S(1)}, u32[]{:S(2)}, u32[]{:S(2)}) collective-permute-start(bf16[32,1280]{1,0:T(8,128)(2,1)S(1)} %copy-done.4), channel_id=1, source_target_pairs={{0,9},{1,8},{2,11},{3,10},{4,13},{5,12},{6,15},{7,14},{8,1},{9,0},... | collective-permute-start | bytes 245768 | tf_op jit(solution)/shard_map/ppermute | solution.py:573
  18.3 0.7 %collective-permute-start.3 = (bf16[32,1280]{1,0:T(8,128)(2,1)S(1)}, bf16[32,1280]{1,0:T(8,128)(2,1)S(1)}, u32[]{:S(2)}, u32[]{:S(2)}) collective-permute-start(bf16[32,1280]{1,0:T(8,128)(2,1)S(1)} %copy-done.3), channel_id=1, source_target_pairs={{0,12},{1,13},{2,14},{3,15},{4,8},{5,9},{6,10},{7,11},{8,4},{9,5},... | collective-permute-start | bytes 245768 | tf_op jit(solution)/shard_map/ppermute | solution.py:573
  19.1 2.3 %collective-permute-start.4 = (bf16[32,1280]{1,0:T(8,128)(2,1)S(1)}, bf16[32,1280]{1,0:T(8,128)(2,1)S(1)}, u32[]{:S(2)}, u32[]{:S(2)}) collective-permute-start(bf16[32,1280]{1,0:T(8,128)(2,1)S(1)} %get-tuple-element.33), channel_id=1, source_target_pairs={{0,11},{1,10},{2,9},{3,8},{4,15},{5,14},{6,13},{7,12},{8,3},{9,2},... | collective-permute-start | bytes 245768 | tf_op jit(solution)/shard_map/ppermute | solution.py:573
  21.3 1.3 %collective-permute-done.refs_1_ = bf16[32,1280]{1,0:T(8,128)(2,1)S(1)} collective-permute-done((bf16[32,1280]{1,0:T(8,128)(2,1)S(1)}, bf16[32,1280]{1,0:T(8,128)(2,1)S(1)}, u32[]{:S(2)}, u32[]{:S(2)}) %collective-permute-start) | collective-permute-done | bytes 81952 | tf_op jit(solution)/shard_map/ppermute | solution.py:573
  22.7 4.8 %collective-permute-start.5 = (bf16[32,1280]{1,0:T(8,128)(2,1)S(1)}, bf16[32,1280]{1,0:T(8,128)(2,1)S(1)}, u32[]{:S(2)}, u32[]{:S(2)}) collective-permute-start(bf16[32,1280]{1,0:T(8,128)(2,1)S(1)} %get-tuple-element.34), channel_id=1, source_target_pairs={{0,14},{1,15},{2,12},{3,13},{4,10},{5,11},{6,8},{7,9},{8,6},{9,7},... | collective-permute-start | bytes 245768 | tf_op jit(solution)/shard_map/ppermute | solution.py:573
  27.5 0.4 collective-permute-done.1.refs_2_
  27.9 2.1 %collective-permute-start.6 = (bf16[32,1280]{1,0:T(8,128)(2,1)S(1)}, bf16[32,1280]{1,0:T(8,128)(2,1)S(1)}, u32[]{:S(2)}, u32[]{:S(2)}) collective-permute-start(bf16[32,1280]{1,0:T(8,128)(2,1)S(1)} %get-tuple-element.35), channel_id=1, source_target_pairs={{0,10},{1,11},{2,8},{3,9},{4,14},{5,15},{6,12},{7,13},{8,2},{9,3},... | collective-permute-start | bytes 245768 | tf_op jit(solution)/shard_map/ppermute | solution.py:573
  30.1 0.0 collective-permute-done.2.refs_3_
  30.1 9.7 %collective-permute-start.7 = (bf16[32,1280]{1,0:T(8,128)(2,1)S(1)}, bf16[32,1280]{1,0:T(8,128)(2,1)S(1)}, u32[]{:S(2)}, u32[]{:S(2)}) collective-permute-start(bf16[32,1280]{1,0:T(8,128)(2,1)S(1)} %get-tuple-element.36), channel_id=1, source_target_pairs={{0,15},{1,14},{2,13},{3,12},{4,11},{5,10},{6,9},{7,8},{8,7},{9,6},... | collective-permute-start | bytes 245768 | tf_op jit(solution)/shard_map/ppermute | solution.py:573
  39.8 0.0 collective-permute-done.3.refs_4_
  39.8 0.0 all-to-all-done.refs_0_
  39.8 3.7 %attend.1 = (f32[4,1024,128]{2,1,0:T(8,128)S(1)}, f32[4,1024,128]{2,1,0:T(8,128)S(1)}, bf16[16,8,1024]{2,1,0:T(8,128)(2,1)}) custom-call(bf16[4,1024,128]{2,1,0:T(8,128)(2,1)S(1)} %get-tuple-element.22.rot_ref, f32[8,512]{1,0:T(8,128)S(1)} %get-tuple-element.23.bias_ref, bf16[8,128,128]{2,1,0:T(8,128)(2,1)S(1)} %get-tuple-element.24.own_ref, ...), custom_call_target="tpu_custom_call" | custom-call | tf_op jit(solution)/shard_map/attend/pallas_call | solution.py:396
  43.5 0.0 collective-permute-done.4.refs_0_
  43.6 0.0 collective-permute-done.5.refs_1_
  43.6 1.6 %collective-permute-done.6.refs_2_ = bf16[32,1280]{1,0:T(8,128)(2,1)S(1)} collective-permute-done((bf16[32,1280]{1,0:T(8,128)(2,1)S(1)}, bf16[32,1280]{1,0:T(8,128)(2,1)S(1)}, u32[]{:S(2)}, u32[]{:S(2)}) %collective-permute-start.6) | collective-permute-done | bytes 81952 | tf_op jit(solution)/shard_map/ppermute | solution.py:573
  45.1 2.6 %attend_late.1 = (bf16[128,4096]{1,0:T(8,128)(2,1)}, bf16[16,8,1024]{2,1,0:T(8,128)(2,1)}) custom-call(bf16[4,1024,128]{2,1,0:T(8,128)(2,1)S(1)} %get-tuple-element.22.rot_ref, f32[8,512]{1,0:T(8,128)S(1)} %get-tuple-element.23.bias_ref, f32[4,1024,128]{2,1,0:T(8,128)S(1)} %get-tuple-element.31.result_ref, ...), custom_call_target="tpu_custom_call", output_to_operand_aliasing={{1}: (9, {})} | custom-call | tf_op jit(solution)/shard_map/attend_late/pallas_call | solution.py:496
  (12 shorter events, 0.0 us)
Async XLA Ops:
  0.6 2.5 %copy-start = (bf16[1,16,32,1024]{3,2,1,0:T(8,128)(2,1)S(1)}, bf16[1,16,32,1024]{3,2,1,0:T(8,128)(2,1)}, u32[]{:S(2)}) copy-start(bf16[1,16,32,1024]{3,2,1,0:T(8,128)(2,1)} %param.10) | copy-start | bytes 3145732
  3.2 1.2 %copy-start.1 = (bf16[1,128,4096]{2,1,0:T(8,128)(2,1)S(1)}, bf16[1,128,4096]{2,1,0:T(8,128)(2,1)}, u32[]{:S(2)}) copy-start(bf16[1,128,4096]{2,1,0:T(8,128)(2,1)} %param.8) | copy-start | bytes 3145732
  4.4 1.1 %copy-start.2 = (f32[1296,128]{1,0:T(8,128)S(1)}, f32[1296,128]{1,0:T(8,128)}, u32[]{:S(2)}) copy-start(f32[1296,128]{1,0:T(8,128)} %get-tuple-element.21.info_ref) | copy-start | bytes 1990660
  5.5 7.0 %copy-start.6 = (bf16[32,1280]{1,0:T(8,128)(2,1)S(1)}, bf16[32,1280]{1,0:T(8,128)(2,1)}, u32[]{:S(2)}) copy-start(bf16[32,1280]{1,0:T(8,128)(2,1)} %get-tuple-element.26) | copy-start | bytes 245764
  5.5 9.7 %copy-start.5 = (bf16[32,1280]{1,0:T(8,128)(2,1)S(1)}, bf16[32,1280]{1,0:T(8,128)(2,1)}, u32[]{:S(2)}) copy-start(bf16[32,1280]{1,0:T(8,128)(2,1)} %get-tuple-element.27) | copy-start | bytes 245764
  5.5 10.9 %copy-start.4 = (bf16[32,1280]{1,0:T(8,128)(2,1)S(1)}, bf16[32,1280]{1,0:T(8,128)(2,1)}, u32[]{:S(2)}) copy-start(bf16[32,1280]{1,0:T(8,128)(2,1)} %get-tuple-element.28) | copy-start | bytes 245764
  5.5 12.8 %copy-start.3 = (bf16[32,1280]{1,0:T(8,128)(2,1)S(1)}, bf16[32,1280]{1,0:T(8,128)(2,1)}, u32[]{:S(2)}) copy-start(bf16[32,1280]{1,0:T(8,128)(2,1)} %get-tuple-element.29) | copy-start | bytes 245764
  7.3 32.5 %all-to-all-start = ((bf16[8,32,1280]{2,1,0:T(8,128)(2,1)}), bf16[8,32,1280]{2,1,0:T(8,128)(2,1)S(1)}, u32[]{:S(2)}, u32[]{:S(2)}) async-start(bf16[8,32,1280]{2,1,0:T(8,128)(2,1)} %get-tuple-element.25), calls=%async_computation | async-start | bytes 1310720 | tf_op jit(solution)/shard_map/all_to_all | solution.py:575
  12.5 10.2 %collective-permute-start = (bf16[32,1280]{1,0:T(8,128)(2,1)S(1)}, bf16[32,1280]{1,0:T(8,128)(2,1)S(1)}, u32[]{:S(2)}, u32[]{:S(2)}) collective-permute-start(bf16[32,1280]{1,0:T(8,128)(2,1)S(1)} %copy-done.6), channel_id=1, source_target_pairs={{0,8},{1,9},{2,10},{3,11},{4,12},{5,13},{6,14},{7,15},{8,0},{9,1},... | collective-permute-start | bytes 245768 | tf_op jit(solution)/shard_map/ppermute | solution.py:573
  15.2 12.7 %collective-permute-start.1 = (bf16[32,1280]{1,0:T(8,128)(2,1)S(1)}, bf16[32,1280]{1,0:T(8,128)(2,1)S(1)}, u32[]{:S(2)}, u32[]{:S(2)}) collective-permute-start(bf16[32,1280]{1,0:T(8,128)(2,1)S(1)} %copy-done.5), channel_id=1, source_target_pairs={{0,13},{1,12},{2,15},{3,14},{4,9},{5,8},{6,11},{7,10},{8,5},{9,4},... | collective-permute-start | bytes 245768 | tf_op jit(solution)/shard_map/ppermute | solution.py:573
  16.4 13.6 %collective-permute-start.2 = (bf16[32,1280]{1,0:T(8,128)(2,1)S(1)}, bf16[32,1280]{1,0:T(8,128)(2,1)S(1)}, u32[]{:S(2)}, u32[]{:S(2)}) collective-permute-start(bf16[32,1280]{1,0:T(8,128)(2,1)S(1)} %copy-done.4), channel_id=1, source_target_pairs={{0,9},{1,8},{2,11},{3,10},{4,13},{5,12},{6,15},{7,14},{8,1},{9,0},... | collective-permute-start | bytes 245768 | tf_op jit(solution)/shard_map/ppermute | solution.py:573
  18.3 21.5 %collective-permute-start.3 = (bf16[32,1280]{1,0:T(8,128)(2,1)S(1)}, bf16[32,1280]{1,0:T(8,128)(2,1)S(1)}, u32[]{:S(2)}, u32[]{:S(2)}) collective-permute-start(bf16[32,1280]{1,0:T(8,128)(2,1)S(1)} %copy-done.3), channel_id=1, source_target_pairs={{0,12},{1,13},{2,14},{3,15},{4,8},{5,9},{6,10},{7,11},{8,4},{9,5},... | collective-permute-start | bytes 245768 | tf_op jit(solution)/shard_map/ppermute | solution.py:573
  19.1 24.5 %collective-permute-start.4 = (bf16[32,1280]{1,0:T(8,128)(2,1)S(1)}, bf16[32,1280]{1,0:T(8,128)(2,1)S(1)}, u32[]{:S(2)}, u32[]{:S(2)}) collective-permute-start(bf16[32,1280]{1,0:T(8,128)(2,1)S(1)} %get-tuple-element.33), channel_id=1, source_target_pairs={{0,11},{1,10},{2,9},{3,8},{4,15},{5,14},{6,13},{7,12},{8,3},{9,2},... | collective-permute-start | bytes 245768 | tf_op jit(solution)/shard_map/ppermute | solution.py:573
  22.7 20.9 %collective-permute-start.5 = (bf16[32,1280]{1,0:T(8,128)(2,1)S(1)}, bf16[32,1280]{1,0:T(8,128)(2,1)S(1)}, u32[]{:S(2)}, u32[]{:S(2)}) collective-permute-start(bf16[32,1280]{1,0:T(8,128)(2,1)S(1)} %get-tuple-element.34), channel_id=1, source_target_pairs={{0,14},{1,15},{2,12},{3,13},{4,10},{5,11},{6,8},{7,9},{8,6},{9,7},... | collective-permute-start | bytes 245768 | tf_op jit(solution)/shard_map/ppermute | solution.py:573
  27.9 17.2 %collective-permute-start.6 = (bf16[32,1280]{1,0:T(8,128)(2,1)S(1)}, bf16[32,1280]{1,0:T(8,128)(2,1)S(1)}, u32[]{:S(2)}, u32[]{:S(2)}) collective-permute-start(bf16[32,1280]{1,0:T(8,128)(2,1)S(1)} %get-tuple-element.35), channel_id=1, source_target_pairs={{0,10},{1,11},{2,8},{3,9},{4,14},{5,15},{6,12},{7,13},{8,2},{9,3},... | collective-permute-start | bytes 245768 | tf_op jit(solution)/shard_map/ppermute | solution.py:573
  30.1 15.1 %collective-permute-start.7 = (bf16[32,1280]{1,0:T(8,128)(2,1)S(1)}, bf16[32,1280]{1,0:T(8,128)(2,1)S(1)}, u32[]{:S(2)}, u32[]{:S(2)}) collective-permute-start(bf16[32,1280]{1,0:T(8,128)(2,1)S(1)} %get-tuple-element.36), channel_id=1, source_target_pairs={{0,15},{1,14},{2,13},{3,12},{4,11},{5,10},{6,9},{7,8},{8,7},{9,6},... | collective-permute-start | bytes 245768 | tf_op jit(solution)/shard_map/ppermute | solution.py:573

commit v3 on v1

--- a/solution.py
+++ b/solution.py
@@ -40,7 +40,7 @@
 def order_of(groups):
     half = groups // 2
     far, near = list(range(half, 2 * half)), list(range(half - 1, 0, -1))
-    order = [(far if kind == "f" else near).pop(0) for kind in "fnfnfnfnfnnffnf"]
+    order = [(far if kind == "f" else near).pop(0) for kind in "ffnfnfnfnfnfnfn"]
     order.insert(groups - LATE - 1, 0)
     return order
 

time: 40.1 us -> 41 us (1.022)
  waiting for transfers between devices: 0.67 us -> 4.09 us
  starting transfers between devices: 26.3 us -> 23.8 us
    ppermute x15, waiting for transfers between devices: 0.67 us -> 4.09 us  [shards(): lax.ppermute(block, 'pg', [(source, source ^ t) for source in range(group...]
    ppermute x15, starting transfers between devices: 26.3 us -> 23.8 us  [shards(): lax.ppermute(block, 'pg', [(source, source ^ t) for source in range(group...]
  transfers between devices with their start and end apart: 15 -> 15, of which waited for: 2 -> 3; matrix products, arithmetic and copies ran while one was open for 0% -> 0% of each run, Pallas kernels for 12% -> 12%
where the time goes in v3:
time: 41 us; the launch traced here: 40.8 us
  starting transfers between devices  23.8 us (58%)
  Pallas kernels  9.89 us (24%)
  waiting for transfers between devices  4.09 us (10%)
  local copies, waits for them, and re-layouts  2.32 us (6%)
  between operations  0.7 us (2%)
    ppermute x15, starting transfers between devices, shards(): lax.ppermute(block, 'pg', [(source, source ^ t) for source in range(group...  23.8 us
    ppermute x15, waiting for transfers between devices, shards(): lax.ppermute(block, 'pg', [(source, source ^ t) for source in range(group...  4.09 us
    pallas_call x1, Pallas kernels, attend(): pl.pallas_call(functools.partial(attend_kernel, len(got), requests is not...  3.87 us
    pallas_call x1, Pallas kernels, attend_late(): pl.pallas_call(functools.partial(late_kernel, len(got), first), out_shape...  2.61 us
    pallas_call x1, Pallas kernels, front(): pl.pallas_call(functools.partial(front_kernel, order), out_shape=[block]...  2.53 us
    unnamed x6, local copies, waits for them, and re-layouts  2.32 us
    pallas_call x1, Pallas kernels, rotate_queries(): pl.pallas_call(functools.partial(query_kernel, order), out_shape=[jax.Sha...  0.88 us
  transfers between devices with their start and end apart: 15, of which 3 were waited for; matrix products, arithmetic and copies ran while one was open for 0% of the time, Pallas kernels for 12%

profile of v3, /device:TPU:0, one launch (start us, length us, event | category | flops | bytes accessed | tf_op | source)
XLA Modules:
  0.0 40.8 jit_solution(12094425083756362277)
XLA Ops:
  0.6 2.5 %front.1 = (bf16[32,1280]{1,0:T(8,128)(2,1)}, bf16[32,1280]{1,0:T(8,128)(2,1)}, bf16[32,1280]{1,0:T(8,128)(2,1)}, bf16[32,1280]{1,0:T(8,128)(2,1)}, f32[1296,128]{1,0:T(8,128)}) custom-call(s32[1]{0:T(128)} %bitcast.me_ref, s32[16]{0:T(128)} %assign_any.1, s32[16]{0:T(128)} %length_any.1, s32[16,16]{1,0:T(8,128)} %owner_any.1, s32[16,16]{1,0:T(8,128)} %stripe_any.1, ...), custom_call_target="tpu_custom_call" | custom-call | tf_op jit(solution)/shard_map/front/pallas_call | solution.py:176
  3.2 4.1 %collective-permute-start = (bf16[32,1280]{1,0:T(8,128)(2,1)}, bf16[32,1280]{1,0:T(8,128)(2,1)S(1)}, u32[]{:S(2)}, u32[]{:S(2)}) collective-permute-start(bf16[32,1280]{1,0:T(8,128)(2,1)} %get-tuple-element.32), channel_id=1, source_target_pairs={{0,8},{1,9},{2,10},{3,11},{4,12},{5,13},{6,14},{7,15},{8,0},{9,1},... | collective-permute-start | bytes 245768 | tf_op jit(solution)/shard_map/ppermute | solution.py:566
  7.3 2.6 %collective-permute-start.2 = (bf16[32,1280]{1,0:T(8,128)(2,1)}, bf16[32,1280]{1,0:T(8,128)(2,1)S(1)}, u32[]{:S(2)}, u32[]{:S(2)}) collective-permute-start(bf16[32,1280]{1,0:T(8,128)(2,1)} %get-tuple-element.34), channel_id=1, source_target_pairs={{0,7},{1,6},{2,5},{3,4},{4,3},{5,2},{6,1},{7,0},{8,15},{9,14},{10,... | collective-permute-start | bytes 245768 | tf_op jit(solution)/shard_map/ppermute | solution.py:566
  9.9 2.5 %collective-permute-start.3 = (bf16[32,1280]{1,0:T(8,128)(2,1)}, bf16[32,1280]{1,0:T(8,128)(2,1)S(1)}, u32[]{:S(2)}, u32[]{:S(2)}) collective-permute-start(bf16[32,1280]{1,0:T(8,128)(2,1)} %get-tuple-element.35), channel_id=1, source_target_pairs={{0,10},{1,11},{2,8},{3,9},{4,14},{5,15},{6,12},{7,13},{8,2},{9,3},... | collective-permute-start | bytes 245768 | tf_op jit(solution)/shard_map/ppermute | solution.py:566
  12.4 1.2 %copy-done.1 = bf16[1,128,4096]{2,1,0:T(8,128)(2,1)S(1)} copy-done((bf16[1,128,4096]{2,1,0:T(8,128)(2,1)S(1)}, bf16[1,128,4096]{2,1,0:T(8,128)(2,1)}, u32[]{:S(2)}) %copy-start.1) | copy-done | bytes 1048600
  13.6 1.1 %copy-done.2 = f32[1296,128]{1,0:T(8,128)S(1)} copy-done((f32[1296,128]{1,0:T(8,128)S(1)}, f32[1296,128]{1,0:T(8,128)}, u32[]{:S(2)}) %copy-start.2) | copy-done | bytes 663576
  14.7 0.9 %rotate_queries.1 = (bf16[32,1280]{1,0:T(8,128)(2,1)S(1)}, bf16[32,1280]{1,0:T(8,128)(2,1)S(1)}, bf16[32,1280]{1,0:T(8,128)(2,1)S(1)}, bf16[32,1280]{1,0:T(8,128...) custom-call(f32[1296,128]{1,0:T(8,128)S(1)} %copy-done.2, ...), custom_call_target="tpu_custom_call" | custom-call | tf_op jit(solution)/shard_map/rotate_queries/pallas_call | solution.py:249
  15.6 1.5 %collective-permute-start.4 = (bf16[32,1280]{1,0:T(8,128)(2,1)S(1)}, bf16[32,1280]{1,0:T(8,128)(2,1)S(1)}, u32[]{:S(2)}, u32[]{:S(2)}) collective-permute-start(bf16[32,1280]{1,0:T(8,128)(2,1)S(1)} %get-tuple-element.36), channel_id=1, source_target_pairs={{0,6},{1,7},{2,4},{3,5},{4,2},{5,3},{6,0},{7,1},{8,14},{9,15},{10,... | collective-permute-start | bytes 245768 | tf_op jit(solution)/shard_map/ppermute | solution.py:566
  17.1 0.0 collective-permute-start.5
  17.1 0.0 collective-permute-done.1.refs_1_
  17.1 1.7 %collective-permute-start.6 = (bf16[32,1280]{1,0:T(8,128)(2,1)S(1)}, bf16[32,1280]{1,0:T(8,128)(2,1)S(1)}, u32[]{:S(2)}, u32[]{:S(2)}) collective-permute-start(bf16[32,1280]{1,0:T(8,128)(2,1)S(1)} %get-tuple-element.38), channel_id=1, source_target_pairs={{0,5},{1,4},{2,7},{3,6},{4,1},{5,0},{6,3},{7,2},{8,13},{9,12},{10,... | collective-permute-start | bytes 245768 | tf_op jit(solution)/shard_map/ppermute | solution.py:566
  18.8 2.4 %collective-permute-start.7 = (bf16[32,1280]{1,0:T(8,128)(2,1)S(1)}, bf16[32,1280]{1,0:T(8,128)(2,1)S(1)}, u32[]{:S(2)}, u32[]{:S(2)}) collective-permute-start(bf16[32,1280]{1,0:T(8,128)(2,1)S(1)} %get-tuple-element.39), channel_id=1, source_target_pairs={{0,12},{1,13},{2,14},{3,15},{4,8},{5,9},{6,10},{7,11},{8,4},{9,5},... | collective-permute-start | bytes 245768 | tf_op jit(solution)/shard_map/ppermute | solution.py:566
  21.1 0.7 %collective-permute-start.8 = (bf16[32,1280]{1,0:T(8,128)(2,1)S(1)}, bf16[32,1280]{1,0:T(8,128)(2,1)S(1)}, u32[]{:S(2)}, u32[]{:S(2)}) collective-permute-start(bf16[32,1280]{1,0:T(8,128)(2,1)S(1)} %get-tuple-element.40), channel_id=1, source_target_pairs={{0,4},{1,5},{2,6},{3,7},{4,0},{5,1},{6,2},{7,3},{8,12},{9,13},{10,... | collective-permute-start | bytes 245768 | tf_op jit(solution)/shard_map/ppermute | solution.py:566
  21.8 1.1 %collective-permute-done.4.refs_4_ = bf16[32,1280]{1,0:T(8,128)(2,1)S(1)} collective-permute-done((bf16[32,1280]{1,0:T(8,128)(2,1)S(1)}, bf16[32,1280]{1,0:T(8,128)(2,1)S(1)}, u32[]{:S(2)}, u32[]{:S(2)}) %collective-permute-start.4) | collective-permute-done | bytes 81952 | tf_op jit(solution)/shard_map/ppermute | solution.py:566
  22.9 0.3 collective-permute-start.9
  23.2 2.0 %collective-permute-done.5.refs_5_ = bf16[32,1280]{1,0:T(8,128)(2,1)S(1)} collective-permute-done((bf16[32,1280]{1,0:T(8,128)(2,1)S(1)}, bf16[32,1280]{1,0:T(8,128)(2,1)S(1)}, u32[]{:S(2)}, u32[]{:S(2)}) %collective-permute-start.5) | collective-permute-done | bytes 81952 | tf_op jit(solution)/shard_map/ppermute | solution.py:566
  25.3 2.0 %collective-permute-start.10 = (bf16[32,1280]{1,0:T(8,128)(2,1)S(1)}, bf16[32,1280]{1,0:T(8,128)(2,1)S(1)}, u32[]{:S(2)}, u32[]{:S(2)}) collective-permute-start(bf16[32,1280]{1,0:T(8,128)(2,1)S(1)} %get-tuple-element.42), channel_id=1, source_target_pairs={{0,3},{1,2},{2,1},{3,0},{4,7},{5,6},{6,5},{7,4},{8,11},{9,10},{10,... | collective-permute-start | bytes 245768 | tf_op jit(solution)/shard_map/ppermute | solution.py:566
  27.2 1.9 %collective-permute-start.11 = (bf16[32,1280]{1,0:T(8,128)(2,1)S(1)}, bf16[32,1280]{1,0:T(8,128)(2,1)S(1)}, u32[]{:S(2)}, u32[]{:S(2)}) collective-permute-start(bf16[32,1280]{1,0:T(8,128)(2,1)S(1)} %get-tuple-element.47), channel_id=1, source_target_pairs={{0,14},{1,15},{2,12},{3,13},{4,10},{5,11},{6,8},{7,9},{8,6},{9,7},... | collective-permute-start | bytes 245768 | tf_op jit(solution)/shard_map/ppermute | solution.py:566
  29.2 1.6 %collective-permute-start.12 = (bf16[32,1280]{1,0:T(8,128)(2,1)S(1)}, bf16[32,1280]{1,0:T(8,128)(2,1)S(1)}, u32[]{:S(2)}, u32[]{:S(2)}) collective-permute-start(bf16[32,1280]{1,0:T(8,128)(2,1)S(1)} %get-tuple-element.48), channel_id=1, source_target_pairs={{0,2},{1,3},{2,0},{3,1},{4,6},{5,7},{6,4},{7,5},{8,10},{9,11},{10,... | collective-permute-start | bytes 245768 | tf_op jit(solution)/shard_map/ppermute | solution.py:566
  30.7 0.7 %collective-permute-start.13 = (bf16[32,1280]{1,0:T(8,128)(2,1)S(1)}, bf16[32,1280]{1,0:T(8,128)(2,1)S(1)}, u32[]{:S(2)}, u32[]{:S(2)}) collective-permute-start(bf16[32,1280]{1,0:T(8,128)(2,1)S(1)} %get-tuple-element.49), channel_id=1, source_target_pairs={{0,15},{1,14},{2,13},{3,12},{4,11},{5,10},{6,9},{7,8},{8,7},{9,6},... | collective-permute-start | bytes 245768 | tf_op jit(solution)/shard_map/ppermute | solution.py:566
  31.5 1.9 %collective-permute-start.14 = (bf16[32,1280]{1,0:T(8,128)(2,1)S(1)}, bf16[32,1280]{1,0:T(8,128)(2,1)S(1)}, u32[]{:S(2)}, u32[]{:S(2)}) collective-permute-start(bf16[32,1280]{1,0:T(8,128)(2,1)S(1)} %get-tuple-element.50), channel_id=1, source_target_pairs={{0,1},{1,0},{2,3},{3,2},{4,5},{5,4},{6,7},{7,6},{8,9},{9,8},{10,11... | collective-permute-start | bytes 245768 | tf_op jit(solution)/shard_map/ppermute | solution.py:566
  33.3 3.9 %attend.1 = (f32[4,1024,128]{2,1,0:T(8,128)S(1)}, f32[4,1024,128]{2,1,0:T(8,128)S(1)}, bf16[16,8,1024]{2,1,0:T(8,128)(2,1)}) custom-call(bf16[4,1024,128]{2,1,0:T(8,128)(2,1)S(1)} %get-tuple-element.29.rot_ref, f32[8,512]{1,0:T(8,128)S(1)} %get-tuple-element.30.bias_ref, bf16[8,160,128]{2,1,0:T(8,128)(2,1)S(1)} %get-tuple-element.31.own_ref, ...), custom_call_target="tpu_custom_call" | custom-call | tf_op jit(solution)/shard_map/attend/pallas_call | solution.py:390
  37.2 0.9 %collective-permute-done.13.refs_2_ = bf16[32,1280]{1,0:T(8,128)(2,1)S(1)} collective-permute-done((bf16[32,1280]{1,0:T(8,128)(2,1)S(1)}, bf16[32,1280]{1,0:T(8,128)(2,1)S(1)}, u32[]{:S(2)}, u32[]{:S(2)}) %collective-permute-start.13) | collective-permute-done | bytes 81952 | tf_op jit(solution)/shard_map/ppermute | solution.py:566
  38.2 2.6 %attend_late.1 = (bf16[128,4096]{1,0:T(8,128)(2,1)}, bf16[16,8,1024]{2,1,0:T(8,128)(2,1)}) custom-call(bf16[4,1024,128]{2,1,0:T(8,128)(2,1)S(1)} %get-tuple-element.29.rot_ref, f32[8,512]{1,0:T(8,128)S(1)} %get-tuple-element.30.bias_ref, f32[4,1024,128]{2,1,0:T(8,128)S(1)} %get-tuple-element.45.result_ref, ...), custom_call_target="tpu_custom_call", output_to_operand_aliasing={{1}: (9, {})} | custom-call | tf_op jit(solution)/shard_map/attend_late/pallas_call | solution.py:490
  (16 shorter events, 0.0 us)
Async XLA Ops:
  0.6 11.8 %copy-start = (bf16[1,16,32,1024]{3,2,1,0:T(8,128)(2,1)S(1)}, bf16[1,16,32,1024]{3,2,1,0:T(8,128)(2,1)}, u32[]{:S(2)}) copy-start(bf16[1,16,32,1024]{3,2,1,0:T(8,128)(2,1)} %param.10) | copy-start | bytes 3145732
  3.2 13.9 %collective-permute-start = (bf16[32,1280]{1,0:T(8,128)(2,1)}, bf16[32,1280]{1,0:T(8,128)(2,1)S(1)}, u32[]{:S(2)}, u32[]{:S(2)}) collective-permute-start(bf16[32,1280]{1,0:T(8,128)(2,1)} %get-tuple-element.32), channel_id=1, source_target_pairs={{0,8},{1,9},{2,10},{3,11},{4,12},{5,13},{6,14},{7,15},{8,0},{9,1},... | collective-permute-start | bytes 245768 | tf_op jit(solution)/shard_map/ppermute | solution.py:566
  7.3 9.8 %collective-permute-start.1 = (bf16[32,1280]{1,0:T(8,128)(2,1)}, bf16[32,1280]{1,0:T(8,128)(2,1)S(1)}, u32[]{:S(2)}, u32[]{:S(2)}) collective-permute-start(bf16[32,1280]{1,0:T(8,128)(2,1)} %get-tuple-element.33), channel_id=1, source_target_pairs={{0,9},{1,8},{2,11},{3,10},{4,13},{5,12},{6,15},{7,14},{8,1},{9,0},... | collective-permute-start | bytes 245768 | tf_op jit(solution)/shard_map/ppermute | solution.py:566
  7.3 11.5 %collective-permute-start.2 = (bf16[32,1280]{1,0:T(8,128)(2,1)}, bf16[32,1280]{1,0:T(8,128)(2,1)S(1)}, u32[]{:S(2)}, u32[]{:S(2)}) collective-permute-start(bf16[32,1280]{1,0:T(8,128)(2,1)} %get-tuple-element.34), channel_id=1, source_target_pairs={{0,7},{1,6},{2,5},{3,4},{4,3},{5,2},{6,1},{7,0},{8,15},{9,14},{10,... | collective-permute-start | bytes 245768 | tf_op jit(solution)/shard_map/ppermute | solution.py:566
  9.9 11.3 %collective-permute-start.3 = (bf16[32,1280]{1,0:T(8,128)(2,1)}, bf16[32,1280]{1,0:T(8,128)(2,1)S(1)}, u32[]{:S(2)}, u32[]{:S(2)}) collective-permute-start(bf16[32,1280]{1,0:T(8,128)(2,1)} %get-tuple-element.35), channel_id=1, source_target_pairs={{0,10},{1,11},{2,8},{3,9},{4,14},{5,15},{6,12},{7,13},{8,2},{9,3},... | collective-permute-start | bytes 245768 | tf_op jit(solution)/shard_map/ppermute | solution.py:566
  12.4 1.2 %copy-start.1 = (bf16[1,128,4096]{2,1,0:T(8,128)(2,1)S(1)}, bf16[1,128,4096]{2,1,0:T(8,128)(2,1)}, u32[]{:S(2)}) copy-start(bf16[1,128,4096]{2,1,0:T(8,128)(2,1)} %param.8) | copy-start | bytes 3145732
  13.6 1.1 %copy-start.2 = (f32[1296,128]{1,0:T(8,128)S(1)}, f32[1296,128]{1,0:T(8,128)}, u32[]{:S(2)}) copy-start(f32[1296,128]{1,0:T(8,128)} %get-tuple-element.28.info_ref) | copy-start | bytes 1990660
  15.6 7.3 %collective-permute-start.4 = (bf16[32,1280]{1,0:T(8,128)(2,1)S(1)}, bf16[32,1280]{1,0:T(8,128)(2,1)S(1)}, u32[]{:S(2)}, u32[]{:S(2)}) collective-permute-start(bf16[32,1280]{1,0:T(8,128)(2,1)S(1)} %get-tuple-element.36), channel_id=1, source_target_pairs={{0,6},{1,7},{2,4},{3,5},{4,2},{5,3},{6,0},{7,1},{8,14},{9,15},{10,... | collective-permute-start | bytes 245768 | tf_op jit(solution)/shard_map/ppermute | solution.py:566
  17.1 8.2 %collective-permute-start.5 = (bf16[32,1280]{1,0:T(8,128)(2,1)S(1)}, bf16[32,1280]{1,0:T(8,128)(2,1)S(1)}, u32[]{:S(2)}, u32[]{:S(2)}) collective-permute-start(bf16[32,1280]{1,0:T(8,128)(2,1)S(1)} %get-tuple-element.37), channel_id=1, source_target_pairs={{0,11},{1,10},{2,9},{3,8},{4,15},{5,14},{6,13},{7,12},{8,3},{9,2},... | collective-permute-start | bytes 245768 | tf_op jit(solution)/shard_map/ppermute | solution.py:566
  17.1 10.2 %collective-permute-start.6 = (bf16[32,1280]{1,0:T(8,128)(2,1)S(1)}, bf16[32,1280]{1,0:T(8,128)(2,1)S(1)}, u32[]{:S(2)}, u32[]{:S(2)}) collective-permute-start(bf16[32,1280]{1,0:T(8,128)(2,1)S(1)} %get-tuple-element.38), channel_id=1, source_target_pairs={{0,5},{1,4},{2,7},{3,6},{4,1},{5,0},{6,3},{7,2},{8,13},{9,12},{10,... | collective-permute-start | bytes 245768 | tf_op jit(solution)/shard_map/ppermute | solution.py:566
  18.8 10.4 %collective-permute-start.7 = (bf16[32,1280]{1,0:T(8,128)(2,1)S(1)}, bf16[32,1280]{1,0:T(8,128)(2,1)S(1)}, u32[]{:S(2)}, u32[]{:S(2)}) collective-permute-start(bf16[32,1280]{1,0:T(8,128)(2,1)S(1)} %get-tuple-element.39), channel_id=1, source_target_pairs={{0,12},{1,13},{2,14},{3,15},{4,8},{5,9},{6,10},{7,11},{8,4},{9,5},... | collective-permute-start | bytes 245768 | tf_op jit(solution)/shard_map/ppermute | solution.py:566
  21.1 9.6 %collective-permute-start.8 = (bf16[32,1280]{1,0:T(8,128)(2,1)S(1)}, bf16[32,1280]{1,0:T(8,128)(2,1)S(1)}, u32[]{:S(2)}, u32[]{:S(2)}) collective-permute-start(bf16[32,1280]{1,0:T(8,128)(2,1)S(1)} %get-tuple-element.40), channel_id=1, source_target_pairs={{0,4},{1,5},{2,6},{3,7},{4,0},{5,1},{6,2},{7,3},{8,12},{9,13},{10,... | collective-permute-start | bytes 245768 | tf_op jit(solution)/shard_map/ppermute | solution.py:566
  22.9 8.5 %collective-permute-start.9 = (bf16[32,1280]{1,0:T(8,128)(2,1)S(1)}, bf16[32,1280]{1,0:T(8,128)(2,1)S(1)}, u32[]{:S(2)}, u32[]{:S(2)}) collective-permute-start(bf16[32,1280]{1,0:T(8,128)(2,1)S(1)} %get-tuple-element.41), channel_id=1, source_target_pairs={{0,13},{1,12},{2,15},{3,14},{4,9},{5,8},{6,11},{7,10},{8,5},{9,4},... | collective-permute-start | bytes 245768 | tf_op jit(solution)/shard_map/ppermute | solution.py:566
  25.3 8.1 %collective-permute-start.10 = (bf16[32,1280]{1,0:T(8,128)(2,1)S(1)}, bf16[32,1280]{1,0:T(8,128)(2,1)S(1)}, u32[]{:S(2)}, u32[]{:S(2)}) collective-permute-start(bf16[32,1280]{1,0:T(8,128)(2,1)S(1)} %get-tuple-element.42), channel_id=1, source_target_pairs={{0,3},{1,2},{2,1},{3,0},{4,7},{5,6},{6,5},{7,4},{8,11},{9,10},{10,... | collective-permute-start | bytes 245768 | tf_op jit(solution)/shard_map/ppermute | solution.py:566
  27.2 10.0 %collective-permute-start.11 = (bf16[32,1280]{1,0:T(8,128)(2,1)S(1)}, bf16[32,1280]{1,0:T(8,128)(2,1)S(1)}, u32[]{:S(2)}, u32[]{:S(2)}) collective-permute-start(bf16[32,1280]{1,0:T(8,128)(2,1)S(1)} %get-tuple-element.47), channel_id=1, source_target_pairs={{0,14},{1,15},{2,12},{3,13},{4,10},{5,11},{6,8},{7,9},{8,6},{9,7},... | collective-permute-start | bytes 245768 | tf_op jit(solution)/shard_map/ppermute | solution.py:566
  29.2 8.1 %collective-permute-start.12 = (bf16[32,1280]{1,0:T(8,128)(2,1)S(1)}, bf16[32,1280]{1,0:T(8,128)(2,1)S(1)}, u32[]{:S(2)}, u32[]{:S(2)}) collective-permute-start(bf16[32,1280]{1,0:T(8,128)(2,1)S(1)} %get-tuple-element.48), channel_id=1, source_target_pairs={{0,2},{1,3},{2,0},{3,1},{4,6},{5,7},{6,4},{7,5},{8,10},{9,11},{10,... | collective-permute-start | bytes 245768 | tf_op jit(solution)/shard_map/ppermute | solution.py:566
  30.7 7.4 %collective-permute-start.13 = (bf16[32,1280]{1,0:T(8,128)(2,1)S(1)}, bf16[32,1280]{1,0:T(8,128)(2,1)S(1)}, u32[]{:S(2)}, u32[]{:S(2)}) collective-permute-start(bf16[32,1280]{1,0:T(8,128)(2,1)S(1)} %get-tuple-element.49), channel_id=1, source_target_pairs={{0,15},{1,14},{2,13},{3,12},{4,11},{5,10},{6,9},{7,8},{8,7},{9,6},... | collective-permute-start | bytes 245768 | tf_op jit(solution)/shard_map/ppermute | solution.py:566
  31.5 6.7 %collective-permute-start.14 = (bf16[32,1280]{1,0:T(8,128)(2,1)S(1)}, bf16[32,1280]{1,0:T(8,128)(2,1)S(1)}, u32[]{:S(2)}, u32[]{:S(2)}) collective-permute-start(bf16[32,1280]{1,0:T(8,128)(2,1)S(1)} %get-tuple-element.50), channel_id=1, source_target_pairs={{0,1},{1,0},{2,3},{3,2},{4,5},{5,4},{6,7},{7,6},{8,9},{9,8},{10,11... | collective-permute-start | bytes 245768 | tf_op jit(solution)/shard_map/ppermute | solution.py:566

commit v4 on v2

--- a/solution.py
+++ b/solution.py
@@ -20,8 +20,10 @@
 MASKED = -1e30
 SCALE = HEAD_DIM ** -0.5 / math.log(2.0)
 CHUNK = 256
+LATE = 4
 LATE_CHUNK = 256
 AHEAD = 4
+AHEAD_OF_QUERIES = 8
 
 SMEM = pl.BlockSpec(memory_space=pltpu.SMEM)
 VMEM = pl.BlockSpec(memory_space=pltpu.VMEM)
@@ -36,18 +38,12 @@
     return slice(head * HEAD_DIM, (head + 1) * HEAD_DIM)
 
 
-def far_partners(groups):
-    quarter = groups // 4
-    next_to, beyond = list(range(2 * quarter, 3 * quarter)), list(range(3 * quarter, 4 * quarter))
-    order = []
-    for at in range(quarter):
-        order += [next_to[at ^ (at >> 1)], beyond[(at ^ (at >> 1)) ^ 1]]
+def order_of(groups):
+    half = groups // 2
+    far, near = list(range(half, 2 * half)), list(range(half - 1, 0, -1))
+    order = [(far if kind == "f" else near).pop(0) for kind in "fnfnfnfnfnnffnf"]
+    order.insert(groups - LATE - 1, 0)
     return order
-
-
-def holder_of(p, me, groups, far):
-    half = groups // 2
-    return me // half * half + p if p < half else me ^ far[p - half]
 
 
 def rotation_tables(rows):
@@ -93,7 +89,7 @@
 
 
 def front_kernel(
-    far, me_ref, assign_any, length_any, owner_any, stripe_any, block_any, table_any, pool_any, *refs
+    order, me_ref, assign_any, length_any, owner_any, stripe_any, block_any, table_any, pool_any, *refs
 ):
     groups, slots, width = pool_any.shape
     send_refs, info_any, refs = refs[:AHEAD], refs[AHEAD], refs[AHEAD + 1 :]
@@ -139,10 +135,10 @@
         copy.wait()
     sends = []
     for p in range(AHEAD):
-        pack_ref[p, :, 0:width] = pool_ref[assign_ref[me ^ far[p]]]
+        pack_ref[p, :, 0:width] = pool_ref[assign_ref[me ^ order[p]]]
         for lanes in range(quarter):
             pack_ref[p, :, width + lanes * HEAD_DIM : width + (lanes + 1) * HEAD_DIM] = fresh_rows(
-                info_ref, at["new"], residue_ref[me ^ far[p]], new_count, count, quarter, lanes
+                info_ref, at["new"], residue_ref[me ^ order[p]], new_count, count, quarter, lanes
             ).astype(jnp.bfloat16)
         sends.append(pltpu.make_async_copy(pack_ref.at[p], send_refs[p], send_sems.at[p]))
         sends[-1].start()
@@ -154,7 +150,7 @@
     piece, slot = row * per_row + lane // slots, lane % slots
     holder, requests, residues = jnp.zeros_like(lane), jnp.zeros_like(lane), jnp.zeros_like(lane)
     for p in range(groups):
-        other = holder_of(p, me, groups, far)
+        other = me ^ order[p]
         holder = jnp.where(piece == p, other, holder)
         requests = jnp.where(lane == p, assign_ref[other], requests)
         residues = jnp.where(lane == p, residue_ref[other], residues)
@@ -172,14 +168,14 @@
     info_copy(1, 0, at["new"]).wait()
 
 
-def front(far, me, assignment, prefix_len, owner_map, stripe_map, block_kv, table, pool):
+def front(order, me, assignment, prefix_len, owner_map, stripe_map, block_kv, table, pool):
     groups, slots, width = pool.shape
     new_count = block_kv.shape[0]
     count = new_count // groups
     block = jax.ShapeDtypeStruct((slots, width + width * count // slots), jnp.bfloat16)
     info = jax.ShapeDtypeStruct((info_rows(new_count)[1], HEAD_DIM), jnp.float32)
     *blocks, info = pl.pallas_call(
-        functools.partial(front_kernel, far),
+        functools.partial(front_kernel, order),
         out_shape=[block] * AHEAD + [info],
         in_specs=[SMEM] + [ANY] * 7,
         out_specs=[ANY] * (AHEAD + 1),
@@ -205,17 +201,42 @@
     return blocks, info
 
 
-def query_kernel(info_ref, q_ref, pool_ref, near_ref, *refs):
+def pack_kernel(info_ref, pool_ref, *refs):
     groups, slots, width = pool_ref.shape
-    half = groups // 2
-    send_refs, refs = refs[: half - AHEAD], refs[half - AHEAD :]
-    rot_ref, own_ref, bias_ref, request_ref, scalar_ref, scalar_sem = refs
-    new_count = q_ref.shape[0]
+    targets, (scalar_ref, scalar_sem) = refs[: groups - AHEAD], refs[groups - AHEAD :]
+    new_count = slots * groups * (targets[0].shape[1] - width) // width
+    at, _ = info_rows(new_count)
     count = new_count // groups
-    quarter = width * count // slots // HEAD_DIM
-    at, _ = info_rows(new_count)
+    quarter = (targets[0].shape[1] - width) // HEAD_DIM
     scalar_copy = pltpu.make_async_copy(info_ref.at[pl.ds(at["scalars"], 8)], scalar_ref, scalar_sem)
     scalar_copy.start()
+    scalar_copy.wait()
+    for p, target in enumerate(targets, AHEAD):
+        target[:, 0:width] = pool_ref[scalar_ref[0, p].astype(jnp.int32)]
+        residue = scalar_ref[1, p].astype(jnp.int32)
+        for lanes in range(quarter):
+            target[:, width + lanes * HEAD_DIM : width + (lanes + 1) * HEAD_DIM] = fresh_rows(
+                info_ref, at["new"], residue, new_count, count, quarter, lanes
+            ).astype(jnp.bfloat16)
+
+
+def pack_others(info, pool, new_count):
+    groups, slots, width = pool.shape
+    block = (slots, width + width * (new_count // groups) // slots)
+    return pl.pallas_call(
+        pack_kernel,
+        out_shape=[jax.ShapeDtypeStruct(block, jnp.bfloat16)] * (groups - AHEAD),
+        in_specs=[VMEM] * 2,
+        out_specs=[VMEM] * (groups - AHEAD),
+        scratch_shapes=[pltpu.SMEM((8, HEAD_DIM), jnp.float32), pltpu.SemaphoreType.DMA],
+        compiler_params=params(32),
+        name="pack_others",
+    )(info, pool)
+
+
+def query_kernel(info_ref, q_ref, rot_ref, own_ref, bias_ref, request_ref):
+    new_count = q_ref.shape[0]
+    at, _ = info_rows(new_count)
     cosine = info_ref[at["cos"] : at["cos"] + new_count]
     sine = info_ref[at["sin"] : at["sin"] + new_count]
     for row in range(bias_ref.shape[1] // HEAD_DIM):
@@ -228,41 +249,23 @@
     for head in range(Q_HEADS):
         rows = slice((head % PER_KV) * new_count, (head % PER_KV + 1) * new_count)
         rot_ref[head // PER_KV, rows, :] = turn(q_ref[:, column(head)], cosine, sine)
-    scalar_copy.wait()
-    targets = [near_ref.at[p] for p in range(half)] + [None] * AHEAD + list(send_refs)
-    for p, target in enumerate(targets):
-        if target is None:
-            continue
-        target[:, 0:width] = pool_ref[scalar_ref[0, p].astype(jnp.int32)]
-        residue = scalar_ref[1, p].astype(jnp.int32)
-        for lanes in range(quarter):
-            target[:, width + lanes * HEAD_DIM : width + (lanes + 1) * HEAD_DIM] = fresh_rows(
-                info_ref, at["new"], residue, new_count, count, quarter, lanes
-            ).astype(jnp.bfloat16)
-
-
-def rotate_queries(info, queries, pool):
-    groups, slots, width = pool.shape
+
+
+def rotate_queries(info, queries, span):
     new_count = queries.shape[0]
-    block = (slots, width + width * (new_count // groups) // slots)
-    sent = groups // 2 - AHEAD
-    near, *outs = pl.pallas_call(
+    return pl.pallas_call(
         query_kernel,
-        out_shape=[jax.ShapeDtypeStruct((groups // 2,) + block, jnp.bfloat16)]
-        + [jax.ShapeDtypeStruct(block, jnp.bfloat16)] * sent
-        + [
+        out_shape=(
             jax.ShapeDtypeStruct((KV_HEADS, PER_KV * new_count, HEAD_DIM), jnp.bfloat16),
             jax.ShapeDtypeStruct((2 * KV_HEADS, new_count, HEAD_DIM), jnp.bfloat16),
-            jax.ShapeDtypeStruct((8, groups * slots), jnp.float32),
+            jax.ShapeDtypeStruct((8, span), jnp.float32),
             jax.ShapeDtypeStruct((8, HEAD_DIM), jnp.int32),
-        ],
-        in_specs=[VMEM] * 3,
-        out_specs=[VMEM] * (sent + 5),
-        scratch_shapes=[pltpu.SMEM((8, HEAD_DIM), jnp.float32), pltpu.SemaphoreType.DMA],
+        ),
+        in_specs=[VMEM] * 2,
+        out_specs=[VMEM] * 4,
         compiler_params=params(32),
         name="rotate_queries",
-    )(info, queries, pool)
-    return near, outs[:sent], outs[sent:]
+    )(info, queries)
 
 
 def quotient(summed, total):
@@ -563,18 +566,19 @@
             me, assignment, prefix_len, stripe_map, owner_map, queries, block_kv, pool
         )
         return (attended[None], decode_kv[None])
-    half = groups // 2
-    far = far_partners(groups)
+    order = order_of(groups)
     table = rotation_tables(new_count)
-    blocks, info = front(far, me, assignment, prefix_len, owner_map, stripe_map, block_kv, table, pool)
-    near, other_blocks, (rot, own, bias, requests) = rotate_queries(info, queries, pool)
-    got = []
-    for block, t in zip(list(blocks) + list(other_blocks), far):
-        got.append(lax.ppermute(block, "pg", [(source, source ^ t) for source in range(groups)]))
-    halves = [list(range(low, low + half)) for low in range(0, groups, half)]
-    got_near = lax.all_to_all(near, "pg", split_axis=0, concat_axis=0, axis_index_groups=halves, tiled=True)
-    result, level, decode_kv = attend(rot, bias, own, [got_near] + got[:AHEAD], requests)
-    attended, decode_kv = attend_late(rot, bias, result, level, got[AHEAD:], half + AHEAD, requests, decode_kv)
+    blocks, info = front(order, me, assignment, prefix_len, owner_map, stripe_map, block_kv, table, pool)
+    blocks = list(blocks) + list(pack_others(info, pool, new_count))
+    rot, own, bias, requests = rotate_queries(info, queries, groups * slots)
+    rot, *blocks[AHEAD_OF_QUERIES:] = lax.optimization_barrier((rot, *blocks[AHEAD_OF_QUERIES:]))
+    got = [
+        lax.ppermute(block, "pg", [(source, source ^ t) for source in range(groups)]) if t else block
+        for block, t in zip(blocks, order)
+    ]
+    soon = groups - LATE
+    result, level, decode_kv = attend(rot, bias, own, got[:soon], requests)
+    attended, decode_kv = attend_late(rot, bias, result, level, got[soon:], soon, requests, decode_kv)
     return (attended[None], decode_kv[None])
 
 

time: 48.1 us -> 39.5 us (0.82)
  starting transfers between devices: 30.8 us -> 26.3 us
  waiting for transfers between devices: 3.34 us -> 0.82 us
  local copies, waits for them, and re-layouts: 2.33 us -> 1.1 us
    all_to_all x1 -> x0, starting transfers between devices: 5.27 us -> none  [shards(): lax.all_to_all(near, 'pg', split_axis=0, concat_axis=0, axis_index_groups...]
    ppermute x8 -> x15, waiting for transfers between devices: 3.34 us -> 0.82 us  [shards(): lax.ppermute(block, 'pg', [(source, source ^ t) for source in range(group...]
    unnamed x14 -> x6, local copies, waits for them, and re-layouts: 2.33 us -> 1.1 us
    ppermute x8 -> x15, starting transfers between devices: 25.5 us -> 26.3 us  [shards(): lax.ppermute(block, 'pg', [(source, source ^ t) for source in range(group...]
    pallas_call x2 -> x3, Pallas kernels: 4.26 us -> 3.92 us  [the longest x1 2.53 us: front(): pl.pallas_call(functools.partial(front_kernel, order), out_shape=[block]...]
  transfers between devices with their start and end apart: 9 -> 15, of which waited for: 3 -> 2; matrix products, arithmetic and copies ran while one was open for 0% -> 0% of each run, Pallas kernels for 8% -> 13%
where the time goes in v4:
time: 39.5 us; the launch traced here: 39.3 us
  starting transfers between devices  26.3 us (67%)
  Pallas kernels  10.4 us (26%)
  local copies, waits for them, and re-layouts  1.1 us (3%)
  waiting for transfers between devices  0.82 us (2%)
  between operations  0.72 us (2%)
    ppermute x15, starting transfers between devices, shards(): lax.ppermute(block, 'pg', [(source, source ^ t) for source in range(group...  26.3 us
    pallas_call x1, Pallas kernels, attend(): pl.pallas_call(functools.partial(attend_kernel, len(got), requests is not...  3.89 us
    pallas_call x1, Pallas kernels, attend_late(): pl.pallas_call(functools.partial(late_kernel, len(got), first), out_shape...  2.62 us
    pallas_call x1, Pallas kernels, front(): pl.pallas_call(functools.partial(front_kernel, order), out_shape=[block]...  2.53 us
    unnamed x6, local copies, waits for them, and re-layouts  1.1 us
    pallas_call x1, Pallas kernels, pack_others(): pl.pallas_call(pack_kernel, out_shape=[jax.ShapeDtypeStruct(block, jnp.bf...  0.87 us
    ppermute x15, waiting for transfers between devices, shards(): lax.ppermute(block, 'pg', [(source, source ^ t) for source in range(group...  0.82 us
  transfers between devices with their start and end apart: 15, of which 2 were waited for; matrix products, arithmetic and copies ran while one was open for 0% of the time, Pallas kernels for 13%

profile of v4, /device:TPU:0, one launch (start us, length us, event | category | flops | bytes accessed | tf_op | source)
XLA Modules:
  0.0 39.3 jit_solution(11210243175129943562)
XLA Ops:
  0.6 2.5 %front.1 = (bf16[32,1280]{1,0:T(8,128)(2,1)}, bf16[32,1280]{1,0:T(8,128)(2,1)}, bf16[32,1280]{1,0:T(8,128)(2,1)}, bf16[32,1280]{1,0:T(8,128)(2,1)}, f32[1296,128]{1,0:T(8,128)}) custom-call(s32[1]{0:T(128)} %bitcast.me_ref, s32[16]{0:T(128)} %assign_any.1, s32[16]{0:T(128)} %length_any.1, s32[16,16]{1,0:T(8,128)} %owner_any.1, s32[16,16]{1,0:T(8,128)} %stripe_any.1, ...), custom_call_target="tpu_custom_call" | custom-call | tf_op jit(solution)/shard_map/front/pallas_call | solution.py:177
  3.2 4.1 %collective-permute-start = (bf16[32,1280]{1,0:T(8,128)(2,1)}, bf16[32,1280]{1,0:T(8,128)(2,1)S(1)}, u32[]{:S(2)}, u32[]{:S(2)}) collective-permute-start(bf16[32,1280]{1,0:T(8,128)(2,1)} %get-tuple-element.50), channel_id=1, source_target_pairs={{0,8},{1,9},{2,10},{3,11},{4,12},{5,13},{6,14},{7,15},{8,0},{9,1},... | collective-permute-start | bytes 245768 | tf_op jit(solution)/shard_map/ppermute | solution.py:576
  7.3 1.7 %collective-permute-start.1 = (bf16[32,1280]{1,0:T(8,128)(2,1)}, bf16[32,1280]{1,0:T(8,128)(2,1)S(1)}, u32[]{:S(2)}, u32[]{:S(2)}) collective-permute-start(bf16[32,1280]{1,0:T(8,128)(2,1)} %get-tuple-element.51), channel_id=1, source_target_pairs={{0,7},{1,6},{2,5},{3,4},{4,3},{5,2},{6,1},{7,0},{8,15},{9,14},{10,... | collective-permute-start | bytes 245768 | tf_op jit(solution)/shard_map/ppermute | solution.py:576
  9.0 0.9 %collective-permute-start.2 = (bf16[32,1280]{1,0:T(8,128)(2,1)}, bf16[32,1280]{1,0:T(8,128)(2,1)S(1)}, u32[]{:S(2)}, u32[]{:S(2)}) collective-permute-start(bf16[32,1280]{1,0:T(8,128)(2,1)} %get-tuple-element.52), channel_id=1, source_target_pairs={{0,9},{1,8},{2,11},{3,10},{4,13},{5,12},{6,15},{7,14},{8,1},{9,0},... | collective-permute-start | bytes 245768 | tf_op jit(solution)/shard_map/ppermute | solution.py:576
  9.9 0.1 collective-permute-start.3
  10.0 1.1 %copy-done.1 = f32[1296,128]{1,0:T(8,128)S(1)} copy-done((f32[1296,128]{1,0:T(8,128)S(1)}, f32[1296,128]{1,0:T(8,128)}, u32[]{:S(2)}) %copy-start.1) | copy-done | bytes 663576
  11.1 0.9 %pack_others.1 = (bf16[32,1280]{1,0:T(8,128)(2,1)S(1)}, bf16[32,1280]{1,0:T(8,128)(2,1)S(1)}, bf16[32,1280]{1,0:T(8,128)(2,1)S(1)}, bf16[32,1280]{1,0:T(8,128)(2...) custom-call(f32[1296,128]{1,0:T(8,128)S(1)} %copy-done.1, ...), custom_call_target="tpu_custom_call" | custom-call | tf_op jit(solution)/shard_map/pack_others/pallas_call | solution.py:226
  12.0 3.9 %collective-permute-start.4 = (bf16[32,1280]{1,0:T(8,128)(2,1)S(1)}, bf16[32,1280]{1,0:T(8,128)(2,1)S(1)}, u32[]{:S(2)}, u32[]{:S(2)}) collective-permute-start(bf16[32,1280]{1,0:T(8,128)(2,1)S(1)} %get-tuple-element.54), channel_id=1, source_target_pairs={{0,10},{1,11},{2,8},{3,9},{4,14},{5,15},{6,12},{7,13},{8,2},{9,3},... | collective-permute-start | bytes 245768 | tf_op jit(solution)/shard_map/ppermute | solution.py:576
  15.8 0.5 %rotate_queries.1 = (bf16[4,1024,128]{2,1,0:T(8,128)(2,1)S(1)}, bf16[8,128,128]{2,1,0:T(8,128)(2,1)S(1)}, f32[8,512]{1,0:T(8,128)S(1)}, s32[8,128]{1,0:T(8,128)S(1)}) custom-call(f32[1296,128]{1,0:T(8,128)S(1)} %copy-done.1, bf16[128,4096]{1,0:T(8,128)(2,1)S(1)} %bitcast.8), custom_call_target="tpu_custom_call" | custom-call | tf_op jit(solution)/shard_map/rotate_queries/pallas_call | solution.py:256
  16.4 0.2 collective-permute-start.5
  16.6 1.4 %collective-permute-start.6 = (bf16[32,1280]{1,0:T(8,128)(2,1)S(1)}, bf16[32,1280]{1,0:T(8,128)(2,1)S(1)}, u32[]{:S(2)}, u32[]{:S(2)}) collective-permute-start(bf16[32,1280]{1,0:T(8,128)(2,1)S(1)} %get-tuple-element.56), channel_id=1, source_target_pairs={{0,11},{1,10},{2,9},{3,8},{4,15},{5,14},{6,13},{7,12},{8,3},{9,2},... | collective-permute-start | bytes 245768 | tf_op jit(solution)/shard_map/ppermute | solution.py:576
  18.0 0.0 collective-permute-done.2.refs_2_
  18.0 0.4 %collective-permute-start.7 = (bf16[32,1280]{1,0:T(8,128)(2,1)S(1)}, bf16[32,1280]{1,0:T(8,128)(2,1)S(1)}, u32[]{:S(2)}, u32[]{:S(2)}) collective-permute-start(bf16[32,1280]{1,0:T(8,128)(2,1)S(1)} %get-tuple-element.57), channel_id=1, source_target_pairs={{0,4},{1,5},{2,6},{3,7},{4,0},{5,1},{6,2},{7,3},{8,12},{9,13},{10,... | collective-permute-start | bytes 245768 | tf_op jit(solution)/shard_map/ppermute | solution.py:576
  18.5 0.0 collective-permute-done.3.refs_3_
  18.5 3.6 %collective-permute-start.8 = (bf16[32,1280]{1,0:T(8,128)(2,1)S(1)}, bf16[32,1280]{1,0:T(8,128)(2,1)S(1)}, u32[]{:S(2)}, u32[]{:S(2)}) collective-permute-start(bf16[32,1280]{1,0:T(8,128)(2,1)S(1)} %get-tuple-element.58), channel_id=1, source_target_pairs={{0,12},{1,13},{2,14},{3,15},{4,8},{5,9},{6,10},{7,11},{8,4},{9,5},... | collective-permute-start | bytes 245768 | tf_op jit(solution)/shard_map/ppermute | solution.py:576
  22.1 0.3 collective-permute-done.5.refs_5_
  22.4 1.3 %collective-permute-start.10 = (bf16[32,1280]{1,0:T(8,128)(2,1)S(1)}, bf16[32,1280]{1,0:T(8,128)(2,1)S(1)}, u32[]{:S(2)}, u32[]{:S(2)}) collective-permute-start(bf16[32,1280]{1,0:T(8,128)(2,1)S(1)} %get-tuple-element.60), channel_id=1, source_target_pairs={{0,2},{1,3},{2,0},{3,1},{4,6},{5,7},{6,4},{7,5},{8,10},{9,11},{10,... | collective-permute-start | bytes 245768 | tf_op jit(solution)/shard_map/ppermute | solution.py:576
  23.7 3.8 %collective-permute-start.11 = (bf16[32,1280]{1,0:T(8,128)(2,1)S(1)}, bf16[32,1280]{1,0:T(8,128)(2,1)S(1)}, u32[]{:S(2)}, u32[]{:S(2)}) collective-permute-start(bf16[32,1280]{1,0:T(8,128)(2,1)S(1)} %get-tuple-element.65), channel_id=1, source_target_pairs={{0,13},{1,12},{2,15},{3,14},{4,9},{5,8},{6,11},{7,10},{8,5},{9,4},... | collective-permute-start | bytes 245768 | tf_op jit(solution)/shard_map/ppermute | solution.py:576
  27.5 2.2 %collective-permute-start.12 = (bf16[32,1280]{1,0:T(8,128)(2,1)S(1)}, bf16[32,1280]{1,0:T(8,128)(2,1)S(1)}, u32[]{:S(2)}, u32[]{:S(2)}) collective-permute-start(bf16[32,1280]{1,0:T(8,128)(2,1)S(1)} %get-tuple-element.66), channel_id=1, source_target_pairs={{0,14},{1,15},{2,12},{3,13},{4,10},{5,11},{6,8},{7,9},{8,6},{9,7},... | collective-permute-start | bytes 245768 | tf_op jit(solution)/shard_map/ppermute | solution.py:576
  29.7 0.0 collective-permute-start.13
  29.7 2.7 %collective-permute-start.14 = (bf16[32,1280]{1,0:T(8,128)(2,1)S(1)}, bf16[32,1280]{1,0:T(8,128)(2,1)S(1)}, u32[]{:S(2)}, u32[]{:S(2)}) collective-permute-start(bf16[32,1280]{1,0:T(8,128)(2,1)S(1)} %get-tuple-element.68), channel_id=1, source_target_pairs={{0,15},{1,14},{2,13},{3,12},{4,11},{5,10},{6,9},{7,8},{8,7},{9,6},... | collective-permute-start | bytes 245768 | tf_op jit(solution)/shard_map/ppermute | solution.py:576
  32.3 3.9 %attend.1 = (f32[4,1024,128]{2,1,0:T(8,128)S(1)}, f32[4,1024,128]{2,1,0:T(8,128)S(1)}, bf16[16,8,1024]{2,1,0:T(8,128)(2,1)}) custom-call(bf16[4,1024,128]{2,1,0:T(8,128)(2,1)S(1)} %get-tuple-element.47.rot_ref, f32[8,512]{1,0:T(8,128)S(1)} %get-tuple-element.48.bias_ref, bf16[8,128,128]{2,1,0:T(8,128)(2,1)S(1)} %get-tuple-element.49.own_ref, ...), custom_call_target="tpu_custom_call" | custom-call | tf_op jit(solution)/shard_map/attend/pallas_call | solution.py:399
  36.3 0.4 %collective-permute-done.14.refs_3_ = bf16[32,1280]{1,0:T(8,128)(2,1)S(1)} collective-permute-done((bf16[32,1280]{1,0:T(8,128)(2,1)S(1)}, bf16[32,1280]{1,0:T(8,128)(2,1)S(1)}, u32[]{:S(2)}, u32[]{:S(2)}) %collective-permute-start.14) | collective-permute-done | bytes 81952 | tf_op jit(solution)/shard_map/ppermute | solution.py:576
  36.7 2.6 %attend_late.1 = (bf16[128,4096]{1,0:T(8,128)(2,1)}, bf16[16,8,1024]{2,1,0:T(8,128)(2,1)}) custom-call(bf16[4,1024,128]{2,1,0:T(8,128)(2,1)S(1)} %get-tuple-element.47.rot_ref, f32[8,512]{1,0:T(8,128)S(1)} %get-tuple-element.48.bias_ref, f32[4,1024,128]{2,1,0:T(8,128)S(1)} %get-tuple-element.63.result_ref, ...), custom_call_target="tpu_custom_call", output_to_operand_aliasing={{1}: (9, {})} | custom-call | tf_op jit(solution)/shard_map/attend_late/pallas_call | solution.py:499
  (17 shorter events, 0.0 us)
Async XLA Ops:
  0.6 9.4 %copy-start = (bf16[1,16,32,1024]{3,2,1,0:T(8,128)(2,1)S(1)}, bf16[1,16,32,1024]{3,2,1,0:T(8,128)(2,1)}, u32[]{:S(2)}) copy-start(bf16[1,16,32,1024]{3,2,1,0:T(8,128)(2,1)} %param.10) | copy-start | bytes 3145732
  3.2 13.2 %collective-permute-start = (bf16[32,1280]{1,0:T(8,128)(2,1)}, bf16[32,1280]{1,0:T(8,128)(2,1)S(1)}, u32[]{:S(2)}, u32[]{:S(2)}) collective-permute-start(bf16[32,1280]{1,0:T(8,128)(2,1)} %get-tuple-element.50), channel_id=1, source_target_pairs={{0,8},{1,9},{2,10},{3,11},{4,12},{5,13},{6,14},{7,15},{8,0},{9,1},... | collective-permute-start | bytes 245768 | tf_op jit(solution)/shard_map/ppermute | solution.py:576
  7.3 9.4 %collective-permute-start.1 = (bf16[32,1280]{1,0:T(8,128)(2,1)}, bf16[32,1280]{1,0:T(8,128)(2,1)S(1)}, u32[]{:S(2)}, u32[]{:S(2)}) collective-permute-start(bf16[32,1280]{1,0:T(8,128)(2,1)} %get-tuple-element.51), channel_id=1, source_target_pairs={{0,7},{1,6},{2,5},{3,4},{4,3},{5,2},{6,1},{7,0},{8,15},{9,14},{10,... | collective-permute-start | bytes 245768 | tf_op jit(solution)/shard_map/ppermute | solution.py:576
  9.0 9.1 %collective-permute-start.2 = (bf16[32,1280]{1,0:T(8,128)(2,1)}, bf16[32,1280]{1,0:T(8,128)(2,1)S(1)}, u32[]{:S(2)}, u32[]{:S(2)}) collective-permute-start(bf16[32,1280]{1,0:T(8,128)(2,1)} %get-tuple-element.52), channel_id=1, source_target_pairs={{0,9},{1,8},{2,11},{3,10},{4,13},{5,12},{6,15},{7,14},{8,1},{9,0},... | collective-permute-start | bytes 245768 | tf_op jit(solution)/shard_map/ppermute | solution.py:576
  9.9 8.6 %collective-permute-start.3 = (bf16[32,1280]{1,0:T(8,128)(2,1)}, bf16[32,1280]{1,0:T(8,128)(2,1)S(1)}, u32[]{:S(2)}, u32[]{:S(2)}) collective-permute-start(bf16[32,1280]{1,0:T(8,128)(2,1)} %get-tuple-element.53), channel_id=1, source_target_pairs={{0,6},{1,7},{2,4},{3,5},{4,2},{5,3},{6,0},{7,1},{8,14},{9,15},{10,... | collective-permute-start | bytes 245768 | tf_op jit(solution)/shard_map/ppermute | solution.py:576
  10.0 1.1 %copy-start.1 = (f32[1296,128]{1,0:T(8,128)S(1)}, f32[1296,128]{1,0:T(8,128)}, u32[]{:S(2)}) copy-start(f32[1296,128]{1,0:T(8,128)} %get-tuple-element.37.info_ref) | copy-start | bytes 1990660
  11.1 4.7 %copy-start.2 = (bf16[1,128,4096]{2,1,0:T(8,128)(2,1)S(1)}, bf16[1,128,4096]{2,1,0:T(8,128)(2,1)}, u32[]{:S(2)}) copy-start(bf16[1,128,4096]{2,1,0:T(8,128)(2,1)} %param.8) | copy-start | bytes 3145732
  12.0 10.1 %collective-permute-start.4 = (bf16[32,1280]{1,0:T(8,128)(2,1)S(1)}, bf16[32,1280]{1,0:T(8,128)(2,1)S(1)}, u32[]{:S(2)}, u32[]{:S(2)}) collective-permute-start(bf16[32,1280]{1,0:T(8,128)(2,1)S(1)} %get-tuple-element.54), channel_id=1, source_target_pairs={{0,10},{1,11},{2,8},{3,9},{4,14},{5,15},{6,12},{7,13},{8,2},{9,3},... | collective-permute-start | bytes 245768 | tf_op jit(solution)/shard_map/ppermute | solution.py:576
  16.4 6.0 %collective-permute-start.5 = (bf16[32,1280]{1,0:T(8,128)(2,1)S(1)}, bf16[32,1280]{1,0:T(8,128)(2,1)S(1)}, u32[]{:S(2)}, u32[]{:S(2)}) collective-permute-start(bf16[32,1280]{1,0:T(8,128)(2,1)S(1)} %get-tuple-element.55), channel_id=1, source_target_pairs={{0,5},{1,4},{2,7},{3,6},{4,1},{5,0},{6,3},{7,2},{8,13},{9,12},{10,... | collective-permute-start | bytes 245768 | tf_op jit(solution)/shard_map/ppermute | solution.py:576
  16.6 7.1 %collective-permute-start.6 = (bf16[32,1280]{1,0:T(8,128)(2,1)S(1)}, bf16[32,1280]{1,0:T(8,128)(2,1)S(1)}, u32[]{:S(2)}, u32[]{:S(2)}) collective-permute-start(bf16[32,1280]{1,0:T(8,128)(2,1)S(1)} %get-tuple-element.56), channel_id=1, source_target_pairs={{0,11},{1,10},{2,9},{3,8},{4,15},{5,14},{6,13},{7,12},{8,3},{9,2},... | collective-permute-start | bytes 245768 | tf_op jit(solution)/shard_map/ppermute | solution.py:576
  18.0 9.4 %collective-permute-start.7 = (bf16[32,1280]{1,0:T(8,128)(2,1)S(1)}, bf16[32,1280]{1,0:T(8,128)(2,1)S(1)}, u32[]{:S(2)}, u32[]{:S(2)}) collective-permute-start(bf16[32,1280]{1,0:T(8,128)(2,1)S(1)} %get-tuple-element.57), channel_id=1, source_target_pairs={{0,4},{1,5},{2,6},{3,7},{4,0},{5,1},{6,2},{7,3},{8,12},{9,13},{10,... | collective-permute-start | bytes 245768 | tf_op jit(solution)/shard_map/ppermute | solution.py:576
  18.5 11.2 %collective-permute-start.8 = (bf16[32,1280]{1,0:T(8,128)(2,1)S(1)}, bf16[32,1280]{1,0:T(8,128)(2,1)S(1)}, u32[]{:S(2)}, u32[]{:S(2)}) collective-permute-start(bf16[32,1280]{1,0:T(8,128)(2,1)S(1)} %get-tuple-element.58), channel_id=1, source_target_pairs={{0,12},{1,13},{2,14},{3,15},{4,8},{5,9},{6,10},{7,11},{8,4},{9,5},... | collective-permute-start | bytes 245768 | tf_op jit(solution)/shard_map/ppermute | solution.py:576
  22.1 7.6 %collective-permute-start.9 = (bf16[32,1280]{1,0:T(8,128)(2,1)S(1)}, bf16[32,1280]{1,0:T(8,128)(2,1)S(1)}, u32[]{:S(2)}, u32[]{:S(2)}) collective-permute-start(bf16[32,1280]{1,0:T(8,128)(2,1)S(1)} %get-tuple-element.59), channel_id=1, source_target_pairs={{0,3},{1,2},{2,1},{3,0},{4,7},{5,6},{6,5},{7,4},{8,11},{9,10},{10,... | collective-permute-start | bytes 245768 | tf_op jit(solution)/shard_map/ppermute | solution.py:576
  22.4 9.9 %collective-permute-start.10 = (bf16[32,1280]{1,0:T(8,128)(2,1)S(1)}, bf16[32,1280]{1,0:T(8,128)(2,1)S(1)}, u32[]{:S(2)}, u32[]{:S(2)}) collective-permute-start(bf16[32,1280]{1,0:T(8,128)(2,1)S(1)} %get-tuple-element.60), channel_id=1, source_target_pairs={{0,2},{1,3},{2,0},{3,1},{4,6},{5,7},{6,4},{7,5},{8,10},{9,11},{10,... | collective-permute-start | bytes 245768 | tf_op jit(solution)/shard_map/ppermute | solution.py:576
  23.7 12.5 %collective-permute-start.11 = (bf16[32,1280]{1,0:T(8,128)(2,1)S(1)}, bf16[32,1280]{1,0:T(8,128)(2,1)S(1)}, u32[]{:S(2)}, u32[]{:S(2)}) collective-permute-start(bf16[32,1280]{1,0:T(8,128)(2,1)S(1)} %get-tuple-element.65), channel_id=1, source_target_pairs={{0,13},{1,12},{2,15},{3,14},{4,9},{5,8},{6,11},{7,10},{8,5},{9,4},... | collective-permute-start | bytes 245768 | tf_op jit(solution)/shard_map/ppermute | solution.py:576
  27.5 8.8 %collective-permute-start.12 = (bf16[32,1280]{1,0:T(8,128)(2,1)S(1)}, bf16[32,1280]{1,0:T(8,128)(2,1)S(1)}, u32[]{:S(2)}, u32[]{:S(2)}) collective-permute-start(bf16[32,1280]{1,0:T(8,128)(2,1)S(1)} %get-tuple-element.66), channel_id=1, source_target_pairs={{0,14},{1,15},{2,12},{3,13},{4,10},{5,11},{6,8},{7,9},{8,6},{9,7},... | collective-permute-start | bytes 245768 | tf_op jit(solution)/shard_map/ppermute | solution.py:576
  29.7 6.6 %collective-permute-start.13 = (bf16[32,1280]{1,0:T(8,128)(2,1)S(1)}, bf16[32,1280]{1,0:T(8,128)(2,1)S(1)}, u32[]{:S(2)}, u32[]{:S(2)}) collective-permute-start(bf16[32,1280]{1,0:T(8,128)(2,1)S(1)} %get-tuple-element.67), channel_id=1, source_target_pairs={{0,1},{1,0},{2,3},{3,2},{4,5},{5,4},{6,7},{7,6},{8,9},{9,8},{10,11... | collective-permute-start | bytes 245768 | tf_op jit(solution)/shard_map/ppermute | solution.py:576
  29.7 7.0 %collective-permute-start.14 = (bf16[32,1280]{1,0:T(8,128)(2,1)S(1)}, bf16[32,1280]{1,0:T(8,128)(2,1)S(1)}, u32[]{:S(2)}, u32[]{:S(2)}) collective-permute-start(bf16[32,1280]{1,0:T(8,128)(2,1)S(1)} %get-tuple-element.68), channel_id=1, source_target_pairs={{0,15},{1,14},{2,13},{3,12},{4,11},{5,10},{6,9},{7,8},{8,7},{9,6},... | collective-permute-start | bytes 245768 | tf_op jit(solution)/shard_map/ppermute | solution.py:576

commit v5 on v4

--- a/solution.py
+++ b/solution.py
@@ -21,7 +21,7 @@
 SCALE = HEAD_DIM ** -0.5 / math.log(2.0)
 CHUNK = 256
 LATE = 4
-LATE_CHUNK = 256
+LATE_CHUNK = 512
 AHEAD = 4
 AHEAD_OF_QUERIES = 8
 
@@ -40,8 +40,8 @@
 
 def order_of(groups):
     half = groups // 2
-    far, near = list(range(half, 2 * half)), list(range(half - 1, 0, -1))
-    order = [(far if kind == "f" else near).pop(0) for kind in "fnfnfnfnfnnffnf"]
+    far, near = [t ^ half // 2 for t in range(half, 2 * half)], list(range(half - 1, 0, -1))
+    order = [(far if kind == "f" else near).pop(0) for kind in "ffnfnfnfnfnfnfn"]
     order.insert(groups - LATE - 1, 0)
     return order
 
@@ -131,17 +131,6 @@
         return pltpu.make_async_copy(info_ref.at[part_rows], info_any.at[part_rows], info_sems.at[part])
 
     info_copy(0, at["new"], rows).start()
-    for copy in pool_copies:
-        copy.wait()
-    sends = []
-    for p in range(AHEAD):
-        pack_ref[p, :, 0:width] = pool_ref[assign_ref[me ^ order[p]]]
-        for lanes in range(quarter):
-            pack_ref[p, :, width + lanes * HEAD_DIM : width + (lanes + 1) * HEAD_DIM] = fresh_rows(
-                info_ref, at["new"], residue_ref[me ^ order[p]], new_count, count, quarter, lanes
-            ).astype(jnp.bfloat16)
-        sends.append(pltpu.make_async_copy(pack_ref.at[p], send_refs[p], send_sems.at[p]))
-        sends[-1].start()
     info_ref[at["cos"] : at["cos"] + new_count] = cosine
     info_ref[at["sin"] : at["sin"] + new_count] = sine
     per_row = HEAD_DIM // slots
@@ -162,6 +151,17 @@
     scalars = jnp.where(row == 0, requests, residues)
     info_ref[at["scalars"] : at["scalars"] + 8] = scalars.astype(jnp.float32)
     info_copy(1, 0, at["new"]).start()
+    for copy in pool_copies:
+        copy.wait()
+    sends = []
+    for p in range(AHEAD):
+        pack_ref[p, :, 0:width] = pool_ref[assign_ref[me ^ order[p]]]
+        for lanes in range(quarter):
+            pack_ref[p, :, width + lanes * HEAD_DIM : width + (lanes + 1) * HEAD_DIM] = fresh_rows(
+                info_ref, at["new"], residue_ref[me ^ order[p]], new_count, count, quarter, lanes
+            ).astype(jnp.bfloat16)
+        sends.append(pltpu.make_async_copy(pack_ref.at[p], send_refs[p], send_sems.at[p]))
+        sends[-1].start()
     for copy in sends:
         copy.wait()
     info_copy(0, at["new"], rows).wait()

time: 39.5 us -> 40.9 us (1.035)
  waiting for transfers between devices: 0.82 us -> 3.73 us
  starting transfers between devices: 26.3 us -> 24.8 us
    ppermute x15, waiting for transfers between devices: 0.82 us -> 3.73 us  [shards(): lax.ppermute(block, 'pg', [(source, source ^ t) for source in range(group...]
    ppermute x15, starting transfers between devices: 26.3 us -> 24.8 us  [shards(): lax.ppermute(block, 'pg', [(source, source ^ t) for source in range(group...]
  transfers between devices with their start and end apart: 15 -> 15, of which waited for: 2 -> 3; matrix products, arithmetic and copies ran while one was open for 0% -> 0% of each run, Pallas kernels for 13% -> 13%
where the time goes in v5:
time: 40.9 us; the launch traced here: 40.7 us
  starting transfers between devices  24.8 us (61%)
  Pallas kernels  10.3 us (25%)
  waiting for transfers between devices  3.73 us (9%)
  local copies, waits for them, and re-layouts  1.1 us (3%)
  between operations  0.74 us (2%)
    ppermute x15, starting transfers between devices, shards(): lax.ppermute(block, 'pg', [(source, source ^ t) for source in range(group...  24.8 us
    pallas_call x1, Pallas kernels, attend(): pl.pallas_call(functools.partial(attend_kernel, len(got), requests is not...  3.89 us
    ppermute x15, waiting for transfers between devices, shards(): lax.ppermute(block, 'pg', [(source, source ^ t) for source in range(group...  3.73 us
    pallas_call x1, Pallas kernels, front(): pl.pallas_call(functools.partial(front_kernel, order), out_shape=[block]...  2.54 us
    pallas_call x1, Pallas kernels, attend_late(): pl.pallas_call(functools.partial(late_kernel, len(got), first), out_shape...  2.52 us
    unnamed x6, local copies, waits for them, and re-layouts  1.1 us
    pallas_call x1, Pallas kernels, pack_others(): pl.pallas_call(pack_kernel, out_shape=[jax.ShapeDtypeStruct(block, jnp.bf...  0.87 us
  transfers between devices with their start and end apart: 15, of which 3 were waited for; matrix products, arithmetic and copies ran while one was open for 0% of the time, Pallas kernels for 13%

profile of v5, /device:TPU:0, one launch (start us, length us, event | category | flops | bytes accessed | tf_op | source)
XLA Modules:
  0.0 40.7 jit_solution(102590485885413779)
XLA Ops:
  0.6 2.5 %front.1 = (bf16[32,1280]{1,0:T(8,128)(2,1)}, bf16[32,1280]{1,0:T(8,128)(2,1)}, bf16[32,1280]{1,0:T(8,128)(2,1)}, bf16[32,1280]{1,0:T(8,128)(2,1)}, f32[1296,128]{1,0:T(8,128)}) custom-call(s32[1]{0:T(128)} %bitcast.me_ref, s32[16]{0:T(128)} %assign_any.1, s32[16]{0:T(128)} %length_any.1, s32[16,16]{1,0:T(8,128)} %owner_any.1, s32[16,16]{1,0:T(8,128)} %stripe_any.1, ...), custom_call_target="tpu_custom_call" | custom-call | tf_op jit(solution)/shard_map/front/pallas_call | solution.py:177
  3.2 5.1 %collective-permute-start = (bf16[32,1280]{1,0:T(8,128)(2,1)}, bf16[32,1280]{1,0:T(8,128)(2,1)S(1)}, u32[]{:S(2)}, u32[]{:S(2)}) collective-permute-start(bf16[32,1280]{1,0:T(8,128)(2,1)} %get-tuple-element.50), channel_id=1, source_target_pairs={{0,12},{1,13},{2,14},{3,15},{4,8},{5,9},{6,10},{7,11},{8,4},{9,5},... | collective-permute-start | bytes 245768 | tf_op jit(solution)/shard_map/ppermute | solution.py:576
  8.3 0.0 collective-permute-start.1
  8.3 0.7 %collective-permute-start.2 = (bf16[32,1280]{1,0:T(8,128)(2,1)}, bf16[32,1280]{1,0:T(8,128)(2,1)S(1)}, u32[]{:S(2)}, u32[]{:S(2)}) collective-permute-start(bf16[32,1280]{1,0:T(8,128)(2,1)} %get-tuple-element.52), channel_id=1, source_target_pairs={{0,7},{1,6},{2,5},{3,4},{4,3},{5,2},{6,1},{7,0},{8,15},{9,14},{10,... | collective-permute-start | bytes 245768 | tf_op jit(solution)/shard_map/ppermute | solution.py:576
  9.0 3.3 %collective-permute-start.3 = (bf16[32,1280]{1,0:T(8,128)(2,1)}, bf16[32,1280]{1,0:T(8,128)(2,1)S(1)}, u32[]{:S(2)}, u32[]{:S(2)}) collective-permute-start(bf16[32,1280]{1,0:T(8,128)(2,1)} %get-tuple-element.53), channel_id=1, source_target_pairs={{0,14},{1,15},{2,12},{3,13},{4,10},{5,11},{6,8},{7,9},{8,6},{9,7},... | collective-permute-start | bytes 245768 | tf_op jit(solution)/shard_map/ppermute | solution.py:576
  12.3 1.1 %copy-done.1 = f32[1296,128]{1,0:T(8,128)S(1)} copy-done((f32[1296,128]{1,0:T(8,128)S(1)}, f32[1296,128]{1,0:T(8,128)}, u32[]{:S(2)}) %copy-start.1) | copy-done | bytes 663576
  13.3 0.9 %pack_others.1 = (bf16[32,1280]{1,0:T(8,128)(2,1)S(1)}, bf16[32,1280]{1,0:T(8,128)(2,1)S(1)}, bf16[32,1280]{1,0:T(8,128)(2,1)S(1)}, bf16[32,1280]{1,0:T(8,128)(2...) custom-call(f32[1296,128]{1,0:T(8,128)S(1)} %copy-done.1, ...), custom_call_target="tpu_custom_call" | custom-call | tf_op jit(solution)/shard_map/pack_others/pallas_call | solution.py:226
  14.2 2.6 %collective-permute-start.4 = (bf16[32,1280]{1,0:T(8,128)(2,1)S(1)}, bf16[32,1280]{1,0:T(8,128)(2,1)S(1)}, u32[]{:S(2)}, u32[]{:S(2)}) collective-permute-start(bf16[32,1280]{1,0:T(8,128)(2,1)S(1)} %get-tuple-element.54), channel_id=1, source_target_pairs={{0,6},{1,7},{2,4},{3,5},{4,2},{5,3},{6,0},{7,1},{8,14},{9,15},{10,... | collective-permute-start | bytes 245768 | tf_op jit(solution)/shard_map/ppermute | solution.py:576
  16.9 0.5 %rotate_queries.1 = (bf16[4,1024,128]{2,1,0:T(8,128)(2,1)S(1)}, bf16[8,128,128]{2,1,0:T(8,128)(2,1)S(1)}, f32[8,512]{1,0:T(8,128)S(1)}, s32[8,128]{1,0:T(8,128)S(1)}) custom-call(f32[1296,128]{1,0:T(8,128)S(1)} %copy-done.1, bf16[128,4096]{1,0:T(8,128)(2,1)S(1)} %bitcast.8), custom_call_target="tpu_custom_call" | custom-call | tf_op jit(solution)/shard_map/rotate_queries/pallas_call | solution.py:256
  17.4 0.0 collective-permute-done.refs_0_
  17.4 0.1 collective-permute-start.5
  17.5 0.0 collective-permute-done.1.refs_1_
  17.5 0.1 collective-permute-start.6
  17.6 3.9 %collective-permute-start.7 = (bf16[32,1280]{1,0:T(8,128)(2,1)S(1)}, bf16[32,1280]{1,0:T(8,128)(2,1)S(1)}, u32[]{:S(2)}, u32[]{:S(2)}) collective-permute-start(bf16[32,1280]{1,0:T(8,128)(2,1)S(1)} %get-tuple-element.57), channel_id=1, source_target_pairs={{0,8},{1,9},{2,10},{3,11},{4,12},{5,13},{6,14},{7,15},{8,0},{9,1},... | collective-permute-start | bytes 245768 | tf_op jit(solution)/shard_map/ppermute | solution.py:576
  21.5 0.8 %collective-permute-start.9 = (bf16[32,1280]{1,0:T(8,128)(2,1)S(1)}, bf16[32,1280]{1,0:T(8,128)(2,1)S(1)}, u32[]{:S(2)}, u32[]{:S(2)}) collective-permute-start(bf16[32,1280]{1,0:T(8,128)(2,1)S(1)} %get-tuple-element.59), channel_id=1, source_target_pairs={{0,9},{1,8},{2,11},{3,10},{4,13},{5,12},{6,15},{7,14},{8,1},{9,0},... | collective-permute-start | bytes 245768 | tf_op jit(solution)/shard_map/ppermute | solution.py:576
  22.3 2.6 %collective-permute-done.5.refs_5_ = bf16[32,1280]{1,0:T(8,128)(2,1)S(1)} collective-permute-done((bf16[32,1280]{1,0:T(8,128)(2,1)S(1)}, bf16[32,1280]{1,0:T(8,128)(2,1)S(1)}, u32[]{:S(2)}, u32[]{:S(2)}) %collective-permute-start.5) | collective-permute-done | bytes 81952 | tf_op jit(solution)/shard_map/ppermute | solution.py:576
  24.9 3.1 %collective-permute-start.11 = (bf16[32,1280]{1,0:T(8,128)(2,1)S(1)}, bf16[32,1280]{1,0:T(8,128)(2,1)S(1)}, u32[]{:S(2)}, u32[]{:S(2)}) collective-permute-start(bf16[32,1280]{1,0:T(8,128)(2,1)S(1)} %get-tuple-element.65), channel_id=1, source_target_pairs={{0,10},{1,11},{2,8},{3,9},{4,14},{5,15},{6,12},{7,13},{8,2},{9,3},... | collective-permute-start | bytes 245768 | tf_op jit(solution)/shard_map/ppermute | solution.py:576
  28.1 0.0 collective-permute-done.7.refs_7_
  28.1 2.3 %collective-permute-start.13 = (bf16[32,1280]{1,0:T(8,128)(2,1)S(1)}, bf16[32,1280]{1,0:T(8,128)(2,1)S(1)}, u32[]{:S(2)}, u32[]{:S(2)}) collective-permute-start(bf16[32,1280]{1,0:T(8,128)(2,1)S(1)} %get-tuple-element.67), channel_id=1, source_target_pairs={{0,11},{1,10},{2,9},{3,8},{4,15},{5,14},{6,13},{7,12},{8,3},{9,2},... | collective-permute-start | bytes 245768 | tf_op jit(solution)/shard_map/ppermute | solution.py:576
  30.4 0.8 %collective-permute-done.9.refs_9_ = bf16[32,1280]{1,0:T(8,128)(2,1)S(1)} collective-permute-done((bf16[32,1280]{1,0:T(8,128)(2,1)S(1)}, bf16[32,1280]{1,0:T(8,128)(2,1)S(1)}, u32[]{:S(2)}, u32[]{:S(2)}) %collective-permute-start.9) | collective-permute-done | bytes 81952 | tf_op jit(solution)/shard_map/ppermute | solution.py:576
  31.2 2.8 %collective-permute-start.14 = (bf16[32,1280]{1,0:T(8,128)(2,1)S(1)}, bf16[32,1280]{1,0:T(8,128)(2,1)S(1)}, u32[]{:S(2)}, u32[]{:S(2)}) collective-permute-start(bf16[32,1280]{1,0:T(8,128)(2,1)S(1)} %get-tuple-element.68), channel_id=1, source_target_pairs={{0,1},{1,0},{2,3},{3,2},{4,5},{5,4},{6,7},{7,6},{8,9},{9,8},{10,11... | collective-permute-start | bytes 245768 | tf_op jit(solution)/shard_map/ppermute | solution.py:576
  34.1 3.9 %attend.1 = (f32[4,1024,128]{2,1,0:T(8,128)S(1)}, f32[4,1024,128]{2,1,0:T(8,128)S(1)}, bf16[16,8,1024]{2,1,0:T(8,128)(2,1)}) custom-call(bf16[4,1024,128]{2,1,0:T(8,128)(2,1)S(1)} %get-tuple-element.47.rot_ref, f32[8,512]{1,0:T(8,128)S(1)} %get-tuple-element.48.bias_ref, bf16[8,128,128]{2,1,0:T(8,128)(2,1)S(1)} %get-tuple-element.49.own_ref, ...), custom_call_target="tpu_custom_call" | custom-call | tf_op jit(solution)/shard_map/attend/pallas_call | solution.py:399
  38.0 0.2 collective-permute-done.13.refs_2_
  38.2 2.5 %attend_late.1 = (bf16[128,4096]{1,0:T(8,128)(2,1)}, bf16[16,8,1024]{2,1,0:T(8,128)(2,1)}) custom-call(bf16[4,1024,128]{2,1,0:T(8,128)(2,1)S(1)} %get-tuple-element.47.rot_ref, f32[8,512]{1,0:T(8,128)S(1)} %get-tuple-element.48.bias_ref, f32[4,1024,128]{2,1,0:T(8,128)S(1)} %get-tuple-element.63.result_ref, ...), custom_call_target="tpu_custom_call", output_to_operand_aliasing={{1}: (9, {})} | custom-call | tf_op jit(solution)/shard_map/attend_late/pallas_call | solution.py:499
  (17 shorter events, 0.0 us)
Async XLA Ops:
  0.6 11.6 %copy-start = (bf16[1,16,32,1024]{3,2,1,0:T(8,128)(2,1)S(1)}, bf16[1,16,32,1024]{3,2,1,0:T(8,128)(2,1)}, u32[]{:S(2)}) copy-start(bf16[1,16,32,1024]{3,2,1,0:T(8,128)(2,1)} %param.10) | copy-start | bytes 3145732
  3.2 14.2 %collective-permute-start = (bf16[32,1280]{1,0:T(8,128)(2,1)}, bf16[32,1280]{1,0:T(8,128)(2,1)S(1)}, u32[]{:S(2)}, u32[]{:S(2)}) collective-permute-start(bf16[32,1280]{1,0:T(8,128)(2,1)} %get-tuple-element.50), channel_id=1, source_target_pairs={{0,12},{1,13},{2,14},{3,15},{4,8},{5,9},{6,10},{7,11},{8,4},{9,5},... | collective-permute-start | bytes 245768 | tf_op jit(solution)/shard_map/ppermute | solution.py:576
  8.3 9.2 %collective-permute-start.1 = (bf16[32,1280]{1,0:T(8,128)(2,1)}, bf16[32,1280]{1,0:T(8,128)(2,1)S(1)}, u32[]{:S(2)}, u32[]{:S(2)}) collective-permute-start(bf16[32,1280]{1,0:T(8,128)(2,1)} %get-tuple-element.51), channel_id=1, source_target_pairs={{0,13},{1,12},{2,15},{3,14},{4,9},{5,8},{6,11},{7,10},{8,5},{9,4},... | collective-permute-start | bytes 245768 | tf_op jit(solution)/shard_map/ppermute | solution.py:576
  8.3 9.3 %collective-permute-start.2 = (bf16[32,1280]{1,0:T(8,128)(2,1)}, bf16[32,1280]{1,0:T(8,128)(2,1)S(1)}, u32[]{:S(2)}, u32[]{:S(2)}) collective-permute-start(bf16[32,1280]{1,0:T(8,128)(2,1)} %get-tuple-element.52), channel_id=1, source_target_pairs={{0,7},{1,6},{2,5},{3,4},{4,3},{5,2},{6,1},{7,0},{8,15},{9,14},{10,... | collective-permute-start | bytes 245768 | tf_op jit(solution)/shard_map/ppermute | solution.py:576
  9.0 12.5 %collective-permute-start.3 = (bf16[32,1280]{1,0:T(8,128)(2,1)}, bf16[32,1280]{1,0:T(8,128)(2,1)S(1)}, u32[]{:S(2)}, u32[]{:S(2)}) collective-permute-start(bf16[32,1280]{1,0:T(8,128)(2,1)} %get-tuple-element.53), channel_id=1, source_target_pairs={{0,14},{1,15},{2,12},{3,13},{4,10},{5,11},{6,8},{7,9},{8,6},{9,7},... | collective-permute-start | bytes 245768 | tf_op jit(solution)/shard_map/ppermute | solution.py:576
  12.3 1.1 %copy-start.1 = (f32[1296,128]{1,0:T(8,128)S(1)}, f32[1296,128]{1,0:T(8,128)}, u32[]{:S(2)}) copy-start(f32[1296,128]{1,0:T(8,128)} %get-tuple-element.37.info_ref) | copy-start | bytes 1990660
  13.3 3.5 %copy-start.2 = (bf16[1,128,4096]{2,1,0:T(8,128)(2,1)S(1)}, bf16[1,128,4096]{2,1,0:T(8,128)(2,1)}, u32[]{:S(2)}) copy-start(bf16[1,128,4096]{2,1,0:T(8,128)(2,1)} %param.8) | copy-start | bytes 3145732
  14.2 7.3 %collective-permute-start.4 = (bf16[32,1280]{1,0:T(8,128)(2,1)S(1)}, bf16[32,1280]{1,0:T(8,128)(2,1)S(1)}, u32[]{:S(2)}, u32[]{:S(2)}) collective-permute-start(bf16[32,1280]{1,0:T(8,128)(2,1)S(1)} %get-tuple-element.54), channel_id=1, source_target_pairs={{0,6},{1,7},{2,4},{3,5},{4,2},{5,3},{6,0},{7,1},{8,14},{9,15},{10,... | collective-permute-start | bytes 245768 | tf_op jit(solution)/shard_map/ppermute | solution.py:576
  17.4 7.5 %collective-permute-start.5 = (bf16[32,1280]{1,0:T(8,128)(2,1)S(1)}, bf16[32,1280]{1,0:T(8,128)(2,1)S(1)}, u32[]{:S(2)}, u32[]{:S(2)}) collective-permute-start(bf16[32,1280]{1,0:T(8,128)(2,1)S(1)} %get-tuple-element.55), channel_id=1, source_target_pairs={{0,15},{1,14},{2,13},{3,12},{4,11},{5,10},{6,9},{7,8},{8,7},{9,6},... | collective-permute-start | bytes 245768 | tf_op jit(solution)/shard_map/ppermute | solution.py:576
  17.5 7.4 %collective-permute-start.6 = (bf16[32,1280]{1,0:T(8,128)(2,1)S(1)}, bf16[32,1280]{1,0:T(8,128)(2,1)S(1)}, u32[]{:S(2)}, u32[]{:S(2)}) collective-permute-start(bf16[32,1280]{1,0:T(8,128)(2,1)S(1)} %get-tuple-element.56), channel_id=1, source_target_pairs={{0,5},{1,4},{2,7},{3,6},{4,1},{5,0},{6,3},{7,2},{8,13},{9,12},{10,... | collective-permute-start | bytes 245768 | tf_op jit(solution)/shard_map/ppermute | solution.py:576
  17.6 10.5 %collective-permute-start.7 = (bf16[32,1280]{1,0:T(8,128)(2,1)S(1)}, bf16[32,1280]{1,0:T(8,128)(2,1)S(1)}, u32[]{:S(2)}, u32[]{:S(2)}) collective-permute-start(bf16[32,1280]{1,0:T(8,128)(2,1)S(1)} %get-tuple-element.57), channel_id=1, source_target_pairs={{0,8},{1,9},{2,10},{3,11},{4,12},{5,13},{6,14},{7,15},{8,0},{9,1},... | collective-permute-start | bytes 245768 | tf_op jit(solution)/shard_map/ppermute | solution.py:576
  21.5 6.6 %collective-permute-start.8 = (bf16[32,1280]{1,0:T(8,128)(2,1)S(1)}, bf16[32,1280]{1,0:T(8,128)(2,1)S(1)}, u32[]{:S(2)}, u32[]{:S(2)}) collective-permute-start(bf16[32,1280]{1,0:T(8,128)(2,1)S(1)} %get-tuple-element.58), channel_id=1, source_target_pairs={{0,4},{1,5},{2,6},{3,7},{4,0},{5,1},{6,2},{7,3},{8,12},{9,13},{10,... | collective-permute-start | bytes 245768 | tf_op jit(solution)/shard_map/ppermute | solution.py:576
  21.5 9.7 %collective-permute-start.9 = (bf16[32,1280]{1,0:T(8,128)(2,1)S(1)}, bf16[32,1280]{1,0:T(8,128)(2,1)S(1)}, u32[]{:S(2)}, u32[]{:S(2)}) collective-permute-start(bf16[32,1280]{1,0:T(8,128)(2,1)S(1)} %get-tuple-element.59), channel_id=1, source_target_pairs={{0,9},{1,8},{2,11},{3,10},{4,13},{5,12},{6,15},{7,14},{8,1},{9,0},... | collective-permute-start | bytes 245768 | tf_op jit(solution)/shard_map/ppermute | solution.py:576
  24.9 9.2 %collective-permute-start.10 = (bf16[32,1280]{1,0:T(8,128)(2,1)S(1)}, bf16[32,1280]{1,0:T(8,128)(2,1)S(1)}, u32[]{:S(2)}, u32[]{:S(2)}) collective-permute-start(bf16[32,1280]{1,0:T(8,128)(2,1)S(1)} %get-tuple-element.60), channel_id=1, source_target_pairs={{0,3},{1,2},{2,1},{3,0},{4,7},{5,6},{6,5},{7,4},{8,11},{9,10},{10,... | collective-permute-start | bytes 245768 | tf_op jit(solution)/shard_map/ppermute | solution.py:576
  24.9 13.1 %collective-permute-start.11 = (bf16[32,1280]{1,0:T(8,128)(2,1)S(1)}, bf16[32,1280]{1,0:T(8,128)(2,1)S(1)}, u32[]{:S(2)}, u32[]{:S(2)}) collective-permute-start(bf16[32,1280]{1,0:T(8,128)(2,1)S(1)} %get-tuple-element.65), channel_id=1, source_target_pairs={{0,10},{1,11},{2,8},{3,9},{4,14},{5,15},{6,12},{7,13},{8,2},{9,3},... | collective-permute-start | bytes 245768 | tf_op jit(solution)/shard_map/ppermute | solution.py:576
  28.1 9.9 %collective-permute-start.12 = (bf16[32,1280]{1,0:T(8,128)(2,1)S(1)}, bf16[32,1280]{1,0:T(8,128)(2,1)S(1)}, u32[]{:S(2)}, u32[]{:S(2)}) collective-permute-start(bf16[32,1280]{1,0:T(8,128)(2,1)S(1)} %get-tuple-element.66), channel_id=1, source_target_pairs={{0,2},{1,3},{2,0},{3,1},{4,6},{5,7},{6,4},{7,5},{8,10},{9,11},{10,... | collective-permute-start | bytes 245768 | tf_op jit(solution)/shard_map/ppermute | solution.py:576
  28.1 10.1 %collective-permute-start.13 = (bf16[32,1280]{1,0:T(8,128)(2,1)S(1)}, bf16[32,1280]{1,0:T(8,128)(2,1)S(1)}, u32[]{:S(2)}, u32[]{:S(2)}) collective-permute-start(bf16[32,1280]{1,0:T(8,128)(2,1)S(1)} %get-tuple-element.67), channel_id=1, source_target_pairs={{0,11},{1,10},{2,9},{3,8},{4,15},{5,14},{6,13},{7,12},{8,3},{9,2},... | collective-permute-start | bytes 245768 | tf_op jit(solution)/shard_map/ppermute | solution.py:576
  31.2 7.0 %collective-permute-start.14 = (bf16[32,1280]{1,0:T(8,128)(2,1)S(1)}, bf16[32,1280]{1,0:T(8,128)(2,1)S(1)}, u32[]{:S(2)}, u32[]{:S(2)}) collective-permute-start(bf16[32,1280]{1,0:T(8,128)(2,1)S(1)} %get-tuple-element.68), channel_id=1, source_target_pairs={{0,1},{1,0},{2,3},{3,2},{4,5},{5,4},{6,7},{7,6},{8,9},{9,8},{10,11... | collective-permute-start | bytes 245768 | tf_op jit(solution)/shard_map/ppermute | solution.py:576

commit v6 on v5

--- a/solution.py
+++ b/solution.py
@@ -40,8 +40,9 @@
 
 def order_of(groups):
     half = groups // 2
-    far, near = [t ^ half // 2 for t in range(half, 2 * half)], list(range(half - 1, 0, -1))
-    order = [(far if kind == "f" else near).pop(0) for kind in "ffnfnfnfnfnfnfn"]
+    near = list(range(half - 1, 0, -1))
+    far = [half + at // 2 + at % 2 * half // 2 for at in range(half)]
+    order = [(far if kind == "f" else near).pop(0) for kind in "fnfnfnfnfnnffnf"]
     order.insert(groups - LATE - 1, 0)
     return order
 

time: 40.9 us -> 40.5 us (level)
  starting transfers between devices: 24.8 us -> 22.4 us
  waiting for transfers between devices: 3.73 us -> 5.78 us
    ppermute x15, starting transfers between devices: 24.8 us -> 22.4 us  [shards(): lax.ppermute(block, 'pg', [(source, source ^ t) for source in range(group...]
    ppermute x15, waiting for transfers between devices: 3.73 us -> 5.78 us  [shards(): lax.ppermute(block, 'pg', [(source, source ^ t) for source in range(group...]
  transfers between devices with their start and end apart: 15 -> 15, of which waited for: 3 -> 2; matrix products, arithmetic and copies ran while one was open for 0% -> 0% of each run, Pallas kernels for 13% -> 13%
where the time goes in v6:
time: 40.5 us; the launch traced here: 40.3 us
  starting transfers between devices  22.4 us (55%)
  Pallas kernels  10.3 us (25%)
  waiting for transfers between devices  5.78 us (14%)
  local copies, waits for them, and re-layouts  1.1 us (3%)
  between operations  0.72 us (2%)
    ppermute x15, starting transfers between devices, shards(): lax.ppermute(block, 'pg', [(source, source ^ t) for source in range(group...  22.4 us
    ppermute x15, waiting for transfers between devices, shards(): lax.ppermute(block, 'pg', [(source, source ^ t) for source in range(group...  5.78 us
    pallas_call x1, Pallas kernels, attend(): pl.pallas_call(functools.partial(attend_kernel, len(got), requests is not...  3.9 us
    pallas_call x1, Pallas kernels, front(): pl.pallas_call(functools.partial(front_kernel, order), out_shape=[block]...  2.54 us
    pallas_call x1, Pallas kernels, attend_late(): pl.pallas_call(functools.partial(late_kernel, len(got), first), out_shape...  2.52 us
    unnamed x6, local copies, waits for them, and re-layouts  1.1 us
    pallas_call x1, Pallas kernels, pack_others(): pl.pallas_call(pack_kernel, out_shape=[jax.ShapeDtypeStruct(block, jnp.bf...  0.87 us
  transfers between devices with their start and end apart: 15, of which 2 were waited for; matrix products, arithmetic and copies ran while one was open for 0% of the time, Pallas kernels for 13%

profile of v6, /device:TPU:0, one launch (start us, length us, event | category | flops | bytes accessed | tf_op | source)
XLA Modules:
  0.0 40.3 jit_solution(9046294733209797772)
XLA Ops:
  0.6 2.5 %front.1 = (bf16[32,1280]{1,0:T(8,128)(2,1)}, bf16[32,1280]{1,0:T(8,128)(2,1)}, bf16[32,1280]{1,0:T(8,128)(2,1)}, bf16[32,1280]{1,0:T(8,128)(2,1)}, f32[1296,128]{1,0:T(8,128)}) custom-call(s32[1]{0:T(128)} %bitcast.me_ref, s32[16]{0:T(128)} %assign_any.1, s32[16]{0:T(128)} %length_any.1, s32[16,16]{1,0:T(8,128)} %owner_any.1, s32[16,16]{1,0:T(8,128)} %stripe_any.1, ...), custom_call_target="tpu_custom_call" | custom-call | tf_op jit(solution)/shard_map/front/pallas_call | solution.py:178
  3.2 4.1 %collective-permute-start = (bf16[32,1280]{1,0:T(8,128)(2,1)}, bf16[32,1280]{1,0:T(8,128)(2,1)S(1)}, u32[]{:S(2)}, u32[]{:S(2)}) collective-permute-start(bf16[32,1280]{1,0:T(8,128)(2,1)} %get-tuple-element.50), channel_id=1, source_target_pairs={{0,8},{1,9},{2,10},{3,11},{4,12},{5,13},{6,14},{7,15},{8,0},{9,1},... | collective-permute-start | bytes 245768 | tf_op jit(solution)/shard_map/ppermute | solution.py:577
  7.3 1.7 %collective-permute-start.1 = (bf16[32,1280]{1,0:T(8,128)(2,1)}, bf16[32,1280]{1,0:T(8,128)(2,1)S(1)}, u32[]{:S(2)}, u32[]{:S(2)}) collective-permute-start(bf16[32,1280]{1,0:T(8,128)(2,1)} %get-tuple-element.51), channel_id=1, source_target_pairs={{0,7},{1,6},{2,5},{3,4},{4,3},{5,2},{6,1},{7,0},{8,15},{9,14},{10,... | collective-permute-start | bytes 245768 | tf_op jit(solution)/shard_map/ppermute | solution.py:577
  9.0 0.2 collective-permute-start.2
  9.2 0.6 %collective-permute-start.3 = (bf16[32,1280]{1,0:T(8,128)(2,1)}, bf16[32,1280]{1,0:T(8,128)(2,1)S(1)}, u32[]{:S(2)}, u32[]{:S(2)}) collective-permute-start(bf16[32,1280]{1,0:T(8,128)(2,1)} %get-tuple-element.53), channel_id=1, source_target_pairs={{0,6},{1,7},{2,4},{3,5},{4,2},{5,3},{6,0},{7,1},{8,14},{9,15},{10,... | collective-permute-start | bytes 245768 | tf_op jit(solution)/shard_map/ppermute | solution.py:577
  9.9 1.1 %copy-done.1 = f32[1296,128]{1,0:T(8,128)S(1)} copy-done((f32[1296,128]{1,0:T(8,128)S(1)}, f32[1296,128]{1,0:T(8,128)}, u32[]{:S(2)}) %copy-start.1) | copy-done | bytes 663576
  11.0 0.9 %pack_others.1 = (bf16[32,1280]{1,0:T(8,128)(2,1)S(1)}, bf16[32,1280]{1,0:T(8,128)(2,1)S(1)}, bf16[32,1280]{1,0:T(8,128)(2,1)S(1)}, bf16[32,1280]{1,0:T(8,128)(2...) custom-call(f32[1296,128]{1,0:T(8,128)S(1)} %copy-done.1, ...), custom_call_target="tpu_custom_call" | custom-call | tf_op jit(solution)/shard_map/pack_others/pallas_call | solution.py:227
  11.8 3.5 %collective-permute-start.4 = (bf16[32,1280]{1,0:T(8,128)(2,1)S(1)}, bf16[32,1280]{1,0:T(8,128)(2,1)S(1)}, u32[]{:S(2)}, u32[]{:S(2)}) collective-permute-start(bf16[32,1280]{1,0:T(8,128)(2,1)S(1)} %get-tuple-element.54), channel_id=1, source_target_pairs={{0,9},{1,8},{2,11},{3,10},{4,13},{5,12},{6,15},{7,14},{8,1},{9,0},... | collective-permute-start | bytes 245768 | tf_op jit(solution)/shard_map/ppermute | solution.py:577
  15.4 0.5 %rotate_queries.1 = (bf16[4,1024,128]{2,1,0:T(8,128)(2,1)S(1)}, bf16[8,128,128]{2,1,0:T(8,128)(2,1)S(1)}, f32[8,512]{1,0:T(8,128)S(1)}, s32[8,128]{1,0:T(8,128)S(1)}) custom-call(f32[1296,128]{1,0:T(8,128)S(1)} %copy-done.1, bf16[128,4096]{1,0:T(8,128)(2,1)S(1)} %bitcast.8), custom_call_target="tpu_custom_call" | custom-call | tf_op jit(solution)/shard_map/rotate_queries/pallas_call | solution.py:257
  15.9 0.0 collective-permute-done.refs_0_
  15.9 0.1 collective-permute-start.5
  16.0 0.0 collective-permute-done.1.refs_1_
  16.0 1.4 %collective-permute-start.6 = (bf16[32,1280]{1,0:T(8,128)(2,1)S(1)}, bf16[32,1280]{1,0:T(8,128)(2,1)S(1)}, u32[]{:S(2)}, u32[]{:S(2)}) collective-permute-start(bf16[32,1280]{1,0:T(8,128)(2,1)S(1)} %get-tuple-element.56), channel_id=1, source_target_pairs={{0,13},{1,12},{2,15},{3,14},{4,9},{5,8},{6,11},{7,10},{8,5},{9,4},... | collective-permute-start | bytes 245768 | tf_op jit(solution)/shard_map/ppermute | solution.py:577
  17.4 0.0 collective-permute-done.2.refs_2_
  17.4 0.4 collective-permute-start.7
  17.8 3.3 %collective-permute-start.8 = (bf16[32,1280]{1,0:T(8,128)(2,1)S(1)}, bf16[32,1280]{1,0:T(8,128)(2,1)S(1)}, u32[]{:S(2)}, u32[]{:S(2)}) collective-permute-start(bf16[32,1280]{1,0:T(8,128)(2,1)S(1)} %get-tuple-element.58), channel_id=1, source_target_pairs={{0,10},{1,11},{2,8},{3,9},{4,14},{5,15},{6,12},{7,13},{8,2},{9,3},... | collective-permute-start | bytes 245768 | tf_op jit(solution)/shard_map/ppermute | solution.py:577
  21.2 3.9 %collective-permute-start.10 = (bf16[32,1280]{1,0:T(8,128)(2,1)S(1)}, bf16[32,1280]{1,0:T(8,128)(2,1)S(1)}, u32[]{:S(2)}, u32[]{:S(2)}) collective-permute-start(bf16[32,1280]{1,0:T(8,128)(2,1)S(1)} %get-tuple-element.60), channel_id=1, source_target_pairs={{0,2},{1,3},{2,0},{3,1},{4,6},{5,7},{6,4},{7,5},{8,10},{9,11},{10,... | collective-permute-start | bytes 245768 | tf_op jit(solution)/shard_map/ppermute | solution.py:577
  25.1 1.0 %collective-permute-start.11 = (bf16[32,1280]{1,0:T(8,128)(2,1)S(1)}, bf16[32,1280]{1,0:T(8,128)(2,1)S(1)}, u32[]{:S(2)}, u32[]{:S(2)}) collective-permute-start(bf16[32,1280]{1,0:T(8,128)(2,1)S(1)} %get-tuple-element.65), channel_id=1, source_target_pairs={{0,14},{1,15},{2,12},{3,13},{4,10},{5,11},{6,8},{7,9},{8,6},{9,7},... | collective-permute-start | bytes 245768 | tf_op jit(solution)/shard_map/ppermute | solution.py:577
  26.1 0.2 collective-permute-start.12
  26.3 2.3 %collective-permute-done.8.refs_8_ = bf16[32,1280]{1,0:T(8,128)(2,1)S(1)} collective-permute-done((bf16[32,1280]{1,0:T(8,128)(2,1)S(1)}, bf16[32,1280]{1,0:T(8,128)(2,1)S(1)}, u32[]{:S(2)}, u32[]{:S(2)}) %collective-permute-start.8) | collective-permute-done | bytes 81952 | tf_op jit(solution)/shard_map/ppermute | solution.py:577
  28.6 1.8 %collective-permute-start.14 = (bf16[32,1280]{1,0:T(8,128)(2,1)S(1)}, bf16[32,1280]{1,0:T(8,128)(2,1)S(1)}, u32[]{:S(2)}, u32[]{:S(2)}) collective-permute-start(bf16[32,1280]{1,0:T(8,128)(2,1)S(1)} %get-tuple-element.68), channel_id=1, source_target_pairs={{0,15},{1,14},{2,13},{3,12},{4,11},{5,10},{6,9},{7,8},{8,7},{9,6},... | collective-permute-start | bytes 245768 | tf_op jit(solution)/shard_map/ppermute | solution.py:577
  30.5 3.9 %attend.1 = (f32[4,1024,128]{2,1,0:T(8,128)S(1)}, f32[4,1024,128]{2,1,0:T(8,128)S(1)}, bf16[16,8,1024]{2,1,0:T(8,128)(2,1)}) custom-call(bf16[4,1024,128]{2,1,0:T(8,128)(2,1)S(1)} %get-tuple-element.47.rot_ref, f32[8,512]{1,0:T(8,128)S(1)} %get-tuple-element.48.bias_ref, bf16[8,128,128]{2,1,0:T(8,128)(2,1)S(1)} %get-tuple-element.49.own_ref, ...), custom_call_target="tpu_custom_call" | custom-call | tf_op jit(solution)/shard_map/attend/pallas_call | solution.py:400
  34.4 3.4 %collective-permute-done.12.refs_1_ = bf16[32,1280]{1,0:T(8,128)(2,1)S(1)} collective-permute-done((bf16[32,1280]{1,0:T(8,128)(2,1)S(1)}, bf16[32,1280]{1,0:T(8,128)(2,1)S(1)}, u32[]{:S(2)}, u32[]{:S(2)}) %collective-permute-start.12) | collective-permute-done | bytes 81952 | tf_op jit(solution)/shard_map/ppermute | solution.py:577
  37.8 2.5 %attend_late.1 = (bf16[128,4096]{1,0:T(8,128)(2,1)}, bf16[16,8,1024]{2,1,0:T(8,128)(2,1)}) custom-call(bf16[4,1024,128]{2,1,0:T(8,128)(2,1)S(1)} %get-tuple-element.47.rot_ref, f32[8,512]{1,0:T(8,128)S(1)} %get-tuple-element.48.bias_ref, f32[4,1024,128]{2,1,0:T(8,128)S(1)} %get-tuple-element.63.result_ref, ...), custom_call_target="tpu_custom_call", output_to_operand_aliasing={{1}: (9, {})} | custom-call | tf_op jit(solution)/shard_map/attend_late/pallas_call | solution.py:500
  (17 shorter events, 0.0 us)
Async XLA Ops:
  0.6 9.2 %copy-start = (bf16[1,16,32,1024]{3,2,1,0:T(8,128)(2,1)S(1)}, bf16[1,16,32,1024]{3,2,1,0:T(8,128)(2,1)}, u32[]{:S(2)}) copy-start(bf16[1,16,32,1024]{3,2,1,0:T(8,128)(2,1)} %param.10) | copy-start | bytes 3145732
  3.2 12.7 %collective-permute-start = (bf16[32,1280]{1,0:T(8,128)(2,1)}, bf16[32,1280]{1,0:T(8,128)(2,1)S(1)}, u32[]{:S(2)}, u32[]{:S(2)}) collective-permute-start(bf16[32,1280]{1,0:T(8,128)(2,1)} %get-tuple-element.50), channel_id=1, source_target_pairs={{0,8},{1,9},{2,10},{3,11},{4,12},{5,13},{6,14},{7,15},{8,0},{9,1},... | collective-permute-start | bytes 245768 | tf_op jit(solution)/shard_map/ppermute | solution.py:577
  7.3 8.7 %collective-permute-start.1 = (bf16[32,1280]{1,0:T(8,128)(2,1)}, bf16[32,1280]{1,0:T(8,128)(2,1)S(1)}, u32[]{:S(2)}, u32[]{:S(2)}) collective-permute-start(bf16[32,1280]{1,0:T(8,128)(2,1)} %get-tuple-element.51), channel_id=1, source_target_pairs={{0,7},{1,6},{2,5},{3,4},{4,3},{5,2},{6,1},{7,0},{8,15},{9,14},{10,... | collective-permute-start | bytes 245768 | tf_op jit(solution)/shard_map/ppermute | solution.py:577
  9.0 8.4 %collective-permute-start.2 = (bf16[32,1280]{1,0:T(8,128)(2,1)}, bf16[32,1280]{1,0:T(8,128)(2,1)S(1)}, u32[]{:S(2)}, u32[]{:S(2)}) collective-permute-start(bf16[32,1280]{1,0:T(8,128)(2,1)} %get-tuple-element.52), channel_id=1, source_target_pairs={{0,12},{1,13},{2,14},{3,15},{4,8},{5,9},{6,10},{7,11},{8,4},{9,5},... | collective-permute-start | bytes 245768 | tf_op jit(solution)/shard_map/ppermute | solution.py:577
  9.2 8.6 %collective-permute-start.3 = (bf16[32,1280]{1,0:T(8,128)(2,1)}, bf16[32,1280]{1,0:T(8,128)(2,1)S(1)}, u32[]{:S(2)}, u32[]{:S(2)}) collective-permute-start(bf16[32,1280]{1,0:T(8,128)(2,1)} %get-tuple-element.53), channel_id=1, source_target_pairs={{0,6},{1,7},{2,4},{3,5},{4,2},{5,3},{6,0},{7,1},{8,14},{9,15},{10,... | collective-permute-start | bytes 245768 | tf_op jit(solution)/shard_map/ppermute | solution.py:577
  9.9 1.1 %copy-start.1 = (f32[1296,128]{1,0:T(8,128)S(1)}, f32[1296,128]{1,0:T(8,128)}, u32[]{:S(2)}) copy-start(f32[1296,128]{1,0:T(8,128)} %get-tuple-element.37.info_ref) | copy-start | bytes 1990660
  11.0 4.4 %copy-start.2 = (bf16[1,128,4096]{2,1,0:T(8,128)(2,1)S(1)}, bf16[1,128,4096]{2,1,0:T(8,128)(2,1)}, u32[]{:S(2)}) copy-start(bf16[1,128,4096]{2,1,0:T(8,128)(2,1)} %param.8) | copy-start | bytes 3145732
  11.8 9.3 %collective-permute-start.4 = (bf16[32,1280]{1,0:T(8,128)(2,1)S(1)}, bf16[32,1280]{1,0:T(8,128)(2,1)S(1)}, u32[]{:S(2)}, u32[]{:S(2)}) collective-permute-start(bf16[32,1280]{1,0:T(8,128)(2,1)S(1)} %get-tuple-element.54), channel_id=1, source_target_pairs={{0,9},{1,8},{2,11},{3,10},{4,13},{5,12},{6,15},{7,14},{8,1},{9,0},... | collective-permute-start | bytes 245768 | tf_op jit(solution)/shard_map/ppermute | solution.py:577
  15.9 5.3 %collective-permute-start.5 = (bf16[32,1280]{1,0:T(8,128)(2,1)S(1)}, bf16[32,1280]{1,0:T(8,128)(2,1)S(1)}, u32[]{:S(2)}, u32[]{:S(2)}) collective-permute-start(bf16[32,1280]{1,0:T(8,128)(2,1)S(1)} %get-tuple-element.55), channel_id=1, source_target_pairs={{0,5},{1,4},{2,7},{3,6},{4,1},{5,0},{6,3},{7,2},{8,13},{9,12},{10,... | collective-permute-start | bytes 245768 | tf_op jit(solution)/shard_map/ppermute | solution.py:577
  16.0 9.1 %collective-permute-start.6 = (bf16[32,1280]{1,0:T(8,128)(2,1)S(1)}, bf16[32,1280]{1,0:T(8,128)(2,1)S(1)}, u32[]{:S(2)}, u32[]{:S(2)}) collective-permute-start(bf16[32,1280]{1,0:T(8,128)(2,1)S(1)} %get-tuple-element.56), channel_id=1, source_target_pairs={{0,13},{1,12},{2,15},{3,14},{4,9},{5,8},{6,11},{7,10},{8,5},{9,4},... | collective-permute-start | bytes 245768 | tf_op jit(solution)/shard_map/ppermute | solution.py:577
  17.4 8.7 %collective-permute-start.7 = (bf16[32,1280]{1,0:T(8,128)(2,1)S(1)}, bf16[32,1280]{1,0:T(8,128)(2,1)S(1)}, u32[]{:S(2)}, u32[]{:S(2)}) collective-permute-start(bf16[32,1280]{1,0:T(8,128)(2,1)S(1)} %get-tuple-element.57), channel_id=1, source_target_pairs={{0,4},{1,5},{2,6},{3,7},{4,0},{5,1},{6,2},{7,3},{8,12},{9,13},{10,... | collective-permute-start | bytes 245768 | tf_op jit(solution)/shard_map/ppermute | solution.py:577
  17.8 10.8 %collective-permute-start.8 = (bf16[32,1280]{1,0:T(8,128)(2,1)S(1)}, bf16[32,1280]{1,0:T(8,128)(2,1)S(1)}, u32[]{:S(2)}, u32[]{:S(2)}) collective-permute-start(bf16[32,1280]{1,0:T(8,128)(2,1)S(1)} %get-tuple-element.58), channel_id=1, source_target_pairs={{0,10},{1,11},{2,8},{3,9},{4,14},{5,15},{6,12},{7,13},{8,2},{9,3},... | collective-permute-start | bytes 245768 | tf_op jit(solution)/shard_map/ppermute | solution.py:577
  21.2 7.5 %collective-permute-start.9 = (bf16[32,1280]{1,0:T(8,128)(2,1)S(1)}, bf16[32,1280]{1,0:T(8,128)(2,1)S(1)}, u32[]{:S(2)}, u32[]{:S(2)}) collective-permute-start(bf16[32,1280]{1,0:T(8,128)(2,1)S(1)} %get-tuple-element.59), channel_id=1, source_target_pairs={{0,3},{1,2},{2,1},{3,0},{4,7},{5,6},{6,5},{7,4},{8,11},{9,10},{10,... | collective-permute-start | bytes 245768 | tf_op jit(solution)/shard_map/ppermute | solution.py:577
  21.2 9.3 %collective-permute-start.10 = (bf16[32,1280]{1,0:T(8,128)(2,1)S(1)}, bf16[32,1280]{1,0:T(8,128)(2,1)S(1)}, u32[]{:S(2)}, u32[]{:S(2)}) collective-permute-start(bf16[32,1280]{1,0:T(8,128)(2,1)S(1)} %get-tuple-element.60), channel_id=1, source_target_pairs={{0,2},{1,3},{2,0},{3,1},{4,6},{5,7},{6,4},{7,5},{8,10},{9,11},{10,... | collective-permute-start | bytes 245768 | tf_op jit(solution)/shard_map/ppermute | solution.py:577
  25.1 9.3 %collective-permute-start.11 = (bf16[32,1280]{1,0:T(8,128)(2,1)S(1)}, bf16[32,1280]{1,0:T(8,128)(2,1)S(1)}, u32[]{:S(2)}, u32[]{:S(2)}) collective-permute-start(bf16[32,1280]{1,0:T(8,128)(2,1)S(1)} %get-tuple-element.65), channel_id=1, source_target_pairs={{0,14},{1,15},{2,12},{3,13},{4,10},{5,11},{6,8},{7,9},{8,6},{9,7},... | collective-permute-start | bytes 245768 | tf_op jit(solution)/shard_map/ppermute | solution.py:577
  26.1 11.7 %collective-permute-start.12 = (bf16[32,1280]{1,0:T(8,128)(2,1)S(1)}, bf16[32,1280]{1,0:T(8,128)(2,1)S(1)}, u32[]{:S(2)}, u32[]{:S(2)}) collective-permute-start(bf16[32,1280]{1,0:T(8,128)(2,1)S(1)} %get-tuple-element.66), channel_id=1, source_target_pairs={{0,11},{1,10},{2,9},{3,8},{4,15},{5,14},{6,13},{7,12},{8,3},{9,2},... | collective-permute-start | bytes 245768 | tf_op jit(solution)/shard_map/ppermute | solution.py:577
  28.6 9.2 %collective-permute-start.13 = (bf16[32,1280]{1,0:T(8,128)(2,1)S(1)}, bf16[32,1280]{1,0:T(8,128)(2,1)S(1)}, u32[]{:S(2)}, u32[]{:S(2)}) collective-permute-start(bf16[32,1280]{1,0:T(8,128)(2,1)S(1)} %get-tuple-element.67), channel_id=1, source_target_pairs={{0,1},{1,0},{2,3},{3,2},{4,5},{5,4},{6,7},{7,6},{8,9},{9,8},{10,11... | collective-permute-start | bytes 245768 | tf_op jit(solution)/shard_map/ppermute | solution.py:577
  28.6 9.2 %collective-permute-start.14 = (bf16[32,1280]{1,0:T(8,128)(2,1)S(1)}, bf16[32,1280]{1,0:T(8,128)(2,1)S(1)}, u32[]{:S(2)}, u32[]{:S(2)}) collective-permute-start(bf16[32,1280]{1,0:T(8,128)(2,1)S(1)} %get-tuple-element.68), channel_id=1, source_target_pairs={{0,15},{1,14},{2,13},{3,12},{4,11},{5,10},{6,9},{7,8},{8,7},{9,6},... | collective-permute-start | bytes 245768 | tf_op jit(solution)/shard_map/ppermute | solution.py:577

commit v7 on v6

--- a/solution.py
+++ b/solution.py
@@ -41,7 +41,8 @@
 def order_of(groups):
     half = groups // 2
     near = list(range(half - 1, 0, -1))
-    far = [half + at // 2 + at % 2 * half // 2 for at in range(half)]
+    quarter, eighth = half // 2, half // 4
+    far = [half + (at // 2 if at % 2 == 0 else quarter + (at // 2 ^ eighth)) for at in range(half)]
     order = [(far if kind == "f" else near).pop(0) for kind in "fnfnfnfnfnnffnf"]
     order.insert(groups - LATE - 1, 0)
     return order

time: 40.5 us -> 40.6 us (level)
  waiting for transfers between devices: 5.78 us -> 9.23 us
  starting transfers between devices: 22.4 us -> 19 us
    ppermute x15, waiting for transfers between devices: 5.78 us -> 9.23 us  [shards(): lax.ppermute(block, 'pg', [(source, source ^ t) for source in range(group...]
    ppermute x15, starting transfers between devices: 22.4 us -> 19 us  [shards(): lax.ppermute(block, 'pg', [(source, source ^ t) for source in range(group...]
  transfers between devices with their start and end apart: 15 -> 15, of which waited for: 2 -> 5; matrix products, arithmetic and copies ran while one was open for 0% -> 0% of each run, Pallas kernels for 13% -> 13%
where the time goes in v7:
time: 40.6 us; the launch traced here: 40.4 us
  starting transfers between devices  19 us (47%)
  Pallas kernels  10.3 us (25%)
  waiting for transfers between devices  9.23 us (23%)
  local copies, waits for them, and re-layouts  1.1 us (3%)
  between operations  0.72 us (2%)
    ppermute x15, starting transfers between devices, shards(): lax.ppermute(block, 'pg', [(source, source ^ t) for source in range(group...  19 us
    ppermute x15, waiting for transfers between devices, shards(): lax.ppermute(block, 'pg', [(source, source ^ t) for source in range(group...  9.23 us
    pallas_call x1, Pallas kernels, attend(): pl.pallas_call(functools.partial(attend_kernel, len(got), requests is not...  3.9 us
    pallas_call x1, Pallas kernels, front(): pl.pallas_call(functools.partial(front_kernel, order), out_shape=[block]...  2.54 us
    pallas_call x1, Pallas kernels, attend_late(): pl.pallas_call(functools.partial(late_kernel, len(got), first), out_shape...  2.52 us
    unnamed x6, local copies, waits for them, and re-layouts  1.1 us
    pallas_call x1, Pallas kernels, pack_others(): pl.pallas_call(pack_kernel, out_shape=[jax.ShapeDtypeStruct(block, jnp.bf...  0.87 us
  transfers between devices with their start and end apart: 15, of which 5 were waited for; matrix products, arithmetic and copies ran while one was open for 0% of the time, Pallas kernels for 13%

profile of v7, /device:TPU:0, one launch (start us, length us, event | category | flops | bytes accessed | tf_op | source)
XLA Modules:
  0.0 40.4 jit_solution(14429314073974053970)
XLA Ops:
  0.6 2.5 %front.1 = (bf16[32,1280]{1,0:T(8,128)(2,1)}, bf16[32,1280]{1,0:T(8,128)(2,1)}, bf16[32,1280]{1,0:T(8,128)(2,1)}, bf16[32,1280]{1,0:T(8,128)(2,1)}, f32[1296,128]{1,0:T(8,128)}) custom-call(s32[1]{0:T(128)} %bitcast.me_ref, s32[16]{0:T(128)} %assign_any.1, s32[16]{0:T(128)} %length_any.1, s32[16,16]{1,0:T(8,128)} %owner_any.1, s32[16,16]{1,0:T(8,128)} %stripe_any.1, ...), custom_call_target="tpu_custom_call" | custom-call | tf_op jit(solution)/shard_map/front/pallas_call | solution.py:179
  3.2 4.1 %collective-permute-start = (bf16[32,1280]{1,0:T(8,128)(2,1)}, bf16[32,1280]{1,0:T(8,128)(2,1)S(1)}, u32[]{:S(2)}, u32[]{:S(2)}) collective-permute-start(bf16[32,1280]{1,0:T(8,128)(2,1)} %get-tuple-element.50), channel_id=1, source_target_pairs={{0,8},{1,9},{2,10},{3,11},{4,12},{5,13},{6,14},{7,15},{8,0},{9,1},... | collective-permute-start | bytes 245768 | tf_op jit(solution)/shard_map/ppermute | solution.py:578
  7.3 1.7 %collective-permute-start.1 = (bf16[32,1280]{1,0:T(8,128)(2,1)}, bf16[32,1280]{1,0:T(8,128)(2,1)S(1)}, u32[]{:S(2)}, u32[]{:S(2)}) collective-permute-start(bf16[32,1280]{1,0:T(8,128)(2,1)} %get-tuple-element.51), channel_id=1, source_target_pairs={{0,7},{1,6},{2,5},{3,4},{4,3},{5,2},{6,1},{7,0},{8,15},{9,14},{10,... | collective-permute-start | bytes 245768 | tf_op jit(solution)/shard_map/ppermute | solution.py:578
  9.0 0.6 %collective-permute-start.2 = (bf16[32,1280]{1,0:T(8,128)(2,1)}, bf16[32,1280]{1,0:T(8,128)(2,1)S(1)}, u32[]{:S(2)}, u32[]{:S(2)}) collective-permute-start(bf16[32,1280]{1,0:T(8,128)(2,1)} %get-tuple-element.52), channel_id=1, source_target_pairs={{0,14},{1,15},{2,12},{3,13},{4,10},{5,11},{6,8},{7,9},{8,6},{9,7},... | collective-permute-start | bytes 245768 | tf_op jit(solution)/shard_map/ppermute | solution.py:578
  9.6 1.2 %collective-permute-start.3 = (bf16[32,1280]{1,0:T(8,128)(2,1)}, bf16[32,1280]{1,0:T(8,128)(2,1)S(1)}, u32[]{:S(2)}, u32[]{:S(2)}) collective-permute-start(bf16[32,1280]{1,0:T(8,128)(2,1)} %get-tuple-element.53), channel_id=1, source_target_pairs={{0,6},{1,7},{2,4},{3,5},{4,2},{5,3},{6,0},{7,1},{8,14},{9,15},{10,... | collective-permute-start | bytes 245768 | tf_op jit(solution)/shard_map/ppermute | solution.py:578
  10.8 1.1 %copy-done.1 = f32[1296,128]{1,0:T(8,128)S(1)} copy-done((f32[1296,128]{1,0:T(8,128)S(1)}, f32[1296,128]{1,0:T(8,128)}, u32[]{:S(2)}) %copy-start.1) | copy-done | bytes 663576
  11.9 0.9 %pack_others.1 = (bf16[32,1280]{1,0:T(8,128)(2,1)S(1)}, bf16[32,1280]{1,0:T(8,128)(2,1)S(1)}, bf16[32,1280]{1,0:T(8,128)(2,1)S(1)}, bf16[32,1280]{1,0:T(8,128)(2...) custom-call(f32[1296,128]{1,0:T(8,128)S(1)} %copy-done.1, ...), custom_call_target="tpu_custom_call" | custom-call | tf_op jit(solution)/shard_map/pack_others/pallas_call | solution.py:228
  12.8 3.5 %collective-permute-start.4 = (bf16[32,1280]{1,0:T(8,128)(2,1)S(1)}, bf16[32,1280]{1,0:T(8,128)(2,1)S(1)}, u32[]{:S(2)}, u32[]{:S(2)}) collective-permute-start(bf16[32,1280]{1,0:T(8,128)(2,1)S(1)} %get-tuple-element.54), channel_id=1, source_target_pairs={{0,9},{1,8},{2,11},{3,10},{4,13},{5,12},{6,15},{7,14},{8,1},{9,0},... | collective-permute-start | bytes 245768 | tf_op jit(solution)/shard_map/ppermute | solution.py:578
  16.3 0.5 %rotate_queries.1 = (bf16[4,1024,128]{2,1,0:T(8,128)(2,1)S(1)}, bf16[8,128,128]{2,1,0:T(8,128)(2,1)S(1)}, f32[8,512]{1,0:T(8,128)S(1)}, s32[8,128]{1,0:T(8,128)S(1)}) custom-call(f32[1296,128]{1,0:T(8,128)S(1)} %copy-done.1, bf16[128,4096]{1,0:T(8,128)(2,1)S(1)} %bitcast.8), custom_call_target="tpu_custom_call" | custom-call | tf_op jit(solution)/shard_map/rotate_queries/pallas_call | solution.py:258
  16.8 0.1 collective-permute-start.5
  16.9 1.4 %collective-permute-start.6 = (bf16[32,1280]{1,0:T(8,128)(2,1)S(1)}, bf16[32,1280]{1,0:T(8,128)(2,1)S(1)}, u32[]{:S(2)}, u32[]{:S(2)}) collective-permute-start(bf16[32,1280]{1,0:T(8,128)(2,1)S(1)} %get-tuple-element.56), channel_id=1, source_target_pairs={{0,15},{1,14},{2,13},{3,12},{4,11},{5,10},{6,9},{7,8},{8,7},{9,6},... | collective-permute-start | bytes 245768 | tf_op jit(solution)/shard_map/ppermute | solution.py:578
  18.3 0.0 collective-permute-done.2.refs_2_
  18.3 0.5 %collective-permute-start.7 = (bf16[32,1280]{1,0:T(8,128)(2,1)S(1)}, bf16[32,1280]{1,0:T(8,128)(2,1)S(1)}, u32[]{:S(2)}, u32[]{:S(2)}) collective-permute-start(bf16[32,1280]{1,0:T(8,128)(2,1)S(1)} %get-tuple-element.57), channel_id=1, source_target_pairs={{0,4},{1,5},{2,6},{3,7},{4,0},{5,1},{6,2},{7,3},{8,12},{9,13},{10,... | collective-permute-start | bytes 245768 | tf_op jit(solution)/shard_map/ppermute | solution.py:578
  18.8 3.3 %collective-permute-start.8 = (bf16[32,1280]{1,0:T(8,128)(2,1)S(1)}, bf16[32,1280]{1,0:T(8,128)(2,1)S(1)}, u32[]{:S(2)}, u32[]{:S(2)}) collective-permute-start(bf16[32,1280]{1,0:T(8,128)(2,1)S(1)} %get-tuple-element.58), channel_id=1, source_target_pairs={{0,10},{1,11},{2,8},{3,9},{4,14},{5,15},{6,12},{7,13},{8,2},{9,3},... | collective-permute-start | bytes 245768 | tf_op jit(solution)/shard_map/ppermute | solution.py:578
  22.1 2.0 %collective-permute-done.5.refs_5_ = bf16[32,1280]{1,0:T(8,128)(2,1)S(1)} collective-permute-done((bf16[32,1280]{1,0:T(8,128)(2,1)S(1)}, bf16[32,1280]{1,0:T(8,128)(2,1)S(1)}, u32[]{:S(2)}, u32[]{:S(2)}) %collective-permute-start.5) | collective-permute-done | bytes 81952 | tf_op jit(solution)/shard_map/ppermute | solution.py:578
  24.1 1.1 %collective-permute-done.6.refs_6_ = bf16[32,1280]{1,0:T(8,128)(2,1)S(1)} collective-permute-done((bf16[32,1280]{1,0:T(8,128)(2,1)S(1)}, bf16[32,1280]{1,0:T(8,128)(2,1)S(1)}, u32[]{:S(2)}, u32[]{:S(2)}) %collective-permute-start.6) | collective-permute-done | bytes 81952 | tf_op jit(solution)/shard_map/ppermute | solution.py:578
  25.1 1.2 %collective-permute-start.11 = (bf16[32,1280]{1,0:T(8,128)(2,1)S(1)}, bf16[32,1280]{1,0:T(8,128)(2,1)S(1)}, u32[]{:S(2)}, u32[]{:S(2)}) collective-permute-start(bf16[32,1280]{1,0:T(8,128)(2,1)S(1)} %get-tuple-element.65), channel_id=1, source_target_pairs={{0,12},{1,13},{2,14},{3,15},{4,8},{5,9},{6,10},{7,11},{8,4},{9,5},... | collective-permute-start | bytes 245768 | tf_op jit(solution)/shard_map/ppermute | solution.py:578
  26.4 0.7 %collective-permute-done.7.refs_7_ = bf16[32,1280]{1,0:T(8,128)(2,1)S(1)} collective-permute-done((bf16[32,1280]{1,0:T(8,128)(2,1)S(1)}, bf16[32,1280]{1,0:T(8,128)(2,1)S(1)}, u32[]{:S(2)}, u32[]{:S(2)}) %collective-permute-start.7) | collective-permute-done | bytes 81952 | tf_op jit(solution)/shard_map/ppermute | solution.py:578
  27.0 0.3 collective-permute-start.12
  27.3 2.1 %collective-permute-done.8.refs_8_ = bf16[32,1280]{1,0:T(8,128)(2,1)S(1)} collective-permute-done((bf16[32,1280]{1,0:T(8,128)(2,1)S(1)}, bf16[32,1280]{1,0:T(8,128)(2,1)S(1)}, u32[]{:S(2)}, u32[]{:S(2)}) %collective-permute-start.8) | collective-permute-done | bytes 81952 | tf_op jit(solution)/shard_map/ppermute | solution.py:578
  29.4 1.2 %collective-permute-start.14 = (bf16[32,1280]{1,0:T(8,128)(2,1)S(1)}, bf16[32,1280]{1,0:T(8,128)(2,1)S(1)}, u32[]{:S(2)}, u32[]{:S(2)}) collective-permute-start(bf16[32,1280]{1,0:T(8,128)(2,1)S(1)} %get-tuple-element.68), channel_id=1, source_target_pairs={{0,13},{1,12},{2,15},{3,14},{4,9},{5,8},{6,11},{7,10},{8,5},{9,4},... | collective-permute-start | bytes 245768 | tf_op jit(solution)/shard_map/ppermute | solution.py:578
  30.6 3.9 %attend.1 = (f32[4,1024,128]{2,1,0:T(8,128)S(1)}, f32[4,1024,128]{2,1,0:T(8,128)S(1)}, bf16[16,8,1024]{2,1,0:T(8,128)(2,1)}) custom-call(bf16[4,1024,128]{2,1,0:T(8,128)(2,1)S(1)} %get-tuple-element.47.rot_ref, f32[8,512]{1,0:T(8,128)S(1)} %get-tuple-element.48.bias_ref, bf16[8,128,128]{2,1,0:T(8,128)(2,1)S(1)} %get-tuple-element.49.own_ref, ...), custom_call_target="tpu_custom_call" | custom-call | tf_op jit(solution)/shard_map/attend/pallas_call | solution.py:401
  34.5 3.4 %collective-permute-done.12.refs_1_ = bf16[32,1280]{1,0:T(8,128)(2,1)S(1)} collective-permute-done((bf16[32,1280]{1,0:T(8,128)(2,1)S(1)}, bf16[32,1280]{1,0:T(8,128)(2,1)S(1)}, u32[]{:S(2)}, u32[]{:S(2)}) %collective-permute-start.12) | collective-permute-done | bytes 81952 | tf_op jit(solution)/shard_map/ppermute | solution.py:578
  37.9 2.5 %attend_late.1 = (bf16[128,4096]{1,0:T(8,128)(2,1)}, bf16[16,8,1024]{2,1,0:T(8,128)(2,1)}) custom-call(bf16[4,1024,128]{2,1,0:T(8,128)(2,1)S(1)} %get-tuple-element.47.rot_ref, f32[8,512]{1,0:T(8,128)S(1)} %get-tuple-element.48.bias_ref, f32[4,1024,128]{2,1,0:T(8,128)S(1)} %get-tuple-element.63.result_ref, ...), custom_call_target="tpu_custom_call", output_to_operand_aliasing={{1}: (9, {})} | custom-call | tf_op jit(solution)/shard_map/attend_late/pallas_call | solution.py:501
  (17 shorter events, 0.0 us)
Async XLA Ops:
  0.6 10.2 %copy-start = (bf16[1,16,32,1024]{3,2,1,0:T(8,128)(2,1)S(1)}, bf16[1,16,32,1024]{3,2,1,0:T(8,128)(2,1)}, u32[]{:S(2)}) copy-start(bf16[1,16,32,1024]{3,2,1,0:T(8,128)(2,1)} %param.10) | copy-start | bytes 3145732
  3.2 13.6 %collective-permute-start = (bf16[32,1280]{1,0:T(8,128)(2,1)}, bf16[32,1280]{1,0:T(8,128)(2,1)S(1)}, u32[]{:S(2)}, u32[]{:S(2)}) collective-permute-start(bf16[32,1280]{1,0:T(8,128)(2,1)} %get-tuple-element.50), channel_id=1, source_target_pairs={{0,8},{1,9},{2,10},{3,11},{4,12},{5,13},{6,14},{7,15},{8,0},{9,1},... | collective-permute-start | bytes 245768 | tf_op jit(solution)/shard_map/ppermute | solution.py:578
  7.3 9.6 %collective-permute-start.1 = (bf16[32,1280]{1,0:T(8,128)(2,1)}, bf16[32,1280]{1,0:T(8,128)(2,1)S(1)}, u32[]{:S(2)}, u32[]{:S(2)}) collective-permute-start(bf16[32,1280]{1,0:T(8,128)(2,1)} %get-tuple-element.51), channel_id=1, source_target_pairs={{0,7},{1,6},{2,5},{3,4},{4,3},{5,2},{6,1},{7,0},{8,15},{9,14},{10,... | collective-permute-start | bytes 245768 | tf_op jit(solution)/shard_map/ppermute | solution.py:578
  9.0 9.3 %collective-permute-start.2 = (bf16[32,1280]{1,0:T(8,128)(2,1)}, bf16[32,1280]{1,0:T(8,128)(2,1)S(1)}, u32[]{:S(2)}, u32[]{:S(2)}) collective-permute-start(bf16[32,1280]{1,0:T(8,128)(2,1)} %get-tuple-element.52), channel_id=1, source_target_pairs={{0,14},{1,15},{2,12},{3,13},{4,10},{5,11},{6,8},{7,9},{8,6},{9,7},... | collective-permute-start | bytes 245768 | tf_op jit(solution)/shard_map/ppermute | solution.py:578
  9.6 9.2 %collective-permute-start.3 = (bf16[32,1280]{1,0:T(8,128)(2,1)}, bf16[32,1280]{1,0:T(8,128)(2,1)S(1)}, u32[]{:S(2)}, u32[]{:S(2)}) collective-permute-start(bf16[32,1280]{1,0:T(8,128)(2,1)} %get-tuple-element.53), channel_id=1, source_target_pairs={{0,6},{1,7},{2,4},{3,5},{4,2},{5,3},{6,0},{7,1},{8,14},{9,15},{10,... | collective-permute-start | bytes 245768 | tf_op jit(solution)/shard_map/ppermute | solution.py:578
  10.8 1.1 %copy-start.1 = (f32[1296,128]{1,0:T(8,128)S(1)}, f32[1296,128]{1,0:T(8,128)}, u32[]{:S(2)}) copy-start(f32[1296,128]{1,0:T(8,128)} %get-tuple-element.37.info_ref) | copy-start | bytes 1990660
  11.9 4.4 %copy-start.2 = (bf16[1,128,4096]{2,1,0:T(8,128)(2,1)S(1)}, bf16[1,128,4096]{2,1,0:T(8,128)(2,1)}, u32[]{:S(2)}) copy-start(bf16[1,128,4096]{2,1,0:T(8,128)(2,1)} %param.8) | copy-start | bytes 3145732
  12.8 9.3 %collective-permute-start.4 = (bf16[32,1280]{1,0:T(8,128)(2,1)S(1)}, bf16[32,1280]{1,0:T(8,128)(2,1)S(1)}, u32[]{:S(2)}, u32[]{:S(2)}) collective-permute-start(bf16[32,1280]{1,0:T(8,128)(2,1)S(1)} %get-tuple-element.54), channel_id=1, source_target_pairs={{0,9},{1,8},{2,11},{3,10},{4,13},{5,12},{6,15},{7,14},{8,1},{9,0},... | collective-permute-start | bytes 245768 | tf_op jit(solution)/shard_map/ppermute | solution.py:578
  16.8 7.2 %collective-permute-start.5 = (bf16[32,1280]{1,0:T(8,128)(2,1)S(1)}, bf16[32,1280]{1,0:T(8,128)(2,1)S(1)}, u32[]{:S(2)}, u32[]{:S(2)}) collective-permute-start(bf16[32,1280]{1,0:T(8,128)(2,1)S(1)} %get-tuple-element.55), channel_id=1, source_target_pairs={{0,5},{1,4},{2,7},{3,6},{4,1},{5,0},{6,3},{7,2},{8,13},{9,12},{10,... | collective-permute-start | bytes 245768 | tf_op jit(solution)/shard_map/ppermute | solution.py:578
  16.9 8.2 %collective-permute-start.6 = (bf16[32,1280]{1,0:T(8,128)(2,1)S(1)}, bf16[32,1280]{1,0:T(8,128)(2,1)S(1)}, u32[]{:S(2)}, u32[]{:S(2)}) collective-permute-start(bf16[32,1280]{1,0:T(8,128)(2,1)S(1)} %get-tuple-element.56), channel_id=1, source_target_pairs={{0,15},{1,14},{2,13},{3,12},{4,11},{5,10},{6,9},{7,8},{8,7},{9,6},... | collective-permute-start | bytes 245768 | tf_op jit(solution)/shard_map/ppermute | solution.py:578
  18.3 8.7 %collective-permute-start.7 = (bf16[32,1280]{1,0:T(8,128)(2,1)S(1)}, bf16[32,1280]{1,0:T(8,128)(2,1)S(1)}, u32[]{:S(2)}, u32[]{:S(2)}) collective-permute-start(bf16[32,1280]{1,0:T(8,128)(2,1)S(1)} %get-tuple-element.57), channel_id=1, source_target_pairs={{0,4},{1,5},{2,6},{3,7},{4,0},{5,1},{6,2},{7,3},{8,12},{9,13},{10,... | collective-permute-start | bytes 245768 | tf_op jit(solution)/shard_map/ppermute | solution.py:578
  18.8 10.6 %collective-permute-start.8 = (bf16[32,1280]{1,0:T(8,128)(2,1)S(1)}, bf16[32,1280]{1,0:T(8,128)(2,1)S(1)}, u32[]{:S(2)}, u32[]{:S(2)}) collective-permute-start(bf16[32,1280]{1,0:T(8,128)(2,1)S(1)} %get-tuple-element.58), channel_id=1, source_target_pairs={{0,10},{1,11},{2,8},{3,9},{4,14},{5,15},{6,12},{7,13},{8,2},{9,3},... | collective-permute-start | bytes 245768 | tf_op jit(solution)/shard_map/ppermute | solution.py:578
  22.1 7.3 %collective-permute-start.9 = (bf16[32,1280]{1,0:T(8,128)(2,1)S(1)}, bf16[32,1280]{1,0:T(8,128)(2,1)S(1)}, u32[]{:S(2)}, u32[]{:S(2)}) collective-permute-start(bf16[32,1280]{1,0:T(8,128)(2,1)S(1)} %get-tuple-element.59), channel_id=1, source_target_pairs={{0,3},{1,2},{2,1},{3,0},{4,7},{5,6},{6,5},{7,4},{8,11},{9,10},{10,... | collective-permute-start | bytes 245768 | tf_op jit(solution)/shard_map/ppermute | solution.py:578
  24.1 6.5 %collective-permute-start.10 = (bf16[32,1280]{1,0:T(8,128)(2,1)S(1)}, bf16[32,1280]{1,0:T(8,128)(2,1)S(1)}, u32[]{:S(2)}, u32[]{:S(2)}) collective-permute-start(bf16[32,1280]{1,0:T(8,128)(2,1)S(1)} %get-tuple-element.60), channel_id=1, source_target_pairs={{0,2},{1,3},{2,0},{3,1},{4,6},{5,7},{6,4},{7,5},{8,10},{9,11},{10,... | collective-permute-start | bytes 245768 | tf_op jit(solution)/shard_map/ppermute | solution.py:578
  25.1 9.3 %collective-permute-start.11 = (bf16[32,1280]{1,0:T(8,128)(2,1)S(1)}, bf16[32,1280]{1,0:T(8,128)(2,1)S(1)}, u32[]{:S(2)}, u32[]{:S(2)}) collective-permute-start(bf16[32,1280]{1,0:T(8,128)(2,1)S(1)} %get-tuple-element.65), channel_id=1, source_target_pairs={{0,12},{1,13},{2,14},{3,15},{4,8},{5,9},{6,10},{7,11},{8,4},{9,5},... | collective-permute-start | bytes 245768 | tf_op jit(solution)/shard_map/ppermute | solution.py:578
  27.0 10.8 %collective-permute-start.12 = (bf16[32,1280]{1,0:T(8,128)(2,1)S(1)}, bf16[32,1280]{1,0:T(8,128)(2,1)S(1)}, u32[]{:S(2)}, u32[]{:S(2)}) collective-permute-start(bf16[32,1280]{1,0:T(8,128)(2,1)S(1)} %get-tuple-element.66), channel_id=1, source_target_pairs={{0,11},{1,10},{2,9},{3,8},{4,15},{5,14},{6,13},{7,12},{8,3},{9,2},... | collective-permute-start | bytes 245768 | tf_op jit(solution)/shard_map/ppermute | solution.py:578
  29.4 8.5 %collective-permute-start.13 = (bf16[32,1280]{1,0:T(8,128)(2,1)S(1)}, bf16[32,1280]{1,0:T(8,128)(2,1)S(1)}, u32[]{:S(2)}, u32[]{:S(2)}) collective-permute-start(bf16[32,1280]{1,0:T(8,128)(2,1)S(1)} %get-tuple-element.67), channel_id=1, source_target_pairs={{0,1},{1,0},{2,3},{3,2},{4,5},{5,4},{6,7},{7,6},{8,9},{9,8},{10,11... | collective-permute-start | bytes 245768 | tf_op jit(solution)/shard_map/ppermute | solution.py:578
  29.4 8.5 %collective-permute-start.14 = (bf16[32,1280]{1,0:T(8,128)(2,1)S(1)}, bf16[32,1280]{1,0:T(8,128)(2,1)S(1)}, u32[]{:S(2)}, u32[]{:S(2)}) collective-permute-start(bf16[32,1280]{1,0:T(8,128)(2,1)S(1)} %get-tuple-element.68), channel_id=1, source_target_pairs={{0,13},{1,12},{2,15},{3,14},{4,9},{5,8},{6,11},{7,10},{8,5},{9,4},... | collective-permute-start | bytes 245768 | tf_op jit(solution)/shard_map/ppermute | solution.py:578

commit v8 on v7

--- a/solution.py
+++ b/solution.py
@@ -43,7 +43,7 @@
     near = list(range(half - 1, 0, -1))
     quarter, eighth = half // 2, half // 4
     far = [half + (at // 2 if at % 2 == 0 else quarter + (at // 2 ^ eighth)) for at in range(half)]
-    order = [(far if kind == "f" else near).pop(0) for kind in "fnfnfnfnfnnffnf"]
+    order = [(far if kind == "f" else near).pop(0) for kind in "ffnfnfnfnfnfnfn"]
     order.insert(groups - LATE - 1, 0)
     return order
 

time: 40.6 us -> 39 us (0.961)
  waiting for transfers between devices: 9.23 us -> 1.08 us
  starting transfers between devices: 19 us -> 25.6 us
    ppermute x15, waiting for transfers between devices: 9.23 us -> 1.08 us  [shards(): lax.ppermute(block, 'pg', [(source, source ^ t) for source in range(group...]
    ppermute x15, starting transfers between devices: 19 us -> 25.6 us  [shards(): lax.ppermute(block, 'pg', [(source, source ^ t) for source in range(group...]
  transfers between devices with their start and end apart: 15 -> 15, of which waited for: 5 -> 2; matrix products, arithmetic and copies ran while one was open for 0% -> 0% of each run, Pallas kernels for 13% -> 14%
where the time goes in v8:
time: 39 us; the launch traced here: 38.8 us
  starting transfers between devices  25.6 us (66%)
  Pallas kernels  10.3 us (26%)
  local copies, waits for them, and re-layouts  1.1 us (3%)
  waiting for transfers between devices  1.08 us (3%)
  between operations  0.7 us (2%)
    ppermute x15, starting transfers between devices, shards(): lax.ppermute(block, 'pg', [(source, source ^ t) for source in range(group...  25.6 us
    pallas_call x1, Pallas kernels, attend(): pl.pallas_call(functools.partial(attend_kernel, len(got), requests is not...  3.89 us
    pallas_call x1, Pallas kernels, front(): pl.pallas_call(functools.partial(front_kernel, order), out_shape=[block]...  2.54 us
    pallas_call x1, Pallas kernels, attend_late(): pl.pallas_call(functools.partial(late_kernel, len(got), first), out_shape...  2.52 us
    unnamed x6, local copies, waits for them, and re-layouts  1.1 us
    ppermute x15, waiting for transfers between devices, shards(): lax.ppermute(block, 'pg', [(source, source ^ t) for source in range(group...  1.08 us
    pallas_call x1, Pallas kernels, pack_others(): pl.pallas_call(pack_kernel, out_shape=[jax.ShapeDtypeStruct(block, jnp.bf...  0.87 us
  transfers between devices with their start and end apart: 15, of which 2 were waited for; matrix products, arithmetic and copies ran while one was open for 0% of the time, Pallas kernels for 14%

profile of v8, /device:TPU:0, one launch (start us, length us, event | category | flops | bytes accessed | tf_op | source)
XLA Modules:
  0.0 38.8 jit_solution(7713441675485888150)
XLA Ops:
  0.6 2.5 %front.1 = (bf16[32,1280]{1,0:T(8,128)(2,1)}, bf16[32,1280]{1,0:T(8,128)(2,1)}, bf16[32,1280]{1,0:T(8,128)(2,1)}, bf16[32,1280]{1,0:T(8,128)(2,1)}, f32[1296,128]{1,0:T(8,128)}) custom-call(s32[1]{0:T(128)} %bitcast.me_ref, s32[16]{0:T(128)} %assign_any.1, s32[16]{0:T(128)} %length_any.1, s32[16,16]{1,0:T(8,128)} %owner_any.1, s32[16,16]{1,0:T(8,128)} %stripe_any.1, ...), custom_call_target="tpu_custom_call" | custom-call | tf_op jit(solution)/shard_map/front/pallas_call | solution.py:179
  3.2 4.1 %collective-permute-start = (bf16[32,1280]{1,0:T(8,128)(2,1)}, bf16[32,1280]{1,0:T(8,128)(2,1)S(1)}, u32[]{:S(2)}, u32[]{:S(2)}) collective-permute-start(bf16[32,1280]{1,0:T(8,128)(2,1)} %get-tuple-element.50), channel_id=1, source_target_pairs={{0,8},{1,9},{2,10},{3,11},{4,12},{5,13},{6,14},{7,15},{8,0},{9,1},... | collective-permute-start | bytes 245768 | tf_op jit(solution)/shard_map/ppermute | solution.py:578
  7.3 2.3 %collective-permute-start.1 = (bf16[32,1280]{1,0:T(8,128)(2,1)}, bf16[32,1280]{1,0:T(8,128)(2,1)S(1)}, u32[]{:S(2)}, u32[]{:S(2)}) collective-permute-start(bf16[32,1280]{1,0:T(8,128)(2,1)} %get-tuple-element.51), channel_id=1, source_target_pairs={{0,14},{1,15},{2,12},{3,13},{4,10},{5,11},{6,8},{7,9},{8,6},{9,7},... | collective-permute-start | bytes 245768 | tf_op jit(solution)/shard_map/ppermute | solution.py:578
  9.6 2.7 %collective-permute-start.3 = (bf16[32,1280]{1,0:T(8,128)(2,1)}, bf16[32,1280]{1,0:T(8,128)(2,1)S(1)}, u32[]{:S(2)}, u32[]{:S(2)}) collective-permute-start(bf16[32,1280]{1,0:T(8,128)(2,1)} %get-tuple-element.53), channel_id=1, source_target_pairs={{0,9},{1,8},{2,11},{3,10},{4,13},{5,12},{6,15},{7,14},{8,1},{9,0},... | collective-permute-start | bytes 245768 | tf_op jit(solution)/shard_map/ppermute | solution.py:578
  12.3 1.1 %copy-done.1 = f32[1296,128]{1,0:T(8,128)S(1)} copy-done((f32[1296,128]{1,0:T(8,128)S(1)}, f32[1296,128]{1,0:T(8,128)}, u32[]{:S(2)}) %copy-start.1) | copy-done | bytes 663576
  13.4 0.9 %pack_others.1 = (bf16[32,1280]{1,0:T(8,128)(2,1)S(1)}, bf16[32,1280]{1,0:T(8,128)(2,1)S(1)}, bf16[32,1280]{1,0:T(8,128)(2,1)S(1)}, bf16[32,1280]{1,0:T(8,128)(2...) custom-call(f32[1296,128]{1,0:T(8,128)S(1)} %copy-done.1, ...), custom_call_target="tpu_custom_call" | custom-call | tf_op jit(solution)/shard_map/pack_others/pallas_call | solution.py:228
  14.3 1.7 %collective-permute-start.4 = (bf16[32,1280]{1,0:T(8,128)(2,1)S(1)}, bf16[32,1280]{1,0:T(8,128)(2,1)S(1)}, u32[]{:S(2)}, u32[]{:S(2)}) collective-permute-start(bf16[32,1280]{1,0:T(8,128)(2,1)S(1)} %get-tuple-element.54), channel_id=1, source_target_pairs={{0,6},{1,7},{2,4},{3,5},{4,2},{5,3},{6,0},{7,1},{8,14},{9,15},{10,... | collective-permute-start | bytes 245768 | tf_op jit(solution)/shard_map/ppermute | solution.py:578
  16.0 0.5 %rotate_queries.1 = (bf16[4,1024,128]{2,1,0:T(8,128)(2,1)S(1)}, bf16[8,128,128]{2,1,0:T(8,128)(2,1)S(1)}, f32[8,512]{1,0:T(8,128)S(1)}, s32[8,128]{1,0:T(8,128)S(1)}) custom-call(f32[1296,128]{1,0:T(8,128)S(1)} %copy-done.1, bf16[128,4096]{1,0:T(8,128)(2,1)S(1)} %bitcast.8), custom_call_target="tpu_custom_call" | custom-call | tf_op jit(solution)/shard_map/rotate_queries/pallas_call | solution.py:258
  16.5 1.4 %collective-permute-start.5 = (bf16[32,1280]{1,0:T(8,128)(2,1)S(1)}, bf16[32,1280]{1,0:T(8,128)(2,1)S(1)}, u32[]{:S(2)}, u32[]{:S(2)}) collective-permute-start(bf16[32,1280]{1,0:T(8,128)(2,1)S(1)} %get-tuple-element.55), channel_id=1, source_target_pairs={{0,15},{1,14},{2,13},{3,12},{4,11},{5,10},{6,9},{7,8},{8,7},{9,6},... | collective-permute-start | bytes 245768 | tf_op jit(solution)/shard_map/ppermute | solution.py:578
  17.9 0.1 collective-permute-start.6
  18.0 3.7 %collective-permute-start.7 = (bf16[32,1280]{1,0:T(8,128)(2,1)S(1)}, bf16[32,1280]{1,0:T(8,128)(2,1)S(1)}, u32[]{:S(2)}, u32[]{:S(2)}) collective-permute-start(bf16[32,1280]{1,0:T(8,128)(2,1)S(1)} %get-tuple-element.57), channel_id=1, source_target_pairs={{0,10},{1,11},{2,8},{3,9},{4,14},{5,15},{6,12},{7,13},{8,2},{9,3},... | collective-permute-start | bytes 245768 | tf_op jit(solution)/shard_map/ppermute | solution.py:578
  21.7 0.0 collective-permute-done.3.refs_3_
  21.7 0.7 %collective-permute-start.8 = (bf16[32,1280]{1,0:T(8,128)(2,1)S(1)}, bf16[32,1280]{1,0:T(8,128)(2,1)S(1)}, u32[]{:S(2)}, u32[]{:S(2)}) collective-permute-start(bf16[32,1280]{1,0:T(8,128)(2,1)S(1)} %get-tuple-element.58), channel_id=1, source_target_pairs={{0,4},{1,5},{2,6},{3,7},{4,0},{5,1},{6,2},{7,3},{8,12},{9,13},{10,... | collective-permute-start | bytes 245768 | tf_op jit(solution)/shard_map/ppermute | solution.py:578
  22.4 0.0 collective-permute-done.4.refs_4_
  22.4 1.3 %collective-permute-start.9 = (bf16[32,1280]{1,0:T(8,128)(2,1)S(1)}, bf16[32,1280]{1,0:T(8,128)(2,1)S(1)}, u32[]{:S(2)}, u32[]{:S(2)}) collective-permute-start(bf16[32,1280]{1,0:T(8,128)(2,1)S(1)} %get-tuple-element.59), channel_id=1, source_target_pairs={{0,12},{1,13},{2,14},{3,15},{4,8},{5,9},{6,10},{7,11},{8,4},{9,5},... | collective-permute-start | bytes 245768 | tf_op jit(solution)/shard_map/ppermute | solution.py:578
  23.7 2.0 %collective-permute-start.10 = (bf16[32,1280]{1,0:T(8,128)(2,1)S(1)}, bf16[32,1280]{1,0:T(8,128)(2,1)S(1)}, u32[]{:S(2)}, u32[]{:S(2)}) collective-permute-start(bf16[32,1280]{1,0:T(8,128)(2,1)S(1)} %get-tuple-element.60), channel_id=1, source_target_pairs={{0,3},{1,2},{2,1},{3,0},{4,7},{5,6},{6,5},{7,4},{8,11},{9,10},{10,... | collective-permute-start | bytes 245768 | tf_op jit(solution)/shard_map/ppermute | solution.py:578
  25.7 1.7 %collective-permute-start.11 = (bf16[32,1280]{1,0:T(8,128)(2,1)S(1)}, bf16[32,1280]{1,0:T(8,128)(2,1)S(1)}, u32[]{:S(2)}, u32[]{:S(2)}) collective-permute-start(bf16[32,1280]{1,0:T(8,128)(2,1)S(1)} %get-tuple-element.65), channel_id=1, source_target_pairs={{0,11},{1,10},{2,9},{3,8},{4,15},{5,14},{6,13},{7,12},{8,3},{9,2},... | collective-permute-start | bytes 245768 | tf_op jit(solution)/shard_map/ppermute | solution.py:578
  27.4 0.9 %collective-permute-start.12 = (bf16[32,1280]{1,0:T(8,128)(2,1)S(1)}, bf16[32,1280]{1,0:T(8,128)(2,1)S(1)}, u32[]{:S(2)}, u32[]{:S(2)}) collective-permute-start(bf16[32,1280]{1,0:T(8,128)(2,1)S(1)} %get-tuple-element.66), channel_id=1, source_target_pairs={{0,2},{1,3},{2,0},{3,1},{4,6},{5,7},{6,4},{7,5},{8,10},{9,11},{10,... | collective-permute-start | bytes 245768 | tf_op jit(solution)/shard_map/ppermute | solution.py:578
  28.3 2.7 %collective-permute-start.13 = (bf16[32,1280]{1,0:T(8,128)(2,1)S(1)}, bf16[32,1280]{1,0:T(8,128)(2,1)S(1)}, u32[]{:S(2)}, u32[]{:S(2)}) collective-permute-start(bf16[32,1280]{1,0:T(8,128)(2,1)S(1)} %get-tuple-element.67), channel_id=1, source_target_pairs={{0,13},{1,12},{2,15},{3,14},{4,9},{5,8},{6,11},{7,10},{8,5},{9,4},... | collective-permute-start | bytes 245768 | tf_op jit(solution)/shard_map/ppermute | solution.py:578
  31.0 0.2 collective-permute-done.9.refs_9_
  31.3 0.3 collective-permute-start.14
  31.5 3.9 %attend.1 = (f32[4,1024,128]{2,1,0:T(8,128)S(1)}, f32[4,1024,128]{2,1,0:T(8,128)S(1)}, bf16[16,8,1024]{2,1,0:T(8,128)(2,1)}) custom-call(bf16[4,1024,128]{2,1,0:T(8,128)(2,1)S(1)} %get-tuple-element.47.rot_ref, f32[8,512]{1,0:T(8,128)S(1)} %get-tuple-element.48.bias_ref, bf16[8,128,128]{2,1,0:T(8,128)(2,1)S(1)} %get-tuple-element.49.own_ref, ...), custom_call_target="tpu_custom_call" | custom-call | tf_op jit(solution)/shard_map/attend/pallas_call | solution.py:401
  35.4 0.8 %collective-permute-done.11.refs_0_ = bf16[32,1280]{1,0:T(8,128)(2,1)S(1)} collective-permute-done((bf16[32,1280]{1,0:T(8,128)(2,1)S(1)}, bf16[32,1280]{1,0:T(8,128)(2,1)S(1)}, u32[]{:S(2)}, u32[]{:S(2)}) %collective-permute-start.11) | collective-permute-done | bytes 81952 | tf_op jit(solution)/shard_map/ppermute | solution.py:578
  36.3 2.5 %attend_late.1 = (bf16[128,4096]{1,0:T(8,128)(2,1)}, bf16[16,8,1024]{2,1,0:T(8,128)(2,1)}) custom-call(bf16[4,1024,128]{2,1,0:T(8,128)(2,1)S(1)} %get-tuple-element.47.rot_ref, f32[8,512]{1,0:T(8,128)S(1)} %get-tuple-element.48.bias_ref, f32[4,1024,128]{2,1,0:T(8,128)S(1)} %get-tuple-element.63.result_ref, ...), custom_call_target="tpu_custom_call", output_to_operand_aliasing={{1}: (9, {})} | custom-call | tf_op jit(solution)/shard_map/attend_late/pallas_call | solution.py:501
  (17 shorter events, 0.0 us)
Async XLA Ops:
  0.6 11.7 %copy-start = (bf16[1,16,32,1024]{3,2,1,0:T(8,128)(2,1)S(1)}, bf16[1,16,32,1024]{3,2,1,0:T(8,128)(2,1)}, u32[]{:S(2)}) copy-start(bf16[1,16,32,1024]{3,2,1,0:T(8,128)(2,1)} %param.10) | copy-start | bytes 3145732
  3.2 13.3 %collective-permute-start = (bf16[32,1280]{1,0:T(8,128)(2,1)}, bf16[32,1280]{1,0:T(8,128)(2,1)S(1)}, u32[]{:S(2)}, u32[]{:S(2)}) collective-permute-start(bf16[32,1280]{1,0:T(8,128)(2,1)} %get-tuple-element.50), channel_id=1, source_target_pairs={{0,8},{1,9},{2,10},{3,11},{4,12},{5,13},{6,14},{7,15},{8,0},{9,1},... | collective-permute-start | bytes 245768 | tf_op jit(solution)/shard_map/ppermute | solution.py:578
  7.3 10.6 %collective-permute-start.1 = (bf16[32,1280]{1,0:T(8,128)(2,1)}, bf16[32,1280]{1,0:T(8,128)(2,1)S(1)}, u32[]{:S(2)}, u32[]{:S(2)}) collective-permute-start(bf16[32,1280]{1,0:T(8,128)(2,1)} %get-tuple-element.51), channel_id=1, source_target_pairs={{0,14},{1,15},{2,12},{3,13},{4,10},{5,11},{6,8},{7,9},{8,6},{9,7},... | collective-permute-start | bytes 245768 | tf_op jit(solution)/shard_map/ppermute | solution.py:578
  9.6 8.4 %collective-permute-start.2 = (bf16[32,1280]{1,0:T(8,128)(2,1)}, bf16[32,1280]{1,0:T(8,128)(2,1)S(1)}, u32[]{:S(2)}, u32[]{:S(2)}) collective-permute-start(bf16[32,1280]{1,0:T(8,128)(2,1)} %get-tuple-element.52), channel_id=1, source_target_pairs={{0,7},{1,6},{2,5},{3,4},{4,3},{5,2},{6,1},{7,0},{8,15},{9,14},{10,... | collective-permute-start | bytes 245768 | tf_op jit(solution)/shard_map/ppermute | solution.py:578
  9.6 12.1 %collective-permute-start.3 = (bf16[32,1280]{1,0:T(8,128)(2,1)}, bf16[32,1280]{1,0:T(8,128)(2,1)S(1)}, u32[]{:S(2)}, u32[]{:S(2)}) collective-permute-start(bf16[32,1280]{1,0:T(8,128)(2,1)} %get-tuple-element.53), channel_id=1, source_target_pairs={{0,9},{1,8},{2,11},{3,10},{4,13},{5,12},{6,15},{7,14},{8,1},{9,0},... | collective-permute-start | bytes 245768 | tf_op jit(solution)/shard_map/ppermute | solution.py:578
  12.3 1.1 %copy-start.1 = (f32[1296,128]{1,0:T(8,128)S(1)}, f32[1296,128]{1,0:T(8,128)}, u32[]{:S(2)}) copy-start(f32[1296,128]{1,0:T(8,128)} %get-tuple-element.37.info_ref) | copy-start | bytes 1990660
  13.4 2.6 %copy-start.2 = (bf16[1,128,4096]{2,1,0:T(8,128)(2,1)S(1)}, bf16[1,128,4096]{2,1,0:T(8,128)(2,1)}, u32[]{:S(2)}) copy-start(bf16[1,128,4096]{2,1,0:T(8,128)(2,1)} %param.8) | copy-start | bytes 3145732
  14.3 8.1 %collective-permute-start.4 = (bf16[32,1280]{1,0:T(8,128)(2,1)S(1)}, bf16[32,1280]{1,0:T(8,128)(2,1)S(1)}, u32[]{:S(2)}, u32[]{:S(2)}) collective-permute-start(bf16[32,1280]{1,0:T(8,128)(2,1)S(1)} %get-tuple-element.54), channel_id=1, source_target_pairs={{0,6},{1,7},{2,4},{3,5},{4,2},{5,3},{6,0},{7,1},{8,14},{9,15},{10,... | collective-permute-start | bytes 245768 | tf_op jit(solution)/shard_map/ppermute | solution.py:578
  16.5 7.2 %collective-permute-start.5 = (bf16[32,1280]{1,0:T(8,128)(2,1)S(1)}, bf16[32,1280]{1,0:T(8,128)(2,1)S(1)}, u32[]{:S(2)}, u32[]{:S(2)}) collective-permute-start(bf16[32,1280]{1,0:T(8,128)(2,1)S(1)} %get-tuple-element.55), channel_id=1, source_target_pairs={{0,15},{1,14},{2,13},{3,12},{4,11},{5,10},{6,9},{7,8},{8,7},{9,6},... | collective-permute-start | bytes 245768 | tf_op jit(solution)/shard_map/ppermute | solution.py:578
  17.9 7.8 %collective-permute-start.6 = (bf16[32,1280]{1,0:T(8,128)(2,1)S(1)}, bf16[32,1280]{1,0:T(8,128)(2,1)S(1)}, u32[]{:S(2)}, u32[]{:S(2)}) collective-permute-start(bf16[32,1280]{1,0:T(8,128)(2,1)S(1)} %get-tuple-element.56), channel_id=1, source_target_pairs={{0,5},{1,4},{2,7},{3,6},{4,1},{5,0},{6,3},{7,2},{8,13},{9,12},{10,... | collective-permute-start | bytes 245768 | tf_op jit(solution)/shard_map/ppermute | solution.py:578
  18.0 9.4 %collective-permute-start.7 = (bf16[32,1280]{1,0:T(8,128)(2,1)S(1)}, bf16[32,1280]{1,0:T(8,128)(2,1)S(1)}, u32[]{:S(2)}, u32[]{:S(2)}) collective-permute-start(bf16[32,1280]{1,0:T(8,128)(2,1)S(1)} %get-tuple-element.57), channel_id=1, source_target_pairs={{0,10},{1,11},{2,8},{3,9},{4,14},{5,15},{6,12},{7,13},{8,2},{9,3},... | collective-permute-start | bytes 245768 | tf_op jit(solution)/shard_map/ppermute | solution.py:578
  21.7 6.6 %collective-permute-start.8 = (bf16[32,1280]{1,0:T(8,128)(2,1)S(1)}, bf16[32,1280]{1,0:T(8,128)(2,1)S(1)}, u32[]{:S(2)}, u32[]{:S(2)}) collective-permute-start(bf16[32,1280]{1,0:T(8,128)(2,1)S(1)} %get-tuple-element.58), channel_id=1, source_target_pairs={{0,4},{1,5},{2,6},{3,7},{4,0},{5,1},{6,2},{7,3},{8,12},{9,13},{10,... | collective-permute-start | bytes 245768 | tf_op jit(solution)/shard_map/ppermute | solution.py:578
  22.4 8.9 %collective-permute-start.9 = (bf16[32,1280]{1,0:T(8,128)(2,1)S(1)}, bf16[32,1280]{1,0:T(8,128)(2,1)S(1)}, u32[]{:S(2)}, u32[]{:S(2)}) collective-permute-start(bf16[32,1280]{1,0:T(8,128)(2,1)S(1)} %get-tuple-element.59), channel_id=1, source_target_pairs={{0,12},{1,13},{2,14},{3,15},{4,8},{5,9},{6,10},{7,11},{8,4},{9,5},... | collective-permute-start | bytes 245768 | tf_op jit(solution)/shard_map/ppermute | solution.py:578
  23.7 7.9 %collective-permute-start.10 = (bf16[32,1280]{1,0:T(8,128)(2,1)S(1)}, bf16[32,1280]{1,0:T(8,128)(2,1)S(1)}, u32[]{:S(2)}, u32[]{:S(2)}) collective-permute-start(bf16[32,1280]{1,0:T(8,128)(2,1)S(1)} %get-tuple-element.60), channel_id=1, source_target_pairs={{0,3},{1,2},{2,1},{3,0},{4,7},{5,6},{6,5},{7,4},{8,11},{9,10},{10,... | collective-permute-start | bytes 245768 | tf_op jit(solution)/shard_map/ppermute | solution.py:578
  25.7 10.6 %collective-permute-start.11 = (bf16[32,1280]{1,0:T(8,128)(2,1)S(1)}, bf16[32,1280]{1,0:T(8,128)(2,1)S(1)}, u32[]{:S(2)}, u32[]{:S(2)}) collective-permute-start(bf16[32,1280]{1,0:T(8,128)(2,1)S(1)} %get-tuple-element.65), channel_id=1, source_target_pairs={{0,11},{1,10},{2,9},{3,8},{4,15},{5,14},{6,13},{7,12},{8,3},{9,2},... | collective-permute-start | bytes 245768 | tf_op jit(solution)/shard_map/ppermute | solution.py:578
  27.4 8.9 %collective-permute-start.12 = (bf16[32,1280]{1,0:T(8,128)(2,1)S(1)}, bf16[32,1280]{1,0:T(8,128)(2,1)S(1)}, u32[]{:S(2)}, u32[]{:S(2)}) collective-permute-start(bf16[32,1280]{1,0:T(8,128)(2,1)S(1)} %get-tuple-element.66), channel_id=1, source_target_pairs={{0,2},{1,3},{2,0},{3,1},{4,6},{5,7},{6,4},{7,5},{8,10},{9,11},{10,... | collective-permute-start | bytes 245768 | tf_op jit(solution)/shard_map/ppermute | solution.py:578
  28.3 8.0 %collective-permute-start.13 = (bf16[32,1280]{1,0:T(8,128)(2,1)S(1)}, bf16[32,1280]{1,0:T(8,128)(2,1)S(1)}, u32[]{:S(2)}, u32[]{:S(2)}) collective-permute-start(bf16[32,1280]{1,0:T(8,128)(2,1)S(1)} %get-tuple-element.67), channel_id=1, source_target_pairs={{0,13},{1,12},{2,15},{3,14},{4,9},{5,8},{6,11},{7,10},{8,5},{9,4},... | collective-permute-start | bytes 245768 | tf_op jit(solution)/shard_map/ppermute | solution.py:578
  31.3 5.0 %collective-permute-start.14 = (bf16[32,1280]{1,0:T(8,128)(2,1)S(1)}, bf16[32,1280]{1,0:T(8,128)(2,1)S(1)}, u32[]{:S(2)}, u32[]{:S(2)}) collective-permute-start(bf16[32,1280]{1,0:T(8,128)(2,1)S(1)} %get-tuple-element.68), channel_id=1, source_target_pairs={{0,1},{1,0},{2,3},{3,2},{4,5},{5,4},{6,7},{7,6},{8,9},{9,8},{10,11... | collective-permute-start | bytes 245768 | tf_op jit(solution)/shard_map/ppermute | solution.py:578

commit v9 on v8

--- a/solution.py
+++ b/solution.py
@@ -43,7 +43,7 @@
     near = list(range(half - 1, 0, -1))
     quarter, eighth = half // 2, half // 4
     far = [half + (at // 2 if at % 2 == 0 else quarter + (at // 2 ^ eighth)) for at in range(half)]
-    order = [(far if kind == "f" else near).pop(0) for kind in "ffnfnfnfnfnfnfn"]
+    order = [(far if kind == "f" else near).pop(0) for kind in "ffnfnfnfnnffnfn"]
     order.insert(groups - LATE - 1, 0)
     return order
 

time: 39 us -> 39.2 us (level)
  no operation moved by 1% of the time
where the time goes in v9:
time: 39.2 us; the launch traced here: 38.8 us
  starting transfers between devices  25.4 us (65%)
  Pallas kernels  10.3 us (26%)
  waiting for transfers between devices  1.31 us (3%)
  local copies, waits for them, and re-layouts  1.1 us (3%)
  between operations  0.7 us (2%)
    ppermute x15, starting transfers between devices, shards(): lax.ppermute(block, 'pg', [(source, source ^ t) for source in range(group...  25.4 us
    pallas_call x1, Pallas kernels, attend(): pl.pallas_call(functools.partial(attend_kernel, len(got), requests is not...  3.89 us
    pallas_call x1, Pallas kernels, front(): pl.pallas_call(functools.partial(front_kernel, order), out_shape=[block]...  2.54 us
    pallas_call x1, Pallas kernels, attend_late(): pl.pallas_call(functools.partial(late_kernel, len(got), first), out_shape...  2.53 us
    ppermute x15, waiting for transfers between devices, shards(): lax.ppermute(block, 'pg', [(source, source ^ t) for source in range(group...  1.31 us
    unnamed x6, local copies, waits for them, and re-layouts  1.1 us
    pallas_call x1, Pallas kernels, pack_others(): pl.pallas_call(pack_kernel, out_shape=[jax.ShapeDtypeStruct(block, jnp.bf...  0.87 us
  transfers between devices with their start and end apart: 15, of which 2 were waited for; matrix products, arithmetic and copies ran while one was open for 0% of the time, Pallas kernels for 14%

profile of v9, /device:TPU:0, one launch (start us, length us, event | category | flops | bytes accessed | tf_op | source)
XLA Modules:
  0.0 38.8 jit_solution(1313956364607027000)
XLA Ops:
  0.6 2.5 %front.1 = (bf16[32,1280]{1,0:T(8,128)(2,1)}, bf16[32,1280]{1,0:T(8,128)(2,1)}, bf16[32,1280]{1,0:T(8,128)(2,1)}, bf16[32,1280]{1,0:T(8,128)(2,1)}, f32[1296,128]{1,0:T(8,128)}) custom-call(s32[1]{0:T(128)} %bitcast.me_ref, s32[16]{0:T(128)} %assign_any.1, s32[16]{0:T(128)} %length_any.1, s32[16,16]{1,0:T(8,128)} %owner_any.1, s32[16,16]{1,0:T(8,128)} %stripe_any.1, ...), custom_call_target="tpu_custom_call" | custom-call | tf_op jit(solution)/shard_map/front/pallas_call | solution.py:179
  3.2 4.1 %collective-permute-start = (bf16[32,1280]{1,0:T(8,128)(2,1)}, bf16[32,1280]{1,0:T(8,128)(2,1)S(1)}, u32[]{:S(2)}, u32[]{:S(2)}) collective-permute-start(bf16[32,1280]{1,0:T(8,128)(2,1)} %get-tuple-element.50), channel_id=1, source_target_pairs={{0,8},{1,9},{2,10},{3,11},{4,12},{5,13},{6,14},{7,15},{8,0},{9,1},... | collective-permute-start | bytes 245768 | tf_op jit(solution)/shard_map/ppermute | solution.py:578
  7.3 2.3 %collective-permute-start.1 = (bf16[32,1280]{1,0:T(8,128)(2,1)}, bf16[32,1280]{1,0:T(8,128)(2,1)S(1)}, u32[]{:S(2)}, u32[]{:S(2)}) collective-permute-start(bf16[32,1280]{1,0:T(8,128)(2,1)} %get-tuple-element.51), channel_id=1, source_target_pairs={{0,14},{1,15},{2,12},{3,13},{4,10},{5,11},{6,8},{7,9},{8,6},{9,7},... | collective-permute-start | bytes 245768 | tf_op jit(solution)/shard_map/ppermute | solution.py:578
  9.6 0.0 collective-permute-start.2
  9.6 2.7 %collective-permute-start.3 = (bf16[32,1280]{1,0:T(8,128)(2,1)}, bf16[32,1280]{1,0:T(8,128)(2,1)S(1)}, u32[]{:S(2)}, u32[]{:S(2)}) collective-permute-start(bf16[32,1280]{1,0:T(8,128)(2,1)} %get-tuple-element.53), channel_id=1, source_target_pairs={{0,9},{1,8},{2,11},{3,10},{4,13},{5,12},{6,15},{7,14},{8,1},{9,0},... | collective-permute-start | bytes 245768 | tf_op jit(solution)/shard_map/ppermute | solution.py:578
  12.3 1.1 %copy-done.1 = f32[1296,128]{1,0:T(8,128)S(1)} copy-done((f32[1296,128]{1,0:T(8,128)S(1)}, f32[1296,128]{1,0:T(8,128)}, u32[]{:S(2)}) %copy-start.1) | copy-done | bytes 663576
  13.4 0.9 %pack_others.1 = (bf16[32,1280]{1,0:T(8,128)(2,1)S(1)}, bf16[32,1280]{1,0:T(8,128)(2,1)S(1)}, bf16[32,1280]{1,0:T(8,128)(2,1)S(1)}, bf16[32,1280]{1,0:T(8,128)(2...) custom-call(f32[1296,128]{1,0:T(8,128)S(1)} %copy-done.1, ...), custom_call_target="tpu_custom_call" | custom-call | tf_op jit(solution)/shard_map/pack_others/pallas_call | solution.py:228
  14.3 1.7 %collective-permute-start.4 = (bf16[32,1280]{1,0:T(8,128)(2,1)S(1)}, bf16[32,1280]{1,0:T(8,128)(2,1)S(1)}, u32[]{:S(2)}, u32[]{:S(2)}) collective-permute-start(bf16[32,1280]{1,0:T(8,128)(2,1)S(1)} %get-tuple-element.54), channel_id=1, source_target_pairs={{0,6},{1,7},{2,4},{3,5},{4,2},{5,3},{6,0},{7,1},{8,14},{9,15},{10,... | collective-permute-start | bytes 245768 | tf_op jit(solution)/shard_map/ppermute | solution.py:578
  16.0 0.5 %rotate_queries.1 = (bf16[4,1024,128]{2,1,0:T(8,128)(2,1)S(1)}, bf16[8,128,128]{2,1,0:T(8,128)(2,1)S(1)}, f32[8,512]{1,0:T(8,128)S(1)}, s32[8,128]{1,0:T(8,128)S(1)}) custom-call(f32[1296,128]{1,0:T(8,128)S(1)} %copy-done.1, bf16[128,4096]{1,0:T(8,128)(2,1)S(1)} %bitcast.8), custom_call_target="tpu_custom_call" | custom-call | tf_op jit(solution)/shard_map/rotate_queries/pallas_call | solution.py:258
  16.5 1.4 %collective-permute-start.5 = (bf16[32,1280]{1,0:T(8,128)(2,1)S(1)}, bf16[32,1280]{1,0:T(8,128)(2,1)S(1)}, u32[]{:S(2)}, u32[]{:S(2)}) collective-permute-start(bf16[32,1280]{1,0:T(8,128)(2,1)S(1)} %get-tuple-element.55), channel_id=1, source_target_pairs={{0,15},{1,14},{2,13},{3,12},{4,11},{5,10},{6,9},{7,8},{8,7},{9,6},... | collective-permute-start | bytes 245768 | tf_op jit(solution)/shard_map/ppermute | solution.py:578
  17.9 0.0 collective-permute-done.1.refs_1_
  17.9 0.1 collective-permute-start.6
  18.0 3.6 %collective-permute-start.7 = (bf16[32,1280]{1,0:T(8,128)(2,1)S(1)}, bf16[32,1280]{1,0:T(8,128)(2,1)S(1)}, u32[]{:S(2)}, u32[]{:S(2)}) collective-permute-start(bf16[32,1280]{1,0:T(8,128)(2,1)S(1)} %get-tuple-element.57), channel_id=1, source_target_pairs={{0,10},{1,11},{2,8},{3,9},{4,14},{5,15},{6,12},{7,13},{8,2},{9,3},... | collective-permute-start | bytes 245768 | tf_op jit(solution)/shard_map/ppermute | solution.py:578
  21.7 0.7 %collective-permute-start.8 = (bf16[32,1280]{1,0:T(8,128)(2,1)S(1)}, bf16[32,1280]{1,0:T(8,128)(2,1)S(1)}, u32[]{:S(2)}, u32[]{:S(2)}) collective-permute-start(bf16[32,1280]{1,0:T(8,128)(2,1)S(1)} %get-tuple-element.58), channel_id=1, source_target_pairs={{0,4},{1,5},{2,6},{3,7},{4,0},{5,1},{6,2},{7,3},{8,12},{9,13},{10,... | collective-permute-start | bytes 245768 | tf_op jit(solution)/shard_map/ppermute | solution.py:578
  22.4 2.4 %collective-permute-start.9 = (bf16[32,1280]{1,0:T(8,128)(2,1)S(1)}, bf16[32,1280]{1,0:T(8,128)(2,1)S(1)}, u32[]{:S(2)}, u32[]{:S(2)}) collective-permute-start(bf16[32,1280]{1,0:T(8,128)(2,1)S(1)} %get-tuple-element.59), channel_id=1, source_target_pairs={{0,3},{1,2},{2,1},{3,0},{4,7},{5,6},{6,5},{7,4},{8,11},{9,10},{10,... | collective-permute-start | bytes 245768 | tf_op jit(solution)/shard_map/ppermute | solution.py:578
  24.8 1.2 %collective-permute-start.10 = (bf16[32,1280]{1,0:T(8,128)(2,1)S(1)}, bf16[32,1280]{1,0:T(8,128)(2,1)S(1)}, u32[]{:S(2)}, u32[]{:S(2)}) collective-permute-start(bf16[32,1280]{1,0:T(8,128)(2,1)S(1)} %get-tuple-element.60), channel_id=1, source_target_pairs={{0,12},{1,13},{2,14},{3,15},{4,8},{5,9},{6,10},{7,11},{8,4},{9,5},... | collective-permute-start | bytes 245768 | tf_op jit(solution)/shard_map/ppermute | solution.py:578
  26.0 0.1 collective-permute-start.11
  26.1 2.0 %collective-permute-start.12 = (bf16[32,1280]{1,0:T(8,128)(2,1)S(1)}, bf16[32,1280]{1,0:T(8,128)(2,1)S(1)}, u32[]{:S(2)}, u32[]{:S(2)}) collective-permute-start(bf16[32,1280]{1,0:T(8,128)(2,1)S(1)} %get-tuple-element.66), channel_id=1, source_target_pairs={{0,2},{1,3},{2,0},{3,1},{4,6},{5,7},{6,4},{7,5},{8,10},{9,11},{10,... | collective-permute-start | bytes 245768 | tf_op jit(solution)/shard_map/ppermute | solution.py:578
  28.1 2.5 %collective-permute-start.13 = (bf16[32,1280]{1,0:T(8,128)(2,1)S(1)}, bf16[32,1280]{1,0:T(8,128)(2,1)S(1)}, u32[]{:S(2)}, u32[]{:S(2)}) collective-permute-start(bf16[32,1280]{1,0:T(8,128)(2,1)S(1)} %get-tuple-element.67), channel_id=1, source_target_pairs={{0,13},{1,12},{2,15},{3,14},{4,9},{5,8},{6,11},{7,10},{8,5},{9,4},... | collective-permute-start | bytes 245768 | tf_op jit(solution)/shard_map/ppermute | solution.py:578
  30.6 0.5 %collective-permute-start.14 = (bf16[32,1280]{1,0:T(8,128)(2,1)S(1)}, bf16[32,1280]{1,0:T(8,128)(2,1)S(1)}, u32[]{:S(2)}, u32[]{:S(2)}) collective-permute-start(bf16[32,1280]{1,0:T(8,128)(2,1)S(1)} %get-tuple-element.68), channel_id=1, source_target_pairs={{0,1},{1,0},{2,3},{3,2},{4,5},{5,4},{6,7},{7,6},{8,9},{9,8},{10,11... | collective-permute-start | bytes 245768 | tf_op jit(solution)/shard_map/ppermute | solution.py:578
  31.1 1.0 %collective-permute-done.10.refs_10_ = bf16[32,1280]{1,0:T(8,128)(2,1)S(1)} collective-permute-done((bf16[32,1280]{1,0:T(8,128)(2,1)S(1)}, bf16[32,1280]{1,0:T(8,128)(2,1)S(1)}, u32[]{:S(2)}, u32[]{:S(2)}) %collective-permute-start.10) | collective-permute-done | bytes 81952 | tf_op jit(solution)/shard_map/ppermute | solution.py:578
  32.1 3.9 %attend.1 = (f32[4,1024,128]{2,1,0:T(8,128)S(1)}, f32[4,1024,128]{2,1,0:T(8,128)S(1)}, bf16[16,8,1024]{2,1,0:T(8,128)(2,1)}) custom-call(bf16[4,1024,128]{2,1,0:T(8,128)(2,1)S(1)} %get-tuple-element.47.rot_ref, f32[8,512]{1,0:T(8,128)S(1)} %get-tuple-element.48.bias_ref, bf16[8,128,128]{2,1,0:T(8,128)(2,1)S(1)} %get-tuple-element.49.own_ref, ...), custom_call_target="tpu_custom_call" | custom-call | tf_op jit(solution)/shard_map/attend/pallas_call | solution.py:401
  36.0 0.3 collective-permute-done.11.refs_0_
  36.3 2.5 %attend_late.1 = (bf16[128,4096]{1,0:T(8,128)(2,1)}, bf16[16,8,1024]{2,1,0:T(8,128)(2,1)}) custom-call(bf16[4,1024,128]{2,1,0:T(8,128)(2,1)S(1)} %get-tuple-element.47.rot_ref, f32[8,512]{1,0:T(8,128)S(1)} %get-tuple-element.48.bias_ref, f32[4,1024,128]{2,1,0:T(8,128)S(1)} %get-tuple-element.63.result_ref, ...), custom_call_target="tpu_custom_call", output_to_operand_aliasing={{1}: (9, {})} | custom-call | tf_op jit(solution)/shard_map/attend_late/pallas_call | solution.py:501
  (17 shorter events, 0.0 us)
Async XLA Ops:
  0.6 11.7 %copy-start = (bf16[1,16,32,1024]{3,2,1,0:T(8,128)(2,1)S(1)}, bf16[1,16,32,1024]{3,2,1,0:T(8,128)(2,1)}, u32[]{:S(2)}) copy-start(bf16[1,16,32,1024]{3,2,1,0:T(8,128)(2,1)} %param.10) | copy-start | bytes 3145732
  3.2 13.3 %collective-permute-start = (bf16[32,1280]{1,0:T(8,128)(2,1)}, bf16[32,1280]{1,0:T(8,128)(2,1)S(1)}, u32[]{:S(2)}, u32[]{:S(2)}) collective-permute-start(bf16[32,1280]{1,0:T(8,128)(2,1)} %get-tuple-element.50), channel_id=1, source_target_pairs={{0,8},{1,9},{2,10},{3,11},{4,12},{5,13},{6,14},{7,15},{8,0},{9,1},... | collective-permute-start | bytes 245768 | tf_op jit(solution)/shard_map/ppermute | solution.py:578
  7.3 10.6 %collective-permute-start.1 = (bf16[32,1280]{1,0:T(8,128)(2,1)}, bf16[32,1280]{1,0:T(8,128)(2,1)S(1)}, u32[]{:S(2)}, u32[]{:S(2)}) collective-permute-start(bf16[32,1280]{1,0:T(8,128)(2,1)} %get-tuple-element.51), channel_id=1, source_target_pairs={{0,14},{1,15},{2,12},{3,13},{4,10},{5,11},{6,8},{7,9},{8,6},{9,7},... | collective-permute-start | bytes 245768 | tf_op jit(solution)/shard_map/ppermute | solution.py:578
  9.6 8.4 %collective-permute-start.2 = (bf16[32,1280]{1,0:T(8,128)(2,1)}, bf16[32,1280]{1,0:T(8,128)(2,1)S(1)}, u32[]{:S(2)}, u32[]{:S(2)}) collective-permute-start(bf16[32,1280]{1,0:T(8,128)(2,1)} %get-tuple-element.52), channel_id=1, source_target_pairs={{0,7},{1,6},{2,5},{3,4},{4,3},{5,2},{6,1},{7,0},{8,15},{9,14},{10,... | collective-permute-start | bytes 245768 | tf_op jit(solution)/shard_map/ppermute | solution.py:578
  9.6 12.1 %collective-permute-start.3 = (bf16[32,1280]{1,0:T(8,128)(2,1)}, bf16[32,1280]{1,0:T(8,128)(2,1)S(1)}, u32[]{:S(2)}, u32[]{:S(2)}) collective-permute-start(bf16[32,1280]{1,0:T(8,128)(2,1)} %get-tuple-element.53), channel_id=1, source_target_pairs={{0,9},{1,8},{2,11},{3,10},{4,13},{5,12},{6,15},{7,14},{8,1},{9,0},... | collective-permute-start | bytes 245768 | tf_op jit(solution)/shard_map/ppermute | solution.py:578
  12.3 1.1 %copy-start.1 = (f32[1296,128]{1,0:T(8,128)S(1)}, f32[1296,128]{1,0:T(8,128)}, u32[]{:S(2)}) copy-start(f32[1296,128]{1,0:T(8,128)} %get-tuple-element.37.info_ref) | copy-start | bytes 1990660
  13.4 2.6 %copy-start.2 = (bf16[1,128,4096]{2,1,0:T(8,128)(2,1)S(1)}, bf16[1,128,4096]{2,1,0:T(8,128)(2,1)}, u32[]{:S(2)}) copy-start(bf16[1,128,4096]{2,1,0:T(8,128)(2,1)} %param.8) | copy-start | bytes 3145732
  14.3 8.1 %collective-permute-start.4 = (bf16[32,1280]{1,0:T(8,128)(2,1)S(1)}, bf16[32,1280]{1,0:T(8,128)(2,1)S(1)}, u32[]{:S(2)}, u32[]{:S(2)}) collective-permute-start(bf16[32,1280]{1,0:T(8,128)(2,1)S(1)} %get-tuple-element.54), channel_id=1, source_target_pairs={{0,6},{1,7},{2,4},{3,5},{4,2},{5,3},{6,0},{7,1},{8,14},{9,15},{10,... | collective-permute-start | bytes 245768 | tf_op jit(solution)/shard_map/ppermute | solution.py:578
  16.5 8.3 %collective-permute-start.5 = (bf16[32,1280]{1,0:T(8,128)(2,1)S(1)}, bf16[32,1280]{1,0:T(8,128)(2,1)S(1)}, u32[]{:S(2)}, u32[]{:S(2)}) collective-permute-start(bf16[32,1280]{1,0:T(8,128)(2,1)S(1)} %get-tuple-element.55), channel_id=1, source_target_pairs={{0,15},{1,14},{2,13},{3,12},{4,11},{5,10},{6,9},{7,8},{8,7},{9,6},... | collective-permute-start | bytes 245768 | tf_op jit(solution)/shard_map/ppermute | solution.py:578
  17.9 8.1 %collective-permute-start.6 = (bf16[32,1280]{1,0:T(8,128)(2,1)S(1)}, bf16[32,1280]{1,0:T(8,128)(2,1)S(1)}, u32[]{:S(2)}, u32[]{:S(2)}) collective-permute-start(bf16[32,1280]{1,0:T(8,128)(2,1)S(1)} %get-tuple-element.56), channel_id=1, source_target_pairs={{0,5},{1,4},{2,7},{3,6},{4,1},{5,0},{6,3},{7,2},{8,13},{9,12},{10,... | collective-permute-start | bytes 245768 | tf_op jit(solution)/shard_map/ppermute | solution.py:578
  18.0 8.1 %collective-permute-start.7 = (bf16[32,1280]{1,0:T(8,128)(2,1)S(1)}, bf16[32,1280]{1,0:T(8,128)(2,1)S(1)}, u32[]{:S(2)}, u32[]{:S(2)}) collective-permute-start(bf16[32,1280]{1,0:T(8,128)(2,1)S(1)} %get-tuple-element.57), channel_id=1, source_target_pairs={{0,10},{1,11},{2,8},{3,9},{4,14},{5,15},{6,12},{7,13},{8,2},{9,3},... | collective-permute-start | bytes 245768 | tf_op jit(solution)/shard_map/ppermute | solution.py:578
  21.7 6.5 %collective-permute-start.8 = (bf16[32,1280]{1,0:T(8,128)(2,1)S(1)}, bf16[32,1280]{1,0:T(8,128)(2,1)S(1)}, u32[]{:S(2)}, u32[]{:S(2)}) collective-permute-start(bf16[32,1280]{1,0:T(8,128)(2,1)S(1)} %get-tuple-element.58), channel_id=1, source_target_pairs={{0,4},{1,5},{2,6},{3,7},{4,0},{5,1},{6,2},{7,3},{8,12},{9,13},{10,... | collective-permute-start | bytes 245768 | tf_op jit(solution)/shard_map/ppermute | solution.py:578
  22.4 8.2 %collective-permute-start.9 = (bf16[32,1280]{1,0:T(8,128)(2,1)S(1)}, bf16[32,1280]{1,0:T(8,128)(2,1)S(1)}, u32[]{:S(2)}, u32[]{:S(2)}) collective-permute-start(bf16[32,1280]{1,0:T(8,128)(2,1)S(1)} %get-tuple-element.59), channel_id=1, source_target_pairs={{0,3},{1,2},{2,1},{3,0},{4,7},{5,6},{6,5},{7,4},{8,11},{9,10},{10,... | collective-permute-start | bytes 245768 | tf_op jit(solution)/shard_map/ppermute | solution.py:578
  24.8 7.3 %collective-permute-start.10 = (bf16[32,1280]{1,0:T(8,128)(2,1)S(1)}, bf16[32,1280]{1,0:T(8,128)(2,1)S(1)}, u32[]{:S(2)}, u32[]{:S(2)}) collective-permute-start(bf16[32,1280]{1,0:T(8,128)(2,1)S(1)} %get-tuple-element.60), channel_id=1, source_target_pairs={{0,12},{1,13},{2,14},{3,15},{4,8},{5,9},{6,10},{7,11},{8,4},{9,5},... | collective-permute-start | bytes 245768 | tf_op jit(solution)/shard_map/ppermute | solution.py:578
  26.0 10.3 %collective-permute-start.11 = (bf16[32,1280]{1,0:T(8,128)(2,1)S(1)}, bf16[32,1280]{1,0:T(8,128)(2,1)S(1)}, u32[]{:S(2)}, u32[]{:S(2)}) collective-permute-start(bf16[32,1280]{1,0:T(8,128)(2,1)S(1)} %get-tuple-element.65), channel_id=1, source_target_pairs={{0,11},{1,10},{2,9},{3,8},{4,15},{5,14},{6,13},{7,12},{8,3},{9,2},... | collective-permute-start | bytes 245768 | tf_op jit(solution)/shard_map/ppermute | solution.py:578
  26.1 10.2 %collective-permute-start.12 = (bf16[32,1280]{1,0:T(8,128)(2,1)S(1)}, bf16[32,1280]{1,0:T(8,128)(2,1)S(1)}, u32[]{:S(2)}, u32[]{:S(2)}) collective-permute-start(bf16[32,1280]{1,0:T(8,128)(2,1)S(1)} %get-tuple-element.66), channel_id=1, source_target_pairs={{0,2},{1,3},{2,0},{3,1},{4,6},{5,7},{6,4},{7,5},{8,10},{9,11},{10,... | collective-permute-start | bytes 245768 | tf_op jit(solution)/shard_map/ppermute | solution.py:578
  28.1 8.1 %collective-permute-start.13 = (bf16[32,1280]{1,0:T(8,128)(2,1)S(1)}, bf16[32,1280]{1,0:T(8,128)(2,1)S(1)}, u32[]{:S(2)}, u32[]{:S(2)}) collective-permute-start(bf16[32,1280]{1,0:T(8,128)(2,1)S(1)} %get-tuple-element.67), channel_id=1, source_target_pairs={{0,13},{1,12},{2,15},{3,14},{4,9},{5,8},{6,11},{7,10},{8,5},{9,4},... | collective-permute-start | bytes 245768 | tf_op jit(solution)/shard_map/ppermute | solution.py:578
  30.6 5.7 %collective-permute-start.14 = (bf16[32,1280]{1,0:T(8,128)(2,1)S(1)}, bf16[32,1280]{1,0:T(8,128)(2,1)S(1)}, u32[]{:S(2)}, u32[]{:S(2)}) collective-permute-start(bf16[32,1280]{1,0:T(8,128)(2,1)S(1)} %get-tuple-element.68), channel_id=1, source_target_pairs={{0,1},{1,0},{2,3},{3,2},{4,5},{5,4},{6,7},{7,6},{8,9},{9,8},{10,11... | collective-permute-start | bytes 245768 | tf_op jit(solution)/shard_map/ppermute | solution.py:578

commit v10 on v9

--- a/solution.py
+++ b/solution.py
@@ -43,7 +43,7 @@
     near = list(range(half - 1, 0, -1))
     quarter, eighth = half // 2, half // 4
     far = [half + (at // 2 if at % 2 == 0 else quarter + (at // 2 ^ eighth)) for at in range(half)]
-    order = [(far if kind == "f" else near).pop(0) for kind in "ffnfnfnfnnffnfn"]
+    order = [(far if kind == "f" else near).pop(0) for kind in "ffnfnfnfnnnffnf"]
     order.insert(groups - LATE - 1, 0)
     return order
 

time: 39.2 us -> 40.6 us (1.036)
  waiting for transfers between devices: 1.31 us -> 3.21 us
    ppermute x15, waiting for transfers between devices: 1.31 us -> 3.21 us  [shards(): lax.ppermute(block, 'pg', [(source, source ^ t) for source in range(group...]
  transfers between devices with their start and end apart: 15 -> 15, of which waited for: 2 -> 2; matrix products, arithmetic and copies ran while one was open for 0% -> 0% of each run, Pallas kernels for 14% -> 13%
where the time goes in v10:
time: 40.6 us; the launch traced here: 40.4 us
  starting transfers between devices  25.1 us (62%)
  Pallas kernels  10.3 us (25%)
  waiting for transfers between devices  3.21 us (8%)
  local copies, waits for them, and re-layouts  1.1 us (3%)
  between operations  0.7 us (2%)
    ppermute x15, starting transfers between devices, shards(): lax.ppermute(block, 'pg', [(source, source ^ t) for source in range(group...  25.1 us
    pallas_call x1, Pallas kernels, attend(): pl.pallas_call(functools.partial(attend_kernel, len(got), requests is not...  3.89 us
    ppermute x15, waiting for transfers between devices, shards(): lax.ppermute(block, 'pg', [(source, source ^ t) for source in range(group...  3.21 us
    pallas_call x1, Pallas kernels, front(): pl.pallas_call(functools.partial(front_kernel, order), out_shape=[block]...  2.54 us
    pallas_call x1, Pallas kernels, attend_late(): pl.pallas_call(functools.partial(late_kernel, len(got), first), out_shape...  2.52 us
    unnamed x6, local copies, waits for them, and re-layouts  1.1 us
    pallas_call x1, Pallas kernels, pack_others(): pl.pallas_call(pack_kernel, out_shape=[jax.ShapeDtypeStruct(block, jnp.bf...  0.87 us
  transfers between devices with their start and end apart: 15, of which 2 were waited for; matrix products, arithmetic and copies ran while one was open for 0% of the time, Pallas kernels for 13%

profile of v10, /device:TPU:0, one launch (start us, length us, event | category | flops | bytes accessed | tf_op | source)
XLA Modules:
  0.0 40.4 jit_solution(10397728278152223022)
XLA Ops:
  0.6 2.5 %front.1 = (bf16[32,1280]{1,0:T(8,128)(2,1)}, bf16[32,1280]{1,0:T(8,128)(2,1)}, bf16[32,1280]{1,0:T(8,128)(2,1)}, bf16[32,1280]{1,0:T(8,128)(2,1)}, f32[1296,128]{1,0:T(8,128)}) custom-call(s32[1]{0:T(128)} %bitcast.me_ref, s32[16]{0:T(128)} %assign_any.1, s32[16]{0:T(128)} %length_any.1, s32[16,16]{1,0:T(8,128)} %owner_any.1, s32[16,16]{1,0:T(8,128)} %stripe_any.1, ...), custom_call_target="tpu_custom_call" | custom-call | tf_op jit(solution)/shard_map/front/pallas_call | solution.py:179
  3.2 4.1 %collective-permute-start = (bf16[32,1280]{1,0:T(8,128)(2,1)}, bf16[32,1280]{1,0:T(8,128)(2,1)S(1)}, u32[]{:S(2)}, u32[]{:S(2)}) collective-permute-start(bf16[32,1280]{1,0:T(8,128)(2,1)} %get-tuple-element.50), channel_id=1, source_target_pairs={{0,8},{1,9},{2,10},{3,11},{4,12},{5,13},{6,14},{7,15},{8,0},{9,1},... | collective-permute-start | bytes 245768 | tf_op jit(solution)/shard_map/ppermute | solution.py:578
  7.3 2.3 %collective-permute-start.1 = (bf16[32,1280]{1,0:T(8,128)(2,1)}, bf16[32,1280]{1,0:T(8,128)(2,1)S(1)}, u32[]{:S(2)}, u32[]{:S(2)}) collective-permute-start(bf16[32,1280]{1,0:T(8,128)(2,1)} %get-tuple-element.51), channel_id=1, source_target_pairs={{0,14},{1,15},{2,12},{3,13},{4,10},{5,11},{6,8},{7,9},{8,6},{9,7},... | collective-permute-start | bytes 245768 | tf_op jit(solution)/shard_map/ppermute | solution.py:578
  9.6 2.7 %collective-permute-start.3 = (bf16[32,1280]{1,0:T(8,128)(2,1)}, bf16[32,1280]{1,0:T(8,128)(2,1)S(1)}, u32[]{:S(2)}, u32[]{:S(2)}) collective-permute-start(bf16[32,1280]{1,0:T(8,128)(2,1)} %get-tuple-element.53), channel_id=1, source_target_pairs={{0,9},{1,8},{2,11},{3,10},{4,13},{5,12},{6,15},{7,14},{8,1},{9,0},... | collective-permute-start | bytes 245768 | tf_op jit(solution)/shard_map/ppermute | solution.py:578
  12.3 1.1 %copy-done.1 = f32[1296,128]{1,0:T(8,128)S(1)} copy-done((f32[1296,128]{1,0:T(8,128)S(1)}, f32[1296,128]{1,0:T(8,128)}, u32[]{:S(2)}) %copy-start.1) | copy-done | bytes 663576
  13.4 0.9 %pack_others.1 = (bf16[32,1280]{1,0:T(8,128)(2,1)S(1)}, bf16[32,1280]{1,0:T(8,128)(2,1)S(1)}, bf16[32,1280]{1,0:T(8,128)(2,1)S(1)}, bf16[32,1280]{1,0:T(8,128)(2...) custom-call(f32[1296,128]{1,0:T(8,128)S(1)} %copy-done.1, ...), custom_call_target="tpu_custom_call" | custom-call | tf_op jit(solution)/shard_map/pack_others/pallas_call | solution.py:228
  14.3 1.7 %collective-permute-start.4 = (bf16[32,1280]{1,0:T(8,128)(2,1)S(1)}, bf16[32,1280]{1,0:T(8,128)(2,1)S(1)}, u32[]{:S(2)}, u32[]{:S(2)}) collective-permute-start(bf16[32,1280]{1,0:T(8,128)(2,1)S(1)} %get-tuple-element.54), channel_id=1, source_target_pairs={{0,6},{1,7},{2,4},{3,5},{4,2},{5,3},{6,0},{7,1},{8,14},{9,15},{10,... | collective-permute-start | bytes 245768 | tf_op jit(solution)/shard_map/ppermute | solution.py:578
  16.0 0.5 %rotate_queries.1 = (bf16[4,1024,128]{2,1,0:T(8,128)(2,1)S(1)}, bf16[8,128,128]{2,1,0:T(8,128)(2,1)S(1)}, f32[8,512]{1,0:T(8,128)S(1)}, s32[8,128]{1,0:T(8,128)S(1)}) custom-call(f32[1296,128]{1,0:T(8,128)S(1)} %copy-done.1, bf16[128,4096]{1,0:T(8,128)(2,1)S(1)} %bitcast.8), custom_call_target="tpu_custom_call" | custom-call | tf_op jit(solution)/shard_map/rotate_queries/pallas_call | solution.py:258
  16.5 0.0 collective-permute-done.refs_0_
  16.5 1.4 %collective-permute-start.5 = (bf16[32,1280]{1,0:T(8,128)(2,1)S(1)}, bf16[32,1280]{1,0:T(8,128)(2,1)S(1)}, u32[]{:S(2)}, u32[]{:S(2)}) collective-permute-start(bf16[32,1280]{1,0:T(8,128)(2,1)S(1)} %get-tuple-element.55), channel_id=1, source_target_pairs={{0,15},{1,14},{2,13},{3,12},{4,11},{5,10},{6,9},{7,8},{8,7},{9,6},... | collective-permute-start | bytes 245768 | tf_op jit(solution)/shard_map/ppermute | solution.py:578
  17.9 0.1 collective-permute-start.6
  18.0 3.6 %collective-permute-start.7 = (bf16[32,1280]{1,0:T(8,128)(2,1)S(1)}, bf16[32,1280]{1,0:T(8,128)(2,1)S(1)}, u32[]{:S(2)}, u32[]{:S(2)}) collective-permute-start(bf16[32,1280]{1,0:T(8,128)(2,1)S(1)} %get-tuple-element.57), channel_id=1, source_target_pairs={{0,10},{1,11},{2,8},{3,9},{4,14},{5,15},{6,12},{7,13},{8,2},{9,3},... | collective-permute-start | bytes 245768 | tf_op jit(solution)/shard_map/ppermute | solution.py:578
  21.7 0.0 collective-permute-done.3.refs_3_
  21.7 0.7 %collective-permute-start.8 = (bf16[32,1280]{1,0:T(8,128)(2,1)S(1)}, bf16[32,1280]{1,0:T(8,128)(2,1)S(1)}, u32[]{:S(2)}, u32[]{:S(2)}) collective-permute-start(bf16[32,1280]{1,0:T(8,128)(2,1)S(1)} %get-tuple-element.58), channel_id=1, source_target_pairs={{0,4},{1,5},{2,6},{3,7},{4,0},{5,1},{6,2},{7,3},{8,12},{9,13},{10,... | collective-permute-start | bytes 245768 | tf_op jit(solution)/shard_map/ppermute | solution.py:578
  22.4 2.4 %collective-permute-start.9 = (bf16[32,1280]{1,0:T(8,128)(2,1)S(1)}, bf16[32,1280]{1,0:T(8,128)(2,1)S(1)}, u32[]{:S(2)}, u32[]{:S(2)}) collective-permute-start(bf16[32,1280]{1,0:T(8,128)(2,1)S(1)} %get-tuple-element.59), channel_id=1, source_target_pairs={{0,3},{1,2},{2,1},{3,0},{4,7},{5,6},{6,5},{7,4},{8,11},{9,10},{10,... | collective-permute-start | bytes 245768 | tf_op jit(solution)/shard_map/ppermute | solution.py:578
  24.8 0.1 collective-permute-start.10
  24.9 0.6 %collective-permute-done.6.refs_6_ = bf16[32,1280]{1,0:T(8,128)(2,1)S(1)} collective-permute-done((bf16[32,1280]{1,0:T(8,128)(2,1)S(1)}, bf16[32,1280]{1,0:T(8,128)(2,1)S(1)}, u32[]{:S(2)}, u32[]{:S(2)}) %collective-permute-start.6) | collective-permute-done | bytes 81952 | tf_op jit(solution)/shard_map/ppermute | solution.py:578
  25.5 1.9 %collective-permute-start.11 = (bf16[32,1280]{1,0:T(8,128)(2,1)S(1)}, bf16[32,1280]{1,0:T(8,128)(2,1)S(1)}, u32[]{:S(2)}, u32[]{:S(2)}) collective-permute-start(bf16[32,1280]{1,0:T(8,128)(2,1)S(1)} %get-tuple-element.65), channel_id=1, source_target_pairs={{0,12},{1,13},{2,14},{3,15},{4,8},{5,9},{6,10},{7,11},{8,4},{9,5},... | collective-permute-start | bytes 245768 | tf_op jit(solution)/shard_map/ppermute | solution.py:578
  27.5 0.5 %collective-permute-start.12 = (bf16[32,1280]{1,0:T(8,128)(2,1)S(1)}, bf16[32,1280]{1,0:T(8,128)(2,1)S(1)}, u32[]{:S(2)}, u32[]{:S(2)}) collective-permute-start(bf16[32,1280]{1,0:T(8,128)(2,1)S(1)} %get-tuple-element.66), channel_id=1, source_target_pairs={{0,11},{1,10},{2,9},{3,8},{4,15},{5,14},{6,13},{7,12},{8,3},{9,2},... | collective-permute-start | bytes 245768 | tf_op jit(solution)/shard_map/ppermute | solution.py:578
  27.9 1.1 %collective-permute-start.13 = (bf16[32,1280]{1,0:T(8,128)(2,1)S(1)}, bf16[32,1280]{1,0:T(8,128)(2,1)S(1)}, u32[]{:S(2)}, u32[]{:S(2)}) collective-permute-start(bf16[32,1280]{1,0:T(8,128)(2,1)S(1)} %get-tuple-element.67), channel_id=1, source_target_pairs={{0,1},{1,0},{2,3},{3,2},{4,5},{5,4},{6,7},{7,6},{8,9},{9,8},{10,11... | collective-permute-start | bytes 245768 | tf_op jit(solution)/shard_map/ppermute | solution.py:578
  29.0 2.4 %collective-permute-start.14 = (bf16[32,1280]{1,0:T(8,128)(2,1)S(1)}, bf16[32,1280]{1,0:T(8,128)(2,1)S(1)}, u32[]{:S(2)}, u32[]{:S(2)}) collective-permute-start(bf16[32,1280]{1,0:T(8,128)(2,1)S(1)} %get-tuple-element.68), channel_id=1, source_target_pairs={{0,13},{1,12},{2,15},{3,14},{4,9},{5,8},{6,11},{7,10},{8,5},{9,4},... | collective-permute-start | bytes 245768 | tf_op jit(solution)/shard_map/ppermute | solution.py:578
  31.4 3.9 %attend.1 = (f32[4,1024,128]{2,1,0:T(8,128)S(1)}, f32[4,1024,128]{2,1,0:T(8,128)S(1)}, bf16[16,8,1024]{2,1,0:T(8,128)(2,1)}) custom-call(bf16[4,1024,128]{2,1,0:T(8,128)(2,1)S(1)} %get-tuple-element.47.rot_ref, f32[8,512]{1,0:T(8,128)S(1)} %get-tuple-element.48.bias_ref, bf16[8,128,128]{2,1,0:T(8,128)(2,1)S(1)} %get-tuple-element.49.own_ref, ...), custom_call_target="tpu_custom_call" | custom-call | tf_op jit(solution)/shard_map/attend/pallas_call | solution.py:401
  35.4 2.5 %collective-permute-done.12.refs_1_ = bf16[32,1280]{1,0:T(8,128)(2,1)S(1)} collective-permute-done((bf16[32,1280]{1,0:T(8,128)(2,1)S(1)}, bf16[32,1280]{1,0:T(8,128)(2,1)S(1)}, u32[]{:S(2)}, u32[]{:S(2)}) %collective-permute-start.12) | collective-permute-done | bytes 81952 | tf_op jit(solution)/shard_map/ppermute | solution.py:578
  37.9 2.5 %attend_late.1 = (bf16[128,4096]{1,0:T(8,128)(2,1)}, bf16[16,8,1024]{2,1,0:T(8,128)(2,1)}) custom-call(bf16[4,1024,128]{2,1,0:T(8,128)(2,1)S(1)} %get-tuple-element.47.rot_ref, f32[8,512]{1,0:T(8,128)S(1)} %get-tuple-element.48.bias_ref, f32[4,1024,128]{2,1,0:T(8,128)S(1)} %get-tuple-element.63.result_ref, ...), custom_call_target="tpu_custom_call", output_to_operand_aliasing={{1}: (9, {})} | custom-call | tf_op jit(solution)/shard_map/attend_late/pallas_call | solution.py:501
  (17 shorter events, 0.0 us)
Async XLA Ops:
  0.6 11.7 %copy-start = (bf16[1,16,32,1024]{3,2,1,0:T(8,128)(2,1)S(1)}, bf16[1,16,32,1024]{3,2,1,0:T(8,128)(2,1)}, u32[]{:S(2)}) copy-start(bf16[1,16,32,1024]{3,2,1,0:T(8,128)(2,1)} %param.10) | copy-start | bytes 3145732
  3.2 13.3 %collective-permute-start = (bf16[32,1280]{1,0:T(8,128)(2,1)}, bf16[32,1280]{1,0:T(8,128)(2,1)S(1)}, u32[]{:S(2)}, u32[]{:S(2)}) collective-permute-start(bf16[32,1280]{1,0:T(8,128)(2,1)} %get-tuple-element.50), channel_id=1, source_target_pairs={{0,8},{1,9},{2,10},{3,11},{4,12},{5,13},{6,14},{7,15},{8,0},{9,1},... | collective-permute-start | bytes 245768 | tf_op jit(solution)/shard_map/ppermute | solution.py:578
  7.3 10.6 %collective-permute-start.1 = (bf16[32,1280]{1,0:T(8,128)(2,1)}, bf16[32,1280]{1,0:T(8,128)(2,1)S(1)}, u32[]{:S(2)}, u32[]{:S(2)}) collective-permute-start(bf16[32,1280]{1,0:T(8,128)(2,1)} %get-tuple-element.51), channel_id=1, source_target_pairs={{0,14},{1,15},{2,12},{3,13},{4,10},{5,11},{6,8},{7,9},{8,6},{9,7},... | collective-permute-start | bytes 245768 | tf_op jit(solution)/shard_map/ppermute | solution.py:578
  9.6 8.4 %collective-permute-start.2 = (bf16[32,1280]{1,0:T(8,128)(2,1)}, bf16[32,1280]{1,0:T(8,128)(2,1)S(1)}, u32[]{:S(2)}, u32[]{:S(2)}) collective-permute-start(bf16[32,1280]{1,0:T(8,128)(2,1)} %get-tuple-element.52), channel_id=1, source_target_pairs={{0,7},{1,6},{2,5},{3,4},{4,3},{5,2},{6,1},{7,0},{8,15},{9,14},{10,... | collective-permute-start | bytes 245768 | tf_op jit(solution)/shard_map/ppermute | solution.py:578
  9.6 12.1 %collective-permute-start.3 = (bf16[32,1280]{1,0:T(8,128)(2,1)}, bf16[32,1280]{1,0:T(8,128)(2,1)S(1)}, u32[]{:S(2)}, u32[]{:S(2)}) collective-permute-start(bf16[32,1280]{1,0:T(8,128)(2,1)} %get-tuple-element.53), channel_id=1, source_target_pairs={{0,9},{1,8},{2,11},{3,10},{4,13},{5,12},{6,15},{7,14},{8,1},{9,0},... | collective-permute-start | bytes 245768 | tf_op jit(solution)/shard_map/ppermute | solution.py:578
  12.3 1.1 %copy-start.1 = (f32[1296,128]{1,0:T(8,128)S(1)}, f32[1296,128]{1,0:T(8,128)}, u32[]{:S(2)}) copy-start(f32[1296,128]{1,0:T(8,128)} %get-tuple-element.37.info_ref) | copy-start | bytes 1990660
  13.4 2.6 %copy-start.2 = (bf16[1,128,4096]{2,1,0:T(8,128)(2,1)S(1)}, bf16[1,128,4096]{2,1,0:T(8,128)(2,1)}, u32[]{:S(2)}) copy-start(bf16[1,128,4096]{2,1,0:T(8,128)(2,1)} %param.8) | copy-start | bytes 3145732
  14.3 8.1 %collective-permute-start.4 = (bf16[32,1280]{1,0:T(8,128)(2,1)S(1)}, bf16[32,1280]{1,0:T(8,128)(2,1)S(1)}, u32[]{:S(2)}, u32[]{:S(2)}) collective-permute-start(bf16[32,1280]{1,0:T(8,128)(2,1)S(1)} %get-tuple-element.54), channel_id=1, source_target_pairs={{0,6},{1,7},{2,4},{3,5},{4,2},{5,3},{6,0},{7,1},{8,14},{9,15},{10,... | collective-permute-start | bytes 245768 | tf_op jit(solution)/shard_map/ppermute | solution.py:578
  16.5 8.3 %collective-permute-start.5 = (bf16[32,1280]{1,0:T(8,128)(2,1)S(1)}, bf16[32,1280]{1,0:T(8,128)(2,1)S(1)}, u32[]{:S(2)}, u32[]{:S(2)}) collective-permute-start(bf16[32,1280]{1,0:T(8,128)(2,1)S(1)} %get-tuple-element.55), channel_id=1, source_target_pairs={{0,15},{1,14},{2,13},{3,12},{4,11},{5,10},{6,9},{7,8},{8,7},{9,6},... | collective-permute-start | bytes 245768 | tf_op jit(solution)/shard_map/ppermute | solution.py:578
  17.9 7.6 %collective-permute-start.6 = (bf16[32,1280]{1,0:T(8,128)(2,1)S(1)}, bf16[32,1280]{1,0:T(8,128)(2,1)S(1)}, u32[]{:S(2)}, u32[]{:S(2)}) collective-permute-start(bf16[32,1280]{1,0:T(8,128)(2,1)S(1)} %get-tuple-element.56), channel_id=1, source_target_pairs={{0,5},{1,4},{2,7},{3,6},{4,1},{5,0},{6,3},{7,2},{8,13},{9,12},{10,... | collective-permute-start | bytes 245768 | tf_op jit(solution)/shard_map/ppermute | solution.py:578
  18.0 9.4 %collective-permute-start.7 = (bf16[32,1280]{1,0:T(8,128)(2,1)S(1)}, bf16[32,1280]{1,0:T(8,128)(2,1)S(1)}, u32[]{:S(2)}, u32[]{:S(2)}) collective-permute-start(bf16[32,1280]{1,0:T(8,128)(2,1)S(1)} %get-tuple-element.57), channel_id=1, source_target_pairs={{0,10},{1,11},{2,8},{3,9},{4,14},{5,15},{6,12},{7,13},{8,2},{9,3},... | collective-permute-start | bytes 245768 | tf_op jit(solution)/shard_map/ppermute | solution.py:578
  21.7 6.3 %collective-permute-start.8 = (bf16[32,1280]{1,0:T(8,128)(2,1)S(1)}, bf16[32,1280]{1,0:T(8,128)(2,1)S(1)}, u32[]{:S(2)}, u32[]{:S(2)}) collective-permute-start(bf16[32,1280]{1,0:T(8,128)(2,1)S(1)} %get-tuple-element.58), channel_id=1, source_target_pairs={{0,4},{1,5},{2,6},{3,7},{4,0},{5,1},{6,2},{7,3},{8,12},{9,13},{10,... | collective-permute-start | bytes 245768 | tf_op jit(solution)/shard_map/ppermute | solution.py:578
  22.4 6.7 %collective-permute-start.9 = (bf16[32,1280]{1,0:T(8,128)(2,1)S(1)}, bf16[32,1280]{1,0:T(8,128)(2,1)S(1)}, u32[]{:S(2)}, u32[]{:S(2)}) collective-permute-start(bf16[32,1280]{1,0:T(8,128)(2,1)S(1)} %get-tuple-element.59), channel_id=1, source_target_pairs={{0,3},{1,2},{2,1},{3,0},{4,7},{5,6},{6,5},{7,4},{8,11},{9,10},{10,... | collective-permute-start | bytes 245768 | tf_op jit(solution)/shard_map/ppermute | solution.py:578
  24.8 6.6 %collective-permute-start.10 = (bf16[32,1280]{1,0:T(8,128)(2,1)S(1)}, bf16[32,1280]{1,0:T(8,128)(2,1)S(1)}, u32[]{:S(2)}, u32[]{:S(2)}) collective-permute-start(bf16[32,1280]{1,0:T(8,128)(2,1)S(1)} %get-tuple-element.60), channel_id=1, source_target_pairs={{0,2},{1,3},{2,0},{3,1},{4,6},{5,7},{6,4},{7,5},{8,10},{9,11},{10,... | collective-permute-start | bytes 245768 | tf_op jit(solution)/shard_map/ppermute | solution.py:578
  25.5 9.8 %collective-permute-start.11 = (bf16[32,1280]{1,0:T(8,128)(2,1)S(1)}, bf16[32,1280]{1,0:T(8,128)(2,1)S(1)}, u32[]{:S(2)}, u32[]{:S(2)}) collective-permute-start(bf16[32,1280]{1,0:T(8,128)(2,1)S(1)} %get-tuple-element.65), channel_id=1, source_target_pairs={{0,12},{1,13},{2,14},{3,15},{4,8},{5,9},{6,10},{7,11},{8,4},{9,5},... | collective-permute-start | bytes 245768 | tf_op jit(solution)/shard_map/ppermute | solution.py:578
  27.5 10.4 %collective-permute-start.12 = (bf16[32,1280]{1,0:T(8,128)(2,1)S(1)}, bf16[32,1280]{1,0:T(8,128)(2,1)S(1)}, u32[]{:S(2)}, u32[]{:S(2)}) collective-permute-start(bf16[32,1280]{1,0:T(8,128)(2,1)S(1)} %get-tuple-element.66), channel_id=1, source_target_pairs={{0,11},{1,10},{2,9},{3,8},{4,15},{5,14},{6,13},{7,12},{8,3},{9,2},... | collective-permute-start | bytes 245768 | tf_op jit(solution)/shard_map/ppermute | solution.py:578
  27.9 9.9 %collective-permute-start.13 = (bf16[32,1280]{1,0:T(8,128)(2,1)S(1)}, bf16[32,1280]{1,0:T(8,128)(2,1)S(1)}, u32[]{:S(2)}, u32[]{:S(2)}) collective-permute-start(bf16[32,1280]{1,0:T(8,128)(2,1)S(1)} %get-tuple-element.67), channel_id=1, source_target_pairs={{0,1},{1,0},{2,3},{3,2},{4,5},{5,4},{6,7},{7,6},{8,9},{9,8},{10,11... | collective-permute-start | bytes 245768 | tf_op jit(solution)/shard_map/ppermute | solution.py:578
  29.0 8.9 %collective-permute-start.14 = (bf16[32,1280]{1,0:T(8,128)(2,1)S(1)}, bf16[32,1280]{1,0:T(8,128)(2,1)S(1)}, u32[]{:S(2)}, u32[]{:S(2)}) collective-permute-start(bf16[32,1280]{1,0:T(8,128)(2,1)S(1)} %get-tuple-element.68), channel_id=1, source_target_pairs={{0,13},{1,12},{2,15},{3,14},{4,9},{5,8},{6,11},{7,10},{8,5},{9,4},... | collective-permute-start | bytes 245768 | tf_op jit(solution)/shard_map/ppermute | solution.py:578

commit v11 on v8

--- a/solution.py
+++ b/solution.py
@@ -19,7 +19,7 @@
 ROPE_BASE = 1000000.0
 MASKED = -1e30
 SCALE = HEAD_DIM ** -0.5 / math.log(2.0)
-CHUNK = 256
+CHUNK = 512
 LATE = 4
 LATE_CHUNK = 512
 AHEAD = 4

time: 39 us -> 39 us (level)
  no operation moved by 1% of the time
where the time goes in v11:
time: 39 us; the launch traced here: 38.8 us
  starting transfers between devices  25.6 us (66%)
  Pallas kernels  10.3 us (26%)
  waiting for transfers between devices  1.12 us (3%)
  local copies, waits for them, and re-layouts  1.1 us (3%)
  between operations  0.7 us (2%)
    ppermute x15, starting transfers between devices, shards(): lax.ppermute(block, 'pg', [(source, source ^ t) for source in range(group...  25.6 us
    pallas_call x1, Pallas kernels, attend(): pl.pallas_call(functools.partial(attend_kernel, len(got), requests is not...  3.85 us
    pallas_call x1, Pallas kernels, front(): pl.pallas_call(functools.partial(front_kernel, order), out_shape=[block]...  2.54 us
    pallas_call x1, Pallas kernels, attend_late(): pl.pallas_call(functools.partial(late_kernel, len(got), first), out_shape...  2.52 us
    ppermute x15, waiting for transfers between devices, shards(): lax.ppermute(block, 'pg', [(source, source ^ t) for source in range(group...  1.12 us
    unnamed x6, local copies, waits for them, and re-layouts  1.1 us
    pallas_call x1, Pallas kernels, pack_others(): pl.pallas_call(pack_kernel, out_shape=[jax.ShapeDtypeStruct(block, jnp.bf...  0.87 us
  transfers between devices with their start and end apart: 15, of which 2 were waited for; matrix products, arithmetic and copies ran while one was open for 0% of the time, Pallas kernels for 14%

profile of v11, /device:TPU:0, one launch (start us, length us, event | category | flops | bytes accessed | tf_op | source)
XLA Modules:
  0.0 38.8 jit_solution(6688500813350283035)
XLA Ops:
  0.6 2.5 %front.1 = (bf16[32,1280]{1,0:T(8,128)(2,1)}, bf16[32,1280]{1,0:T(8,128)(2,1)}, bf16[32,1280]{1,0:T(8,128)(2,1)}, bf16[32,1280]{1,0:T(8,128)(2,1)}, f32[1296,128]{1,0:T(8,128)}) custom-call(s32[1]{0:T(128)} %bitcast.me_ref, s32[16]{0:T(128)} %assign_any.1, s32[16]{0:T(128)} %length_any.1, s32[16,16]{1,0:T(8,128)} %owner_any.1, s32[16,16]{1,0:T(8,128)} %stripe_any.1, ...), custom_call_target="tpu_custom_call" | custom-call | tf_op jit(solution)/shard_map/front/pallas_call | solution.py:179
  3.2 4.1 %collective-permute-start = (bf16[32,1280]{1,0:T(8,128)(2,1)}, bf16[32,1280]{1,0:T(8,128)(2,1)S(1)}, u32[]{:S(2)}, u32[]{:S(2)}) collective-permute-start(bf16[32,1280]{1,0:T(8,128)(2,1)} %get-tuple-element.50), channel_id=1, source_target_pairs={{0,8},{1,9},{2,10},{3,11},{4,12},{5,13},{6,14},{7,15},{8,0},{9,1},... | collective-permute-start | bytes 245768 | tf_op jit(solution)/shard_map/ppermute | solution.py:578
  7.3 2.3 %collective-permute-start.1 = (bf16[32,1280]{1,0:T(8,128)(2,1)}, bf16[32,1280]{1,0:T(8,128)(2,1)S(1)}, u32[]{:S(2)}, u32[]{:S(2)}) collective-permute-start(bf16[32,1280]{1,0:T(8,128)(2,1)} %get-tuple-element.51), channel_id=1, source_target_pairs={{0,14},{1,15},{2,12},{3,13},{4,10},{5,11},{6,8},{7,9},{8,6},{9,7},... | collective-permute-start | bytes 245768 | tf_op jit(solution)/shard_map/ppermute | solution.py:578
  9.6 2.7 %collective-permute-start.3 = (bf16[32,1280]{1,0:T(8,128)(2,1)}, bf16[32,1280]{1,0:T(8,128)(2,1)S(1)}, u32[]{:S(2)}, u32[]{:S(2)}) collective-permute-start(bf16[32,1280]{1,0:T(8,128)(2,1)} %get-tuple-element.53), channel_id=1, source_target_pairs={{0,9},{1,8},{2,11},{3,10},{4,13},{5,12},{6,15},{7,14},{8,1},{9,0},... | collective-permute-start | bytes 245768 | tf_op jit(solution)/shard_map/ppermute | solution.py:578
  12.3 1.1 %copy-done.1 = f32[1296,128]{1,0:T(8,128)S(1)} copy-done((f32[1296,128]{1,0:T(8,128)S(1)}, f32[1296,128]{1,0:T(8,128)}, u32[]{:S(2)}) %copy-start.1) | copy-done | bytes 663576
  13.4 0.9 %pack_others.1 = (bf16[32,1280]{1,0:T(8,128)(2,1)S(1)}, bf16[32,1280]{1,0:T(8,128)(2,1)S(1)}, bf16[32,1280]{1,0:T(8,128)(2,1)S(1)}, bf16[32,1280]{1,0:T(8,128)(2...) custom-call(f32[1296,128]{1,0:T(8,128)S(1)} %copy-done.1, ...), custom_call_target="tpu_custom_call" | custom-call | tf_op jit(solution)/shard_map/pack_others/pallas_call | solution.py:228
  14.3 1.7 %collective-permute-start.4 = (bf16[32,1280]{1,0:T(8,128)(2,1)S(1)}, bf16[32,1280]{1,0:T(8,128)(2,1)S(1)}, u32[]{:S(2)}, u32[]{:S(2)}) collective-permute-start(bf16[32,1280]{1,0:T(8,128)(2,1)S(1)} %get-tuple-element.54), channel_id=1, source_target_pairs={{0,6},{1,7},{2,4},{3,5},{4,2},{5,3},{6,0},{7,1},{8,14},{9,15},{10,... | collective-permute-start | bytes 245768 | tf_op jit(solution)/shard_map/ppermute | solution.py:578
  16.0 0.5 %rotate_queries.1 = (bf16[4,1024,128]{2,1,0:T(8,128)(2,1)S(1)}, bf16[8,128,128]{2,1,0:T(8,128)(2,1)S(1)}, f32[8,512]{1,0:T(8,128)S(1)}, s32[8,128]{1,0:T(8,128)S(1)}) custom-call(f32[1296,128]{1,0:T(8,128)S(1)} %copy-done.1, bf16[128,4096]{1,0:T(8,128)(2,1)S(1)} %bitcast.8), custom_call_target="tpu_custom_call" | custom-call | tf_op jit(solution)/shard_map/rotate_queries/pallas_call | solution.py:258
  16.5 1.4 %collective-permute-start.5 = (bf16[32,1280]{1,0:T(8,128)(2,1)S(1)}, bf16[32,1280]{1,0:T(8,128)(2,1)S(1)}, u32[]{:S(2)}, u32[]{:S(2)}) collective-permute-start(bf16[32,1280]{1,0:T(8,128)(2,1)S(1)} %get-tuple-element.55), channel_id=1, source_target_pairs={{0,15},{1,14},{2,13},{3,12},{4,11},{5,10},{6,9},{7,8},{8,7},{9,6},... | collective-permute-start | bytes 245768 | tf_op jit(solution)/shard_map/ppermute | solution.py:578
  17.9 0.1 collective-permute-start.6
  18.0 0.0 collective-permute-done.2.refs_2_
  18.0 3.6 %collective-permute-start.7 = (bf16[32,1280]{1,0:T(8,128)(2,1)S(1)}, bf16[32,1280]{1,0:T(8,128)(2,1)S(1)}, u32[]{:S(2)}, u32[]{:S(2)}) collective-permute-start(bf16[32,1280]{1,0:T(8,128)(2,1)S(1)} %get-tuple-element.57), channel_id=1, source_target_pairs={{0,10},{1,11},{2,8},{3,9},{4,14},{5,15},{6,12},{7,13},{8,2},{9,3},... | collective-permute-start | bytes 245768 | tf_op jit(solution)/shard_map/ppermute | solution.py:578
  21.7 0.0 collective-permute-done.3.refs_3_
  21.7 0.7 %collective-permute-start.8 = (bf16[32,1280]{1,0:T(8,128)(2,1)S(1)}, bf16[32,1280]{1,0:T(8,128)(2,1)S(1)}, u32[]{:S(2)}, u32[]{:S(2)}) collective-permute-start(bf16[32,1280]{1,0:T(8,128)(2,1)S(1)} %get-tuple-element.58), channel_id=1, source_target_pairs={{0,4},{1,5},{2,6},{3,7},{4,0},{5,1},{6,2},{7,3},{8,12},{9,13},{10,... | collective-permute-start | bytes 245768 | tf_op jit(solution)/shard_map/ppermute | solution.py:578
  22.4 1.3 %collective-permute-start.9 = (bf16[32,1280]{1,0:T(8,128)(2,1)S(1)}, bf16[32,1280]{1,0:T(8,128)(2,1)S(1)}, u32[]{:S(2)}, u32[]{:S(2)}) collective-permute-start(bf16[32,1280]{1,0:T(8,128)(2,1)S(1)} %get-tuple-element.59), channel_id=1, source_target_pairs={{0,12},{1,13},{2,14},{3,15},{4,8},{5,9},{6,10},{7,11},{8,4},{9,5},... | collective-permute-start | bytes 245768 | tf_op jit(solution)/shard_map/ppermute | solution.py:578
  23.7 2.0 %collective-permute-start.10 = (bf16[32,1280]{1,0:T(8,128)(2,1)S(1)}, bf16[32,1280]{1,0:T(8,128)(2,1)S(1)}, u32[]{:S(2)}, u32[]{:S(2)}) collective-permute-start(bf16[32,1280]{1,0:T(8,128)(2,1)S(1)} %get-tuple-element.60), channel_id=1, source_target_pairs={{0,3},{1,2},{2,1},{3,0},{4,7},{5,6},{6,5},{7,4},{8,11},{9,10},{10,... | collective-permute-start | bytes 245768 | tf_op jit(solution)/shard_map/ppermute | solution.py:578
  25.7 1.7 %collective-permute-start.11 = (bf16[32,1280]{1,0:T(8,128)(2,1)S(1)}, bf16[32,1280]{1,0:T(8,128)(2,1)S(1)}, u32[]{:S(2)}, u32[]{:S(2)}) collective-permute-start(bf16[32,1280]{1,0:T(8,128)(2,1)S(1)} %get-tuple-element.65), channel_id=1, source_target_pairs={{0,11},{1,10},{2,9},{3,8},{4,15},{5,14},{6,13},{7,12},{8,3},{9,2},... | collective-permute-start | bytes 245768 | tf_op jit(solution)/shard_map/ppermute | solution.py:578
  27.4 0.9 %collective-permute-start.12 = (bf16[32,1280]{1,0:T(8,128)(2,1)S(1)}, bf16[32,1280]{1,0:T(8,128)(2,1)S(1)}, u32[]{:S(2)}, u32[]{:S(2)}) collective-permute-start(bf16[32,1280]{1,0:T(8,128)(2,1)S(1)} %get-tuple-element.66), channel_id=1, source_target_pairs={{0,2},{1,3},{2,0},{3,1},{4,6},{5,7},{6,4},{7,5},{8,10},{9,11},{10,... | collective-permute-start | bytes 245768 | tf_op jit(solution)/shard_map/ppermute | solution.py:578
  28.3 2.7 %collective-permute-start.13 = (bf16[32,1280]{1,0:T(8,128)(2,1)S(1)}, bf16[32,1280]{1,0:T(8,128)(2,1)S(1)}, u32[]{:S(2)}, u32[]{:S(2)}) collective-permute-start(bf16[32,1280]{1,0:T(8,128)(2,1)S(1)} %get-tuple-element.67), channel_id=1, source_target_pairs={{0,13},{1,12},{2,15},{3,14},{4,9},{5,8},{6,11},{7,10},{8,5},{9,4},... | collective-permute-start | bytes 245768 | tf_op jit(solution)/shard_map/ppermute | solution.py:578
  31.0 0.2 collective-permute-done.9.refs_9_
  31.3 0.3 collective-permute-start.14
  31.5 3.9 %attend.1 = (f32[4,1024,128]{2,1,0:T(8,128)S(1)}, f32[4,1024,128]{2,1,0:T(8,128)S(1)}, bf16[16,8,1024]{2,1,0:T(8,128)(2,1)}) custom-call(bf16[4,1024,128]{2,1,0:T(8,128)(2,1)S(1)} %get-tuple-element.47.rot_ref, f32[8,512]{1,0:T(8,128)S(1)} %get-tuple-element.48.bias_ref, bf16[8,128,128]{2,1,0:T(8,128)(2,1)S(1)} %get-tuple-element.49.own_ref, ...), custom_call_target="tpu_custom_call" | custom-call | tf_op jit(solution)/shard_map/attend/pallas_call | solution.py:401
  35.4 0.9 %collective-permute-done.11.refs_0_ = bf16[32,1280]{1,0:T(8,128)(2,1)S(1)} collective-permute-done((bf16[32,1280]{1,0:T(8,128)(2,1)S(1)}, bf16[32,1280]{1,0:T(8,128)(2,1)S(1)}, u32[]{:S(2)}, u32[]{:S(2)}) %collective-permute-start.11) | collective-permute-done | bytes 81952 | tf_op jit(solution)/shard_map/ppermute | solution.py:578
  36.3 2.5 %attend_late.1 = (bf16[128,4096]{1,0:T(8,128)(2,1)}, bf16[16,8,1024]{2,1,0:T(8,128)(2,1)}) custom-call(bf16[4,1024,128]{2,1,0:T(8,128)(2,1)S(1)} %get-tuple-element.47.rot_ref, f32[8,512]{1,0:T(8,128)S(1)} %get-tuple-element.48.bias_ref, f32[4,1024,128]{2,1,0:T(8,128)S(1)} %get-tuple-element.63.result_ref, ...), custom_call_target="tpu_custom_call", output_to_operand_aliasing={{1}: (9, {})} | custom-call | tf_op jit(solution)/shard_map/attend_late/pallas_call | solution.py:501
  (17 shorter events, 0.0 us)
Async XLA Ops:
  0.6 11.7 %copy-start = (bf16[1,16,32,1024]{3,2,1,0:T(8,128)(2,1)S(1)}, bf16[1,16,32,1024]{3,2,1,0:T(8,128)(2,1)}, u32[]{:S(2)}) copy-start(bf16[1,16,32,1024]{3,2,1,0:T(8,128)(2,1)} %param.10) | copy-start | bytes 3145732
  3.2 13.3 %collective-permute-start = (bf16[32,1280]{1,0:T(8,128)(2,1)}, bf16[32,1280]{1,0:T(8,128)(2,1)S(1)}, u32[]{:S(2)}, u32[]{:S(2)}) collective-permute-start(bf16[32,1280]{1,0:T(8,128)(2,1)} %get-tuple-element.50), channel_id=1, source_target_pairs={{0,8},{1,9},{2,10},{3,11},{4,12},{5,13},{6,14},{7,15},{8,0},{9,1},... | collective-permute-start | bytes 245768 | tf_op jit(solution)/shard_map/ppermute | solution.py:578
  7.3 10.6 %collective-permute-start.1 = (bf16[32,1280]{1,0:T(8,128)(2,1)}, bf16[32,1280]{1,0:T(8,128)(2,1)S(1)}, u32[]{:S(2)}, u32[]{:S(2)}) collective-permute-start(bf16[32,1280]{1,0:T(8,128)(2,1)} %get-tuple-element.51), channel_id=1, source_target_pairs={{0,14},{1,15},{2,12},{3,13},{4,10},{5,11},{6,8},{7,9},{8,6},{9,7},... | collective-permute-start | bytes 245768 | tf_op jit(solution)/shard_map/ppermute | solution.py:578
  9.6 8.4 %collective-permute-start.2 = (bf16[32,1280]{1,0:T(8,128)(2,1)}, bf16[32,1280]{1,0:T(8,128)(2,1)S(1)}, u32[]{:S(2)}, u32[]{:S(2)}) collective-permute-start(bf16[32,1280]{1,0:T(8,128)(2,1)} %get-tuple-element.52), channel_id=1, source_target_pairs={{0,7},{1,6},{2,5},{3,4},{4,3},{5,2},{6,1},{7,0},{8,15},{9,14},{10,... | collective-permute-start | bytes 245768 | tf_op jit(solution)/shard_map/ppermute | solution.py:578
  9.6 12.1 %collective-permute-start.3 = (bf16[32,1280]{1,0:T(8,128)(2,1)}, bf16[32,1280]{1,0:T(8,128)(2,1)S(1)}, u32[]{:S(2)}, u32[]{:S(2)}) collective-permute-start(bf16[32,1280]{1,0:T(8,128)(2,1)} %get-tuple-element.53), channel_id=1, source_target_pairs={{0,9},{1,8},{2,11},{3,10},{4,13},{5,12},{6,15},{7,14},{8,1},{9,0},... | collective-permute-start | bytes 245768 | tf_op jit(solution)/shard_map/ppermute | solution.py:578
  12.3 1.1 %copy-start.1 = (f32[1296,128]{1,0:T(8,128)S(1)}, f32[1296,128]{1,0:T(8,128)}, u32[]{:S(2)}) copy-start(f32[1296,128]{1,0:T(8,128)} %get-tuple-element.37.info_ref) | copy-start | bytes 1990660
  13.4 2.6 %copy-start.2 = (bf16[1,128,4096]{2,1,0:T(8,128)(2,1)S(1)}, bf16[1,128,4096]{2,1,0:T(8,128)(2,1)}, u32[]{:S(2)}) copy-start(bf16[1,128,4096]{2,1,0:T(8,128)(2,1)} %param.8) | copy-start | bytes 3145732
  14.3 8.1 %collective-permute-start.4 = (bf16[32,1280]{1,0:T(8,128)(2,1)S(1)}, bf16[32,1280]{1,0:T(8,128)(2,1)S(1)}, u32[]{:S(2)}, u32[]{:S(2)}) collective-permute-start(bf16[32,1280]{1,0:T(8,128)(2,1)S(1)} %get-tuple-element.54), channel_id=1, source_target_pairs={{0,6},{1,7},{2,4},{3,5},{4,2},{5,3},{6,0},{7,1},{8,14},{9,15},{10,... | collective-permute-start | bytes 245768 | tf_op jit(solution)/shard_map/ppermute | solution.py:578
  16.5 7.2 %collective-permute-start.5 = (bf16[32,1280]{1,0:T(8,128)(2,1)S(1)}, bf16[32,1280]{1,0:T(8,128)(2,1)S(1)}, u32[]{:S(2)}, u32[]{:S(2)}) collective-permute-start(bf16[32,1280]{1,0:T(8,128)(2,1)S(1)} %get-tuple-element.55), channel_id=1, source_target_pairs={{0,15},{1,14},{2,13},{3,12},{4,11},{5,10},{6,9},{7,8},{8,7},{9,6},... | collective-permute-start | bytes 245768 | tf_op jit(solution)/shard_map/ppermute | solution.py:578
  17.9 7.8 %collective-permute-start.6 = (bf16[32,1280]{1,0:T(8,128)(2,1)S(1)}, bf16[32,1280]{1,0:T(8,128)(2,1)S(1)}, u32[]{:S(2)}, u32[]{:S(2)}) collective-permute-start(bf16[32,1280]{1,0:T(8,128)(2,1)S(1)} %get-tuple-element.56), channel_id=1, source_target_pairs={{0,5},{1,4},{2,7},{3,6},{4,1},{5,0},{6,3},{7,2},{8,13},{9,12},{10,... | collective-permute-start | bytes 245768 | tf_op jit(solution)/shard_map/ppermute | solution.py:578
  18.0 9.4 %collective-permute-start.7 = (bf16[32,1280]{1,0:T(8,128)(2,1)S(1)}, bf16[32,1280]{1,0:T(8,128)(2,1)S(1)}, u32[]{:S(2)}, u32[]{:S(2)}) collective-permute-start(bf16[32,1280]{1,0:T(8,128)(2,1)S(1)} %get-tuple-element.57), channel_id=1, source_target_pairs={{0,10},{1,11},{2,8},{3,9},{4,14},{5,15},{6,12},{7,13},{8,2},{9,3},... | collective-permute-start | bytes 245768 | tf_op jit(solution)/shard_map/ppermute | solution.py:578
  21.7 6.6 %collective-permute-start.8 = (bf16[32,1280]{1,0:T(8,128)(2,1)S(1)}, bf16[32,1280]{1,0:T(8,128)(2,1)S(1)}, u32[]{:S(2)}, u32[]{:S(2)}) collective-permute-start(bf16[32,1280]{1,0:T(8,128)(2,1)S(1)} %get-tuple-element.58), channel_id=1, source_target_pairs={{0,4},{1,5},{2,6},{3,7},{4,0},{5,1},{6,2},{7,3},{8,12},{9,13},{10,... | collective-permute-start | bytes 245768 | tf_op jit(solution)/shard_map/ppermute | solution.py:578
  22.4 8.9 %collective-permute-start.9 = (bf16[32,1280]{1,0:T(8,128)(2,1)S(1)}, bf16[32,1280]{1,0:T(8,128)(2,1)S(1)}, u32[]{:S(2)}, u32[]{:S(2)}) collective-permute-start(bf16[32,1280]{1,0:T(8,128)(2,1)S(1)} %get-tuple-element.59), channel_id=1, source_target_pairs={{0,12},{1,13},{2,14},{3,15},{4,8},{5,9},{6,10},{7,11},{8,4},{9,5},... | collective-permute-start | bytes 245768 | tf_op jit(solution)/shard_map/ppermute | solution.py:578
  23.7 7.9 %collective-permute-start.10 = (bf16[32,1280]{1,0:T(8,128)(2,1)S(1)}, bf16[32,1280]{1,0:T(8,128)(2,1)S(1)}, u32[]{:S(2)}, u32[]{:S(2)}) collective-permute-start(bf16[32,1280]{1,0:T(8,128)(2,1)S(1)} %get-tuple-element.60), channel_id=1, source_target_pairs={{0,3},{1,2},{2,1},{3,0},{4,7},{5,6},{6,5},{7,4},{8,11},{9,10},{10,... | collective-permute-start | bytes 245768 | tf_op jit(solution)/shard_map/ppermute | solution.py:578
  25.7 10.6 %collective-permute-start.11 = (bf16[32,1280]{1,0:T(8,128)(2,1)S(1)}, bf16[32,1280]{1,0:T(8,128)(2,1)S(1)}, u32[]{:S(2)}, u32[]{:S(2)}) collective-permute-start(bf16[32,1280]{1,0:T(8,128)(2,1)S(1)} %get-tuple-element.65), channel_id=1, source_target_pairs={{0,11},{1,10},{2,9},{3,8},{4,15},{5,14},{6,13},{7,12},{8,3},{9,2},... | collective-permute-start | bytes 245768 | tf_op jit(solution)/shard_map/ppermute | solution.py:578
  27.4 8.9 %collective-permute-start.12 = (bf16[32,1280]{1,0:T(8,128)(2,1)S(1)}, bf16[32,1280]{1,0:T(8,128)(2,1)S(1)}, u32[]{:S(2)}, u32[]{:S(2)}) collective-permute-start(bf16[32,1280]{1,0:T(8,128)(2,1)S(1)} %get-tuple-element.66), channel_id=1, source_target_pairs={{0,2},{1,3},{2,0},{3,1},{4,6},{5,7},{6,4},{7,5},{8,10},{9,11},{10,... | collective-permute-start | bytes 245768 | tf_op jit(solution)/shard_map/ppermute | solution.py:578
  28.3 8.0 %collective-permute-start.13 = (bf16[32,1280]{1,0:T(8,128)(2,1)S(1)}, bf16[32,1280]{1,0:T(8,128)(2,1)S(1)}, u32[]{:S(2)}, u32[]{:S(2)}) collective-permute-start(bf16[32,1280]{1,0:T(8,128)(2,1)S(1)} %get-tuple-element.67), channel_id=1, source_target_pairs={{0,13},{1,12},{2,15},{3,14},{4,9},{5,8},{6,11},{7,10},{8,5},{9,4},... | collective-permute-start | bytes 245768 | tf_op jit(solution)/shard_map/ppermute | solution.py:578
  31.3 5.0 %collective-permute-start.14 = (bf16[32,1280]{1,0:T(8,128)(2,1)S(1)}, bf16[32,1280]{1,0:T(8,128)(2,1)S(1)}, u32[]{:S(2)}, u32[]{:S(2)}) collective-permute-start(bf16[32,1280]{1,0:T(8,128)(2,1)S(1)} %get-tuple-element.68), channel_id=1, source_target_pairs={{0,1},{1,0},{2,3},{3,2},{4,5},{5,4},{6,7},{7,6},{8,9},{9,8},{10,11... | collective-permute-start | bytes 245768 | tf_op jit(solution)/shard_map/ppermute | solution.py:578

commit v12 on v8

--- a/solution.py
+++ b/solution.py
@@ -43,6 +43,7 @@
     near = list(range(half - 1, 0, -1))
     quarter, eighth = half // 2, half // 4
     far = [half + (at // 2 if at % 2 == 0 else quarter + (at // 2 ^ eighth)) for at in range(half)]
+    far[-2:] = far[:-3:-1]
     order = [(far if kind == "f" else near).pop(0) for kind in "ffnfnfnfnfnfnfn"]
     order.insert(groups - LATE - 1, 0)
     return order

time: 39 us -> 40.1 us (1.028)
  waiting for transfers between devices: 1.08 us -> 2.09 us
    ppermute x15, waiting for transfers between devices: 1.08 us -> 2.09 us  [shards(): lax.ppermute(block, 'pg', [(source, source ^ t) for source in range(group...]
  transfers between devices with their start and end apart: 15 -> 15, of which waited for: 2 -> 1; matrix products, arithmetic and copies ran while one was open for 0% -> 0% of each run, Pallas kernels for 14% -> 13%
where the time goes in v12:
time: 40.1 us; the launch traced here: 39.9 us
  starting transfers between devices  25.6 us (64%)
  Pallas kernels  10.3 us (26%)
  waiting for transfers between devices  2.09 us (5%)
  local copies, waits for them, and re-layouts  1.1 us (3%)
  between operations  0.73 us (2%)
    ppermute x15, starting transfers between devices, shards(): lax.ppermute(block, 'pg', [(source, source ^ t) for source in range(group...  25.6 us
    pallas_call x1, Pallas kernels, attend(): pl.pallas_call(functools.partial(attend_kernel, len(got), requests is not...  3.9 us
    pallas_call x1, Pallas kernels, front(): pl.pallas_call(functools.partial(front_kernel, order), out_shape=[block]...  2.54 us
    pallas_call x1, Pallas kernels, attend_late(): pl.pallas_call(functools.partial(late_kernel, len(got), first), out_shape...  2.52 us
    ppermute x15, waiting for transfers between devices, shards(): lax.ppermute(block, 'pg', [(source, source ^ t) for source in range(group...  2.09 us
    unnamed x6, local copies, waits for them, and re-layouts  1.1 us
    pallas_call x1, Pallas kernels, pack_others(): pl.pallas_call(pack_kernel, out_shape=[jax.ShapeDtypeStruct(block, jnp.bf...  0.86 us
  transfers between devices with their start and end apart: 15, of which 1 were waited for; matrix products, arithmetic and copies ran while one was open for 0% of the time, Pallas kernels for 13%

profile of v12, /device:TPU:0, one launch (start us, length us, event | category | flops | bytes accessed | tf_op | source)
XLA Modules:
  0.0 39.9 jit_solution(17810616782120080915)
XLA Ops:
  0.6 2.5 %front.1 = (bf16[32,1280]{1,0:T(8,128)(2,1)}, bf16[32,1280]{1,0:T(8,128)(2,1)}, bf16[32,1280]{1,0:T(8,128)(2,1)}, bf16[32,1280]{1,0:T(8,128)(2,1)}, f32[1296,128]{1,0:T(8,128)}) custom-call(s32[1]{0:T(128)} %bitcast.me_ref, s32[16]{0:T(128)} %assign_any.1, s32[16]{0:T(128)} %length_any.1, s32[16,16]{1,0:T(8,128)} %owner_any.1, s32[16,16]{1,0:T(8,128)} %stripe_any.1, ...), custom_call_target="tpu_custom_call" | custom-call | tf_op jit(solution)/shard_map/front/pallas_call | solution.py:180
  3.2 4.1 %collective-permute-start = (bf16[32,1280]{1,0:T(8,128)(2,1)}, bf16[32,1280]{1,0:T(8,128)(2,1)S(1)}, u32[]{:S(2)}, u32[]{:S(2)}) collective-permute-start(bf16[32,1280]{1,0:T(8,128)(2,1)} %get-tuple-element.50), channel_id=1, source_target_pairs={{0,8},{1,9},{2,10},{3,11},{4,12},{5,13},{6,14},{7,15},{8,0},{9,1},... | collective-permute-start | bytes 245768 | tf_op jit(solution)/shard_map/ppermute | solution.py:579
  7.3 2.3 %collective-permute-start.1 = (bf16[32,1280]{1,0:T(8,128)(2,1)}, bf16[32,1280]{1,0:T(8,128)(2,1)S(1)}, u32[]{:S(2)}, u32[]{:S(2)}) collective-permute-start(bf16[32,1280]{1,0:T(8,128)(2,1)} %get-tuple-element.51), channel_id=1, source_target_pairs={{0,14},{1,15},{2,12},{3,13},{4,10},{5,11},{6,8},{7,9},{8,6},{9,7},... | collective-permute-start | bytes 245768 | tf_op jit(solution)/shard_map/ppermute | solution.py:579
  9.6 2.7 %collective-permute-start.3 = (bf16[32,1280]{1,0:T(8,128)(2,1)}, bf16[32,1280]{1,0:T(8,128)(2,1)S(1)}, u32[]{:S(2)}, u32[]{:S(2)}) collective-permute-start(bf16[32,1280]{1,0:T(8,128)(2,1)} %get-tuple-element.53), channel_id=1, source_target_pairs={{0,9},{1,8},{2,11},{3,10},{4,13},{5,12},{6,15},{7,14},{8,1},{9,0},... | collective-permute-start | bytes 245768 | tf_op jit(solution)/shard_map/ppermute | solution.py:579
  12.3 1.1 %copy-done.1 = f32[1296,128]{1,0:T(8,128)S(1)} copy-done((f32[1296,128]{1,0:T(8,128)S(1)}, f32[1296,128]{1,0:T(8,128)}, u32[]{:S(2)}) %copy-start.1) | copy-done | bytes 663576
  13.4 0.9 %pack_others.1 = (bf16[32,1280]{1,0:T(8,128)(2,1)S(1)}, bf16[32,1280]{1,0:T(8,128)(2,1)S(1)}, bf16[32,1280]{1,0:T(8,128)(2,1)S(1)}, bf16[32,1280]{1,0:T(8,128)(2...) custom-call(f32[1296,128]{1,0:T(8,128)S(1)} %copy-done.1, ...), custom_call_target="tpu_custom_call" | custom-call | tf_op jit(solution)/shard_map/pack_others/pallas_call | solution.py:229
  14.3 1.7 %collective-permute-start.4 = (bf16[32,1280]{1,0:T(8,128)(2,1)S(1)}, bf16[32,1280]{1,0:T(8,128)(2,1)S(1)}, u32[]{:S(2)}, u32[]{:S(2)}) collective-permute-start(bf16[32,1280]{1,0:T(8,128)(2,1)S(1)} %get-tuple-element.54), channel_id=1, source_target_pairs={{0,6},{1,7},{2,4},{3,5},{4,2},{5,3},{6,0},{7,1},{8,14},{9,15},{10,... | collective-permute-start | bytes 245768 | tf_op jit(solution)/shard_map/ppermute | solution.py:579
  16.0 0.5 %rotate_queries.1 = (bf16[4,1024,128]{2,1,0:T(8,128)(2,1)S(1)}, bf16[8,128,128]{2,1,0:T(8,128)(2,1)S(1)}, f32[8,512]{1,0:T(8,128)S(1)}, s32[8,128]{1,0:T(8,128)S(1)}) custom-call(f32[1296,128]{1,0:T(8,128)S(1)} %copy-done.1, bf16[128,4096]{1,0:T(8,128)(2,1)S(1)} %bitcast.8), custom_call_target="tpu_custom_call" | custom-call | tf_op jit(solution)/shard_map/rotate_queries/pallas_call | solution.py:259
  16.5 1.4 %collective-permute-start.5 = (bf16[32,1280]{1,0:T(8,128)(2,1)S(1)}, bf16[32,1280]{1,0:T(8,128)(2,1)S(1)}, u32[]{:S(2)}, u32[]{:S(2)}) collective-permute-start(bf16[32,1280]{1,0:T(8,128)(2,1)S(1)} %get-tuple-element.55), channel_id=1, source_target_pairs={{0,15},{1,14},{2,13},{3,12},{4,11},{5,10},{6,9},{7,8},{8,7},{9,6},... | collective-permute-start | bytes 245768 | tf_op jit(solution)/shard_map/ppermute | solution.py:579
  17.9 0.0 collective-permute-done.1.refs_1_
  17.9 0.1 collective-permute-start.6
  18.0 0.0 collective-permute-done.2.refs_2_
  18.0 3.6 %collective-permute-start.7 = (bf16[32,1280]{1,0:T(8,128)(2,1)S(1)}, bf16[32,1280]{1,0:T(8,128)(2,1)S(1)}, u32[]{:S(2)}, u32[]{:S(2)}) collective-permute-start(bf16[32,1280]{1,0:T(8,128)(2,1)S(1)} %get-tuple-element.57), channel_id=1, source_target_pairs={{0,10},{1,11},{2,8},{3,9},{4,14},{5,15},{6,12},{7,13},{8,2},{9,3},... | collective-permute-start | bytes 245768 | tf_op jit(solution)/shard_map/ppermute | solution.py:579
  21.7 0.7 %collective-permute-start.8 = (bf16[32,1280]{1,0:T(8,128)(2,1)S(1)}, bf16[32,1280]{1,0:T(8,128)(2,1)S(1)}, u32[]{:S(2)}, u32[]{:S(2)}) collective-permute-start(bf16[32,1280]{1,0:T(8,128)(2,1)S(1)} %get-tuple-element.58), channel_id=1, source_target_pairs={{0,4},{1,5},{2,6},{3,7},{4,0},{5,1},{6,2},{7,3},{8,12},{9,13},{10,... | collective-permute-start | bytes 245768 | tf_op jit(solution)/shard_map/ppermute | solution.py:579
  22.4 1.3 %collective-permute-start.9 = (bf16[32,1280]{1,0:T(8,128)(2,1)S(1)}, bf16[32,1280]{1,0:T(8,128)(2,1)S(1)}, u32[]{:S(2)}, u32[]{:S(2)}) collective-permute-start(bf16[32,1280]{1,0:T(8,128)(2,1)S(1)} %get-tuple-element.59), channel_id=1, source_target_pairs={{0,12},{1,13},{2,14},{3,15},{4,8},{5,9},{6,10},{7,11},{8,4},{9,5},... | collective-permute-start | bytes 245768 | tf_op jit(solution)/shard_map/ppermute | solution.py:579
  23.7 2.0 %collective-permute-start.10 = (bf16[32,1280]{1,0:T(8,128)(2,1)S(1)}, bf16[32,1280]{1,0:T(8,128)(2,1)S(1)}, u32[]{:S(2)}, u32[]{:S(2)}) collective-permute-start(bf16[32,1280]{1,0:T(8,128)(2,1)S(1)} %get-tuple-element.60), channel_id=1, source_target_pairs={{0,3},{1,2},{2,1},{3,0},{4,7},{5,6},{6,5},{7,4},{8,11},{9,10},{10,... | collective-permute-start | bytes 245768 | tf_op jit(solution)/shard_map/ppermute | solution.py:579
  25.7 2.7 %collective-permute-start.11 = (bf16[32,1280]{1,0:T(8,128)(2,1)S(1)}, bf16[32,1280]{1,0:T(8,128)(2,1)S(1)}, u32[]{:S(2)}, u32[]{:S(2)}) collective-permute-start(bf16[32,1280]{1,0:T(8,128)(2,1)S(1)} %get-tuple-element.65), channel_id=1, source_target_pairs={{0,13},{1,12},{2,15},{3,14},{4,9},{5,8},{6,11},{7,10},{8,5},{9,4},... | collective-permute-start | bytes 245768 | tf_op jit(solution)/shard_map/ppermute | solution.py:579
  28.4 0.0 collective-permute-done.7.refs_7_
  28.4 0.0 collective-permute-start.12
  28.4 0.8 %collective-permute-start.13 = (bf16[32,1280]{1,0:T(8,128)(2,1)S(1)}, bf16[32,1280]{1,0:T(8,128)(2,1)S(1)}, u32[]{:S(2)}, u32[]{:S(2)}) collective-permute-start(bf16[32,1280]{1,0:T(8,128)(2,1)S(1)} %get-tuple-element.67), channel_id=1, source_target_pairs={{0,11},{1,10},{2,9},{3,8},{4,15},{5,14},{6,13},{7,12},{8,3},{9,2},... | collective-permute-start | bytes 245768 | tf_op jit(solution)/shard_map/ppermute | solution.py:579
  29.2 2.1 %collective-permute-done.9.refs_9_ = bf16[32,1280]{1,0:T(8,128)(2,1)S(1)} collective-permute-done((bf16[32,1280]{1,0:T(8,128)(2,1)S(1)}, bf16[32,1280]{1,0:T(8,128)(2,1)S(1)}, u32[]{:S(2)}, u32[]{:S(2)}) %collective-permute-start.9) | collective-permute-done | bytes 81952 | tf_op jit(solution)/shard_map/ppermute | solution.py:579
  31.3 2.1 %collective-permute-start.14 = (bf16[32,1280]{1,0:T(8,128)(2,1)S(1)}, bf16[32,1280]{1,0:T(8,128)(2,1)S(1)}, u32[]{:S(2)}, u32[]{:S(2)}) collective-permute-start(bf16[32,1280]{1,0:T(8,128)(2,1)S(1)} %get-tuple-element.68), channel_id=1, source_target_pairs={{0,1},{1,0},{2,3},{3,2},{4,5},{5,4},{6,7},{7,6},{8,9},{9,8},{10,11... | collective-permute-start | bytes 245768 | tf_op jit(solution)/shard_map/ppermute | solution.py:579
  33.4 3.9 %attend.1 = (f32[4,1024,128]{2,1,0:T(8,128)S(1)}, f32[4,1024,128]{2,1,0:T(8,128)S(1)}, bf16[16,8,1024]{2,1,0:T(8,128)(2,1)}) custom-call(bf16[4,1024,128]{2,1,0:T(8,128)(2,1)S(1)} %get-tuple-element.47.rot_ref, f32[8,512]{1,0:T(8,128)S(1)} %get-tuple-element.48.bias_ref, bf16[8,128,128]{2,1,0:T(8,128)(2,1)S(1)} %get-tuple-element.49.own_ref, ...), custom_call_target="tpu_custom_call" | custom-call | tf_op jit(solution)/shard_map/attend/pallas_call | solution.py:402
  37.3 2.5 %attend_late.1 = (bf16[128,4096]{1,0:T(8,128)(2,1)}, bf16[16,8,1024]{2,1,0:T(8,128)(2,1)}) custom-call(bf16[4,1024,128]{2,1,0:T(8,128)(2,1)S(1)} %get-tuple-element.47.rot_ref, f32[8,512]{1,0:T(8,128)S(1)} %get-tuple-element.48.bias_ref, f32[4,1024,128]{2,1,0:T(8,128)S(1)} %get-tuple-element.63.result_ref, ...), custom_call_target="tpu_custom_call", output_to_operand_aliasing={{1}: (9, {})} | custom-call | tf_op jit(solution)/shard_map/attend_late/pallas_call | solution.py:502
  (17 shorter events, 0.0 us)
Async XLA Ops:
  0.6 11.7 %copy-start = (bf16[1,16,32,1024]{3,2,1,0:T(8,128)(2,1)S(1)}, bf16[1,16,32,1024]{3,2,1,0:T(8,128)(2,1)}, u32[]{:S(2)}) copy-start(bf16[1,16,32,1024]{3,2,1,0:T(8,128)(2,1)} %param.10) | copy-start | bytes 3145732
  3.2 13.3 %collective-permute-start = (bf16[32,1280]{1,0:T(8,128)(2,1)}, bf16[32,1280]{1,0:T(8,128)(2,1)S(1)}, u32[]{:S(2)}, u32[]{:S(2)}) collective-permute-start(bf16[32,1280]{1,0:T(8,128)(2,1)} %get-tuple-element.50), channel_id=1, source_target_pairs={{0,8},{1,9},{2,10},{3,11},{4,12},{5,13},{6,14},{7,15},{8,0},{9,1},... | collective-permute-start | bytes 245768 | tf_op jit(solution)/shard_map/ppermute | solution.py:579
  7.3 10.6 %collective-permute-start.1 = (bf16[32,1280]{1,0:T(8,128)(2,1)}, bf16[32,1280]{1,0:T(8,128)(2,1)S(1)}, u32[]{:S(2)}, u32[]{:S(2)}) collective-permute-start(bf16[32,1280]{1,0:T(8,128)(2,1)} %get-tuple-element.51), channel_id=1, source_target_pairs={{0,14},{1,15},{2,12},{3,13},{4,10},{5,11},{6,8},{7,9},{8,6},{9,7},... | collective-permute-start | bytes 245768 | tf_op jit(solution)/shard_map/ppermute | solution.py:579
  9.6 8.4 %collective-permute-start.2 = (bf16[32,1280]{1,0:T(8,128)(2,1)}, bf16[32,1280]{1,0:T(8,128)(2,1)S(1)}, u32[]{:S(2)}, u32[]{:S(2)}) collective-permute-start(bf16[32,1280]{1,0:T(8,128)(2,1)} %get-tuple-element.52), channel_id=1, source_target_pairs={{0,7},{1,6},{2,5},{3,4},{4,3},{5,2},{6,1},{7,0},{8,15},{9,14},{10,... | collective-permute-start | bytes 245768 | tf_op jit(solution)/shard_map/ppermute | solution.py:579
  9.6 12.1 %collective-permute-start.3 = (bf16[32,1280]{1,0:T(8,128)(2,1)}, bf16[32,1280]{1,0:T(8,128)(2,1)S(1)}, u32[]{:S(2)}, u32[]{:S(2)}) collective-permute-start(bf16[32,1280]{1,0:T(8,128)(2,1)} %get-tuple-element.53), channel_id=1, source_target_pairs={{0,9},{1,8},{2,11},{3,10},{4,13},{5,12},{6,15},{7,14},{8,1},{9,0},... | collective-permute-start | bytes 245768 | tf_op jit(solution)/shard_map/ppermute | solution.py:579
  12.3 1.1 %copy-start.1 = (f32[1296,128]{1,0:T(8,128)S(1)}, f32[1296,128]{1,0:T(8,128)}, u32[]{:S(2)}) copy-start(f32[1296,128]{1,0:T(8,128)} %get-tuple-element.37.info_ref) | copy-start | bytes 1990660
  13.4 2.6 %copy-start.2 = (bf16[1,128,4096]{2,1,0:T(8,128)(2,1)S(1)}, bf16[1,128,4096]{2,1,0:T(8,128)(2,1)}, u32[]{:S(2)}) copy-start(bf16[1,128,4096]{2,1,0:T(8,128)(2,1)} %param.8) | copy-start | bytes 3145732
  14.3 8.1 %collective-permute-start.4 = (bf16[32,1280]{1,0:T(8,128)(2,1)S(1)}, bf16[32,1280]{1,0:T(8,128)(2,1)S(1)}, u32[]{:S(2)}, u32[]{:S(2)}) collective-permute-start(bf16[32,1280]{1,0:T(8,128)(2,1)S(1)} %get-tuple-element.54), channel_id=1, source_target_pairs={{0,6},{1,7},{2,4},{3,5},{4,2},{5,3},{6,0},{7,1},{8,14},{9,15},{10,... | collective-permute-start | bytes 245768 | tf_op jit(solution)/shard_map/ppermute | solution.py:579
  16.5 7.2 %collective-permute-start.5 = (bf16[32,1280]{1,0:T(8,128)(2,1)S(1)}, bf16[32,1280]{1,0:T(8,128)(2,1)S(1)}, u32[]{:S(2)}, u32[]{:S(2)}) collective-permute-start(bf16[32,1280]{1,0:T(8,128)(2,1)S(1)} %get-tuple-element.55), channel_id=1, source_target_pairs={{0,15},{1,14},{2,13},{3,12},{4,11},{5,10},{6,9},{7,8},{8,7},{9,6},... | collective-permute-start | bytes 245768 | tf_op jit(solution)/shard_map/ppermute | solution.py:579
  17.9 7.8 %collective-permute-start.6 = (bf16[32,1280]{1,0:T(8,128)(2,1)S(1)}, bf16[32,1280]{1,0:T(8,128)(2,1)S(1)}, u32[]{:S(2)}, u32[]{:S(2)}) collective-permute-start(bf16[32,1280]{1,0:T(8,128)(2,1)S(1)} %get-tuple-element.56), channel_id=1, source_target_pairs={{0,5},{1,4},{2,7},{3,6},{4,1},{5,0},{6,3},{7,2},{8,13},{9,12},{10,... | collective-permute-start | bytes 245768 | tf_op jit(solution)/shard_map/ppermute | solution.py:579
  18.0 10.4 %collective-permute-start.7 = (bf16[32,1280]{1,0:T(8,128)(2,1)S(1)}, bf16[32,1280]{1,0:T(8,128)(2,1)S(1)}, u32[]{:S(2)}, u32[]{:S(2)}) collective-permute-start(bf16[32,1280]{1,0:T(8,128)(2,1)S(1)} %get-tuple-element.57), channel_id=1, source_target_pairs={{0,10},{1,11},{2,8},{3,9},{4,14},{5,15},{6,12},{7,13},{8,2},{9,3},... | collective-permute-start | bytes 245768 | tf_op jit(solution)/shard_map/ppermute | solution.py:579
  21.7 6.7 %collective-permute-start.8 = (bf16[32,1280]{1,0:T(8,128)(2,1)S(1)}, bf16[32,1280]{1,0:T(8,128)(2,1)S(1)}, u32[]{:S(2)}, u32[]{:S(2)}) collective-permute-start(bf16[32,1280]{1,0:T(8,128)(2,1)S(1)} %get-tuple-element.58), channel_id=1, source_target_pairs={{0,4},{1,5},{2,6},{3,7},{4,0},{5,1},{6,2},{7,3},{8,12},{9,13},{10,... | collective-permute-start | bytes 245768 | tf_op jit(solution)/shard_map/ppermute | solution.py:579
  22.4 8.9 %collective-permute-start.9 = (bf16[32,1280]{1,0:T(8,128)(2,1)S(1)}, bf16[32,1280]{1,0:T(8,128)(2,1)S(1)}, u32[]{:S(2)}, u32[]{:S(2)}) collective-permute-start(bf16[32,1280]{1,0:T(8,128)(2,1)S(1)} %get-tuple-element.59), channel_id=1, source_target_pairs={{0,12},{1,13},{2,14},{3,15},{4,8},{5,9},{6,10},{7,11},{8,4},{9,5},... | collective-permute-start | bytes 245768 | tf_op jit(solution)/shard_map/ppermute | solution.py:579
  23.7 9.7 %collective-permute-start.10 = (bf16[32,1280]{1,0:T(8,128)(2,1)S(1)}, bf16[32,1280]{1,0:T(8,128)(2,1)S(1)}, u32[]{:S(2)}, u32[]{:S(2)}) collective-permute-start(bf16[32,1280]{1,0:T(8,128)(2,1)S(1)} %get-tuple-element.60), channel_id=1, source_target_pairs={{0,3},{1,2},{2,1},{3,0},{4,7},{5,6},{6,5},{7,4},{8,11},{9,10},{10,... | collective-permute-start | bytes 245768 | tf_op jit(solution)/shard_map/ppermute | solution.py:579
  25.7 11.6 %collective-permute-start.11 = (bf16[32,1280]{1,0:T(8,128)(2,1)S(1)}, bf16[32,1280]{1,0:T(8,128)(2,1)S(1)}, u32[]{:S(2)}, u32[]{:S(2)}) collective-permute-start(bf16[32,1280]{1,0:T(8,128)(2,1)S(1)} %get-tuple-element.65), channel_id=1, source_target_pairs={{0,13},{1,12},{2,15},{3,14},{4,9},{5,8},{6,11},{7,10},{8,5},{9,4},... | collective-permute-start | bytes 245768 | tf_op jit(solution)/shard_map/ppermute | solution.py:579
  28.4 8.9 %collective-permute-start.12 = (bf16[32,1280]{1,0:T(8,128)(2,1)S(1)}, bf16[32,1280]{1,0:T(8,128)(2,1)S(1)}, u32[]{:S(2)}, u32[]{:S(2)}) collective-permute-start(bf16[32,1280]{1,0:T(8,128)(2,1)S(1)} %get-tuple-element.66), channel_id=1, source_target_pairs={{0,2},{1,3},{2,0},{3,1},{4,6},{5,7},{6,4},{7,5},{8,10},{9,11},{10,... | collective-permute-start | bytes 245768 | tf_op jit(solution)/shard_map/ppermute | solution.py:579
  28.4 8.9 %collective-permute-start.13 = (bf16[32,1280]{1,0:T(8,128)(2,1)S(1)}, bf16[32,1280]{1,0:T(8,128)(2,1)S(1)}, u32[]{:S(2)}, u32[]{:S(2)}) collective-permute-start(bf16[32,1280]{1,0:T(8,128)(2,1)S(1)} %get-tuple-element.67), channel_id=1, source_target_pairs={{0,11},{1,10},{2,9},{3,8},{4,15},{5,14},{6,13},{7,12},{8,3},{9,2},... | collective-permute-start | bytes 245768 | tf_op jit(solution)/shard_map/ppermute | solution.py:579
  31.3 6.1 %collective-permute-start.14 = (bf16[32,1280]{1,0:T(8,128)(2,1)S(1)}, bf16[32,1280]{1,0:T(8,128)(2,1)S(1)}, u32[]{:S(2)}, u32[]{:S(2)}) collective-permute-start(bf16[32,1280]{1,0:T(8,128)(2,1)S(1)} %get-tuple-element.68), channel_id=1, source_target_pairs={{0,1},{1,0},{2,3},{3,2},{4,5},{5,4},{6,7},{7,6},{8,9},{9,8},{10,11... | collective-permute-start | bytes 245768 | tf_op jit(solution)/shard_map/ppermute | solution.py:579

commit v13 on v8

--- a/solution.py
+++ b/solution.py
@@ -22,7 +22,7 @@
 CHUNK = 256
 LATE = 4
 LATE_CHUNK = 512
-AHEAD = 4
+AHEAD = 5
 AHEAD_OF_QUERIES = 8
 
 SMEM = pl.BlockSpec(memory_space=pltpu.SMEM)

time: 39 us -> 39.2 us (level)
  starting transfers between devices: 25.6 us -> 24 us
  waiting for transfers between devices: 1.08 us -> 2.4 us
    ppermute x15, starting transfers between devices: 25.6 us -> 24 us  [shards(): lax.ppermute(block, 'pg', [(source, source ^ t) for source in range(group...]
    ppermute x15, waiting for transfers between devices: 1.08 us -> 2.4 us  [shards(): lax.ppermute(block, 'pg', [(source, source ^ t) for source in range(group...]
  transfers between devices with their start and end apart: 15 -> 15, of which waited for: 2 -> 4; matrix products, arithmetic and copies ran while one was open for 0% -> 0% of each run, Pallas kernels for 14% -> 14%
where the time goes in v13:
time: 39.2 us; the launch traced here: 38.9 us
  starting transfers between devices  24 us (61%)
  Pallas kernels  10.3 us (26%)
  waiting for transfers between devices  2.4 us (6%)
  local copies, waits for them, and re-layouts  1.46 us (4%)
  between operations  0.7 us (2%)
    ppermute x15, starting transfers between devices, shards(): lax.ppermute(block, 'pg', [(source, source ^ t) for source in range(group...  24 us
    pallas_call x1, Pallas kernels, attend(): pl.pallas_call(functools.partial(attend_kernel, len(got), requests is not...  3.89 us
    pallas_call x1, Pallas kernels, front(): pl.pallas_call(functools.partial(front_kernel, order), out_shape=[block]...  2.57 us
    pallas_call x1, Pallas kernels, attend_late(): pl.pallas_call(functools.partial(late_kernel, len(got), first), out_shape...  2.52 us
    ppermute x15, waiting for transfers between devices, shards(): lax.ppermute(block, 'pg', [(source, source ^ t) for source in range(group...  2.4 us
    unnamed x6, local copies, waits for them, and re-layouts  1.46 us
    pallas_call x1, Pallas kernels, pack_others(): pl.pallas_call(pack_kernel, out_shape=[jax.ShapeDtypeStruct(block, jnp.bf...  0.85 us
  transfers between devices with their start and end apart: 15, of which 4 were waited for; matrix products, arithmetic and copies ran while one was open for 0% of the time, Pallas kernels for 14%

profile of v13, /device:TPU:0, one launch (start us, length us, event | category | flops | bytes accessed | tf_op | source)
XLA Modules:
  0.0 38.9 jit_solution(8181038598990161951)
XLA Ops:
  0.6 2.6 %front.1 = (bf16[32,1280]{1,0:T(8,128)(2,1)}, bf16[32,1280]{1,0:T(8,128)(2,1)}, bf16[32,1280]{1,0:T(8,128)(2,1)}, bf16[32,1280]{1,0:T(8,128)(2,1)}, bf16[32,1280]{1,0:T(8,128)(2,1)}, /*index=5*/f32[1296,128]{1,0:T(8,128)}) custom-call(s32[1]{0:T(128)} %bitcast.me_ref, s32[16]{0:T(128)} %assign_any.1, s32[16]{0:T(128)} %length_any.1, s32[16,16]{1,0:T(8,128)} %owner_any.1, ...), custom_call_target="tpu_custom_call" | custom-call | tf_op jit(solution)/shard_map/front/pallas_call | solution.py:179
  3.2 4.1 %collective-permute-start = (bf16[32,1280]{1,0:T(8,128)(2,1)}, bf16[32,1280]{1,0:T(8,128)(2,1)S(1)}, u32[]{:S(2)}, u32[]{:S(2)}) collective-permute-start(bf16[32,1280]{1,0:T(8,128)(2,1)} %get-tuple-element.50), channel_id=1, source_target_pairs={{0,8},{1,9},{2,10},{3,11},{4,12},{5,13},{6,14},{7,15},{8,0},{9,1},... | collective-permute-start | bytes 245768 | tf_op jit(solution)/shard_map/ppermute | solution.py:578
  7.3 2.3 %collective-permute-start.1 = (bf16[32,1280]{1,0:T(8,128)(2,1)}, bf16[32,1280]{1,0:T(8,128)(2,1)S(1)}, u32[]{:S(2)}, u32[]{:S(2)}) collective-permute-start(bf16[32,1280]{1,0:T(8,128)(2,1)} %get-tuple-element.51), channel_id=1, source_target_pairs={{0,14},{1,15},{2,12},{3,13},{4,10},{5,11},{6,8},{7,9},{8,6},{9,7},... | collective-permute-start | bytes 245768 | tf_op jit(solution)/shard_map/ppermute | solution.py:578
  9.6 2.7 %collective-permute-start.3 = (bf16[32,1280]{1,0:T(8,128)(2,1)}, bf16[32,1280]{1,0:T(8,128)(2,1)S(1)}, u32[]{:S(2)}, u32[]{:S(2)}) collective-permute-start(bf16[32,1280]{1,0:T(8,128)(2,1)} %get-tuple-element.53), channel_id=1, source_target_pairs={{0,9},{1,8},{2,11},{3,10},{4,13},{5,12},{6,15},{7,14},{8,1},{9,0},... | collective-permute-start | bytes 245768 | tf_op jit(solution)/shard_map/ppermute | solution.py:578
  12.3 1.6 %collective-permute-start.4 = (bf16[32,1280]{1,0:T(8,128)(2,1)}, bf16[32,1280]{1,0:T(8,128)(2,1)S(1)}, u32[]{:S(2)}, u32[]{:S(2)}) collective-permute-start(bf16[32,1280]{1,0:T(8,128)(2,1)} %get-tuple-element.54), channel_id=1, source_target_pairs={{0,6},{1,7},{2,4},{3,5},{4,2},{5,3},{6,0},{7,1},{8,14},{9,15},{10,... | collective-permute-start | bytes 245768 | tf_op jit(solution)/shard_map/ppermute | solution.py:578
  14.0 1.1 %copy-done.1 = f32[1296,128]{1,0:T(8,128)S(1)} copy-done((f32[1296,128]{1,0:T(8,128)S(1)}, f32[1296,128]{1,0:T(8,128)}, u32[]{:S(2)}) %copy-start.1) | copy-done | bytes 663576
  15.1 0.8 %pack_others.1 = (bf16[32,1280]{1,0:T(8,128)(2,1)S(1)}, bf16[32,1280]{1,0:T(8,128)(2,1)S(1)}, bf16[32,1280]{1,0:T(8,128)(2,1)S(1)}, bf16[32,1280]{1,0:T(8,128)(2...) custom-call(f32[1296,128]{1,0:T(8,128)S(1)} %copy-done.1, ...), custom_call_target="tpu_custom_call" | custom-call | tf_op jit(solution)/shard_map/pack_others/pallas_call | solution.py:228
  15.9 0.4 copy-done.2
  16.3 0.5 %rotate_queries.1 = (bf16[4,1024,128]{2,1,0:T(8,128)(2,1)S(1)}, bf16[8,128,128]{2,1,0:T(8,128)(2,1)S(1)}, f32[8,512]{1,0:T(8,128)S(1)}, s32[8,128]{1,0:T(8,128)S(1)}) custom-call(f32[1296,128]{1,0:T(8,128)S(1)} %copy-done.1, bf16[128,4096]{1,0:T(8,128)(2,1)S(1)} %bitcast.8), custom_call_target="tpu_custom_call" | custom-call | tf_op jit(solution)/shard_map/rotate_queries/pallas_call | solution.py:258
  16.8 1.1 %collective-permute-start.5 = (bf16[32,1280]{1,0:T(8,128)(2,1)S(1)}, bf16[32,1280]{1,0:T(8,128)(2,1)S(1)}, u32[]{:S(2)}, u32[]{:S(2)}) collective-permute-start(bf16[32,1280]{1,0:T(8,128)(2,1)S(1)} %get-tuple-element.55), channel_id=1, source_target_pairs={{0,15},{1,14},{2,13},{3,12},{4,11},{5,10},{6,9},{7,8},{8,7},{9,6},... | collective-permute-start | bytes 245768 | tf_op jit(solution)/shard_map/ppermute | solution.py:578
  17.9 0.4 %collective-permute-start.6 = (bf16[32,1280]{1,0:T(8,128)(2,1)S(1)}, bf16[32,1280]{1,0:T(8,128)(2,1)S(1)}, u32[]{:S(2)}, u32[]{:S(2)}) collective-permute-start(bf16[32,1280]{1,0:T(8,128)(2,1)S(1)} %get-tuple-element.56), channel_id=1, source_target_pairs={{0,5},{1,4},{2,7},{3,6},{4,1},{5,0},{6,3},{7,2},{8,13},{9,12},{10,... | collective-permute-start | bytes 245768 | tf_op jit(solution)/shard_map/ppermute | solution.py:578
  18.3 3.5 %collective-permute-start.7 = (bf16[32,1280]{1,0:T(8,128)(2,1)S(1)}, bf16[32,1280]{1,0:T(8,128)(2,1)S(1)}, u32[]{:S(2)}, u32[]{:S(2)}) collective-permute-start(bf16[32,1280]{1,0:T(8,128)(2,1)S(1)} %get-tuple-element.57), channel_id=1, source_target_pairs={{0,10},{1,11},{2,8},{3,9},{4,14},{5,15},{6,12},{7,13},{8,2},{9,3},... | collective-permute-start | bytes 245768 | tf_op jit(solution)/shard_map/ppermute | solution.py:578
  21.9 0.5 %collective-permute-start.8 = (bf16[32,1280]{1,0:T(8,128)(2,1)S(1)}, bf16[32,1280]{1,0:T(8,128)(2,1)S(1)}, u32[]{:S(2)}, u32[]{:S(2)}) collective-permute-start(bf16[32,1280]{1,0:T(8,128)(2,1)S(1)} %get-tuple-element.58), channel_id=1, source_target_pairs={{0,4},{1,5},{2,6},{3,7},{4,0},{5,1},{6,2},{7,3},{8,12},{9,13},{10,... | collective-permute-start | bytes 245768 | tf_op jit(solution)/shard_map/ppermute | solution.py:578
  22.3 1.3 %collective-permute-start.9 = (bf16[32,1280]{1,0:T(8,128)(2,1)S(1)}, bf16[32,1280]{1,0:T(8,128)(2,1)S(1)}, u32[]{:S(2)}, u32[]{:S(2)}) collective-permute-start(bf16[32,1280]{1,0:T(8,128)(2,1)S(1)} %get-tuple-element.59), channel_id=1, source_target_pairs={{0,12},{1,13},{2,14},{3,15},{4,8},{5,9},{6,10},{7,11},{8,4},{9,5},... | collective-permute-start | bytes 245768 | tf_op jit(solution)/shard_map/ppermute | solution.py:578
  23.8 0.8 %collective-permute-start.10 = (bf16[32,1280]{1,0:T(8,128)(2,1)S(1)}, bf16[32,1280]{1,0:T(8,128)(2,1)S(1)}, u32[]{:S(2)}, u32[]{:S(2)}) collective-permute-start(bf16[32,1280]{1,0:T(8,128)(2,1)S(1)} %get-tuple-element.60), channel_id=1, source_target_pairs={{0,3},{1,2},{2,1},{3,0},{4,7},{5,6},{6,5},{7,4},{8,11},{9,10},{10,... | collective-permute-start | bytes 245768 | tf_op jit(solution)/shard_map/ppermute | solution.py:578
  24.6 1.0 %collective-permute-done.6.refs_6_ = bf16[32,1280]{1,0:T(8,128)(2,1)S(1)} collective-permute-done((bf16[32,1280]{1,0:T(8,128)(2,1)S(1)}, bf16[32,1280]{1,0:T(8,128)(2,1)S(1)}, u32[]{:S(2)}, u32[]{:S(2)}) %collective-permute-start.6) | collective-permute-done | bytes 81952 | tf_op jit(solution)/shard_map/ppermute | solution.py:578
  25.6 1.4 %collective-permute-start.11 = (bf16[32,1280]{1,0:T(8,128)(2,1)S(1)}, bf16[32,1280]{1,0:T(8,128)(2,1)S(1)}, u32[]{:S(2)}, u32[]{:S(2)}) collective-permute-start(bf16[32,1280]{1,0:T(8,128)(2,1)S(1)} %get-tuple-element.65), channel_id=1, source_target_pairs={{0,11},{1,10},{2,9},{3,8},{4,15},{5,14},{6,13},{7,12},{8,3},{9,2},... | collective-permute-start | bytes 245768 | tf_op jit(solution)/shard_map/ppermute | solution.py:578
  27.1 1.0 %collective-permute-start.12 = (bf16[32,1280]{1,0:T(8,128)(2,1)S(1)}, bf16[32,1280]{1,0:T(8,128)(2,1)S(1)}, u32[]{:S(2)}, u32[]{:S(2)}) collective-permute-start(bf16[32,1280]{1,0:T(8,128)(2,1)S(1)} %get-tuple-element.66), channel_id=1, source_target_pairs={{0,2},{1,3},{2,0},{3,1},{4,6},{5,7},{6,4},{7,5},{8,10},{9,11},{10,... | collective-permute-start | bytes 245768 | tf_op jit(solution)/shard_map/ppermute | solution.py:578
  28.0 2.4 %collective-permute-start.13 = (bf16[32,1280]{1,0:T(8,128)(2,1)S(1)}, bf16[32,1280]{1,0:T(8,128)(2,1)S(1)}, u32[]{:S(2)}, u32[]{:S(2)}) collective-permute-start(bf16[32,1280]{1,0:T(8,128)(2,1)S(1)} %get-tuple-element.67), channel_id=1, source_target_pairs={{0,13},{1,12},{2,15},{3,14},{4,9},{5,8},{6,11},{7,10},{8,5},{9,4},... | collective-permute-start | bytes 245768 | tf_op jit(solution)/shard_map/ppermute | solution.py:578
  30.5 0.2 collective-permute-done.9.refs_9_
  30.7 0.8 %collective-permute-start.14 = (bf16[32,1280]{1,0:T(8,128)(2,1)S(1)}, bf16[32,1280]{1,0:T(8,128)(2,1)S(1)}, u32[]{:S(2)}, u32[]{:S(2)}) collective-permute-start(bf16[32,1280]{1,0:T(8,128)(2,1)S(1)} %get-tuple-element.68), channel_id=1, source_target_pairs={{0,1},{1,0},{2,3},{3,2},{4,5},{5,4},{6,7},{7,6},{8,9},{9,8},{10,11... | collective-permute-start | bytes 245768 | tf_op jit(solution)/shard_map/ppermute | solution.py:578
  31.5 3.9 %attend.1 = (f32[4,1024,128]{2,1,0:T(8,128)S(1)}, f32[4,1024,128]{2,1,0:T(8,128)S(1)}, bf16[16,8,1024]{2,1,0:T(8,128)(2,1)}) custom-call(bf16[4,1024,128]{2,1,0:T(8,128)(2,1)S(1)} %get-tuple-element.47.rot_ref, f32[8,512]{1,0:T(8,128)S(1)} %get-tuple-element.48.bias_ref, bf16[8,128,128]{2,1,0:T(8,128)(2,1)S(1)} %get-tuple-element.49.own_ref, ...), custom_call_target="tpu_custom_call" | custom-call | tf_op jit(solution)/shard_map/attend/pallas_call | solution.py:401
  35.4 1.0 %collective-permute-done.11.refs_0_ = bf16[32,1280]{1,0:T(8,128)(2,1)S(1)} collective-permute-done((bf16[32,1280]{1,0:T(8,128)(2,1)S(1)}, bf16[32,1280]{1,0:T(8,128)(2,1)S(1)}, u32[]{:S(2)}, u32[]{:S(2)}) %collective-permute-start.11) | collective-permute-done | bytes 81952 | tf_op jit(solution)/shard_map/ppermute | solution.py:578
  36.4 2.5 %attend_late.1 = (bf16[128,4096]{1,0:T(8,128)(2,1)}, bf16[16,8,1024]{2,1,0:T(8,128)(2,1)}) custom-call(bf16[4,1024,128]{2,1,0:T(8,128)(2,1)S(1)} %get-tuple-element.47.rot_ref, f32[8,512]{1,0:T(8,128)S(1)} %get-tuple-element.48.bias_ref, f32[4,1024,128]{2,1,0:T(8,128)S(1)} %get-tuple-element.63.result_ref, ...), custom_call_target="tpu_custom_call", output_to_operand_aliasing={{1}: (9, {})} | custom-call | tf_op jit(solution)/shard_map/attend_late/pallas_call | solution.py:501
  (17 shorter events, 0.2 us)
Async XLA Ops:
  0.6 13.3 %copy-start = (bf16[1,16,32,1024]{3,2,1,0:T(8,128)(2,1)S(1)}, bf16[1,16,32,1024]{3,2,1,0:T(8,128)(2,1)}, u32[]{:S(2)}) copy-start(bf16[1,16,32,1024]{3,2,1,0:T(8,128)(2,1)} %param.10) | copy-start | bytes 3145732
  3.2 13.6 %collective-permute-start = (bf16[32,1280]{1,0:T(8,128)(2,1)}, bf16[32,1280]{1,0:T(8,128)(2,1)S(1)}, u32[]{:S(2)}, u32[]{:S(2)}) collective-permute-start(bf16[32,1280]{1,0:T(8,128)(2,1)} %get-tuple-element.50), channel_id=1, source_target_pairs={{0,8},{1,9},{2,10},{3,11},{4,12},{5,13},{6,14},{7,15},{8,0},{9,1},... | collective-permute-start | bytes 245768 | tf_op jit(solution)/shard_map/ppermute | solution.py:578
  7.3 10.6 %collective-permute-start.1 = (bf16[32,1280]{1,0:T(8,128)(2,1)}, bf16[32,1280]{1,0:T(8,128)(2,1)S(1)}, u32[]{:S(2)}, u32[]{:S(2)}) collective-permute-start(bf16[32,1280]{1,0:T(8,128)(2,1)} %get-tuple-element.51), channel_id=1, source_target_pairs={{0,14},{1,15},{2,12},{3,13},{4,10},{5,11},{6,8},{7,9},{8,6},{9,7},... | collective-permute-start | bytes 245768 | tf_op jit(solution)/shard_map/ppermute | solution.py:578
  9.6 8.7 %collective-permute-start.2 = (bf16[32,1280]{1,0:T(8,128)(2,1)}, bf16[32,1280]{1,0:T(8,128)(2,1)S(1)}, u32[]{:S(2)}, u32[]{:S(2)}) collective-permute-start(bf16[32,1280]{1,0:T(8,128)(2,1)} %get-tuple-element.52), channel_id=1, source_target_pairs={{0,7},{1,6},{2,5},{3,4},{4,3},{5,2},{6,1},{7,0},{8,15},{9,14},{10,... | collective-permute-start | bytes 245768 | tf_op jit(solution)/shard_map/ppermute | solution.py:578
  9.6 12.3 %collective-permute-start.3 = (bf16[32,1280]{1,0:T(8,128)(2,1)}, bf16[32,1280]{1,0:T(8,128)(2,1)S(1)}, u32[]{:S(2)}, u32[]{:S(2)}) collective-permute-start(bf16[32,1280]{1,0:T(8,128)(2,1)} %get-tuple-element.53), channel_id=1, source_target_pairs={{0,9},{1,8},{2,11},{3,10},{4,13},{5,12},{6,15},{7,14},{8,1},{9,0},... | collective-permute-start | bytes 245768 | tf_op jit(solution)/shard_map/ppermute | solution.py:578
  12.3 10.0 %collective-permute-start.4 = (bf16[32,1280]{1,0:T(8,128)(2,1)}, bf16[32,1280]{1,0:T(8,128)(2,1)S(1)}, u32[]{:S(2)}, u32[]{:S(2)}) collective-permute-start(bf16[32,1280]{1,0:T(8,128)(2,1)} %get-tuple-element.54), channel_id=1, source_target_pairs={{0,6},{1,7},{2,4},{3,5},{4,2},{5,3},{6,0},{7,1},{8,14},{9,15},{10,... | collective-permute-start | bytes 245768 | tf_op jit(solution)/shard_map/ppermute | solution.py:578
  14.0 1.1 %copy-start.1 = (f32[1296,128]{1,0:T(8,128)S(1)}, f32[1296,128]{1,0:T(8,128)}, u32[]{:S(2)}) copy-start(f32[1296,128]{1,0:T(8,128)} %get-tuple-element.37.info_ref) | copy-start | bytes 1990660
  15.1 1.2 %copy-start.2 = (bf16[1,128,4096]{2,1,0:T(8,128)(2,1)S(1)}, bf16[1,128,4096]{2,1,0:T(8,128)(2,1)}, u32[]{:S(2)}) copy-start(bf16[1,128,4096]{2,1,0:T(8,128)(2,1)} %param.8) | copy-start | bytes 3145732
  16.8 7.0 %collective-permute-start.5 = (bf16[32,1280]{1,0:T(8,128)(2,1)S(1)}, bf16[32,1280]{1,0:T(8,128)(2,1)S(1)}, u32[]{:S(2)}, u32[]{:S(2)}) collective-permute-start(bf16[32,1280]{1,0:T(8,128)(2,1)S(1)} %get-tuple-element.55), channel_id=1, source_target_pairs={{0,15},{1,14},{2,13},{3,12},{4,11},{5,10},{6,9},{7,8},{8,7},{9,6},... | collective-permute-start | bytes 245768 | tf_op jit(solution)/shard_map/ppermute | solution.py:578
  17.9 7.7 %collective-permute-start.6 = (bf16[32,1280]{1,0:T(8,128)(2,1)S(1)}, bf16[32,1280]{1,0:T(8,128)(2,1)S(1)}, u32[]{:S(2)}, u32[]{:S(2)}) collective-permute-start(bf16[32,1280]{1,0:T(8,128)(2,1)S(1)} %get-tuple-element.56), channel_id=1, source_target_pairs={{0,5},{1,4},{2,7},{3,6},{4,1},{5,0},{6,3},{7,2},{8,13},{9,12},{10,... | collective-permute-start | bytes 245768 | tf_op jit(solution)/shard_map/ppermute | solution.py:578
  18.3 8.7 %collective-permute-start.7 = (bf16[32,1280]{1,0:T(8,128)(2,1)S(1)}, bf16[32,1280]{1,0:T(8,128)(2,1)S(1)}, u32[]{:S(2)}, u32[]{:S(2)}) collective-permute-start(bf16[32,1280]{1,0:T(8,128)(2,1)S(1)} %get-tuple-element.57), channel_id=1, source_target_pairs={{0,10},{1,11},{2,8},{3,9},{4,14},{5,15},{6,12},{7,13},{8,2},{9,3},... | collective-permute-start | bytes 245768 | tf_op jit(solution)/shard_map/ppermute | solution.py:578
  21.9 6.2 %collective-permute-start.8 = (bf16[32,1280]{1,0:T(8,128)(2,1)S(1)}, bf16[32,1280]{1,0:T(8,128)(2,1)S(1)}, u32[]{:S(2)}, u32[]{:S(2)}) collective-permute-start(bf16[32,1280]{1,0:T(8,128)(2,1)S(1)} %get-tuple-element.58), channel_id=1, source_target_pairs={{0,4},{1,5},{2,6},{3,7},{4,0},{5,1},{6,2},{7,3},{8,12},{9,13},{10,... | collective-permute-start | bytes 245768 | tf_op jit(solution)/shard_map/ppermute | solution.py:578
  22.3 8.4 %collective-permute-start.9 = (bf16[32,1280]{1,0:T(8,128)(2,1)S(1)}, bf16[32,1280]{1,0:T(8,128)(2,1)S(1)}, u32[]{:S(2)}, u32[]{:S(2)}) collective-permute-start(bf16[32,1280]{1,0:T(8,128)(2,1)S(1)} %get-tuple-element.59), channel_id=1, source_target_pairs={{0,12},{1,13},{2,14},{3,15},{4,8},{5,9},{6,10},{7,11},{8,4},{9,5},... | collective-permute-start | bytes 245768 | tf_op jit(solution)/shard_map/ppermute | solution.py:578
  23.8 7.7 %collective-permute-start.10 = (bf16[32,1280]{1,0:T(8,128)(2,1)S(1)}, bf16[32,1280]{1,0:T(8,128)(2,1)S(1)}, u32[]{:S(2)}, u32[]{:S(2)}) collective-permute-start(bf16[32,1280]{1,0:T(8,128)(2,1)S(1)} %get-tuple-element.60), channel_id=1, source_target_pairs={{0,3},{1,2},{2,1},{3,0},{4,7},{5,6},{6,5},{7,4},{8,11},{9,10},{10,... | collective-permute-start | bytes 245768 | tf_op jit(solution)/shard_map/ppermute | solution.py:578
  25.6 10.8 %collective-permute-start.11 = (bf16[32,1280]{1,0:T(8,128)(2,1)S(1)}, bf16[32,1280]{1,0:T(8,128)(2,1)S(1)}, u32[]{:S(2)}, u32[]{:S(2)}) collective-permute-start(bf16[32,1280]{1,0:T(8,128)(2,1)S(1)} %get-tuple-element.65), channel_id=1, source_target_pairs={{0,11},{1,10},{2,9},{3,8},{4,15},{5,14},{6,13},{7,12},{8,3},{9,2},... | collective-permute-start | bytes 245768 | tf_op jit(solution)/shard_map/ppermute | solution.py:578
  27.1 9.3 %collective-permute-start.12 = (bf16[32,1280]{1,0:T(8,128)(2,1)S(1)}, bf16[32,1280]{1,0:T(8,128)(2,1)S(1)}, u32[]{:S(2)}, u32[]{:S(2)}) collective-permute-start(bf16[32,1280]{1,0:T(8,128)(2,1)S(1)} %get-tuple-element.66), channel_id=1, source_target_pairs={{0,2},{1,3},{2,0},{3,1},{4,6},{5,7},{6,4},{7,5},{8,10},{9,11},{10,... | collective-permute-start | bytes 245768 | tf_op jit(solution)/shard_map/ppermute | solution.py:578
  28.0 8.3 %collective-permute-start.13 = (bf16[32,1280]{1,0:T(8,128)(2,1)S(1)}, bf16[32,1280]{1,0:T(8,128)(2,1)S(1)}, u32[]{:S(2)}, u32[]{:S(2)}) collective-permute-start(bf16[32,1280]{1,0:T(8,128)(2,1)S(1)} %get-tuple-element.67), channel_id=1, source_target_pairs={{0,13},{1,12},{2,15},{3,14},{4,9},{5,8},{6,11},{7,10},{8,5},{9,4},... | collective-permute-start | bytes 245768 | tf_op jit(solution)/shard_map/ppermute | solution.py:578
  30.7 5.7 %collective-permute-start.14 = (bf16[32,1280]{1,0:T(8,128)(2,1)S(1)}, bf16[32,1280]{1,0:T(8,128)(2,1)S(1)}, u32[]{:S(2)}, u32[]{:S(2)}) collective-permute-start(bf16[32,1280]{1,0:T(8,128)(2,1)S(1)} %get-tuple-element.68), channel_id=1, source_target_pairs={{0,1},{1,0},{2,3},{3,2},{4,5},{5,4},{6,7},{7,6},{8,9},{9,8},{10,11... | collective-permute-start | bytes 245768 | tf_op jit(solution)/shard_map/ppermute | solution.py:578

commit v14 on v8

--- a/solution.py
+++ b/solution.py
@@ -41,8 +41,8 @@
 def order_of(groups):
     half = groups // 2
     near = list(range(half - 1, 0, -1))
-    quarter, eighth = half // 2, half // 4
-    far = [half + (at // 2 if at % 2 == 0 else quarter + (at // 2 ^ eighth)) for at in range(half)]
+    quarter = half // 2
+    far = [half + (at // 2 if at % 2 == 0 else quarter + (at // 2 ^ (quarter - 1))) for at in range(half)]
     order = [(far if kind == "f" else near).pop(0) for kind in "ffnfnfnfnfnfnfn"]
     order.insert(groups - LATE - 1, 0)
     return order

time: 39 us -> 40.9 us (1.049)
  waiting for transfers between devices: 1.08 us -> 2.69 us
    ppermute x15, waiting for transfers between devices: 1.08 us -> 2.69 us  [shards(): lax.ppermute(block, 'pg', [(source, source ^ t) for source in range(group...]
  transfers between devices with their start and end apart: 15 -> 15, of which waited for: 2 -> 3; matrix products, arithmetic and copies ran while one was open for 0% -> 0% of each run, Pallas kernels for 14% -> 13%
where the time goes in v14:
time: 40.9 us; the launch traced here: 40.7 us
  starting transfers between devices  25.8 us (63%)
  Pallas kernels  10.4 us (25%)
  waiting for transfers between devices  2.69 us (7%)
  local copies, waits for them, and re-layouts  1.1 us (3%)
  between operations  0.73 us (2%)
    ppermute x15, starting transfers between devices, shards(): lax.ppermute(block, 'pg', [(source, source ^ t) for source in range(group...  25.8 us
    pallas_call x1, Pallas kernels, attend(): pl.pallas_call(functools.partial(attend_kernel, len(got), requests is not...  3.9 us
    ppermute x15, waiting for transfers between devices, shards(): lax.ppermute(block, 'pg', [(source, source ^ t) for source in range(group...  2.69 us
    pallas_call x1, Pallas kernels, front(): pl.pallas_call(functools.partial(front_kernel, order), out_shape=[block]...  2.54 us
    pallas_call x1, Pallas kernels, attend_late(): pl.pallas_call(functools.partial(late_kernel, len(got), first), out_shape...  2.52 us
    unnamed x6, local copies, waits for them, and re-layouts  1.1 us
    pallas_call x1, Pallas kernels, pack_others(): pl.pallas_call(pack_kernel, out_shape=[jax.ShapeDtypeStruct(block, jnp.bf...  0.88 us
  transfers between devices with their start and end apart: 15, of which 3 were waited for; matrix products, arithmetic and copies ran while one was open for 0% of the time, Pallas kernels for 13%

profile of v14, /device:TPU:0, one launch (start us, length us, event | category | flops | bytes accessed | tf_op | source)
XLA Modules:
  0.0 40.7 jit_solution(9251938186591207506)
XLA Ops:
  0.6 2.5 %front.1 = (bf16[32,1280]{1,0:T(8,128)(2,1)}, bf16[32,1280]{1,0:T(8,128)(2,1)}, bf16[32,1280]{1,0:T(8,128)(2,1)}, bf16[32,1280]{1,0:T(8,128)(2,1)}, f32[1296,128]{1,0:T(8,128)}) custom-call(s32[1]{0:T(128)} %bitcast.me_ref, s32[16]{0:T(128)} %assign_any.1, s32[16]{0:T(128)} %length_any.1, s32[16,16]{1,0:T(8,128)} %owner_any.1, s32[16,16]{1,0:T(8,128)} %stripe_any.1, ...), custom_call_target="tpu_custom_call" | custom-call | tf_op jit(solution)/shard_map/front/pallas_call | solution.py:179
  3.2 4.1 %collective-permute-start = (bf16[32,1280]{1,0:T(8,128)(2,1)}, bf16[32,1280]{1,0:T(8,128)(2,1)S(1)}, u32[]{:S(2)}, u32[]{:S(2)}) collective-permute-start(bf16[32,1280]{1,0:T(8,128)(2,1)} %get-tuple-element.50), channel_id=1, source_target_pairs={{0,8},{1,9},{2,10},{3,11},{4,12},{5,13},{6,14},{7,15},{8,0},{9,1},... | collective-permute-start | bytes 245768 | tf_op jit(solution)/shard_map/ppermute | solution.py:578
  7.3 1.5 %collective-permute-start.1 = (bf16[32,1280]{1,0:T(8,128)(2,1)}, bf16[32,1280]{1,0:T(8,128)(2,1)S(1)}, u32[]{:S(2)}, u32[]{:S(2)}) collective-permute-start(bf16[32,1280]{1,0:T(8,128)(2,1)} %get-tuple-element.51), channel_id=1, source_target_pairs={{0,15},{1,14},{2,13},{3,12},{4,11},{5,10},{6,9},{7,8},{8,7},{9,6},... | collective-permute-start | bytes 245768 | tf_op jit(solution)/shard_map/ppermute | solution.py:578
  8.8 0.2 collective-permute-start.2
  9.0 2.5 %collective-permute-start.3 = (bf16[32,1280]{1,0:T(8,128)(2,1)}, bf16[32,1280]{1,0:T(8,128)(2,1)S(1)}, u32[]{:S(2)}, u32[]{:S(2)}) collective-permute-start(bf16[32,1280]{1,0:T(8,128)(2,1)} %get-tuple-element.53), channel_id=1, source_target_pairs={{0,9},{1,8},{2,11},{3,10},{4,13},{5,12},{6,15},{7,14},{8,1},{9,0},... | collective-permute-start | bytes 245768 | tf_op jit(solution)/shard_map/ppermute | solution.py:578
  11.5 1.1 %copy-done.1 = f32[1296,128]{1,0:T(8,128)S(1)} copy-done((f32[1296,128]{1,0:T(8,128)S(1)}, f32[1296,128]{1,0:T(8,128)}, u32[]{:S(2)}) %copy-start.1) | copy-done | bytes 663576
  12.6 0.9 %pack_others.1 = (bf16[32,1280]{1,0:T(8,128)(2,1)S(1)}, bf16[32,1280]{1,0:T(8,128)(2,1)S(1)}, bf16[32,1280]{1,0:T(8,128)(2,1)S(1)}, bf16[32,1280]{1,0:T(8,128)(2...) custom-call(f32[1296,128]{1,0:T(8,128)S(1)} %copy-done.1, ...), custom_call_target="tpu_custom_call" | custom-call | tf_op jit(solution)/shard_map/pack_others/pallas_call | solution.py:228
  13.4 1.7 %collective-permute-start.4 = (bf16[32,1280]{1,0:T(8,128)(2,1)S(1)}, bf16[32,1280]{1,0:T(8,128)(2,1)S(1)}, u32[]{:S(2)}, u32[]{:S(2)}) collective-permute-start(bf16[32,1280]{1,0:T(8,128)(2,1)S(1)} %get-tuple-element.54), channel_id=1, source_target_pairs={{0,6},{1,7},{2,4},{3,5},{4,2},{5,3},{6,0},{7,1},{8,14},{9,15},{10,... | collective-permute-start | bytes 245768 | tf_op jit(solution)/shard_map/ppermute | solution.py:578
  15.1 0.5 %rotate_queries.1 = (bf16[4,1024,128]{2,1,0:T(8,128)(2,1)S(1)}, bf16[8,128,128]{2,1,0:T(8,128)(2,1)S(1)}, f32[8,512]{1,0:T(8,128)S(1)}, s32[8,128]{1,0:T(8,128)S(1)}) custom-call(f32[1296,128]{1,0:T(8,128)S(1)} %copy-done.1, bf16[128,4096]{1,0:T(8,128)(2,1)S(1)} %bitcast.8), custom_call_target="tpu_custom_call" | custom-call | tf_op jit(solution)/shard_map/rotate_queries/pallas_call | solution.py:258
  15.7 0.0 collective-permute-done.refs_0_
  15.7 2.6 %collective-permute-start.5 = (bf16[32,1280]{1,0:T(8,128)(2,1)S(1)}, bf16[32,1280]{1,0:T(8,128)(2,1)S(1)}, u32[]{:S(2)}, u32[]{:S(2)}) collective-permute-start(bf16[32,1280]{1,0:T(8,128)(2,1)S(1)} %get-tuple-element.55), channel_id=1, source_target_pairs={{0,14},{1,15},{2,12},{3,13},{4,10},{5,11},{6,8},{7,9},{8,6},{9,7},... | collective-permute-start | bytes 245768 | tf_op jit(solution)/shard_map/ppermute | solution.py:578
  18.3 0.0 collective-permute-done.1.refs_1_
  18.3 0.4 %collective-permute-start.6 = (bf16[32,1280]{1,0:T(8,128)(2,1)S(1)}, bf16[32,1280]{1,0:T(8,128)(2,1)S(1)}, u32[]{:S(2)}, u32[]{:S(2)}) collective-permute-start(bf16[32,1280]{1,0:T(8,128)(2,1)S(1)} %get-tuple-element.56), channel_id=1, source_target_pairs={{0,5},{1,4},{2,7},{3,6},{4,1},{5,0},{6,3},{7,2},{8,13},{9,12},{10,... | collective-permute-start | bytes 245768 | tf_op jit(solution)/shard_map/ppermute | solution.py:578
  18.7 0.0 collective-permute-done.2.refs_2_
  18.7 2.4 %collective-permute-start.7 = (bf16[32,1280]{1,0:T(8,128)(2,1)S(1)}, bf16[32,1280]{1,0:T(8,128)(2,1)S(1)}, u32[]{:S(2)}, u32[]{:S(2)}) collective-permute-start(bf16[32,1280]{1,0:T(8,128)(2,1)S(1)} %get-tuple-element.57), channel_id=1, source_target_pairs={{0,10},{1,11},{2,8},{3,9},{4,14},{5,15},{6,12},{7,13},{8,2},{9,3},... | collective-permute-start | bytes 245768 | tf_op jit(solution)/shard_map/ppermute | solution.py:578
  21.1 1.9 %collective-permute-start.8 = (bf16[32,1280]{1,0:T(8,128)(2,1)S(1)}, bf16[32,1280]{1,0:T(8,128)(2,1)S(1)}, u32[]{:S(2)}, u32[]{:S(2)}) collective-permute-start(bf16[32,1280]{1,0:T(8,128)(2,1)S(1)} %get-tuple-element.58), channel_id=1, source_target_pairs={{0,4},{1,5},{2,6},{3,7},{4,0},{5,1},{6,2},{7,3},{8,12},{9,13},{10,... | collective-permute-start | bytes 245768 | tf_op jit(solution)/shard_map/ppermute | solution.py:578
  23.0 0.8 %collective-permute-done.5.refs_5_ = bf16[32,1280]{1,0:T(8,128)(2,1)S(1)} collective-permute-done((bf16[32,1280]{1,0:T(8,128)(2,1)S(1)}, bf16[32,1280]{1,0:T(8,128)(2,1)S(1)}, u32[]{:S(2)}, u32[]{:S(2)}) %collective-permute-start.5) | collective-permute-done | bytes 81952 | tf_op jit(solution)/shard_map/ppermute | solution.py:578
  23.8 1.3 %collective-permute-start.10 = (bf16[32,1280]{1,0:T(8,128)(2,1)S(1)}, bf16[32,1280]{1,0:T(8,128)(2,1)S(1)}, u32[]{:S(2)}, u32[]{:S(2)}) collective-permute-start(bf16[32,1280]{1,0:T(8,128)(2,1)S(1)} %get-tuple-element.60), channel_id=1, source_target_pairs={{0,3},{1,2},{2,1},{3,0},{4,7},{5,6},{6,5},{7,4},{8,11},{9,10},{10,... | collective-permute-start | bytes 245768 | tf_op jit(solution)/shard_map/ppermute | solution.py:578
  25.1 1.1 %collective-permute-done.6.refs_6_ = bf16[32,1280]{1,0:T(8,128)(2,1)S(1)} collective-permute-done((bf16[32,1280]{1,0:T(8,128)(2,1)S(1)}, bf16[32,1280]{1,0:T(8,128)(2,1)S(1)}, u32[]{:S(2)}, u32[]{:S(2)}) %collective-permute-start.6) | collective-permute-done | bytes 81952 | tf_op jit(solution)/shard_map/ppermute | solution.py:578
  26.2 1.0 %collective-permute-start.11 = (bf16[32,1280]{1,0:T(8,128)(2,1)S(1)}, bf16[32,1280]{1,0:T(8,128)(2,1)S(1)}, u32[]{:S(2)}, u32[]{:S(2)}) collective-permute-start(bf16[32,1280]{1,0:T(8,128)(2,1)S(1)} %get-tuple-element.65), channel_id=1, source_target_pairs={{0,11},{1,10},{2,9},{3,8},{4,15},{5,14},{6,13},{7,12},{8,3},{9,2},... | collective-permute-start | bytes 245768 | tf_op jit(solution)/shard_map/ppermute | solution.py:578
  27.2 0.8 %collective-permute-done.7.refs_7_ = bf16[32,1280]{1,0:T(8,128)(2,1)S(1)} collective-permute-done((bf16[32,1280]{1,0:T(8,128)(2,1)S(1)}, bf16[32,1280]{1,0:T(8,128)(2,1)S(1)}, u32[]{:S(2)}, u32[]{:S(2)}) %collective-permute-start.7) | collective-permute-done | bytes 81952 | tf_op jit(solution)/shard_map/ppermute | solution.py:578
  28.0 6.2 %collective-permute-start.13 = (bf16[32,1280]{1,0:T(8,128)(2,1)S(1)}, bf16[32,1280]{1,0:T(8,128)(2,1)S(1)}, u32[]{:S(2)}, u32[]{:S(2)}) collective-permute-start(bf16[32,1280]{1,0:T(8,128)(2,1)S(1)} %get-tuple-element.67), channel_id=1, source_target_pairs={{0,12},{1,13},{2,14},{3,15},{4,8},{5,9},{6,10},{7,11},{8,4},{9,5},... | collective-permute-start | bytes 245768 | tf_op jit(solution)/shard_map/ppermute | solution.py:578
  34.2 3.9 %attend.1 = (f32[4,1024,128]{2,1,0:T(8,128)S(1)}, f32[4,1024,128]{2,1,0:T(8,128)S(1)}, bf16[16,8,1024]{2,1,0:T(8,128)(2,1)}) custom-call(bf16[4,1024,128]{2,1,0:T(8,128)(2,1)S(1)} %get-tuple-element.47.rot_ref, f32[8,512]{1,0:T(8,128)S(1)} %get-tuple-element.48.bias_ref, bf16[8,128,128]{2,1,0:T(8,128)(2,1)S(1)} %get-tuple-element.49.own_ref, ...), custom_call_target="tpu_custom_call" | custom-call | tf_op jit(solution)/shard_map/attend/pallas_call | solution.py:401
  38.2 2.5 %attend_late.1 = (bf16[128,4096]{1,0:T(8,128)(2,1)}, bf16[16,8,1024]{2,1,0:T(8,128)(2,1)}) custom-call(bf16[4,1024,128]{2,1,0:T(8,128)(2,1)S(1)} %get-tuple-element.47.rot_ref, f32[8,512]{1,0:T(8,128)S(1)} %get-tuple-element.48.bias_ref, f32[4,1024,128]{2,1,0:T(8,128)S(1)} %get-tuple-element.63.result_ref, ...), custom_call_target="tpu_custom_call", output_to_operand_aliasing={{1}: (9, {})} | custom-call | tf_op jit(solution)/shard_map/attend_late/pallas_call | solution.py:501
  (17 shorter events, 0.0 us)
Async XLA Ops:
  0.6 10.8 %copy-start = (bf16[1,16,32,1024]{3,2,1,0:T(8,128)(2,1)S(1)}, bf16[1,16,32,1024]{3,2,1,0:T(8,128)(2,1)}, u32[]{:S(2)}) copy-start(bf16[1,16,32,1024]{3,2,1,0:T(8,128)(2,1)} %param.10) | copy-start | bytes 3145732
  3.2 12.5 %collective-permute-start = (bf16[32,1280]{1,0:T(8,128)(2,1)}, bf16[32,1280]{1,0:T(8,128)(2,1)S(1)}, u32[]{:S(2)}, u32[]{:S(2)}) collective-permute-start(bf16[32,1280]{1,0:T(8,128)(2,1)} %get-tuple-element.50), channel_id=1, source_target_pairs={{0,8},{1,9},{2,10},{3,11},{4,12},{5,13},{6,14},{7,15},{8,0},{9,1},... | collective-permute-start | bytes 245768 | tf_op jit(solution)/shard_map/ppermute | solution.py:578
  7.3 11.0 %collective-permute-start.1 = (bf16[32,1280]{1,0:T(8,128)(2,1)}, bf16[32,1280]{1,0:T(8,128)(2,1)S(1)}, u32[]{:S(2)}, u32[]{:S(2)}) collective-permute-start(bf16[32,1280]{1,0:T(8,128)(2,1)} %get-tuple-element.51), channel_id=1, source_target_pairs={{0,15},{1,14},{2,13},{3,12},{4,11},{5,10},{6,9},{7,8},{8,7},{9,6},... | collective-permute-start | bytes 245768 | tf_op jit(solution)/shard_map/ppermute | solution.py:578
  8.8 9.9 %collective-permute-start.2 = (bf16[32,1280]{1,0:T(8,128)(2,1)}, bf16[32,1280]{1,0:T(8,128)(2,1)S(1)}, u32[]{:S(2)}, u32[]{:S(2)}) collective-permute-start(bf16[32,1280]{1,0:T(8,128)(2,1)} %get-tuple-element.52), channel_id=1, source_target_pairs={{0,7},{1,6},{2,5},{3,4},{4,3},{5,2},{6,1},{7,0},{8,15},{9,14},{10,... | collective-permute-start | bytes 245768 | tf_op jit(solution)/shard_map/ppermute | solution.py:578
  9.0 12.1 %collective-permute-start.3 = (bf16[32,1280]{1,0:T(8,128)(2,1)}, bf16[32,1280]{1,0:T(8,128)(2,1)S(1)}, u32[]{:S(2)}, u32[]{:S(2)}) collective-permute-start(bf16[32,1280]{1,0:T(8,128)(2,1)} %get-tuple-element.53), channel_id=1, source_target_pairs={{0,9},{1,8},{2,11},{3,10},{4,13},{5,12},{6,15},{7,14},{8,1},{9,0},... | collective-permute-start | bytes 245768 | tf_op jit(solution)/shard_map/ppermute | solution.py:578
  11.5 1.1 %copy-start.1 = (f32[1296,128]{1,0:T(8,128)S(1)}, f32[1296,128]{1,0:T(8,128)}, u32[]{:S(2)}) copy-start(f32[1296,128]{1,0:T(8,128)} %get-tuple-element.37.info_ref) | copy-start | bytes 1990660
  12.6 2.6 %copy-start.2 = (bf16[1,128,4096]{2,1,0:T(8,128)(2,1)S(1)}, bf16[1,128,4096]{2,1,0:T(8,128)(2,1)}, u32[]{:S(2)}) copy-start(bf16[1,128,4096]{2,1,0:T(8,128)(2,1)} %param.8) | copy-start | bytes 3145732
  13.4 9.6 %collective-permute-start.4 = (bf16[32,1280]{1,0:T(8,128)(2,1)S(1)}, bf16[32,1280]{1,0:T(8,128)(2,1)S(1)}, u32[]{:S(2)}, u32[]{:S(2)}) collective-permute-start(bf16[32,1280]{1,0:T(8,128)(2,1)S(1)} %get-tuple-element.54), channel_id=1, source_target_pairs={{0,6},{1,7},{2,4},{3,5},{4,2},{5,3},{6,0},{7,1},{8,14},{9,15},{10,... | collective-permute-start | bytes 245768 | tf_op jit(solution)/shard_map/ppermute | solution.py:578
  15.7 8.1 %collective-permute-start.5 = (bf16[32,1280]{1,0:T(8,128)(2,1)S(1)}, bf16[32,1280]{1,0:T(8,128)(2,1)S(1)}, u32[]{:S(2)}, u32[]{:S(2)}) collective-permute-start(bf16[32,1280]{1,0:T(8,128)(2,1)S(1)} %get-tuple-element.55), channel_id=1, source_target_pairs={{0,14},{1,15},{2,12},{3,13},{4,10},{5,11},{6,8},{7,9},{8,6},{9,7},... | collective-permute-start | bytes 245768 | tf_op jit(solution)/shard_map/ppermute | solution.py:578
  18.3 7.9 %collective-permute-start.6 = (bf16[32,1280]{1,0:T(8,128)(2,1)S(1)}, bf16[32,1280]{1,0:T(8,128)(2,1)S(1)}, u32[]{:S(2)}, u32[]{:S(2)}) collective-permute-start(bf16[32,1280]{1,0:T(8,128)(2,1)S(1)} %get-tuple-element.56), channel_id=1, source_target_pairs={{0,5},{1,4},{2,7},{3,6},{4,1},{5,0},{6,3},{7,2},{8,13},{9,12},{10,... | collective-permute-start | bytes 245768 | tf_op jit(solution)/shard_map/ppermute | solution.py:578
  18.7 9.3 %collective-permute-start.7 = (bf16[32,1280]{1,0:T(8,128)(2,1)S(1)}, bf16[32,1280]{1,0:T(8,128)(2,1)S(1)}, u32[]{:S(2)}, u32[]{:S(2)}) collective-permute-start(bf16[32,1280]{1,0:T(8,128)(2,1)S(1)} %get-tuple-element.57), channel_id=1, source_target_pairs={{0,10},{1,11},{2,8},{3,9},{4,14},{5,15},{6,12},{7,13},{8,2},{9,3},... | collective-permute-start | bytes 245768 | tf_op jit(solution)/shard_map/ppermute | solution.py:578
  21.1 7.0 %collective-permute-start.8 = (bf16[32,1280]{1,0:T(8,128)(2,1)S(1)}, bf16[32,1280]{1,0:T(8,128)(2,1)S(1)}, u32[]{:S(2)}, u32[]{:S(2)}) collective-permute-start(bf16[32,1280]{1,0:T(8,128)(2,1)S(1)} %get-tuple-element.58), channel_id=1, source_target_pairs={{0,4},{1,5},{2,6},{3,7},{4,0},{5,1},{6,2},{7,3},{8,12},{9,13},{10,... | collective-permute-start | bytes 245768 | tf_op jit(solution)/shard_map/ppermute | solution.py:578
  23.0 11.2 %collective-permute-start.9 = (bf16[32,1280]{1,0:T(8,128)(2,1)S(1)}, bf16[32,1280]{1,0:T(8,128)(2,1)S(1)}, u32[]{:S(2)}, u32[]{:S(2)}) collective-permute-start(bf16[32,1280]{1,0:T(8,128)(2,1)S(1)} %get-tuple-element.59), channel_id=1, source_target_pairs={{0,13},{1,12},{2,15},{3,14},{4,9},{5,8},{6,11},{7,10},{8,5},{9,4},... | collective-permute-start | bytes 245768 | tf_op jit(solution)/shard_map/ppermute | solution.py:578
  23.8 10.5 %collective-permute-start.10 = (bf16[32,1280]{1,0:T(8,128)(2,1)S(1)}, bf16[32,1280]{1,0:T(8,128)(2,1)S(1)}, u32[]{:S(2)}, u32[]{:S(2)}) collective-permute-start(bf16[32,1280]{1,0:T(8,128)(2,1)S(1)} %get-tuple-element.60), channel_id=1, source_target_pairs={{0,3},{1,2},{2,1},{3,0},{4,7},{5,6},{6,5},{7,4},{8,11},{9,10},{10,... | collective-permute-start | bytes 245768 | tf_op jit(solution)/shard_map/ppermute | solution.py:578
  26.2 11.9 %collective-permute-start.11 = (bf16[32,1280]{1,0:T(8,128)(2,1)S(1)}, bf16[32,1280]{1,0:T(8,128)(2,1)S(1)}, u32[]{:S(2)}, u32[]{:S(2)}) collective-permute-start(bf16[32,1280]{1,0:T(8,128)(2,1)S(1)} %get-tuple-element.65), channel_id=1, source_target_pairs={{0,11},{1,10},{2,9},{3,8},{4,15},{5,14},{6,13},{7,12},{8,3},{9,2},... | collective-permute-start | bytes 245768 | tf_op jit(solution)/shard_map/ppermute | solution.py:578
  28.0 10.1 %collective-permute-start.12 = (bf16[32,1280]{1,0:T(8,128)(2,1)S(1)}, bf16[32,1280]{1,0:T(8,128)(2,1)S(1)}, u32[]{:S(2)}, u32[]{:S(2)}) collective-permute-start(bf16[32,1280]{1,0:T(8,128)(2,1)S(1)} %get-tuple-element.66), channel_id=1, source_target_pairs={{0,2},{1,3},{2,0},{3,1},{4,6},{5,7},{6,4},{7,5},{8,10},{9,11},{10,... | collective-permute-start | bytes 245768 | tf_op jit(solution)/shard_map/ppermute | solution.py:578
  28.0 10.1 %collective-permute-start.13 = (bf16[32,1280]{1,0:T(8,128)(2,1)S(1)}, bf16[32,1280]{1,0:T(8,128)(2,1)S(1)}, u32[]{:S(2)}, u32[]{:S(2)}) collective-permute-start(bf16[32,1280]{1,0:T(8,128)(2,1)S(1)} %get-tuple-element.67), channel_id=1, source_target_pairs={{0,12},{1,13},{2,14},{3,15},{4,8},{5,9},{6,10},{7,11},{8,4},{9,5},... | collective-permute-start | bytes 245768 | tf_op jit(solution)/shard_map/ppermute | solution.py:578
  34.2 4.0 %collective-permute-start.14 = (bf16[32,1280]{1,0:T(8,128)(2,1)S(1)}, bf16[32,1280]{1,0:T(8,128)(2,1)S(1)}, u32[]{:S(2)}, u32[]{:S(2)}) collective-permute-start(bf16[32,1280]{1,0:T(8,128)(2,1)S(1)} %get-tuple-element.68), channel_id=1, source_target_pairs={{0,1},{1,0},{2,3},{3,2},{4,5},{5,4},{6,7},{7,6},{8,9},{9,8},{10,11... | collective-permute-start | bytes 245768 | tf_op jit(solution)/shard_map/ppermute | solution.py:578

commit v15 on v8

--- a/solution.py
+++ b/solution.py
@@ -21,7 +21,7 @@
 SCALE = HEAD_DIM ** -0.5 / math.log(2.0)
 CHUNK = 256
 LATE = 4
-LATE_CHUNK = 512
+LATE_CHUNK = 1024
 AHEAD = 4
 AHEAD_OF_QUERIES = 8
 

time: 39 us -> 39 us (level)
  no operation moved by 1% of the time
where the time goes in v15:
time: 39 us; the launch traced here: 38.8 us
  starting transfers between devices  25.6 us (66%)
  Pallas kernels  10.3 us (26%)
  local copies, waits for them, and re-layouts  1.1 us (3%)
  waiting for transfers between devices  1.08 us (3%)
  between operations  0.7 us (2%)
    ppermute x15, starting transfers between devices, shards(): lax.ppermute(block, 'pg', [(source, source ^ t) for source in range(group...  25.6 us
    pallas_call x1, Pallas kernels, attend(): pl.pallas_call(functools.partial(attend_kernel, len(got), requests is not...  3.89 us
    pallas_call x1, Pallas kernels, front(): pl.pallas_call(functools.partial(front_kernel, order), out_shape=[block]...  2.54 us
    pallas_call x1, Pallas kernels, attend_late(): pl.pallas_call(functools.partial(late_kernel, len(got), first), out_shape...  2.52 us
    unnamed x6, local copies, waits for them, and re-layouts  1.1 us
    ppermute x15, waiting for transfers between devices, shards(): lax.ppermute(block, 'pg', [(source, source ^ t) for source in range(group...  1.08 us
    pallas_call x1, Pallas kernels, pack_others(): pl.pallas_call(pack_kernel, out_shape=[jax.ShapeDtypeStruct(block, jnp.bf...  0.87 us
  transfers between devices with their start and end apart: 15, of which 2 were waited for; matrix products, arithmetic and copies ran while one was open for 0% of the time, Pallas kernels for 14%

profile of v15, /device:TPU:0, one launch (start us, length us, event | category | flops | bytes accessed | tf_op | source)
XLA Modules:
  0.0 38.8 jit_solution(10891755014939902994)
XLA Ops:
  0.6 2.5 %front.1 = (bf16[32,1280]{1,0:T(8,128)(2,1)}, bf16[32,1280]{1,0:T(8,128)(2,1)}, bf16[32,1280]{1,0:T(8,128)(2,1)}, bf16[32,1280]{1,0:T(8,128)(2,1)}, f32[1296,128]{1,0:T(8,128)}) custom-call(s32[1]{0:T(128)} %bitcast.me_ref, s32[16]{0:T(128)} %assign_any.1, s32[16]{0:T(128)} %length_any.1, s32[16,16]{1,0:T(8,128)} %owner_any.1, s32[16,16]{1,0:T(8,128)} %stripe_any.1, ...), custom_call_target="tpu_custom_call" | custom-call | tf_op jit(solution)/shard_map/front/pallas_call | solution.py:179
  3.2 4.1 %collective-permute-start = (bf16[32,1280]{1,0:T(8,128)(2,1)}, bf16[32,1280]{1,0:T(8,128)(2,1)S(1)}, u32[]{:S(2)}, u32[]{:S(2)}) collective-permute-start(bf16[32,1280]{1,0:T(8,128)(2,1)} %get-tuple-element.50), channel_id=1, source_target_pairs={{0,8},{1,9},{2,10},{3,11},{4,12},{5,13},{6,14},{7,15},{8,0},{9,1},... | collective-permute-start | bytes 245768 | tf_op jit(solution)/shard_map/ppermute | solution.py:578
  7.3 2.3 %collective-permute-start.1 = (bf16[32,1280]{1,0:T(8,128)(2,1)}, bf16[32,1280]{1,0:T(8,128)(2,1)S(1)}, u32[]{:S(2)}, u32[]{:S(2)}) collective-permute-start(bf16[32,1280]{1,0:T(8,128)(2,1)} %get-tuple-element.51), channel_id=1, source_target_pairs={{0,14},{1,15},{2,12},{3,13},{4,10},{5,11},{6,8},{7,9},{8,6},{9,7},... | collective-permute-start | bytes 245768 | tf_op jit(solution)/shard_map/ppermute | solution.py:578
  9.6 0.0 collective-permute-start.2
  9.6 2.7 %collective-permute-start.3 = (bf16[32,1280]{1,0:T(8,128)(2,1)}, bf16[32,1280]{1,0:T(8,128)(2,1)S(1)}, u32[]{:S(2)}, u32[]{:S(2)}) collective-permute-start(bf16[32,1280]{1,0:T(8,128)(2,1)} %get-tuple-element.53), channel_id=1, source_target_pairs={{0,9},{1,8},{2,11},{3,10},{4,13},{5,12},{6,15},{7,14},{8,1},{9,0},... | collective-permute-start | bytes 245768 | tf_op jit(solution)/shard_map/ppermute | solution.py:578
  12.3 1.1 %copy-done.1 = f32[1296,128]{1,0:T(8,128)S(1)} copy-done((f32[1296,128]{1,0:T(8,128)S(1)}, f32[1296,128]{1,0:T(8,128)}, u32[]{:S(2)}) %copy-start.1) | copy-done | bytes 663576
  13.4 0.9 %pack_others.1 = (bf16[32,1280]{1,0:T(8,128)(2,1)S(1)}, bf16[32,1280]{1,0:T(8,128)(2,1)S(1)}, bf16[32,1280]{1,0:T(8,128)(2,1)S(1)}, bf16[32,1280]{1,0:T(8,128)(2...) custom-call(f32[1296,128]{1,0:T(8,128)S(1)} %copy-done.1, ...), custom_call_target="tpu_custom_call" | custom-call | tf_op jit(solution)/shard_map/pack_others/pallas_call | solution.py:228
  14.3 1.7 %collective-permute-start.4 = (bf16[32,1280]{1,0:T(8,128)(2,1)S(1)}, bf16[32,1280]{1,0:T(8,128)(2,1)S(1)}, u32[]{:S(2)}, u32[]{:S(2)}) collective-permute-start(bf16[32,1280]{1,0:T(8,128)(2,1)S(1)} %get-tuple-element.54), channel_id=1, source_target_pairs={{0,6},{1,7},{2,4},{3,5},{4,2},{5,3},{6,0},{7,1},{8,14},{9,15},{10,... | collective-permute-start | bytes 245768 | tf_op jit(solution)/shard_map/ppermute | solution.py:578
  16.0 0.5 %rotate_queries.1 = (bf16[4,1024,128]{2,1,0:T(8,128)(2,1)S(1)}, bf16[8,128,128]{2,1,0:T(8,128)(2,1)S(1)}, f32[8,512]{1,0:T(8,128)S(1)}, s32[8,128]{1,0:T(8,128)S(1)}) custom-call(f32[1296,128]{1,0:T(8,128)S(1)} %copy-done.1, bf16[128,4096]{1,0:T(8,128)(2,1)S(1)} %bitcast.8), custom_call_target="tpu_custom_call" | custom-call | tf_op jit(solution)/shard_map/rotate_queries/pallas_call | solution.py:258
  16.5 0.0 collective-permute-done.refs_0_
  16.5 1.4 %collective-permute-start.5 = (bf16[32,1280]{1,0:T(8,128)(2,1)S(1)}, bf16[32,1280]{1,0:T(8,128)(2,1)S(1)}, u32[]{:S(2)}, u32[]{:S(2)}) collective-permute-start(bf16[32,1280]{1,0:T(8,128)(2,1)S(1)} %get-tuple-element.55), channel_id=1, source_target_pairs={{0,15},{1,14},{2,13},{3,12},{4,11},{5,10},{6,9},{7,8},{8,7},{9,6},... | collective-permute-start | bytes 245768 | tf_op jit(solution)/shard_map/ppermute | solution.py:578
  17.9 0.1 collective-permute-start.6
  18.0 3.6 %collective-permute-start.7 = (bf16[32,1280]{1,0:T(8,128)(2,1)S(1)}, bf16[32,1280]{1,0:T(8,128)(2,1)S(1)}, u32[]{:S(2)}, u32[]{:S(2)}) collective-permute-start(bf16[32,1280]{1,0:T(8,128)(2,1)S(1)} %get-tuple-element.57), channel_id=1, source_target_pairs={{0,10},{1,11},{2,8},{3,9},{4,14},{5,15},{6,12},{7,13},{8,2},{9,3},... | collective-permute-start | bytes 245768 | tf_op jit(solution)/shard_map/ppermute | solution.py:578
  21.7 0.7 %collective-permute-start.8 = (bf16[32,1280]{1,0:T(8,128)(2,1)S(1)}, bf16[32,1280]{1,0:T(8,128)(2,1)S(1)}, u32[]{:S(2)}, u32[]{:S(2)}) collective-permute-start(bf16[32,1280]{1,0:T(8,128)(2,1)S(1)} %get-tuple-element.58), channel_id=1, source_target_pairs={{0,4},{1,5},{2,6},{3,7},{4,0},{5,1},{6,2},{7,3},{8,12},{9,13},{10,... | collective-permute-start | bytes 245768 | tf_op jit(solution)/shard_map/ppermute | solution.py:578
  22.4 1.3 %collective-permute-start.9 = (bf16[32,1280]{1,0:T(8,128)(2,1)S(1)}, bf16[32,1280]{1,0:T(8,128)(2,1)S(1)}, u32[]{:S(2)}, u32[]{:S(2)}) collective-permute-start(bf16[32,1280]{1,0:T(8,128)(2,1)S(1)} %get-tuple-element.59), channel_id=1, source_target_pairs={{0,12},{1,13},{2,14},{3,15},{4,8},{5,9},{6,10},{7,11},{8,4},{9,5},... | collective-permute-start | bytes 245768 | tf_op jit(solution)/shard_map/ppermute | solution.py:578
  23.7 2.0 %collective-permute-start.10 = (bf16[32,1280]{1,0:T(8,128)(2,1)S(1)}, bf16[32,1280]{1,0:T(8,128)(2,1)S(1)}, u32[]{:S(2)}, u32[]{:S(2)}) collective-permute-start(bf16[32,1280]{1,0:T(8,128)(2,1)S(1)} %get-tuple-element.60), channel_id=1, source_target_pairs={{0,3},{1,2},{2,1},{3,0},{4,7},{5,6},{6,5},{7,4},{8,11},{9,10},{10,... | collective-permute-start | bytes 245768 | tf_op jit(solution)/shard_map/ppermute | solution.py:578
  25.7 1.7 %collective-permute-start.11 = (bf16[32,1280]{1,0:T(8,128)(2,1)S(1)}, bf16[32,1280]{1,0:T(8,128)(2,1)S(1)}, u32[]{:S(2)}, u32[]{:S(2)}) collective-permute-start(bf16[32,1280]{1,0:T(8,128)(2,1)S(1)} %get-tuple-element.65), channel_id=1, source_target_pairs={{0,11},{1,10},{2,9},{3,8},{4,15},{5,14},{6,13},{7,12},{8,3},{9,2},... | collective-permute-start | bytes 245768 | tf_op jit(solution)/shard_map/ppermute | solution.py:578
  27.4 0.9 %collective-permute-start.12 = (bf16[32,1280]{1,0:T(8,128)(2,1)S(1)}, bf16[32,1280]{1,0:T(8,128)(2,1)S(1)}, u32[]{:S(2)}, u32[]{:S(2)}) collective-permute-start(bf16[32,1280]{1,0:T(8,128)(2,1)S(1)} %get-tuple-element.66), channel_id=1, source_target_pairs={{0,2},{1,3},{2,0},{3,1},{4,6},{5,7},{6,4},{7,5},{8,10},{9,11},{10,... | collective-permute-start | bytes 245768 | tf_op jit(solution)/shard_map/ppermute | solution.py:578
  28.3 2.7 %collective-permute-start.13 = (bf16[32,1280]{1,0:T(8,128)(2,1)S(1)}, bf16[32,1280]{1,0:T(8,128)(2,1)S(1)}, u32[]{:S(2)}, u32[]{:S(2)}) collective-permute-start(bf16[32,1280]{1,0:T(8,128)(2,1)S(1)} %get-tuple-element.67), channel_id=1, source_target_pairs={{0,13},{1,12},{2,15},{3,14},{4,9},{5,8},{6,11},{7,10},{8,5},{9,4},... | collective-permute-start | bytes 245768 | tf_op jit(solution)/shard_map/ppermute | solution.py:578
  31.0 0.2 collective-permute-done.9.refs_9_
  31.3 0.3 collective-permute-start.14
  31.5 3.9 %attend.1 = (f32[4,1024,128]{2,1,0:T(8,128)S(1)}, f32[4,1024,128]{2,1,0:T(8,128)S(1)}, bf16[16,8,1024]{2,1,0:T(8,128)(2,1)}) custom-call(bf16[4,1024,128]{2,1,0:T(8,128)(2,1)S(1)} %get-tuple-element.47.rot_ref, f32[8,512]{1,0:T(8,128)S(1)} %get-tuple-element.48.bias_ref, bf16[8,128,128]{2,1,0:T(8,128)(2,1)S(1)} %get-tuple-element.49.own_ref, ...), custom_call_target="tpu_custom_call" | custom-call | tf_op jit(solution)/shard_map/attend/pallas_call | solution.py:401
  35.4 0.8 %collective-permute-done.11.refs_0_ = bf16[32,1280]{1,0:T(8,128)(2,1)S(1)} collective-permute-done((bf16[32,1280]{1,0:T(8,128)(2,1)S(1)}, bf16[32,1280]{1,0:T(8,128)(2,1)S(1)}, u32[]{:S(2)}, u32[]{:S(2)}) %collective-permute-start.11) | collective-permute-done | bytes 81952 | tf_op jit(solution)/shard_map/ppermute | solution.py:578
  36.3 2.5 %attend_late.1 = (bf16[128,4096]{1,0:T(8,128)(2,1)}, bf16[16,8,1024]{2,1,0:T(8,128)(2,1)}) custom-call(bf16[4,1024,128]{2,1,0:T(8,128)(2,1)S(1)} %get-tuple-element.47.rot_ref, f32[8,512]{1,0:T(8,128)S(1)} %get-tuple-element.48.bias_ref, f32[4,1024,128]{2,1,0:T(8,128)S(1)} %get-tuple-element.63.result_ref, ...), custom_call_target="tpu_custom_call", output_to_operand_aliasing={{1}: (9, {})} | custom-call | tf_op jit(solution)/shard_map/attend_late/pallas_call | solution.py:501
  (17 shorter events, 0.0 us)
Async XLA Ops:
  0.6 11.7 %copy-start = (bf16[1,16,32,1024]{3,2,1,0:T(8,128)(2,1)S(1)}, bf16[1,16,32,1024]{3,2,1,0:T(8,128)(2,1)}, u32[]{:S(2)}) copy-start(bf16[1,16,32,1024]{3,2,1,0:T(8,128)(2,1)} %param.10) | copy-start | bytes 3145732
  3.2 13.3 %collective-permute-start = (bf16[32,1280]{1,0:T(8,128)(2,1)}, bf16[32,1280]{1,0:T(8,128)(2,1)S(1)}, u32[]{:S(2)}, u32[]{:S(2)}) collective-permute-start(bf16[32,1280]{1,0:T(8,128)(2,1)} %get-tuple-element.50), channel_id=1, source_target_pairs={{0,8},{1,9},{2,10},{3,11},{4,12},{5,13},{6,14},{7,15},{8,0},{9,1},... | collective-permute-start | bytes 245768 | tf_op jit(solution)/shard_map/ppermute | solution.py:578
  7.3 10.6 %collective-permute-start.1 = (bf16[32,1280]{1,0:T(8,128)(2,1)}, bf16[32,1280]{1,0:T(8,128)(2,1)S(1)}, u32[]{:S(2)}, u32[]{:S(2)}) collective-permute-start(bf16[32,1280]{1,0:T(8,128)(2,1)} %get-tuple-element.51), channel_id=1, source_target_pairs={{0,14},{1,15},{2,12},{3,13},{4,10},{5,11},{6,8},{7,9},{8,6},{9,7},... | collective-permute-start | bytes 245768 | tf_op jit(solution)/shard_map/ppermute | solution.py:578
  9.6 8.4 %collective-permute-start.2 = (bf16[32,1280]{1,0:T(8,128)(2,1)}, bf16[32,1280]{1,0:T(8,128)(2,1)S(1)}, u32[]{:S(2)}, u32[]{:S(2)}) collective-permute-start(bf16[32,1280]{1,0:T(8,128)(2,1)} %get-tuple-element.52), channel_id=1, source_target_pairs={{0,7},{1,6},{2,5},{3,4},{4,3},{5,2},{6,1},{7,0},{8,15},{9,14},{10,... | collective-permute-start | bytes 245768 | tf_op jit(solution)/shard_map/ppermute | solution.py:578
  9.6 12.1 %collective-permute-start.3 = (bf16[32,1280]{1,0:T(8,128)(2,1)}, bf16[32,1280]{1,0:T(8,128)(2,1)S(1)}, u32[]{:S(2)}, u32[]{:S(2)}) collective-permute-start(bf16[32,1280]{1,0:T(8,128)(2,1)} %get-tuple-element.53), channel_id=1, source_target_pairs={{0,9},{1,8},{2,11},{3,10},{4,13},{5,12},{6,15},{7,14},{8,1},{9,0},... | collective-permute-start | bytes 245768 | tf_op jit(solution)/shard_map/ppermute | solution.py:578
  12.3 1.1 %copy-start.1 = (f32[1296,128]{1,0:T(8,128)S(1)}, f32[1296,128]{1,0:T(8,128)}, u32[]{:S(2)}) copy-start(f32[1296,128]{1,0:T(8,128)} %get-tuple-element.37.info_ref) | copy-start | bytes 1990660
  13.4 2.6 %copy-start.2 = (bf16[1,128,4096]{2,1,0:T(8,128)(2,1)S(1)}, bf16[1,128,4096]{2,1,0:T(8,128)(2,1)}, u32[]{:S(2)}) copy-start(bf16[1,128,4096]{2,1,0:T(8,128)(2,1)} %param.8) | copy-start | bytes 3145732
  14.3 8.1 %collective-permute-start.4 = (bf16[32,1280]{1,0:T(8,128)(2,1)S(1)}, bf16[32,1280]{1,0:T(8,128)(2,1)S(1)}, u32[]{:S(2)}, u32[]{:S(2)}) collective-permute-start(bf16[32,1280]{1,0:T(8,128)(2,1)S(1)} %get-tuple-element.54), channel_id=1, source_target_pairs={{0,6},{1,7},{2,4},{3,5},{4,2},{5,3},{6,0},{7,1},{8,14},{9,15},{10,... | collective-permute-start | bytes 245768 | tf_op jit(solution)/shard_map/ppermute | solution.py:578
  16.5 7.2 %collective-permute-start.5 = (bf16[32,1280]{1,0:T(8,128)(2,1)S(1)}, bf16[32,1280]{1,0:T(8,128)(2,1)S(1)}, u32[]{:S(2)}, u32[]{:S(2)}) collective-permute-start(bf16[32,1280]{1,0:T(8,128)(2,1)S(1)} %get-tuple-element.55), channel_id=1, source_target_pairs={{0,15},{1,14},{2,13},{3,12},{4,11},{5,10},{6,9},{7,8},{8,7},{9,6},... | collective-permute-start | bytes 245768 | tf_op jit(solution)/shard_map/ppermute | solution.py:578
  17.9 7.8 %collective-permute-start.6 = (bf16[32,1280]{1,0:T(8,128)(2,1)S(1)}, bf16[32,1280]{1,0:T(8,128)(2,1)S(1)}, u32[]{:S(2)}, u32[]{:S(2)}) collective-permute-start(bf16[32,1280]{1,0:T(8,128)(2,1)S(1)} %get-tuple-element.56), channel_id=1, source_target_pairs={{0,5},{1,4},{2,7},{3,6},{4,1},{5,0},{6,3},{7,2},{8,13},{9,12},{10,... | collective-permute-start | bytes 245768 | tf_op jit(solution)/shard_map/ppermute | solution.py:578
  18.0 9.4 %collective-permute-start.7 = (bf16[32,1280]{1,0:T(8,128)(2,1)S(1)}, bf16[32,1280]{1,0:T(8,128)(2,1)S(1)}, u32[]{:S(2)}, u32[]{:S(2)}) collective-permute-start(bf16[32,1280]{1,0:T(8,128)(2,1)S(1)} %get-tuple-element.57), channel_id=1, source_target_pairs={{0,10},{1,11},{2,8},{3,9},{4,14},{5,15},{6,12},{7,13},{8,2},{9,3},... | collective-permute-start | bytes 245768 | tf_op jit(solution)/shard_map/ppermute | solution.py:578
  21.7 6.6 %collective-permute-start.8 = (bf16[32,1280]{1,0:T(8,128)(2,1)S(1)}, bf16[32,1280]{1,0:T(8,128)(2,1)S(1)}, u32[]{:S(2)}, u32[]{:S(2)}) collective-permute-start(bf16[32,1280]{1,0:T(8,128)(2,1)S(1)} %get-tuple-element.58), channel_id=1, source_target_pairs={{0,4},{1,5},{2,6},{3,7},{4,0},{5,1},{6,2},{7,3},{8,12},{9,13},{10,... | collective-permute-start | bytes 245768 | tf_op jit(solution)/shard_map/ppermute | solution.py:578
  22.4 8.9 %collective-permute-start.9 = (bf16[32,1280]{1,0:T(8,128)(2,1)S(1)}, bf16[32,1280]{1,0:T(8,128)(2,1)S(1)}, u32[]{:S(2)}, u32[]{:S(2)}) collective-permute-start(bf16[32,1280]{1,0:T(8,128)(2,1)S(1)} %get-tuple-element.59), channel_id=1, source_target_pairs={{0,12},{1,13},{2,14},{3,15},{4,8},{5,9},{6,10},{7,11},{8,4},{9,5},... | collective-permute-start | bytes 245768 | tf_op jit(solution)/shard_map/ppermute | solution.py:578
  23.7 7.9 %collective-permute-start.10 = (bf16[32,1280]{1,0:T(8,128)(2,1)S(1)}, bf16[32,1280]{1,0:T(8,128)(2,1)S(1)}, u32[]{:S(2)}, u32[]{:S(2)}) collective-permute-start(bf16[32,1280]{1,0:T(8,128)(2,1)S(1)} %get-tuple-element.60), channel_id=1, source_target_pairs={{0,3},{1,2},{2,1},{3,0},{4,7},{5,6},{6,5},{7,4},{8,11},{9,10},{10,... | collective-permute-start | bytes 245768 | tf_op jit(solution)/shard_map/ppermute | solution.py:578
  25.7 10.6 %collective-permute-start.11 = (bf16[32,1280]{1,0:T(8,128)(2,1)S(1)}, bf16[32,1280]{1,0:T(8,128)(2,1)S(1)}, u32[]{:S(2)}, u32[]{:S(2)}) collective-permute-start(bf16[32,1280]{1,0:T(8,128)(2,1)S(1)} %get-tuple-element.65), channel_id=1, source_target_pairs={{0,11},{1,10},{2,9},{3,8},{4,15},{5,14},{6,13},{7,12},{8,3},{9,2},... | collective-permute-start | bytes 245768 | tf_op jit(solution)/shard_map/ppermute | solution.py:578
  27.4 8.9 %collective-permute-start.12 = (bf16[32,1280]{1,0:T(8,128)(2,1)S(1)}, bf16[32,1280]{1,0:T(8,128)(2,1)S(1)}, u32[]{:S(2)}, u32[]{:S(2)}) collective-permute-start(bf16[32,1280]{1,0:T(8,128)(2,1)S(1)} %get-tuple-element.66), channel_id=1, source_target_pairs={{0,2},{1,3},{2,0},{3,1},{4,6},{5,7},{6,4},{7,5},{8,10},{9,11},{10,... | collective-permute-start | bytes 245768 | tf_op jit(solution)/shard_map/ppermute | solution.py:578
  28.3 8.0 %collective-permute-start.13 = (bf16[32,1280]{1,0:T(8,128)(2,1)S(1)}, bf16[32,1280]{1,0:T(8,128)(2,1)S(1)}, u32[]{:S(2)}, u32[]{:S(2)}) collective-permute-start(bf16[32,1280]{1,0:T(8,128)(2,1)S(1)} %get-tuple-element.67), channel_id=1, source_target_pairs={{0,13},{1,12},{2,15},{3,14},{4,9},{5,8},{6,11},{7,10},{8,5},{9,4},... | collective-permute-start | bytes 245768 | tf_op jit(solution)/shard_map/ppermute | solution.py:578
  31.3 5.0 %collective-permute-start.14 = (bf16[32,1280]{1,0:T(8,128)(2,1)S(1)}, bf16[32,1280]{1,0:T(8,128)(2,1)S(1)}, u32[]{:S(2)}, u32[]{:S(2)}) collective-permute-start(bf16[32,1280]{1,0:T(8,128)(2,1)S(1)} %get-tuple-element.68), channel_id=1, source_target_pairs={{0,1},{1,0},{2,3},{3,2},{4,5},{5,4},{6,7},{7,6},{8,9},{9,8},{10,11... | collective-permute-start | bytes 245768 | tf_op jit(solution)/shard_map/ppermute | solution.py:578
